TPU v7x, 32 devices: a whole 2x2x4 slice. The times are simulated.
32 devices in a mesh: box: 8 (over z, y), panel: 4 (over x, core).
Axes of the slice: x: 2, y: 2, z: 4, core: 2. Of those that a mesh axis runs over, the one named last changes fastest.
Arguments:
- field_start: float32 [2048, 2048], P('box', 'panel'), may hold values from -6 to 6
- fluid_mask: int32 [2048, 2048], P('box', 'panel'), may hold values 0 or 1
- base_visc: float32 [2048, 2048], P('box', 'panel'), may hold values from 0.02 to 0.1
- panel_cell: int32 [4096], P(('box', 'panel')), may hold values from 0 to 131071
- amplitude: bfloat16 [4096, 4096], P('box', 'panel'), may hold values from 0.049804688 to 0.5
- delay_bin: int32 [4096, 4096], P('box', 'panel'), may hold values from 0 to 2044
Outputs:
- field_end: float32 [2048, 2048], P('box', 'panel')
- signals: float32 [4096, 2048], P('panel', 'box')
Inputs may be any that keep to these rules, and one draw needn't show every extreme that they name: `panel_cell`: an index, row-major, into the 256 x 512 block of the device that owns the panel.
All inputs are finite; a program needn't handle non-finite values. No bound on the sum of `fluid_mask` on one device may be relied on, other than what follows from the above.
Results may differ from a plain program's by a relative error of at most 0.0029.
Values may be sent and summed in bfloat16 or wider, within the bound.
No kernel may reach another device: no remote copies, remote signals or barrier semaphores. Data moves between devices by JAX's collectives and lax.ppermute only.
A program may use at most 64 MiB of HBM per device.

v0:
```python
import math

import jax
import jax.numpy as jnp
from jax import lax
from jax.sharding import PartitionSpec as P

STEPS = 4
NB = 2048


def with_halo(x, sides, width):
    for axis, dim in sides:
        peers, length = (lax.axis_size(axis), x.shape[dim])
        up = [(i, (i + 1) % peers) for i in range(peers - 1)]
        down = [(j, i) for i, j in up]
        last = lax.slice_in_dim(x, length - width, length, axis=dim)
        initial = lax.slice_in_dim(x, 0, width, axis=dim)
        before = lax.ppermute(last, axis, up)
        after = lax.ppermute(initial, axis, down)
        x = jnp.concatenate([before, x, after], axis=dim)
    return x


def advance(ext, mask_c, base_c):
    center = ext[1:-1, 1:-1]
    west = ext[:-2, 1:-1]
    east = ext[2:, 1:-1]
    south = ext[1:-1, :-2]
    north = ext[1:-1, 2:]
    grad_x = 0.5 * (east - west)
    grad_y = 0.5 * (north - south)
    grad_norm = jnp.sqrt(grad_x * grad_x + grad_y * grad_y)
    viscosity = base_c + 0.05 * grad_norm / (1.0 + grad_norm)
    update = center + viscosity * (east + west + north + south - 4.0 * center)
    update = update - 0.15 * (center - west) - 0.1 * (center - south)
    return mask_c * update


def signal_terms(amplitude, delay_bin, sample):
    panels, observers = amplitude.shape
    groups = NB // 128
    width = math.gcd(observers, max(1, 32768 // panels))
    blocks = observers // width
    amp_blocks = amplitude.reshape(panels, blocks, width).transpose(1, 0, 2)
    bin_blocks = delay_bin.reshape(panels, blocks, width).transpose(1, 0, 2)
    high_ids = jnp.arange(groups, dtype=jnp.int32)
    low_ids = jnp.arange(128, dtype=jnp.int32)

    def one_block(pair):
        amp_rows, bin_rows = pair
        weight = (amp_rows.astype(jnp.float32)[None, :, :] * sample[:, :, None]).astype(
            jnp.bfloat16
        )
        high = bin_rows // 128
        low = bin_rows % 128
        chosen = high[:, :, None] == high_ids[None, None, :]
        left = jnp.where(chosen[None], weight[:, :, :, None], jnp.zeros((), jnp.bfloat16))
        right = (low[:, :, None] == low_ids[None, None, :]).astype(jnp.bfloat16)
        binned = jnp.einsum("tpoh,pol->othl", left, right, preferred_element_type=jnp.float32)
        binned = binned.reshape(width, STEPS, NB)
        total = binned[:, 0, :]
        for step in range(1, STEPS):
            total = total + jnp.pad(binned[:, step, : NB - step], ((0, 0), (step, 0)))
        return total

    result = lax.map(one_block, (amp_blocks, bin_blocks))
    return result.reshape(observers, NB)


def on_device(field_start, fluid_mask, base_visc, panel_cell, amplitude, delay_bin):
    maskf = fluid_mask.astype(jnp.float32)
    taken = []
    field = field_start
    for step in range(STEPS):
        extended = with_halo(field, (("box", 0), ("panel", 1)), 1)
        field = advance(extended, maskf, base_visc)
        taken.append(field.reshape(-1)[panel_cell])
    sample = jnp.stack(taken)
    every = lax.all_gather(sample, ("box", "panel"), axis=1, tiled=True)
    amp_all = lax.all_to_all(amplitude, "box", split_axis=1, concat_axis=0, tiled=True)
    bin_all = lax.all_to_all(delay_bin, "box", split_axis=1, concat_axis=0, tiled=True)
    finished = signal_terms(amp_all, bin_all, every)
    signals = lax.all_to_all(finished, "box", split_axis=1, concat_axis=0, tiled=True)
    return (field, signals)


def solution(mesh):
    placed = (
        P("box", "panel"),
        P("box", "panel"),
        P("box", "panel"),
        P(("box", "panel")),
        P("box", "panel"),
        P("box", "panel"),
    )
    return jax.shard_map(
        on_device,
        mesh=mesh,
        in_specs=placed,
        out_specs=(P("box", "panel"), P("panel", "box")),
        check_vma=False,
    )
```

profile of v0, /device:TPU:0, one launch (start us, length us, event | category | flops | bytes accessed | tf_op | source)
XLA Modules:
  0.0 399.4 jit_solution(5120583995772502488)
XLA Ops:
  3.1 7.3 %all-to-all-start.1 = ((bf16[512,8,128]{0,2,1:T(8,128)(2,1)}), bf16[512,8,128]{0,2,1:T(8,128)(2,1)S(1)}, u32[]{:S(2)}, u32[]{:S(2)}) async-start(bf16[512,8,128]{0,2,1:T(8,128)(2,1)} %bitcast.3), calls=%async_computation.1 | async-start | bytes 2097152 | tf_op jit(solution)/shard_map/all_to_all | solution.py:81
  12.2 23.9 %all-to-all-done.1 = bf16[512,8,128]{0,2,1:T(8,128)(2,1)S(1)} async-done(((bf16[512,8,128]{0,2,1:T(8,128)(2,1)}), bf16[512,8,128]{0,2,1:T(8,128)(2,1)S(1)}, u32[]{:S(2)}, u32[]{:S(2)}) %all-to-all-start.1) | async-done | bytes 1048608 | tf_op jit(solution)/shard_map/all_to_all | solution.py:81
  37.1 4.5 %all-to-all-start = ((s32[512,8,128]{0,2,1:T(8,128)}), s32[512,8,128]{0,2,1:T(8,128)}, u32[]{:S(2)}, u32[]{:S(2)}) async-start(s32[512,8,128]{0,2,1:T(8,128)} %bitcast), calls=%async_computation | async-start | bytes 4194304 | tf_op jit(solution)/shard_map/all_to_all | solution.py:82
  43.0 4.5 %collective-permute-start.1 = (f32[1,512]{1,0:T(1,128)S(1)}, f32[1,512]{1,0:T(1,128)S(1)}, u32[]{:S(2)}, u32[]{:S(2)}) collective-permute-start(f32[1,512]{1,0:T(1,128)S(1)} %get-tuple-element.136), channel_id=1, source_target_pairs={{0,4},{4,8},{8,12},{12,16},{16,20},{20,24},{24,28},{1,5},{5,9},{9,... | collective-permute-start | bytes 6152 | tf_op jit(solution)/shard_map/ppermute | solution.py:19
  47.5 3.1 collective-permute-done
  50.6 7.6 %collective-permute-done.1 = f32[1,512]{1,0:T(1,128)S(1)} collective-permute-done((f32[1,512]{1,0:T(1,128)S(1)}, f32[1,512]{1,0:T(1,128)S(1)}, u32[]{:S(2)}, u32[]{:S(2)}) %collective-permute-start.1) | collective-permute-done | bytes 2080 | tf_op jit(solution)/shard_map/ppermute | solution.py:19
  59.6 3.0 collective-permute-start.3
  65.8 21.4 %collective-permute-start.5 = (f32[1,512]{1,0:T(1,128)S(1)}, f32[1,512]{1,0:T(1,128)S(1)}, u32[]{:S(2)}, u32[]{:S(2)}) collective-permute-start(f32[1,512]{1,0:T(1,128)S(1)} %get-tuple-element.134), channel_id=1, source_target_pairs={{0,4},{4,8},{8,12},{12,16},{16,20},{20,24},{24,28},{1,5},{5,9},{9,... | collective-permute-start | bytes 6152 | tf_op jit(solution)/shard_map/ppermute | solution.py:19
  89.9 3.8 collective-permute-start.7
  96.8 5.8 %collective-permute-start.9 = (f32[1,512]{1,0:T(1,128)S(1)}, f32[1,512]{1,0:T(1,128)S(1)}, u32[]{:S(2)}, u32[]{:S(2)}) collective-permute-start(f32[1,512]{1,0:T(1,128)S(1)} %get-tuple-element.132), channel_id=1, source_target_pairs={{0,4},{4,8},{8,12},{12,16},{16,20},{20,24},{24,28},{1,5},{5,9},{9,... | collective-permute-start | bytes 6152 | tf_op jit(solution)/shard_map/ppermute | solution.py:19
  105.3 6.0 %collective-permute-start.11 = (f32[258,1]{1,0:T(8,128)S(1)}, f32[258,1]{1,0:T(8,128)S(1)}, u32[]{:S(2)}, u32[]{:S(2)}) collective-permute-start(f32[258,1]{1,0:T(8,128)S(1)} %get-tuple-element.123), channel_id=1, source_target_pairs={{0,1},{1,2},{2,3},{4,5},{5,6},{6,7},{8,9},{9,10},{10,11},{12,13},{... | collective-permute-start | bytes 3104 | tf_op jit(solution)/shard_map/ppermute | solution.py:19
  114.4 15.0 %collective-permute-start.13 = (f32[1,512]{1,0:T(1,128)S(1)}, f32[1,512]{1,0:T(1,128)S(1)}, u32[]{:S(2)}, u32[]{:S(2)}) collective-permute-start(f32[1,512]{1,0:T(1,128)S(1)} %get-tuple-element.130), channel_id=1, source_target_pairs={{0,4},{4,8},{8,12},{12,16},{16,20},{20,24},{24,28},{1,5},{5,9},{9,... | collective-permute-start | bytes 6152 | tf_op jit(solution)/shard_map/ppermute | solution.py:19
  132.7 6.0 %collective-permute-start.15 = (f32[258,1]{1,0:T(8,128)S(1)}, f32[258,1]{1,0:T(8,128)S(1)}, u32[]{:S(2)}, u32[]{:S(2)}) collective-permute-start(f32[258,1]{1,0:T(8,128)S(1)} %get-tuple-element.121), channel_id=1, source_target_pairs={{0,1},{1,2},{2,3},{4,5},{5,6},{6,7},{8,9},{9,10},{10,11},{12,13},{... | collective-permute-start | bytes 3104 | tf_op jit(solution)/shard_map/ppermute | solution.py:19
  147.7 49.8 %all_gather.3 = f32[4,4096]{1,0:T(4,128)S(1)} all-gather(f32[4,128]{1,0:T(4,128)S(1)} %pad_maximum_fusion.44), channel_id=1, replica_groups=mesh['box'=8,'panel'=4] {'box','panel'}, dimensions={1}, use_global_device_ids=true | all-gather | bytes 67584 | tf_op jit(solution)/shard_map/all_gather | solution.py:80
  203.9 165.0 %while.13 = (s32[]{:T(128)}, f32[16,8,2048]{2,1,0:T(8,128)S(1)}, s32[16,4096,8]{1,2,0:T(8,128)}, bf16[16,4096,8]{1,2,0:T(8,128)(2,1)}, f32[4,4096]{1,0:T(4,128)S(1)}, /*index=5*/s32[]{:T(128)}) while((s32[]{:T(128)}, f32[16,8,2048]{2,1,0:T(8,128)S(1)}, s32[16,4096,8]{1,2,0:T(8,128)}, bf16[16,4096,8]{1,2,0:T(8,128)(2,1)}, ...), condition=%wide.region_1.2_spmd.clone, body=%wide.region_0.1_spmd.clone.sunk | while | flops 544849920 | bytes 4848981 | solution.py:67
  207.1 6.4 %fusion.95 = f32[8,4,16,128]{3,2,1,0:T(8,128)S(1)} fusion(s32[4096,8]{0,1:T(8,128)S(1)} %add_select_fusion.5, pred[4096,8,16]{0,2,1:T(8,128)(4,1)S(1)} %iota_compare_fusion.3, bf16[4,4096,8]{1,0,2:T(4,128)(2,1)S(1)} %multiply_convert_fusion.2), kind=kOutput, calls=%fused_computation.8.clone.1 | convolution fusion | flops 543162368 | bytes 1179648 | tf_op jit(solution)/shard_map/while/body/eval_jaxpr/tpoh,pol->othl/dot_general | solution.py:60
  217.4 6.4 %fusion.95 = f32[8,4,16,128]{3,2,1,0:T(8,128)S(1)} fusion(s32[4096,8]{0,1:T(8,128)S(1)} %add_select_fusion.5, pred[4096,8,16]{0,2,1:T(8,128)(4,1)S(1)} %iota_compare_fusion.3, bf16[4,4096,8]{1,0,2:T(4,128)(2,1)S(1)} %multiply_convert_fusion.2), kind=kOutput, calls=%fused_computation.8.clone.1 | convolution fusion | flops 543162368 | bytes 1179648 | tf_op jit(solution)/shard_map/while/body/eval_jaxpr/tpoh,pol->othl/dot_general | solution.py:60
  227.7 6.4 %fusion.95 = f32[8,4,16,128]{3,2,1,0:T(8,128)S(1)} fusion(s32[4096,8]{0,1:T(8,128)S(1)} %add_select_fusion.5, pred[4096,8,16]{0,2,1:T(8,128)(4,1)S(1)} %iota_compare_fusion.3, bf16[4,4096,8]{1,0,2:T(4,128)(2,1)S(1)} %multiply_convert_fusion.2), kind=kOutput, calls=%fused_computation.8.clone.1 | convolution fusion | flops 543162368 | bytes 1179648 | tf_op jit(solution)/shard_map/while/body/eval_jaxpr/tpoh,pol->othl/dot_general | solution.py:60
  238.0 6.4 %fusion.95 = f32[8,4,16,128]{3,2,1,0:T(8,128)S(1)} fusion(s32[4096,8]{0,1:T(8,128)S(1)} %add_select_fusion.5, pred[4096,8,16]{0,2,1:T(8,128)(4,1)S(1)} %iota_compare_fusion.3, bf16[4,4096,8]{1,0,2:T(4,128)(2,1)S(1)} %multiply_convert_fusion.2), kind=kOutput, calls=%fused_computation.8.clone.1 | convolution fusion | flops 543162368 | bytes 1179648 | tf_op jit(solution)/shard_map/while/body/eval_jaxpr/tpoh,pol->othl/dot_general | solution.py:60
  248.3 6.4 %fusion.95 = f32[8,4,16,128]{3,2,1,0:T(8,128)S(1)} fusion(s32[4096,8]{0,1:T(8,128)S(1)} %add_select_fusion.5, pred[4096,8,16]{0,2,1:T(8,128)(4,1)S(1)} %iota_compare_fusion.3, bf16[4,4096,8]{1,0,2:T(4,128)(2,1)S(1)} %multiply_convert_fusion.2), kind=kOutput, calls=%fused_computation.8.clone.1 | convolution fusion | flops 543162368 | bytes 1179648 | tf_op jit(solution)/shard_map/while/body/eval_jaxpr/tpoh,pol->othl/dot_general | solution.py:60
  258.6 6.4 %fusion.95 = f32[8,4,16,128]{3,2,1,0:T(8,128)S(1)} fusion(s32[4096,8]{0,1:T(8,128)S(1)} %add_select_fusion.5, pred[4096,8,16]{0,2,1:T(8,128)(4,1)S(1)} %iota_compare_fusion.3, bf16[4,4096,8]{1,0,2:T(4,128)(2,1)S(1)} %multiply_convert_fusion.2), kind=kOutput, calls=%fused_computation.8.clone.1 | convolution fusion | flops 543162368 | bytes 1179648 | tf_op jit(solution)/shard_map/while/body/eval_jaxpr/tpoh,pol->othl/dot_general | solution.py:60
  269.0 6.4 %fusion.95 = f32[8,4,16,128]{3,2,1,0:T(8,128)S(1)} fusion(s32[4096,8]{0,1:T(8,128)S(1)} %add_select_fusion.5, pred[4096,8,16]{0,2,1:T(8,128)(4,1)S(1)} %iota_compare_fusion.3, bf16[4,4096,8]{1,0,2:T(4,128)(2,1)S(1)} %multiply_convert_fusion.2), kind=kOutput, calls=%fused_computation.8.clone.1 | convolution fusion | flops 543162368 | bytes 1179648 | tf_op jit(solution)/shard_map/while/body/eval_jaxpr/tpoh,pol->othl/dot_general | solution.py:60
  279.3 6.4 %fusion.95 = f32[8,4,16,128]{3,2,1,0:T(8,128)S(1)} fusion(s32[4096,8]{0,1:T(8,128)S(1)} %add_select_fusion.5, pred[4096,8,16]{0,2,1:T(8,128)(4,1)S(1)} %iota_compare_fusion.3, bf16[4,4096,8]{1,0,2:T(4,128)(2,1)S(1)} %multiply_convert_fusion.2), kind=kOutput, calls=%fused_computation.8.clone.1 | convolution fusion | flops 543162368 | bytes 1179648 | tf_op jit(solution)/shard_map/while/body/eval_jaxpr/tpoh,pol->othl/dot_general | solution.py:60
  289.6 6.4 %fusion.95 = f32[8,4,16,128]{3,2,1,0:T(8,128)S(1)} fusion(s32[4096,8]{0,1:T(8,128)S(1)} %add_select_fusion.5, pred[4096,8,16]{0,2,1:T(8,128)(4,1)S(1)} %iota_compare_fusion.3, bf16[4,4096,8]{1,0,2:T(4,128)(2,1)S(1)} %multiply_convert_fusion.2), kind=kOutput, calls=%fused_computation.8.clone.1 | convolution fusion | flops 543162368 | bytes 1179648 | tf_op jit(solution)/shard_map/while/body/eval_jaxpr/tpoh,pol->othl/dot_general | solution.py:60
  299.9 6.4 %fusion.95 = f32[8,4,16,128]{3,2,1,0:T(8,128)S(1)} fusion(s32[4096,8]{0,1:T(8,128)S(1)} %add_select_fusion.5, pred[4096,8,16]{0,2,1:T(8,128)(4,1)S(1)} %iota_compare_fusion.3, bf16[4,4096,8]{1,0,2:T(4,128)(2,1)S(1)} %multiply_convert_fusion.2), kind=kOutput, calls=%fused_computation.8.clone.1 | convolution fusion | flops 543162368 | bytes 1179648 | tf_op jit(solution)/shard_map/while/body/eval_jaxpr/tpoh,pol->othl/dot_general | solution.py:60
  310.2 6.4 %fusion.95 = f32[8,4,16,128]{3,2,1,0:T(8,128)S(1)} fusion(s32[4096,8]{0,1:T(8,128)S(1)} %add_select_fusion.5, pred[4096,8,16]{0,2,1:T(8,128)(4,1)S(1)} %iota_compare_fusion.3, bf16[4,4096,8]{1,0,2:T(4,128)(2,1)S(1)} %multiply_convert_fusion.2), kind=kOutput, calls=%fused_computation.8.clone.1 | convolution fusion | flops 543162368 | bytes 1179648 | tf_op jit(solution)/shard_map/while/body/eval_jaxpr/tpoh,pol->othl/dot_general | solution.py:60
  320.5 6.4 %fusion.95 = f32[8,4,16,128]{3,2,1,0:T(8,128)S(1)} fusion(s32[4096,8]{0,1:T(8,128)S(1)} %add_select_fusion.5, pred[4096,8,16]{0,2,1:T(8,128)(4,1)S(1)} %iota_compare_fusion.3, bf16[4,4096,8]{1,0,2:T(4,128)(2,1)S(1)} %multiply_convert_fusion.2), kind=kOutput, calls=%fused_computation.8.clone.1 | convolution fusion | flops 543162368 | bytes 1179648 | tf_op jit(solution)/shard_map/while/body/eval_jaxpr/tpoh,pol->othl/dot_general | solution.py:60
  330.8 6.4 %fusion.95 = f32[8,4,16,128]{3,2,1,0:T(8,128)S(1)} fusion(s32[4096,8]{0,1:T(8,128)S(1)} %add_select_fusion.5, pred[4096,8,16]{0,2,1:T(8,128)(4,1)S(1)} %iota_compare_fusion.3, bf16[4,4096,8]{1,0,2:T(4,128)(2,1)S(1)} %multiply_convert_fusion.2), kind=kOutput, calls=%fused_computation.8.clone.1 | convolution fusion | flops 543162368 | bytes 1179648 | tf_op jit(solution)/shard_map/while/body/eval_jaxpr/tpoh,pol->othl/dot_general | solution.py:60
  341.2 6.4 %fusion.95 = f32[8,4,16,128]{3,2,1,0:T(8,128)S(1)} fusion(s32[4096,8]{0,1:T(8,128)S(1)} %add_select_fusion.5, pred[4096,8,16]{0,2,1:T(8,128)(4,1)S(1)} %iota_compare_fusion.3, bf16[4,4096,8]{1,0,2:T(4,128)(2,1)S(1)} %multiply_convert_fusion.2), kind=kOutput, calls=%fused_computation.8.clone.1 | convolution fusion | flops 543162368 | bytes 1179648 | tf_op jit(solution)/shard_map/while/body/eval_jaxpr/tpoh,pol->othl/dot_general | solution.py:60
  351.5 6.4 %fusion.95 = f32[8,4,16,128]{3,2,1,0:T(8,128)S(1)} fusion(s32[4096,8]{0,1:T(8,128)S(1)} %add_select_fusion.5, pred[4096,8,16]{0,2,1:T(8,128)(4,1)S(1)} %iota_compare_fusion.3, bf16[4,4096,8]{1,0,2:T(4,128)(2,1)S(1)} %multiply_convert_fusion.2), kind=kOutput, calls=%fused_computation.8.clone.1 | convolution fusion | flops 543162368 | bytes 1179648 | tf_op jit(solution)/shard_map/while/body/eval_jaxpr/tpoh,pol->othl/dot_general | solution.py:60
  361.8 6.4 %fusion.95 = f32[8,4,16,128]{3,2,1,0:T(8,128)S(1)} fusion(s32[4096,8]{0,1:T(8,128)S(1)} %add_select_fusion.5, pred[4096,8,16]{0,2,1:T(8,128)(4,1)S(1)} %iota_compare_fusion.3, bf16[4,4096,8]{1,0,2:T(4,128)(2,1)S(1)} %multiply_convert_fusion.2), kind=kOutput, calls=%fused_computation.8.clone.1 | convolution fusion | flops 543162368 | bytes 1179648 | tf_op jit(solution)/shard_map/while/body/eval_jaxpr/tpoh,pol->othl/dot_general | solution.py:60
  369.5 28.9 %all_to_all.51 = f32[128,8,256]{2,0,1:T(8,128)S(1)} all-to-all(f32[128,8,256]{2,0,1:T(8,128)S(1)} %copy.37), channel_id=1, replica_groups=mesh['box'=8,'panel'=4] {'box'}, dimensions={1} | all-to-all | bytes 2097152 | tf_op jit(solution)/shard_map/all_to_all | solution.py:84
  (304 shorter events, 102.8 us)
Async XLA Ops:
  0.6 9.7 %copy-start.5 = (s32[512,1024]{1,0:T(8,128)S(1)}, s32[512,1024]{1,0:T(8,128)}, u32[]{:S(2)}) copy-start(s32[512,1024]{1,0:T(8,128)} %param.13) | copy-start | bytes 6291460
  3.1 33.0 %all-to-all-start.1 = ((bf16[512,8,128]{0,2,1:T(8,128)(2,1)}), bf16[512,8,128]{0,2,1:T(8,128)(2,1)S(1)}, u32[]{:S(2)}, u32[]{:S(2)}) async-start(bf16[512,8,128]{0,2,1:T(8,128)(2,1)} %bitcast.3), calls=%async_computation.1 | async-start | bytes 2097152 | tf_op jit(solution)/shard_map/all_to_all | solution.py:81
  36.1 1.0 copy-start.2
  37.1 4.5 %copy-start.4 = (f32[256,512]{1,0:T(8,128)S(1)}, f32[256,512]{1,0:T(8,128)}, u32[]{:S(2)}) copy-start(f32[256,512]{1,0:T(8,128)} %param.8) | copy-start | bytes 1572868
  37.1 26.5 %copy-start = (f32[256,512]{1,0:T(8,128)S(1)}, f32[256,512]{1,0:T(8,128)}, u32[]{:S(2)}) copy-start(f32[256,512]{1,0:T(8,128)} %param.10) | copy-start | bytes 1572868
  37.1 26.5 %copy-start.1 = (s32[256,512]{1,0:T(8,128)S(1)}, s32[256,512]{1,0:T(8,128)}, u32[]{:S(2)}) copy-start(s32[256,512]{1,0:T(8,128)} %param.9) | copy-start | bytes 1572868
  37.1 162.3 %all-to-all-start = ((s32[512,8,128]{0,2,1:T(8,128)}), s32[512,8,128]{0,2,1:T(8,128)}, u32[]{:S(2)}, u32[]{:S(2)}) async-start(s32[512,8,128]{0,2,1:T(8,128)} %bitcast), calls=%async_computation | async-start | bytes 4194304 | tf_op jit(solution)/shard_map/all_to_all | solution.py:82
  41.7 8.9 %collective-permute-start = (f32[1,512]{1,0:T(1,128)S(1)}, f32[1,512]{1,0:T(1,128)S(1)}, u32[]{:S(2)}, u32[]{:S(2)}) collective-permute-start(f32[1,512]{1,0:T(1,128)S(1)} %get-tuple-element.135), channel_id=1, source_target_pairs={{4,0},{8,4},{12,8},{16,12},{20,16},{24,20},{28,24},{5,1},{9,5},{13... | collective-permute-start | bytes 6152 | tf_op jit(solution)/shard_map/ppermute | solution.py:20
  43.0 15.2 %collective-permute-start.1 = (f32[1,512]{1,0:T(1,128)S(1)}, f32[1,512]{1,0:T(1,128)S(1)}, u32[]{:S(2)}, u32[]{:S(2)}) collective-permute-start(f32[1,512]{1,0:T(1,128)S(1)} %get-tuple-element.136), channel_id=1, source_target_pairs={{0,4},{4,8},{8,12},{12,16},{16,20},{20,24},{24,28},{1,5},{5,9},{9,... | collective-permute-start | bytes 6152 | tf_op jit(solution)/shard_map/ppermute | solution.py:19
  58.3 4.3 %collective-permute-start.2 = (f32[258,1]{1,0:T(8,128)S(1)}, f32[258,1]{1,0:T(8,128)S(1)}, u32[]{:S(2)}, u32[]{:S(2)}) collective-permute-start(f32[258,1]{1,0:T(8,128)S(1)} %get-tuple-element.128), channel_id=1, source_target_pairs={{1,0},{2,1},{3,2},{5,4},{6,5},{7,6},{9,8},{10,9},{11,10},{13,12},{... | collective-permute-start | bytes 3104 | tf_op jit(solution)/shard_map/ppermute | solution.py:20
  59.6 4.0 %collective-permute-start.3 = (f32[258,1]{1,0:T(8,128)S(1)}, f32[258,1]{1,0:T(8,128)S(1)}, u32[]{:S(2)}, u32[]{:S(2)}) collective-permute-start(f32[258,1]{1,0:T(8,128)S(1)} %get-tuple-element.127), channel_id=1, source_target_pairs={{0,1},{1,2},{2,3},{4,5},{5,6},{6,7},{8,9},{9,10},{10,11},{12,13},{... | collective-permute-start | bytes 3104 | tf_op jit(solution)/shard_map/ppermute | solution.py:19
  64.5 22.7 %collective-permute-start.4 = (f32[1,512]{1,0:T(1,128)S(1)}, f32[1,512]{1,0:T(1,128)S(1)}, u32[]{:S(2)}, u32[]{:S(2)}) collective-permute-start(f32[1,512]{1,0:T(1,128)S(1)} %get-tuple-element.133), channel_id=1, source_target_pairs={{4,0},{8,4},{12,8},{16,12},{20,16},{24,20},{28,24},{5,1},{9,5},{13... | collective-permute-start | bytes 6152 | tf_op jit(solution)/shard_map/ppermute | solution.py:20
  65.8 22.7 %collective-permute-start.5 = (f32[1,512]{1,0:T(1,128)S(1)}, f32[1,512]{1,0:T(1,128)S(1)}, u32[]{:S(2)}, u32[]{:S(2)}) collective-permute-start(f32[1,512]{1,0:T(1,128)S(1)} %get-tuple-element.134), channel_id=1, source_target_pairs={{0,4},{4,8},{8,12},{12,16},{16,20},{20,24},{24,28},{1,5},{5,9},{9,... | collective-permute-start | bytes 6152 | tf_op jit(solution)/shard_map/ppermute | solution.py:19
  88.6 5.1 %collective-permute-start.6 = (f32[258,1]{1,0:T(8,128)S(1)}, f32[258,1]{1,0:T(8,128)S(1)}, u32[]{:S(2)}, u32[]{:S(2)}) collective-permute-start(f32[258,1]{1,0:T(8,128)S(1)} %get-tuple-element.126), channel_id=1, source_target_pairs={{1,0},{2,1},{3,2},{5,4},{6,5},{7,6},{9,8},{10,9},{11,10},{13,12},{... | collective-permute-start | bytes 3104 | tf_op jit(solution)/shard_map/ppermute | solution.py:20
  89.9 4.8 %collective-permute-start.7 = (f32[258,1]{1,0:T(8,128)S(1)}, f32[258,1]{1,0:T(8,128)S(1)}, u32[]{:S(2)}, u32[]{:S(2)}) collective-permute-start(f32[258,1]{1,0:T(8,128)S(1)} %get-tuple-element.125), channel_id=1, source_target_pairs={{0,1},{1,2},{2,3},{4,5},{5,6},{6,7},{8,9},{9,10},{10,11},{12,13},{... | collective-permute-start | bytes 3104 | tf_op jit(solution)/shard_map/ppermute | solution.py:19
  95.5 34.0 %copy-start.11 = (s32[128]{0:T(128)S(1)}, s32[128]{0:T(128)}, u32[]{:S(2)}) copy-start(s32[128]{0:T(128)} %param.11) | copy-start | bytes 1540
  95.5 7.1 %collective-permute-start.8 = (f32[1,512]{1,0:T(1,128)S(1)}, f32[1,512]{1,0:T(1,128)S(1)}, u32[]{:S(2)}, u32[]{:S(2)}) collective-permute-start(f32[1,512]{1,0:T(1,128)S(1)} %get-tuple-element.131), channel_id=1, source_target_pairs={{4,0},{8,4},{12,8},{16,12},{20,16},{24,20},{28,24},{5,1},{9,5},{13... | collective-permute-start | bytes 6152 | tf_op jit(solution)/shard_map/ppermute | solution.py:20
  96.8 7.1 %collective-permute-start.9 = (f32[1,512]{1,0:T(1,128)S(1)}, f32[1,512]{1,0:T(1,128)S(1)}, u32[]{:S(2)}, u32[]{:S(2)}) collective-permute-start(f32[1,512]{1,0:T(1,128)S(1)} %get-tuple-element.132), channel_id=1, source_target_pairs={{0,4},{4,8},{8,12},{12,16},{16,20},{20,24},{24,28},{1,5},{5,9},{9,... | collective-permute-start | bytes 6152 | tf_op jit(solution)/shard_map/ppermute | solution.py:19
  104.0 7.3 %collective-permute-start.10 = (f32[258,1]{1,0:T(8,128)S(1)}, f32[258,1]{1,0:T(8,128)S(1)}, u32[]{:S(2)}, u32[]{:S(2)}) collective-permute-start(f32[258,1]{1,0:T(8,128)S(1)} %get-tuple-element.124), channel_id=1, source_target_pairs={{1,0},{2,1},{3,2},{5,4},{6,5},{7,6},{9,8},{10,9},{11,10},{13,12},{... | collective-permute-start | bytes 3104 | tf_op jit(solution)/shard_map/ppermute | solution.py:20
  105.3 7.0 %collective-permute-start.11 = (f32[258,1]{1,0:T(8,128)S(1)}, f32[258,1]{1,0:T(8,128)S(1)}, u32[]{:S(2)}, u32[]{:S(2)}) collective-permute-start(f32[258,1]{1,0:T(8,128)S(1)} %get-tuple-element.123), channel_id=1, source_target_pairs={{0,1},{1,2},{2,3},{4,5},{5,6},{6,7},{8,9},{9,10},{10,11},{12,13},{... | collective-permute-start | bytes 3104 | tf_op jit(solution)/shard_map/ppermute | solution.py:19
  113.1 16.3 %collective-permute-start.12 = (f32[1,512]{1,0:T(1,128)S(1)}, f32[1,512]{1,0:T(1,128)S(1)}, u32[]{:S(2)}, u32[]{:S(2)}) collective-permute-start(f32[1,512]{1,0:T(1,128)S(1)} %get-tuple-element.129), channel_id=1, source_target_pairs={{4,0},{8,4},{12,8},{16,12},{20,16},{24,20},{28,24},{5,1},{9,5},{13... | collective-permute-start | bytes 6152 | tf_op jit(solution)/shard_map/ppermute | solution.py:20
  114.4 16.3 %collective-permute-start.13 = (f32[1,512]{1,0:T(1,128)S(1)}, f32[1,512]{1,0:T(1,128)S(1)}, u32[]{:S(2)}, u32[]{:S(2)}) collective-permute-start(f32[1,512]{1,0:T(1,128)S(1)} %get-tuple-element.130), channel_id=1, source_target_pairs={{0,4},{4,8},{8,12},{12,16},{16,20},{20,24},{24,28},{1,5},{5,9},{9,... | collective-permute-start | bytes 6152 | tf_op jit(solution)/shard_map/ppermute | solution.py:19
  129.5 9.3 %copy-start.8 = (f32[1,512]{1,0:T(1,128)}, f32[1,512]{1,0:T(1,128)S(1)}, u32[]{:S(2)}) copy-start(f32[1,512]{1,0:T(1,128)S(1)} %collective-permute-done.12) | copy-start | bytes 6148
  130.7 8.0 %copy-start.9 = (f32[1,512]{1,0:T(1,128)}, f32[1,512]{1,0:T(1,128)S(1)}, u32[]{:S(2)}) copy-start(f32[1,512]{1,0:T(1,128)S(1)} %collective-permute-done.13) | copy-start | bytes 6148
  131.4 12.8 %collective-permute-start.14 = (f32[258,1]{1,0:T(8,128)}, f32[258,1]{1,0:T(8,128)S(1)}, u32[]{:S(2)}, u32[]{:S(2)}) collective-permute-start(f32[258,1]{1,0:T(8,128)} %get-tuple-element.122), channel_id=1, source_target_pairs={{1,0},{2,1},{3,2},{5,4},{6,5},{7,6},{9,8},{10,9},{11,10},{13,12},{... | collective-permute-start | bytes 3104 | tf_op jit(solution)/shard_map/ppermute | solution.py:20
  132.7 11.5 %collective-permute-start.15 = (f32[258,1]{1,0:T(8,128)S(1)}, f32[258,1]{1,0:T(8,128)S(1)}, u32[]{:S(2)}, u32[]{:S(2)}) collective-permute-start(f32[258,1]{1,0:T(8,128)S(1)} %get-tuple-element.121), channel_id=1, source_target_pairs={{0,1},{1,2},{2,3},{4,5},{5,6},{6,7},{8,9},{9,10},{10,11},{12,13},{... | collective-permute-start | bytes 3104 | tf_op jit(solution)/shard_map/ppermute | solution.py:19
  144.2 53.3 %copy-start.3 = (bf16[512,8,128]{0,2,1:T(8,128)(2,1)S(1)}, bf16[512,8,128]{0,2,1:T(8,128)(2,1)}, u32[]{:S(2)}) copy-start(bf16[512,8,128]{0,2,1:T(8,128)(2,1)} %copy-done.2) | copy-start | bytes 3145732
  144.3 2.8 copy-start.10
  145.8 53.7 %copy-start.6 = (f32[256,512]{1,0:T(8,128)}, f32[256,512]{1,0:T(8,128)S(1)}, u32[]{:S(2)}) copy-start(f32[256,512]{1,0:T(8,128)S(1)} %fusion.27) | copy-start | bytes 1572868
  202.3 1.6 copy-start.7
where the time goes:
time: 401 us; the launch traced here: 399 us
  matrix products  103 us (26%)
  starting transfers between devices  87.7 us (22%)
  blocking collectives  78.7 us (20%)
  other arithmetic  58.9 us (15%)
  waiting for transfers between devices  41.3 us (10%)
  local copies, waits for them, and re-layouts  26.8 us (7%)
    dot_general x16, matrix products, one_block(): jnp.einsum('tpoh,pol->othl', left, right, preferred_element_type=jnp.floa...  103 us
    ppermute x8, starting transfers between devices, with_halo(): before = lax.ppermute(last, axis, up)  65.6 us
    all_gather x1, blocking collectives, on_device(): every = lax.all_gather(sample, ('box', 'panel'), axis=1, tiled=True)  49.8 us
    all_to_all x1, blocking collectives, on_device(): lax.all_to_all(finished, 'box', split_axis=1, concat_axis=0, tiled=True)  28.9 us
    all_to_all x1, waiting for transfers between devices, on_device(): lax.all_to_all(amplitude, 'box', split_axis=1, concat_axis=0, tiled=True)  23.9 us
    select_n x16, other arithmetic, one_block(): high = bin_rows // 128  15.9 us
    select_n x16, other arithmetic, one_block(): low = bin_rows % 128  15.5 us
    ppermute x8, waiting for transfers between devices, with_halo(): before = lax.ppermute(last, axis, up)  14.3 us
  transfers between devices with their start and end apart: 18, of which 9 were waited for; matrix products, arithmetic and copies ran while one was open for 4% of the time, Pallas kernels for 0%

commit v1 on v0

v1 whole, which is shorter than its diff:
```python
import functools

import jax
import jax.numpy as jnp
from jax import lax
from jax.experimental import pallas as pl
from jax.experimental.pallas import tpu as pltpu
from jax.sharding import PartitionSpec as P

F32 = jnp.float32
BF16 = jnp.bfloat16
STEPS = 4
NB = 2048
LOW = 32
LANES = 128
EDGE = 2 * STEPS
PAD = 16
AMP_SCALE = 4096.0
CHUNKS = 2
UNROLL = 4
VMEM = pl.BlockSpec(memory_space=pltpu.VMEM)
SMEM = pl.BlockSpec(memory_space=pltpu.SMEM)


def params(mib):
    return pltpu.CompilerParams(vmem_limit_bytes=mib << 20)


def cost(flops, size):
    return pl.CostEstimate(flops=flops, bytes_accessed=size, transcendentals=0)


def pack_kernel(amp_ref, bin_ref, *outs):
    scaled = (amp_ref[...].astype(F32) * AMP_SCALE).astype(jnp.int32)
    word = jnp.transpose((scaled << 16) | bin_ref[...])
    peers, width, rows = outs[0].shape
    for dest in range(peers):
        for c, out in enumerate(outs):
            first = (dest * len(outs) + c) * width
            out[dest] = word[first : first + width]


def pack(amplitude, delay_bin, peers, chunks):
    panels, observers = amplitude.shape
    width = observers // peers // chunks
    block = pl.BlockSpec((LANES, observers), lambda i: (i, 0))
    out = jax.ShapeDtypeStruct((peers, width, panels), jnp.int32)
    return pl.pallas_call(
        pack_kernel,
        grid=(panels // LANES,),
        in_specs=[block, block],
        out_specs=[pl.BlockSpec((peers, width, LANES), lambda i: (0, 0, i))] * chunks,
        out_shape=[out] * chunks,
        compiler_params=params(32),
        cost_estimate=cost(panels * observers, 10 * panels * observers),
    )(amplitude, delay_bin)


def rows_kernel(field_ref, mask_ref, visc_ref, coded_ref, first_ref, last_ref):
    length = field_ref.shape[0]
    coded = jnp.where(mask_ref[...] != 0, visc_ref[...], 0.0)
    coded_ref[...] = coded
    first_ref[:STEPS] = field_ref[:STEPS]
    first_ref[STEPS:] = coded[:STEPS]
    last_ref[:STEPS] = field_ref[length - STEPS :]
    last_ref[STEPS:] = coded[length - STEPS :]


def columns_kernel(field_ref, coded_ref, before_ref, after_ref, first_ref, last_ref, tall):
    rows, cols = field_ref.shape
    tall[...] = jnp.zeros_like(tall)
    for part, ref in enumerate((field_ref, coded_ref)):
        halo = slice(part * STEPS, (part + 1) * STEPS)
        for start, low, out in ((0, 0, first_ref), (cols - LANES, LANES - STEPS, last_ref)):
            lanes = slice(start, start + LANES)
            tall[:rows] = ref[:, lanes]
            tall[rows : rows + STEPS] = after_ref[halo, lanes]
            tall[rows + STEPS : rows + EDGE] = before_ref[halo, lanes]
            out[halo] = jnp.transpose(tall[...])[low : low + STEPS]


def step_kernel(
    cell_smem,
    cell_ref,
    field_ref,
    coded_ref,
    before_ref,
    after_ref,
    south_ref,
    north_ref,
    end_ref,
    sample_ref,
    fields,
    visc,
    wide,
    picked,
):
    rows, cols = field_ref.shape
    panels = cell_ref.shape[1]
    height, width = visc.shape
    wide[...] = jnp.zeros_like(wide)
    blank = jnp.zeros((PAD, width), F32)
    for part, (ref, buf) in enumerate(((field_ref, fields.at[0]), (coded_ref, visc))):
        halo = slice(part * STEPS, (part + 1) * STEPS)
        wide[:STEPS] = north_ref[halo]
        wide[LANES - STEPS :] = south_ref[halo]
        side = jnp.transpose(wide[...])
        buf[:PAD] = blank
        buf[PAD + rows :] = blank
        buf[PAD : PAD + rows, :cols] = ref[...]
        buf[PAD + rows : PAD + rows + STEPS, :cols] = after_ref[halo]
        buf[PAD - STEPS : PAD, :cols] = before_ref[halo]
        buf[PAD : PAD + rows, cols:] = side[:rows]
        buf[PAD + rows : PAD + rows + STEPS, cols:] = side[rows : rows + STEPS]
        buf[PAD - STEPS : PAD, cols:] = side[rows + STEPS : rows + EDGE]

    strip = 16
    for step in range(STEPS):
        old, new = fields.at[step], fields.at[step + 1]
        new[:8] = jnp.zeros((8, width), F32)
        new[height - 8 :] = jnp.zeros((8, width), F32)

        def one_strip(i, carry):
            top = pl.multiple_of(i * strip, 8)
            window = old[pl.ds(top, strip + 16), :]
            base = visc[pl.ds(top + 8, strip), :]
            center = window[8 : 8 + strip]
            west = window[7 : 7 + strip]
            east = window[9 : 9 + strip]
            south = pltpu.roll(center, 1, 1)
            north = pltpu.roll(center, width - 1, 1)
            grad_x = 0.5 * (east - west)
            grad_y = 0.5 * (north - south)
            grad_norm = jnp.sqrt(grad_x * grad_x + grad_y * grad_y)
            viscosity = base + 0.05 * grad_norm / (1.0 + grad_norm)
            update = center + viscosity * (east + west + north + south - 4.0 * center)
            update = update - 0.15 * (center - west) - 0.1 * (center - south)
            new[pl.ds(top + 8, strip), :] = jnp.where(base > 0.0, update, 0.0)
            return carry

        lax.fori_loop(0, (height - 16) // strip, one_strip, 0)
    end_ref[...] = fields[STEPS, PAD : PAD + rows, :cols]

    def one_panel(k, carry):
        cell = cell_smem[0, k]
        row = cell // cols + PAD
        for step in range(STEPS):
            picked[step, pl.ds(k, 1), :] = fields[step + 1, pl.ds(row, 1), :cols]
        return carry

    lax.fori_loop(0, panels, one_panel, 0, unroll=4)
    column = lax.rem(cell_ref[...], cols)
    chosen = lax.broadcasted_iota(jnp.int32, (cols, panels), 0) == column
    for step in range(STEPS):
        turned = jnp.transpose(picked[step])
        value = jnp.sum(jnp.where(chosen, turned, 0.0), axis=0, keepdims=True)
        sample_ref[:, step, :] = jnp.broadcast_to(value, (sample_ref.shape[0], panels))


def field_window(field, mask, visc, panel_cell):
    rows, cols = field.shape
    tall = -(-(rows + EDGE) // LANES) * LANES
    edge_rows = jax.ShapeDtypeStruct((EDGE, cols), F32)
    edge_cols = jax.ShapeDtypeStruct((EDGE, tall), F32)

    def shifted(axis, first, last):
        peers = lax.axis_size(axis)
        up = [(i, i + 1) for i in range(peers - 1)]
        down = [(i + 1, i) for i in range(peers - 1)]
        return lax.ppermute(last, axis, up), lax.ppermute(first, axis, down)

    coded, first, last = pl.pallas_call(
        rows_kernel,
        in_specs=[VMEM] * 3,
        out_specs=[VMEM] * 3,
        out_shape=[jax.ShapeDtypeStruct((rows, cols), F32), edge_rows, edge_rows],
        compiler_params=params(16),
        cost_estimate=cost(rows * cols, 16 * rows * cols),
    )(field, mask, visc)
    before, after = shifted("box", first, last)
    first, last = pl.pallas_call(
        columns_kernel,
        in_specs=[VMEM] * 4,
        out_specs=[VMEM] * 2,
        out_shape=[edge_cols, edge_cols],
        scratch_shapes=[pltpu.VMEM((tall, LANES), F32)],
        compiler_params=params(16),
        cost_estimate=cost(rows * cols, 4 * rows * cols),
    )(field, coded, before, after)
    south, north = shifted("panel", first, last)
    devices = lax.axis_size("box") * lax.axis_size("panel")
    panels = panel_cell.shape[0]
    cells = panel_cell.reshape(1, panels)
    height, width = rows + 2 * PAD, cols + LANES
    return pl.pallas_call(
        step_kernel,
        in_specs=[SMEM] + [VMEM] * 7,
        out_specs=[VMEM] * 2,
        out_shape=[
            jax.ShapeDtypeStruct((rows, cols), F32),
            jax.ShapeDtypeStruct((devices, STEPS, panels), F32),
        ],
        scratch_shapes=[
            pltpu.VMEM((STEPS + 1, height, width), F32),
            pltpu.VMEM((height, width), F32),
            pltpu.VMEM((LANES, tall), F32),
            pltpu.VMEM((STEPS, panels, cols), F32),
        ],
        compiler_params=params(24),
        cost_estimate=cost(100 * rows * cols, 80 * rows * cols),
    )(cells, cells, field, coded, before, after, south, north)


def bin_kernel(word_ref, sample_ref, out_ref, low_s, high_s, weight_s, acc_s, sig_s):
    sources, block, local = word_ref.shape
    parts = local // LANES
    high = NB // LOW
    span = LOW + 16
    depth = 2 * LANES
    shift = LOW.bit_length() - 1
    for s in range(sources):
        for j in range(parts):
            word = word_ref[s, :, j * LANES : (j + 1) * LANES]
            at = slice((s * parts + j) * LANES, (s * parts + j + 1) * LANES)
            low_s[:, at] = (word & (LOW - 1)).astype(F32)
            high_s[:, at] = ((word >> shift) & (high - 1)).astype(F32)
            amp = (word >> 16).astype(F32) * (1.0 / AMP_SCALE)
            for t in range(STEPS):
                weight_s[t, :, at] = amp * sample_ref[s * parts + j, t : t + 1, :]

    one = jnp.ones((), BF16)
    zero = jnp.zeros((), BF16)
    high_ids = lax.broadcasted_iota(jnp.int32, (high, depth), 0).astype(F32).astype(BF16)
    low_ids = [
        (lax.broadcasted_iota(jnp.int32, (span, depth), 0) - t).astype(F32).astype(BF16)
        for t in range(STEPS)
    ]
    lane = lax.broadcasted_iota(jnp.int32, (NB // LANES, LANES), 1)
    acc_s[...] = jnp.zeros_like(acc_s)

    def spread(row):
        return jnp.broadcast_to(row, (16, depth)).astype(BF16)

    def one_observer(o, u):
        acc = None
        for c in range(sources * local // depth):
            at = slice(c * depth, (c + 1) * depth)
            low_row = spread(low_s[pl.ds(o, 1), at])
            high_row = spread(high_s[pl.ds(o, 1), at])
            weights = [spread(weight_s[t, pl.ds(o, 1), at]) for t in range(STEPS)]
            left = jnp.concatenate(
                [jnp.where(high_ids[k : k + 16] == high_row, one, zero) for k in range(0, high, 16)]
            )
            right = []
            for k in range(0, span, 16):
                placed = zero
                for t in range(1 if k >= LOW else 0, STEPS):
                    placed = jnp.where(low_ids[t][k : k + 16] == low_row, weights[t], placed)
                right.append(placed)
            term = lax.dot_general(
                left, jnp.concatenate(right), (((1,), (1,)), ((), ())), preferred_element_type=F32
            )
            acc = term if acc is None else acc + term
        acc_s[u, :, :span] = acc
        per_row = LANES // LOW
        total = None
        for j in range(per_row):
            x = acc_s[u, pl.ds(j, NB // LANES, stride=per_row), :]
            if j:
                x = pltpu.roll(x, LOW * j, 1)
            if j == per_row - 1:
                x = jnp.where(lane < 16, pltpu.roll(x, 1, 0), x)
            total = x if total is None else total + x
        sig_s[:, pl.ds(o, 1), :] = total[:, None, :]

    unroll = acc_s.shape[0]

    def some_observers(i, carry):
        for u in range(unroll):
            one_observer(i * unroll + u, u)
        return carry

    lax.fori_loop(0, block // unroll, some_observers, 0)
    owners, _, bins = out_ref.shape
    for d in range(owners):
        for r in range(bins // LANES):
            out_ref[d, :, r * LANES : (r + 1) * LANES] = sig_s[d * (bins // LANES) + r].astype(BF16)


def binned(words, samples, owners):
    sources, observers, local = words.shape
    block = 16
    panels = sources * local
    return pl.pallas_call(
        bin_kernel,
        grid=(observers // block,),
        in_specs=[
            pl.BlockSpec((sources, block, local), lambda i: (0, i, 0)),
            pl.BlockSpec(samples.shape, lambda i: (0, 0, 0)),
        ],
        out_specs=pl.BlockSpec((owners, block, NB // owners), lambda i: (0, i, 0)),
        out_shape=jax.ShapeDtypeStruct((owners, observers, NB // owners), BF16),
        scratch_shapes=[
            pltpu.VMEM((block, panels), F32),
            pltpu.VMEM((block, panels), F32),
            pltpu.VMEM((STEPS, block, panels), F32),
            pltpu.VMEM((UNROLL, NB // LOW, LANES), F32),
            pltpu.VMEM((NB // LANES, block, LANES), F32),
        ],
        compiler_params=params(40),
        cost_estimate=cost(65536 * observers * panels, 8 * observers * panels),
    )(words, samples)


def on_device(field_start, fluid_mask, base_visc, panel_cell, amplitude, delay_bin):
    peers = lax.axis_size("box")
    swap = functools.partial(
        lax.all_to_all, axis_name="box", split_axis=0, concat_axis=0, tiled=True
    )
    packed = pack(amplitude, delay_bin, peers, CHUNKS)
    packed, field_start = lax.optimization_barrier((packed, field_start))
    words = [swap(w) for w in packed]
    field, sample = field_window(field_start, fluid_mask, base_visc, panel_cell)
    words[0], sample = lax.optimization_barrier((words[0], sample))
    samples = lax.all_to_all(sample, ("box", "panel"), split_axis=0, concat_axis=0, tiled=True)
    finished = [swap(binned(w, samples, peers)) for w in words]
    signals = jnp.concatenate(finished, axis=1).astype(F32)
    return (field, signals.reshape(-1, signals.shape[-1]))


def solution(mesh):
    placed = (
        P("box", "panel"),
        P("box", "panel"),
        P("box", "panel"),
        P(("box", "panel")),
        P("box", "panel"),
        P("box", "panel"),
    )
    return jax.shard_map(
        on_device,
        mesh=mesh,
        in_specs=placed,
        out_specs=(P("box", "panel"), P("panel", "box")),
        check_vma=False,
    )
```

time: 401 us -> 134 us (0.33)
  matrix products: 103 us -> 0 us
  starting transfers between devices: 87.7 us -> 22.4 us
  other arithmetic: 58.9 us -> 1.11 us
  Pallas kernels: 0 us -> 46 us
  blocking collectives: 78.7 us -> 41.8 us
  local copies, waits for them, and re-layouts: 26.8 us -> 2.88 us
  waiting for transfers between devices: 41.3 us -> 18.6 us
    dot_general x16 -> x0, matrix products: 103 us -> none  [one_block(): jnp.einsum('tpoh,pol->othl', left, right, preferred_element_type=jnp.floa...]
    ppermute x16 -> x4, starting transfers between devices: 75.9 us -> 7.79 us  [shifted(): return (lax.ppermute(last, axis, up), lax.ppermute(first, axis, down))]
    all_gather x1 -> x0, blocking collectives: 49.8 us -> none  [on_device(): every = lax.all_gather(sample, ('box', 'panel'), axis=1, tiled=True)]
    pallas_call x0 -> x6, Pallas kernels: none -> 46 us  [the longest x2 30.5 us: binned(): pl.pallas_call(bin_kernel, grid=(observers // block,), in_specs=[pl.Block...]
    select_n x33 -> x0, other arithmetic: 31.4 us -> none  [the longest x16 15.9 us: one_block(): high = bin_rows // 128]
    mul x20 -> x0, other arithmetic: 17.7 us -> none  [the longest x16 13.7 us: one_block(): amp_rows.astype(jnp.float32)[None, :, :] * sample[:, :, None]]
    all_to_all x2 -> x3, waiting for transfers between devices: 23.9 us -> 10.7 us  [the longest x2 10.7 us: on_device(): words = [swap(w) for w in packed]]
    all_to_all x1 -> x2, blocking collectives: 28.9 us -> 41.8 us  [the longest x1 27.5 us: on_device(): lax.all_to_all(sample, ('box', 'panel'), split_axis=0, concat_axis=0, til...]
  transfers between devices with their start and end apart: 18 -> 7, of which waited for: 9 -> 4; matrix products, arithmetic and copies ran while one was open for 4% -> 0% of each run, Pallas kernels for 0% -> 33%
where the time goes in v1:
time: 134 us
  Pallas kernels  46 us (34%)
  blocking collectives  41.8 us (31%)
  starting transfers between devices  22.4 us (17%)
  waiting for transfers between devices  18.6 us (14%)
  local copies, waits for them, and re-layouts  2.88 us (2%)
    pallas_call x2, Pallas kernels, binned(): pl.pallas_call(bin_kernel, grid=(observers // block,), in_specs=[pl.Block...  30.5 us
    all_to_all x1, blocking collectives, on_device(): lax.all_to_all(sample, ('box', 'panel'), split_axis=0, concat_axis=0, til...  27.5 us
    all_to_all x1, blocking collectives, on_device(): finished = [swap(binned(w, samples, peers)) for w in words]  14.3 us
    pallas_call x1, Pallas kernels, field_window(): pl.pallas_call(step_kernel, in_specs=[SMEM] + [VMEM] * 7, out_specs=[VMEM...  13 us
    all_to_all x2, starting transfers between devices, on_device(): words = [swap(w) for w in packed]  11 us
    all_to_all x2, waiting for transfers between devices, on_device(): words = [swap(w) for w in packed]  10.7 us
    ppermute x4, waiting for transfers between devices, shifted(): return (lax.ppermute(last, axis, up), lax.ppermute(first, axis, down))  7.91 us
    ppermute x4, starting transfers between devices, shifted(): return (lax.ppermute(last, axis, up), lax.ppermute(first, axis, down))  7.79 us
  transfers between devices with their start and end apart: 7, of which 4 were waited for; matrix products, arithmetic and copies ran while one was open for 0% of the time, Pallas kernels for 33%

profile of v1, /device:TPU:0, one launch (start us, length us, event | category | flops | bytes accessed | tf_op | source)
XLA Modules:
  0.0 133.5 jit_solution(5057995802246557565)
XLA Ops:
  0.6 0.0 copy-start
  0.6 0.0 copy-start.1
  0.7 1.6 %copy-done.1 = s32[512,1024]{1,0:T(8,128)S(1)} copy-done((s32[512,1024]{1,0:T(8,128)S(1)}, s32[512,1024]{1,0:T(8,128)}, u32[]{:S(2)}) %copy-start.1) | copy-done | bytes 2097176
  2.3 1.2 copy-done.2
  3.5 0.0 copy-start.3
  3.5 2.2 %shard_map.77 = (s32[8,64,512]{2,1,0:T(8,128)}, s32[8,64,512]{2,1,0:T(8,128)}) custom-call(bf16[512,1024]{1,0:T(8,128)(2,1)S(1)} %copy-done.2, s32[512,1024]{1,0:T(8,128)S(1)} %copy-done.1), custom_call_target="tpu_custom_call" | custom-call | flops 524288 | bytes 5242880 | tf_op jit(solution)/shard_map/pallas_call | solution.py:48
  5.8 7.4 %all-to-all-start = ((s32[8,64,512]{2,1,0:T(8,128)}), s32[8,64,512]{2,1,0:T(8,128)S(1)}, u32[]{:S(2)}, u32[]{:S(2)}) async-start(s32[8,64,512]{2,1,0:T(8,128)} %get-tuple-element.25), calls=%async_computation | async-start | bytes 2097152 | tf_op jit(solution)/shard_map/all_to_all | solution.py:322
  13.2 0.0 copy-done
  13.2 0.0 copy-done.3
  13.2 0.0 copy-done.4
  13.2 0.1 shard_map.78
  13.3 3.9 %collective-permute-start = (f32[8,512]{1,0:T(8,128)S(1)}, f32[8,512]{1,0:T(8,128)S(1)}, u32[]{:S(2)}, u32[]{:S(2)}) collective-permute-start(f32[8,512]{1,0:T(8,128)S(1)} %get-tuple-element.20), channel_id=1, source_target_pairs={{0,4},{4,8},{8,12},{12,16},{16,20},{20,24},{24,28},{1,5},{5,9},{9,... | collective-permute-start | bytes 49160 | tf_op jit(solution)/shard_map/ppermute | solution.py:170
  17.2 1.3 collective-permute-start.1
  18.5 2.2 %collective-permute-done.before_ref = f32[8,512]{1,0:T(8,128)S(1)} collective-permute-done((f32[8,512]{1,0:T(8,128)S(1)}, f32[8,512]{1,0:T(8,128)S(1)}, u32[]{:S(2)}, u32[]{:S(2)}) %collective-permute-start) | collective-permute-done | bytes 16416 | tf_op jit(solution)/shard_map/ppermute | solution.py:170
  20.7 2.2 %collective-permute-done.1.after_ref = f32[8,512]{1,0:T(8,128)S(1)} collective-permute-done((f32[8,512]{1,0:T(8,128)S(1)}, f32[8,512]{1,0:T(8,128)S(1)}, u32[]{:S(2)}, u32[]{:S(2)}) %collective-permute-start.1) | collective-permute-done | bytes 16416 | tf_op jit(solution)/shard_map/ppermute | solution.py:170
  22.9 0.3 shard_map.79
  23.2 1.3 collective-permute-start.2
  24.5 1.3 collective-permute-start.3
  25.8 0.0 collective-permute-done.2.south_ref
  25.8 3.5 %collective-permute-done.3.north_ref = f32[8,384]{1,0:T(8,128)S(1)} collective-permute-done((f32[8,384]{1,0:T(8,128)S(1)}, f32[8,384]{1,0:T(8,128)S(1)}, u32[]{:S(2)}, u32[]{:S(2)}) %collective-permute-start.3) | collective-permute-done | bytes 12320 | tf_op jit(solution)/shard_map/ppermute | solution.py:170
  29.3 0.0 copy-done.5
  29.3 13.0 %shard_map.80 = (f32[256,512]{1,0:T(8,128)}, f32[32,4,128]{2,1,0:T(4,128)S(1)}) custom-call(s32[1,128]{1,0:T(1,128)S(1)} %bitcast.4, s32[1,128]{1,0:T(1,128)S(1)} %bitcast.5, f32[256,512]{1,0:T(8,128)S(1)} %copy-done, f32[256,512]{1,0:T(8,128)S(1)} %get-tuple-element.19.coded_ref, f32[8,512]{1,0:T(8,128)S(1)} %collective-permute-done.before_ref, ...), custom_call_target="tpu_custom_call" | custom-call | flops 13107200 | bytes 10485760 | tf_op jit(solution)/shard_map/pallas_call | solution.py:195
  42.3 0.0 all-to-all-done.word_ref
  42.3 27.5 %all_to_all.25.sample_ref = f32[32,4,128]{2,1,0:T(4,128)S(1)} all-to-all(f32[32,4,128]{2,1,0:T(4,128)S(1)} %get-tuple-element.28), channel_id=1, replica_groups=mesh['box'=8,'panel'=4] {'box','panel'}, dimensions={0} | all-to-all | bytes 131072 | tf_op jit(solution)/shard_map/all_to_all | solution.py:325
  69.7 3.6 %all-to-all-start.3 = ((s32[8,64,512]{2,1,0:T(8,128)}), s32[8,64,512]{2,1,0:T(8,128)S(1)}, u32[]{:S(2)}, u32[]{:S(2)}) async-start(s32[8,64,512]{2,1,0:T(8,128)} %get-tuple-element.29), calls=%async_computation.3 | async-start | bytes 2097152 | tf_op jit(solution)/shard_map/all_to_all | solution.py:322
  73.3 15.5 %shard_map.81 = bf16[8,64,256]{2,1,0:T(8,128)(2,1)} custom-call(s32[8,64,512]{2,1,0:T(8,128)S(1)} %all-to-all-done.word_ref, f32[32,4,128]{2,1,0:T(4,128)S(1)} %all_to_all.25.sample_ref), custom_call_target="tpu_custom_call" | custom-call | flops 17179869184 | bytes 2097152 | tf_op jit(solution)/shard_map/pallas_call | solution.py:294
  88.8 10.7 %all-to-all-done.3.word_ref = s32[8,64,512]{2,1,0:T(8,128)S(1)} async-done(((s32[8,64,512]{2,1,0:T(8,128)}), s32[8,64,512]{2,1,0:T(8,128)S(1)}, u32[]{:S(2)}, u32[]{:S(2)}) %all-to-all-start.3) | async-done | bytes 1048608 | tf_op jit(solution)/shard_map/all_to_all | solution.py:322
  99.5 3.6 %all-to-all-start.2 = ((bf16[8,64,256]{2,1,0:T(8,128)(2,1)}), bf16[8,64,256]{2,1,0:T(8,128)(2,1)S(1)}, u32[]{:S(2)}, u32[]{:S(2)}) async-start(bf16[8,64,256]{2,1,0:T(8,128)(2,1)} %shard_map.81), calls=%async_computation.2 | async-start | bytes 524288 | tf_op jit(solution)/shard_map/all_to_all | solution.py:326
  103.1 14.9 %shard_map.82 = bf16[8,64,256]{2,1,0:T(8,128)(2,1)S(1)} custom-call(s32[8,64,512]{2,1,0:T(8,128)S(1)} %all-to-all-done.3.word_ref, f32[32,4,128]{2,1,0:T(4,128)S(1)} %all_to_all.25.sample_ref), custom_call_target="tpu_custom_call" | custom-call | flops 17179869184 | bytes 2097152 | tf_op jit(solution)/shard_map/pallas_call | solution.py:294
  118.1 0.0 all-to-all-done.2
  118.1 14.3 %all_to_all.26 = bf16[8,64,256]{2,1,0:T(8,128)(2,1)S(1)} all-to-all(bf16[8,64,256]{2,1,0:T(8,128)(2,1)S(1)} %shard_map.82), channel_id=1, replica_groups=mesh['box'=8,'panel'=4] {'box'}, dimensions={0} | all-to-all | bytes 524288 | tf_op jit(solution)/shard_map/all_to_all | solution.py:326
  132.5 1.1 bitcast_convert_fusion
  (4 shorter events, 0.0 us)
Async XLA Ops:
  0.6 12.5 %copy-start = (f32[256,512]{1,0:T(8,128)S(1)}, f32[256,512]{1,0:T(8,128)}, u32[]{:S(2)}) copy-start(f32[256,512]{1,0:T(8,128)} %field_ref.2) | copy-start | bytes 1572868
  0.6 1.6 %copy-start.1 = (s32[512,1024]{1,0:T(8,128)S(1)}, s32[512,1024]{1,0:T(8,128)}, u32[]{:S(2)}) copy-start(s32[512,1024]{1,0:T(8,128)} %bin_ref.1) | copy-start | bytes 6291460
  2.3 1.2 copy-start.2
  3.5 9.7 %copy-start.3 = (s32[256,512]{1,0:T(8,128)S(1)}, s32[256,512]{1,0:T(8,128)}, u32[]{:S(2)}) copy-start(s32[256,512]{1,0:T(8,128)} %mask_ref.1) | copy-start | bytes 1572868
  3.5 9.7 %copy-start.4 = (f32[256,512]{1,0:T(8,128)S(1)}, f32[256,512]{1,0:T(8,128)}, u32[]{:S(2)}) copy-start(f32[256,512]{1,0:T(8,128)} %visc_ref.1) | copy-start | bytes 1572868
  5.8 23.5 %copy-start.5 = (s32[128]{0:T(128)S(1)}, s32[128]{0:T(128)}, u32[]{:S(2)}) copy-start(s32[128]{0:T(128)} %param.9) | copy-start | bytes 1540
  5.8 36.5 %all-to-all-start = ((s32[8,64,512]{2,1,0:T(8,128)}), s32[8,64,512]{2,1,0:T(8,128)S(1)}, u32[]{:S(2)}, u32[]{:S(2)}) async-start(s32[8,64,512]{2,1,0:T(8,128)} %get-tuple-element.25), calls=%async_computation | async-start | bytes 2097152 | tf_op jit(solution)/shard_map/all_to_all | solution.py:322
  13.3 7.4 %collective-permute-start = (f32[8,512]{1,0:T(8,128)S(1)}, f32[8,512]{1,0:T(8,128)S(1)}, u32[]{:S(2)}, u32[]{:S(2)}) collective-permute-start(f32[8,512]{1,0:T(8,128)S(1)} %get-tuple-element.20), channel_id=1, source_target_pairs={{0,4},{4,8},{8,12},{12,16},{16,20},{20,24},{24,28},{1,5},{5,9},{9,... | collective-permute-start | bytes 49160 | tf_op jit(solution)/shard_map/ppermute | solution.py:170
  17.2 5.7 %collective-permute-start.1 = (f32[8,512]{1,0:T(8,128)S(1)}, f32[8,512]{1,0:T(8,128)S(1)}, u32[]{:S(2)}, u32[]{:S(2)}) collective-permute-start(f32[8,512]{1,0:T(8,128)S(1)} %get-tuple-element.21), channel_id=1, source_target_pairs={{4,0},{8,4},{12,8},{16,12},{20,16},{24,20},{28,24},{5,1},{9,5},{13... | collective-permute-start | bytes 49160 | tf_op jit(solution)/shard_map/ppermute | solution.py:170
  23.2 2.6 %collective-permute-start.2 = (f32[8,384]{1,0:T(8,128)S(1)}, f32[8,384]{1,0:T(8,128)S(1)}, u32[]{:S(2)}, u32[]{:S(2)}) collective-permute-start(f32[8,384]{1,0:T(8,128)S(1)} %get-tuple-element.22), channel_id=1, source_target_pairs={{0,1},{1,2},{2,3},{4,5},{5,6},{6,7},{8,9},{9,10},{10,11},{12,13},{... | collective-permute-start | bytes 36872 | tf_op jit(solution)/shard_map/ppermute | solution.py:170
  24.5 4.8 %collective-permute-start.3 = (f32[8,384]{1,0:T(8,128)S(1)}, f32[8,384]{1,0:T(8,128)S(1)}, u32[]{:S(2)}, u32[]{:S(2)}) collective-permute-start(f32[8,384]{1,0:T(8,128)S(1)} %get-tuple-element.23), channel_id=1, source_target_pairs={{1,0},{2,1},{3,2},{5,4},{6,5},{7,6},{9,8},{10,9},{11,10},{13,12},{... | collective-permute-start | bytes 36872 | tf_op jit(solution)/shard_map/ppermute | solution.py:170
  69.7 29.8 %all-to-all-start.3 = ((s32[8,64,512]{2,1,0:T(8,128)}), s32[8,64,512]{2,1,0:T(8,128)S(1)}, u32[]{:S(2)}, u32[]{:S(2)}) async-start(s32[8,64,512]{2,1,0:T(8,128)} %get-tuple-element.29), calls=%async_computation.3 | async-start | bytes 2097152 | tf_op jit(solution)/shard_map/all_to_all | solution.py:322
  99.5 18.5 %all-to-all-start.2 = ((bf16[8,64,256]{2,1,0:T(8,128)(2,1)}), bf16[8,64,256]{2,1,0:T(8,128)(2,1)S(1)}, u32[]{:S(2)}, u32[]{:S(2)}) async-start(bf16[8,64,256]{2,1,0:T(8,128)(2,1)} %shard_map.81), calls=%async_computation.2 | async-start | bytes 524288 | tf_op jit(solution)/shard_map/all_to_all | solution.py:326

commit v2 on v1

--- a/solution.py
+++ b/solution.py
@@ -16,7 +16,7 @@
 EDGE = 2 * STEPS
 PAD = 16
 AMP_SCALE = 4096.0
-CHUNKS = 2
+LAST = 6
 UNROLL = 4
 VMEM = pl.BlockSpec(memory_space=pltpu.VMEM)
 SMEM = pl.BlockSpec(memory_space=pltpu.SMEM)
@@ -30,30 +30,31 @@
     return pl.CostEstimate(flops=flops, bytes_accessed=size, transcendentals=0)
 
 
-def pack_kernel(amp_ref, bin_ref, *outs):
+def pack_kernel(me_ref, amp_ref, bin_ref, *refs):
+    outs, turned = refs[:-1], refs[-1]
     scaled = (amp_ref[...].astype(F32) * AMP_SCALE).astype(jnp.int32)
-    word = jnp.transpose((scaled << 16) | bin_ref[...])
-    peers, width, rows = outs[0].shape
-    for dest in range(peers):
-        for c, out in enumerate(outs):
-            first = (dest * len(outs) + c) * width
-            out[dest] = word[first : first + width]
-
-
-def pack(amplitude, delay_bin, peers, chunks):
+    turned[...] = jnp.transpose((scaled << 16) | bin_ref[...])
+    width = outs[0].shape[0]
+    for k, out in enumerate(outs):
+        first = pl.multiple_of(lax.rem(me_ref[0] + k, len(outs)) * width, 8)
+        out[...] = turned[pl.ds(first, width), :]
+
+
+def pack(me, amplitude, delay_bin, members):
     panels, observers = amplitude.shape
-    width = observers // peers // chunks
+    width = observers // members
     block = pl.BlockSpec((LANES, observers), lambda i: (i, 0))
-    out = jax.ShapeDtypeStruct((peers, width, panels), jnp.int32)
+    out = jax.ShapeDtypeStruct((width, panels), jnp.int32)
     return pl.pallas_call(
         pack_kernel,
         grid=(panels // LANES,),
-        in_specs=[block, block],
-        out_specs=[pl.BlockSpec((peers, width, LANES), lambda i: (0, 0, i))] * chunks,
-        out_shape=[out] * chunks,
-        compiler_params=params(32),
+        in_specs=[SMEM, block, block],
+        out_specs=[pl.BlockSpec((width, LANES), lambda i: (0, i))] * members,
+        out_shape=[out] * members,
+        scratch_shapes=[pltpu.VMEM((observers, LANES), jnp.int32)],
+        compiler_params=params(56),
         cost_estimate=cost(panels * observers, 10 * panels * observers),
-    )(amplitude, delay_bin)
+    )(me, amplitude, delay_bin)
 
 
 def rows_kernel(field_ref, mask_ref, visc_ref, coded_ref, first_ref, last_ref):
@@ -154,22 +155,13 @@
     for step in range(STEPS):
         turned = jnp.transpose(picked[step])
         value = jnp.sum(jnp.where(chosen, turned, 0.0), axis=0, keepdims=True)
-        sample_ref[:, step, :] = jnp.broadcast_to(value, (sample_ref.shape[0], panels))
-
-
-def field_window(field, mask, visc, panel_cell):
+        sample_ref[step : step + 1, :] = value
+
+
+def edges(field, mask, visc):
     rows, cols = field.shape
-    tall = -(-(rows + EDGE) // LANES) * LANES
     edge_rows = jax.ShapeDtypeStruct((EDGE, cols), F32)
-    edge_cols = jax.ShapeDtypeStruct((EDGE, tall), F32)
-
-    def shifted(axis, first, last):
-        peers = lax.axis_size(axis)
-        up = [(i, i + 1) for i in range(peers - 1)]
-        down = [(i + 1, i) for i in range(peers - 1)]
-        return lax.ppermute(last, axis, up), lax.ppermute(first, axis, down)
-
-    coded, first, last = pl.pallas_call(
+    return pl.pallas_call(
         rows_kernel,
         in_specs=[VMEM] * 3,
         out_specs=[VMEM] * 3,
@@ -177,7 +169,20 @@
         compiler_params=params(16),
         cost_estimate=cost(rows * cols, 16 * rows * cols),
     )(field, mask, visc)
-    before, after = shifted("box", first, last)
+
+
+def shifted(axis, first, last):
+    peers = lax.axis_size(axis)
+    up = [(i, i + 1) for i in range(peers - 1)]
+    down = [(i + 1, i) for i in range(peers - 1)]
+    return lax.ppermute(last, axis, up), lax.ppermute(first, axis, down)
+
+
+def field_window(field, coded, before, after, panel_cell):
+    rows, cols = field.shape
+    tall = -(-(rows + EDGE) // LANES) * LANES
+    edge_cols = jax.ShapeDtypeStruct((EDGE, tall), F32)
+
     first, last = pl.pallas_call(
         columns_kernel,
         in_specs=[VMEM] * 4,
@@ -188,7 +193,6 @@
         cost_estimate=cost(rows * cols, 4 * rows * cols),
     )(field, coded, before, after)
     south, north = shifted("panel", first, last)
-    devices = lax.axis_size("box") * lax.axis_size("panel")
     panels = panel_cell.shape[0]
     cells = panel_cell.reshape(1, panels)
     height, width = rows + 2 * PAD, cols + LANES
@@ -198,7 +202,7 @@
         out_specs=[VMEM] * 2,
         out_shape=[
             jax.ShapeDtypeStruct((rows, cols), F32),
-            jax.ShapeDtypeStruct((devices, STEPS, panels), F32),
+            jax.ShapeDtypeStruct((STEPS, panels), F32),
         ],
         scratch_shapes=[
             pltpu.VMEM((STEPS + 1, height, width), F32),
@@ -207,26 +211,29 @@
             pltpu.VMEM((STEPS, panels, cols), F32),
         ],
         compiler_params=params(24),
-        cost_estimate=cost(100 * rows * cols, 80 * rows * cols),
+        cost_estimate=cost(100 * rows * cols, 800 * rows * cols),
     )(cells, cells, field, coded, before, after, south, north)
 
 
-def bin_kernel(word_ref, sample_ref, out_ref, low_s, high_s, weight_s, acc_s, sig_s):
-    sources, block, local = word_ref.shape
+def bin_kernel(half_ref, *refs):
+    members = (len(refs) - 7) // 2
+    words, samples = refs[:members], refs[members : 2 * members]
+    keep_ref, send_ref, low_s, high_s, weight_s, acc_s, sig_s = refs[2 * members :]
+    block, local = words[0].shape
     parts = local // LANES
     high = NB // LOW
     span = LOW + 16
     depth = 2 * LANES
     shift = LOW.bit_length() - 1
-    for s in range(sources):
+    for s in range(members):
         for j in range(parts):
-            word = word_ref[s, :, j * LANES : (j + 1) * LANES]
+            word = words[s][:, j * LANES : (j + 1) * LANES]
             at = slice((s * parts + j) * LANES, (s * parts + j + 1) * LANES)
             low_s[:, at] = (word & (LOW - 1)).astype(F32)
             high_s[:, at] = ((word >> shift) & (high - 1)).astype(F32)
             amp = (word >> 16).astype(F32) * (1.0 / AMP_SCALE)
             for t in range(STEPS):
-                weight_s[t, :, at] = amp * sample_ref[s * parts + j, t : t + 1, :]
+                weight_s[t, :, at] = amp * samples[s][j, t : t + 1, :]
 
     one = jnp.ones((), BF16)
     zero = jnp.zeros((), BF16)
@@ -243,7 +250,7 @@
 
     def one_observer(o, u):
         acc = None
-        for c in range(sources * local // depth):
+        for c in range(members * local // depth):
             at = slice(c * depth, (c + 1) * depth)
             low_row = spread(low_s[pl.ds(o, 1), at])
             high_row = spread(high_s[pl.ds(o, 1), at])
@@ -281,25 +288,33 @@
         return carry
 
     lax.fori_loop(0, block // unroll, some_observers, 0)
-    owners, _, bins = out_ref.shape
-    for d in range(owners):
-        for r in range(bins // LANES):
-            out_ref[d, :, r * LANES : (r + 1) * LANES] = sig_s[d * (bins // LANES) + r].astype(BF16)
-
-
-def binned(words, samples, owners):
-    sources, observers, local = words.shape
+    tiles = NB // LANES // 2
+    per_owner = tiles // keep_ref.shape[0]
+    for r in range(tiles):
+        lanes = slice(r % per_owner * LANES, (r % per_owner + 1) * LANES)
+        keep_ref[r // per_owner, :, lanes] = sig_s[half_ref[0] * tiles + r]
+        sent = sig_s[(1 - half_ref[0]) * tiles + r]
+        send_ref[r // per_owner, :, lanes] = sent.astype(BF16)
+
+
+def binned(half, words, samples, first, count):
+    members = len(words)
+    local = words[0].shape[1]
     block = 16
-    panels = sources * local
+    panels = members * local
+    bins = NB // 2 // members
+    out = pl.BlockSpec((members, block, bins), lambda i: (0, i, 0))
     return pl.pallas_call(
         bin_kernel,
-        grid=(observers // block,),
-        in_specs=[
-            pl.BlockSpec((sources, block, local), lambda i: (0, i, 0)),
-            pl.BlockSpec(samples.shape, lambda i: (0, 0, 0)),
+        grid=(count // block,),
+        in_specs=[SMEM]
+        + [pl.BlockSpec((block, local), lambda i: (first // block + i, 0))] * members
+        + [pl.BlockSpec(samples[0].shape, lambda i: (0, 0, 0))] * members,
+        out_specs=[out, out],
+        out_shape=[
+            jax.ShapeDtypeStruct((members, count, bins), F32),
+            jax.ShapeDtypeStruct((members, count, bins), BF16),
         ],
-        out_specs=pl.BlockSpec((owners, block, NB // owners), lambda i: (0, i, 0)),
-        out_shape=jax.ShapeDtypeStruct((owners, observers, NB // owners), BF16),
         scratch_shapes=[
             pltpu.VMEM((block, panels), F32),
             pltpu.VMEM((block, panels), F32),
@@ -308,24 +323,82 @@
             pltpu.VMEM((NB // LANES, block, LANES), F32),
         ],
         compiler_params=params(40),
-        cost_estimate=cost(65536 * observers * panels, 8 * observers * panels),
-    )(words, samples)
+        cost_estimate=cost(65536 * count * panels, 8 * count * panels),
+    )(half, *words, *samples)
+
+
+def join_kernel(me_ref, keep_ref, got_ref, *outs):
+    for k, out in enumerate(outs):
+        owner = lax.rem(me_ref[0] + k, len(outs))
+        out[...] = (keep_ref[owner] + got_ref[owner].astype(F32)).astype(BF16)
+
+
+def join(me, keep, got):
+    members, count, bins = keep.shape
+    return pl.pallas_call(
+        join_kernel,
+        in_specs=[SMEM, VMEM, VMEM],
+        out_specs=[VMEM] * members,
+        out_shape=[jax.ShapeDtypeStruct((count, bins), BF16)] * members,
+        compiler_params=params(16),
+        cost_estimate=cost(keep.size, 8 * keep.size),
+    )(me, keep, got)
+
+
+def place_kernel(firsts, width, me_ref, *refs):
+    out_ref, members = refs[-1], (len(refs) - 1) // len(firsts)
+    for c, first in enumerate(firsts):
+        for k in range(members):
+            ref = refs[c * members + k]
+            owner = lax.rem(me_ref[0] - k + members, members)
+            start = pl.multiple_of(owner * width + first, 16)
+            out_ref[pl.ds(start, ref.shape[0]), :] = ref[...].astype(F32)
 
 
 def on_device(field_start, fluid_mask, base_visc, panel_cell, amplitude, delay_bin):
     peers = lax.axis_size("box")
-    swap = functools.partial(
-        lax.all_to_all, axis_name="box", split_axis=0, concat_axis=0, tiled=True
-    )
-    packed = pack(amplitude, delay_bin, peers, CHUNKS)
-    packed, field_start = lax.optimization_barrier((packed, field_start))
-    words = [swap(w) for w in packed]
-    field, sample = field_window(field_start, fluid_mask, base_visc, panel_cell)
-    words[0], sample = lax.optimization_barrier((words[0], sample))
-    samples = lax.all_to_all(sample, ("box", "panel"), split_axis=0, concat_axis=0, tiled=True)
-    finished = [swap(binned(w, samples, peers)) for w in words]
-    signals = jnp.concatenate(finished, axis=1).astype(F32)
-    return (field, signals.reshape(-1, signals.shape[-1]))
+    members = peers // 2
+    index = lax.axis_index("box").astype(jnp.int32).reshape(1)
+    me, half = lax.rem(index, members), index // members
+
+    def spread(parts):
+        def perm(k):
+            return [(i, i // members * members + (i + k) % members) for i in range(peers)]
+
+        return [lax.ppermute(x, "box", perm(k)) if k else x for k, x in enumerate(parts)]
+
+    coded, *ends = edges(field_start, fluid_mask, base_visc)
+    amplitude, delay_bin, *ends = lax.optimization_barrier((amplitude, delay_bin, *ends))
+    before, after = shifted("box", *ends)
+    packed = pack(me, amplitude, delay_bin, members)
+    before, after, *packed = lax.optimization_barrier((before, after, *packed))
+    words = spread(packed)
+    field, sample = field_window(field_start, coded, before, after, panel_cell)
+    samples = spread([lax.all_gather(sample, "panel")] * members)
+    observers = words[0].shape[0]
+    across = [(i, (i + members) % peers) for i in range(peers)]
+    pieces, firsts, first = [], [], 0
+    for count in sizes(observers):
+        keep, send = binned(half, words, samples, first, count)
+        got = lax.ppermute(send, "box", across)
+        if pieces:
+            got, *pieces = lax.optimization_barrier((got, *pieces))
+        pieces += spread(join(me, keep, got))
+        firsts.append(first)
+        first += count
+    signals = pl.pallas_call(
+        functools.partial(place_kernel, firsts, observers),
+        in_specs=[SMEM] + [VMEM] * len(pieces),
+        out_specs=VMEM,
+        out_shape=jax.ShapeDtypeStruct((observers * members, pieces[0].shape[1]), F32),
+        compiler_params=params(16),
+    )(me, *pieces)
+    return (field, signals)
+
+
+def sizes(observers):
+    last = -(-observers * LAST // 16 // 16) * 16
+    return [observers - last, last]
 
 
 def solution(mesh):

time: 134 us -> 113 us (0.84)
  blocking collectives: 41.8 us -> 6.53 us
  Pallas kernels: 46 us -> 56.4 us
  starting transfers between devices: 22.4 us -> 25.7 us
    all_to_all x2 -> x0, blocking collectives: 41.8 us -> none  [the longest x1 27.5 us: on_device(): lax.all_to_all(sample, ('box', 'panel'), split_axis=0, concat_axis=0, til...]
    ppermute x0 -> x14, starting transfers between devices: none -> 16.8 us  [the longest x12 13.7 us: spread(): lax.ppermute(x, 'box', perm(k))]
    ppermute x0 -> x14, waiting for transfers between devices: none -> 16.2 us  [the longest x12 10.2 us: spread(): lax.ppermute(x, 'box', perm(k))]
    all_to_all x3 -> x0, starting transfers between devices: 14.6 us -> none  [the longest x2 11 us: on_device(): words = [swap(w) for w in packed]]
    all_to_all x3 -> x0, waiting for transfers between devices: 10.7 us -> none  [the longest x2 10.7 us: on_device(): words = [swap(w) for w in packed]]
    pallas_call x4 -> x7, Pallas kernels: 32.8 us -> 43.2 us  [the longest x2 37.5 us: binned(): pl.pallas_call(bin_kernel, grid=(count // block,), in_specs=[SMEM] + [pl....]
    all_gather x0 -> x1, blocking collectives: none -> 6.53 us  [on_device(): samples = spread([lax.all_gather(sample, 'panel')] * members)]
    ppermute x4, waiting for transfers between devices: 7.91 us -> 3.5 us  [shifted(): return (lax.ppermute(last, axis, up), lax.ppermute(first, axis, down))]
  transfers between devices with their start and end apart: 7 -> 18, of which waited for: 4 -> 6; matrix products, arithmetic and copies ran while one was open for 0% -> 0% of each run, Pallas kernels for 33% -> 28%
where the time goes in v2:
time: 113 us; the launch traced here: 112 us
  Pallas kernels  56.4 us (50%)
  starting transfers between devices  25.7 us (23%)
  waiting for transfers between devices  19.7 us (17%)
  blocking collectives  6.53 us (6%)
  local copies, waits for them, and re-layouts  3.13 us (3%)
    pallas_call x2, Pallas kernels, binned(): pl.pallas_call(bin_kernel, grid=(count // block,), in_specs=[SMEM] + [pl....  37.5 us
    ppermute x12, starting transfers between devices, spread(): lax.ppermute(x, 'box', perm(k))  13.7 us
    pallas_call x1, Pallas kernels, field_window(): pl.pallas_call(step_kernel, in_specs=[SMEM] + [VMEM] * 7, out_specs=[VMEM...  13 us
    ppermute x12, waiting for transfers between devices, spread(): lax.ppermute(x, 'box', perm(k))  10.2 us
    ppermute x4, starting transfers between devices, shifted(): return (lax.ppermute(last, axis, up), lax.ppermute(first, axis, down))  8.88 us
    all_gather x1, blocking collectives, on_device(): samples = spread([lax.all_gather(sample, 'panel')] * members)  6.53 us
    ppermute x2, waiting for transfers between devices, on_device(): got = lax.ppermute(send, 'box', across)  6 us
    pallas_call x1, Pallas kernels, pack(): pl.pallas_call(pack_kernel, grid=(panels // LANES,), in_specs=[SMEM, bloc...  4.47 us
  transfers between devices with their start and end apart: 18, of which 6 were waited for; matrix products, arithmetic and copies ran while one was open for 0% of the time, Pallas kernels for 28%

profile of v2, /device:TPU:0, one launch (start us, length us, event | category | flops | bytes accessed | tf_op | source)
XLA Modules:
  0.0 112.2 jit_solution(4576261288549084577)
XLA Ops:
  0.6 1.0 copy-done
  1.7 1.0 copy-done.2
  2.7 1.0 copy-done.3
  3.8 0.1 shard_map.77
  3.8 5.0 %collective-permute-start = (f32[8,512]{1,0:T(8,128)S(1)}, f32[8,512]{1,0:T(8,128)S(1)}, u32[]{:S(2)}, u32[]{:S(2)}) collective-permute-start(f32[8,512]{1,0:T(8,128)S(1)} %get-tuple-element.43), channel_id=1, source_target_pairs={{0,4},{4,8},{8,12},{12,16},{16,20},{20,24},{24,28},{1,5},{5,9},{9,... | collective-permute-start | bytes 49160 | tf_op jit(solution)/shard_map/ppermute | solution.py:178
  8.8 1.3 %collective-permute-start.1 = (f32[8,512]{1,0:T(8,128)S(1)}, f32[8,512]{1,0:T(8,128)S(1)}, u32[]{:S(2)}, u32[]{:S(2)}) collective-permute-start(f32[8,512]{1,0:T(8,128)S(1)} %get-tuple-element.44), channel_id=1, source_target_pairs={{4,0},{8,4},{12,8},{16,12},{20,16},{24,20},{28,24},{5,1},{9,5},{13... | collective-permute-start | bytes 49160 | tf_op jit(solution)/shard_map/ppermute | solution.py:178
  10.2 4.5 %shard_map.78 = (s32[256,512]{1,0:T(8,128)}, s32[256,512]{1,0:T(8,128)}, s32[256,512]{1,0:T(8,128)}, s32[256,512]{1,0:T(8,128)}) custom-call(s32[1]{0:T(128)S(6)} %rem.22.me_ref, bf16[512,1024]{1,0:T(8,128)(2,1)} %amp_ref, s32[512,1024]{1,0:T(8,128)} %bin_ref), custom_call_target="tpu_custom_call" | custom-call | flops 524288 | bytes 5242880 | tf_op jit(solution)/shard_map/pallas_call | solution.py:48
  14.6 2.7 %collective-permute-start.4 = (s32[256,512]{1,0:T(8,128)}, s32[256,512]{1,0:T(8,128)S(1)}, u32[]{:S(2)}, u32[]{:S(2)}) collective-permute-start(s32[256,512]{1,0:T(8,128)} %get-tuple-element.57), channel_id=1, source_target_pairs={{0,4},{4,8},{8,12},{12,0},{16,20},{20,24},{24,28},{28,16},{1,5},{5... | collective-permute-start | bytes 1572872 | tf_op jit(solution)/shard_map/ppermute | solution.py:368
  17.3 1.6 %collective-permute-start.5 = (s32[256,512]{1,0:T(8,128)}, s32[256,512]{1,0:T(8,128)S(1)}, u32[]{:S(2)}, u32[]{:S(2)}) collective-permute-start(s32[256,512]{1,0:T(8,128)} %get-tuple-element.58), channel_id=1, source_target_pairs={{0,8},{4,12},{8,0},{12,4},{16,24},{20,28},{24,16},{28,20},{1,9},{5... | collective-permute-start | bytes 1572872 | tf_op jit(solution)/shard_map/ppermute | solution.py:368
  18.9 2.3 %collective-permute-start.6 = (s32[256,512]{1,0:T(8,128)}, s32[256,512]{1,0:T(8,128)S(1)}, u32[]{:S(2)}, u32[]{:S(2)}) collective-permute-start(s32[256,512]{1,0:T(8,128)} %get-tuple-element.59), channel_id=1, source_target_pairs={{0,12},{4,0},{8,4},{12,8},{16,28},{20,16},{24,20},{28,24},{1,13},{... | collective-permute-start | bytes 1572872 | tf_op jit(solution)/shard_map/ppermute | solution.py:368
  21.2 0.3 shard_map.79
  21.5 1.3 %collective-permute-start.2 = (f32[8,384]{1,0:T(8,128)S(1)}, f32[8,384]{1,0:T(8,128)S(1)}, u32[]{:S(2)}, u32[]{:S(2)}) collective-permute-start(f32[8,384]{1,0:T(8,128)S(1)} %get-tuple-element.53), channel_id=1, source_target_pairs={{0,1},{1,2},{2,3},{4,5},{5,6},{6,7},{8,9},{9,10},{10,11},{12,13},{... | collective-permute-start | bytes 36872 | tf_op jit(solution)/shard_map/ppermute | solution.py:178
  22.8 1.3 %collective-permute-start.3 = (f32[8,384]{1,0:T(8,128)S(1)}, f32[8,384]{1,0:T(8,128)S(1)}, u32[]{:S(2)}, u32[]{:S(2)}) collective-permute-start(f32[8,384]{1,0:T(8,128)S(1)} %get-tuple-element.54), channel_id=1, source_target_pairs={{1,0},{2,1},{3,2},{5,4},{6,5},{7,6},{9,8},{10,9},{11,10},{13,12},{... | collective-permute-start | bytes 36872 | tf_op jit(solution)/shard_map/ppermute | solution.py:178
  24.1 3.5 %collective-permute-done.3.north_ref = f32[8,384]{1,0:T(8,128)S(1)} collective-permute-done((f32[8,384]{1,0:T(8,128)S(1)}, f32[8,384]{1,0:T(8,128)S(1)}, u32[]{:S(2)}, u32[]{:S(2)}) %collective-permute-start.3) | collective-permute-done | bytes 12320 | tf_op jit(solution)/shard_map/ppermute | solution.py:178
  27.6 13.0 %shard_map.80 = (f32[256,512]{1,0:T(8,128)}, f32[4,128]{1,0:T(4,128)S(1)}) custom-call(s32[1,128]{1,0:T(1,128)S(1)} %bitcast.3, s32[1,128]{1,0:T(1,128)S(1)} %bitcast.4, f32[256,512]{1,0:T(8,128)S(1)} %copy-done.1, f32[256,512]{1,0:T(8,128)S(1)} %get-tuple-element.40.coded_ref, f32[8,512]{1,0:T(8,128)S(1)} %collective-permute-done.before_ref, ...), custom_call_target="tpu_custom_call" | custom-call | flops 13107200 | bytes 104857600 | tf_op jit(solution)/shard_map/pallas_call | solution.py:199
  40.6 6.5 %all-gather.1.refs_4_ = f32[4,4,128]{2,1,0:T(4,128)S(1)} all-gather(f32[1,4,128]{2,1,0:T(4,128)S(1)} %bitcast.5), channel_id=2, replica_groups=mesh['box'=8,'panel'=4] {'panel'}, dimensions={0}, use_global_device_ids=true | all-gather | bytes 10240 | tf_op jit(solution)/shard_map/all_gather | solution.py:377
  47.1 0.6 collective-permute-start.8
  47.7 4.0 %collective-permute-done.7.refs_5_ = f32[4,4,128]{2,1,0:T(4,128)S(1)} collective-permute-done((f32[4,4,128]{2,1,0:T(4,128)S(1)}, f32[4,4,128]{2,1,0:T(4,128)S(1)}, u32[]{:S(2)}, u32[]{:S(2)}) %collective-permute-start.7) | collective-permute-done | bytes 8224 | tf_op jit(solution)/shard_map/ppermute | solution.py:368
  51.6 3.6 %collective-permute-done.9.refs_7_ = f32[4,4,128]{2,1,0:T(4,128)S(1)} collective-permute-done((f32[4,4,128]{2,1,0:T(4,128)S(1)}, f32[4,4,128]{2,1,0:T(4,128)S(1)}, u32[]{:S(2)}, u32[]{:S(2)}) %collective-permute-start.9) | collective-permute-done | bytes 8224 | tf_op jit(solution)/shard_map/ppermute | solution.py:368
  55.3 23.4 %shard_map.82 = (f32[4,160,256]{2,1,0:T(8,128)S(1)}, bf16[4,160,256]{2,1,0:T(8,128)(2,1)S(1)}) custom-call(s32[1]{0:T(128)S(6)} %select_n.5.half_ref, s32[256,512]{1,0:T(8,128)S(1)} %copy-done.5, s32[256,512]{1,0:T(8,128)S(1)} %collective-permute-done.4.refs_1_, s32[256,512]{1,0:T(8,128)S(1)} %collective-permute-done.5.refs_2_, ...), custom_call_target="tpu_custom_call" | custom-call | flops 21474836480 | bytes 2621440 | tf_op jit(solution)/shard_map/pallas_call | solution.py:307
  78.8 2.7 %collective-permute-start.11 = (bf16[4,160,256]{2,1,0:T(8,128)(2,1)S(1)}, bf16[4,160,256]{2,1,0:T(8,128)(2,1)S(1)}, u32[]{:S(2)}, u32[]{:S(2)}) collective-permute-start(bf16[4,160,256]{2,1,0:T(8,128)(2,1)S(1)} %get-tuple-element.63), channel_id=1, source_target_pairs={{0,16},{4,20},{8,24},{12,28},{16,0},{20,4},{24,8},{28,12},{1,17},{... | collective-permute-start | bytes 983048 | tf_op jit(solution)/shard_map/ppermute | solution.py:383
  81.4 14.0 %shard_map.81 = (f32[4,96,256]{2,1,0:T(8,128)S(1)}, bf16[4,96,256]{2,1,0:T(8,128)(2,1)S(1)}) custom-call(s32[1]{0:T(128)S(6)} %select_n.5.half_ref, s32[256,512]{1,0:T(8,128)S(1)} %copy-done.5, s32[256,512]{1,0:T(8,128)S(1)} %collective-permute-done.4.refs_1_, s32[256,512]{1,0:T(8,128)S(1)} %collective-permute-done.5.refs_2_, ...), custom_call_target="tpu_custom_call" | custom-call | flops 12884901888 | bytes 1572864 | tf_op jit(solution)/shard_map/pallas_call | solution.py:307
  95.5 0.4 collective-permute-start.10
  96.0 0.1 collective-permute-start.12
  96.0 1.5 %collective-permute-start.13 = (bf16[160,256]{1,0:T(8,128)(2,1)S(1)}, bf16[160,256]{1,0:T(8,128)(2,1)S(1)}, u32[]{:S(2)}, u32[]{:S(2)}) collective-permute-start(bf16[160,256]{1,0:T(8,128)(2,1)S(1)} %get-tuple-element.66), channel_id=1, source_target_pairs={{0,8},{4,12},{8,0},{12,4},{16,24},{20,28},{24,16},{28,20},{1,9},{5... | collective-permute-start | bytes 245768 | tf_op jit(solution)/shard_map/ppermute | solution.py:368
  97.5 1.6 %collective-permute-start.14 = (bf16[160,256]{1,0:T(8,128)(2,1)S(1)}, bf16[160,256]{1,0:T(8,128)(2,1)S(1)}, u32[]{:S(2)}, u32[]{:S(2)}) collective-permute-start(bf16[160,256]{1,0:T(8,128)(2,1)S(1)} %get-tuple-element.67), channel_id=1, source_target_pairs={{0,12},{4,0},{8,4},{12,8},{16,28},{20,16},{24,20},{28,24},{1,13},{... | collective-permute-start | bytes 245768 | tf_op jit(solution)/shard_map/ppermute | solution.py:368
  99.1 6.0 %collective-permute-done.10.got_ref = bf16[4,96,256]{2,1,0:T(8,128)(2,1)S(1)} collective-permute-done((bf16[4,96,256]{2,1,0:T(8,128)(2,1)S(1)}, bf16[4,96,256]{2,1,0:T(8,128)(2,1)S(1)}, u32[]{:S(2)}, u32[]{:S(2)}) %collective-permute-start.10) | collective-permute-done | bytes 196640 | tf_op jit(solution)/shard_map/ppermute | solution.py:383
  105.2 1.9 %collective-permute-start.15 = (bf16[96,256]{1,0:T(8,128)(2,1)S(1)}, bf16[96,256]{1,0:T(8,128)(2,1)S(1)}, u32[]{:S(2)}, u32[]{:S(2)}) collective-permute-start(bf16[96,256]{1,0:T(8,128)(2,1)S(1)} %get-tuple-element.75), channel_id=1, source_target_pairs={{0,4},{4,8},{8,12},{12,0},{16,20},{20,24},{24,28},{28,16},{1,5},{5... | collective-permute-start | bytes 147464 | tf_op jit(solution)/shard_map/ppermute | solution.py:368
  107.1 1.5 %collective-permute-start.17 = (bf16[96,256]{1,0:T(8,128)(2,1)S(1)}, bf16[96,256]{1,0:T(8,128)(2,1)S(1)}, u32[]{:S(2)}, u32[]{:S(2)}) collective-permute-start(bf16[96,256]{1,0:T(8,128)(2,1)S(1)} %get-tuple-element.77), channel_id=1, source_target_pairs={{0,12},{4,0},{8,4},{12,8},{16,28},{20,16},{24,20},{28,24},{1,13},{... | collective-permute-start | bytes 147464 | tf_op jit(solution)/shard_map/ppermute | solution.py:368
  108.6 1.6 %collective-permute-done.15.refs_5_ = bf16[96,256]{1,0:T(8,128)(2,1)S(1)} collective-permute-done((bf16[96,256]{1,0:T(8,128)(2,1)S(1)}, bf16[96,256]{1,0:T(8,128)(2,1)S(1)}, u32[]{:S(2)}, u32[]{:S(2)}) %collective-permute-start.15) | collective-permute-done | bytes 49184 | tf_op jit(solution)/shard_map/ppermute | solution.py:368
  110.2 1.0 collective-permute-done.16.refs_6_
  111.2 1.0 shard_map.85
  (26 shorter events, 0.2 us)
Async XLA Ops:
  0.6 1.0 copy-start
  1.7 1.0 copy-start.2
  2.7 1.0 copy-start.3
  3.8 17.5 %copy-start.1 = (f32[256,512]{1,0:T(8,128)S(1)}, f32[256,512]{1,0:T(8,128)}, u32[]{:S(2)}) copy-start(f32[256,512]{1,0:T(8,128)} %field_ref.5) | copy-start | bytes 1572868
  3.8 10.8 %collective-permute-start = (f32[8,512]{1,0:T(8,128)S(1)}, f32[8,512]{1,0:T(8,128)S(1)}, u32[]{:S(2)}, u32[]{:S(2)}) collective-permute-start(f32[8,512]{1,0:T(8,128)S(1)} %get-tuple-element.43), channel_id=1, source_target_pairs={{0,4},{4,8},{8,12},{12,16},{16,20},{20,24},{24,28},{1,5},{5,9},{9,... | collective-permute-start | bytes 49160 | tf_op jit(solution)/shard_map/ppermute | solution.py:178
  8.8 5.8 %collective-permute-start.1 = (f32[8,512]{1,0:T(8,128)S(1)}, f32[8,512]{1,0:T(8,128)S(1)}, u32[]{:S(2)}, u32[]{:S(2)}) collective-permute-start(f32[8,512]{1,0:T(8,128)S(1)} %get-tuple-element.44), channel_id=1, source_target_pairs={{4,0},{8,4},{12,8},{16,12},{20,16},{24,20},{28,24},{5,1},{9,5},{13... | collective-permute-start | bytes 49160 | tf_op jit(solution)/shard_map/ppermute | solution.py:178
  10.1 17.5 %copy-start.4 = (s32[128]{0:T(128)S(1)}, s32[128]{0:T(128)}, u32[]{:S(2)}) copy-start(s32[128]{0:T(128)} %param.9) | copy-start | bytes 1540
  14.6 40.7 %copy-start.5 = (s32[256,512]{1,0:T(8,128)S(1)}, s32[256,512]{1,0:T(8,128)}, u32[]{:S(2)}) copy-start(s32[256,512]{1,0:T(8,128)} %get-tuple-element.56.refs_0_) | copy-start | bytes 1572868
  14.6 40.7 %collective-permute-start.4 = (s32[256,512]{1,0:T(8,128)}, s32[256,512]{1,0:T(8,128)S(1)}, u32[]{:S(2)}, u32[]{:S(2)}) collective-permute-start(s32[256,512]{1,0:T(8,128)} %get-tuple-element.57), channel_id=1, source_target_pairs={{0,4},{4,8},{8,12},{12,0},{16,20},{20,24},{24,28},{28,16},{1,5},{5... | collective-permute-start | bytes 1572872 | tf_op jit(solution)/shard_map/ppermute | solution.py:368
  17.3 38.0 %collective-permute-start.5 = (s32[256,512]{1,0:T(8,128)}, s32[256,512]{1,0:T(8,128)S(1)}, u32[]{:S(2)}, u32[]{:S(2)}) collective-permute-start(s32[256,512]{1,0:T(8,128)} %get-tuple-element.58), channel_id=1, source_target_pairs={{0,8},{4,12},{8,0},{12,4},{16,24},{20,28},{24,16},{28,20},{1,9},{5... | collective-permute-start | bytes 1572872 | tf_op jit(solution)/shard_map/ppermute | solution.py:368
  18.9 36.4 %collective-permute-start.6 = (s32[256,512]{1,0:T(8,128)}, s32[256,512]{1,0:T(8,128)S(1)}, u32[]{:S(2)}, u32[]{:S(2)}) collective-permute-start(s32[256,512]{1,0:T(8,128)} %get-tuple-element.59), channel_id=1, source_target_pairs={{0,12},{4,0},{8,4},{12,8},{16,28},{20,16},{24,20},{28,24},{1,13},{... | collective-permute-start | bytes 1572872 | tf_op jit(solution)/shard_map/ppermute | solution.py:368
  21.5 2.6 %collective-permute-start.2 = (f32[8,384]{1,0:T(8,128)S(1)}, f32[8,384]{1,0:T(8,128)S(1)}, u32[]{:S(2)}, u32[]{:S(2)}) collective-permute-start(f32[8,384]{1,0:T(8,128)S(1)} %get-tuple-element.53), channel_id=1, source_target_pairs={{0,1},{1,2},{2,3},{4,5},{5,6},{6,7},{8,9},{9,10},{10,11},{12,13},{... | collective-permute-start | bytes 36872 | tf_op jit(solution)/shard_map/ppermute | solution.py:178
  22.8 4.8 %collective-permute-start.3 = (f32[8,384]{1,0:T(8,128)S(1)}, f32[8,384]{1,0:T(8,128)S(1)}, u32[]{:S(2)}, u32[]{:S(2)}) collective-permute-start(f32[8,384]{1,0:T(8,128)S(1)} %get-tuple-element.54), channel_id=1, source_target_pairs={{1,0},{2,1},{3,2},{5,4},{6,5},{7,6},{9,8},{10,9},{11,10},{13,12},{... | collective-permute-start | bytes 36872 | tf_op jit(solution)/shard_map/ppermute | solution.py:178
  47.1 4.6 %collective-permute-start.7 = (f32[4,4,128]{2,1,0:T(4,128)S(1)}, f32[4,4,128]{2,1,0:T(4,128)S(1)}, u32[]{:S(2)}, u32[]{:S(2)}) collective-permute-start(f32[4,4,128]{2,1,0:T(4,128)S(1)} %all-gather.1.refs_4_), channel_id=1, source_target_pairs={{0,4},{4,8},{8,12},{12,0},{16,20},{20,24},{24,28},{28,16},{1,5},{5... | collective-permute-start | bytes 24584 | tf_op jit(solution)/shard_map/ppermute | solution.py:368
  47.1 4.6 %collective-permute-start.8 = (f32[4,4,128]{2,1,0:T(4,128)S(1)}, f32[4,4,128]{2,1,0:T(4,128)S(1)}, u32[]{:S(2)}, u32[]{:S(2)}) collective-permute-start(f32[4,4,128]{2,1,0:T(4,128)S(1)} %all-gather.1.refs_4_), channel_id=1, source_target_pairs={{0,8},{4,12},{8,0},{12,4},{16,24},{20,28},{24,16},{28,20},{1,9},{5... | collective-permute-start | bytes 24584 | tf_op jit(solution)/shard_map/ppermute | solution.py:368
  51.6 3.7 %collective-permute-start.9 = (f32[4,4,128]{2,1,0:T(4,128)S(1)}, f32[4,4,128]{2,1,0:T(4,128)S(1)}, u32[]{:S(2)}, u32[]{:S(2)}) collective-permute-start(f32[4,4,128]{2,1,0:T(4,128)S(1)} %all-gather.1.refs_4_), channel_id=1, source_target_pairs={{0,12},{4,0},{8,4},{12,8},{16,28},{20,16},{24,20},{28,24},{1,13},{... | collective-permute-start | bytes 24584 | tf_op jit(solution)/shard_map/ppermute | solution.py:368
  78.8 17.1 %collective-permute-start.11 = (bf16[4,160,256]{2,1,0:T(8,128)(2,1)S(1)}, bf16[4,160,256]{2,1,0:T(8,128)(2,1)S(1)}, u32[]{:S(2)}, u32[]{:S(2)}) collective-permute-start(bf16[4,160,256]{2,1,0:T(8,128)(2,1)S(1)} %get-tuple-element.63), channel_id=1, source_target_pairs={{0,16},{4,20},{8,24},{12,28},{16,0},{20,4},{24,8},{28,12},{1,17},{... | collective-permute-start | bytes 983048 | tf_op jit(solution)/shard_map/ppermute | solution.py:383
  95.5 9.6 %collective-permute-start.10 = (bf16[4,96,256]{2,1,0:T(8,128)(2,1)S(1)}, bf16[4,96,256]{2,1,0:T(8,128)(2,1)S(1)}, u32[]{:S(2)}, u32[]{:S(2)}) collective-permute-start(bf16[4,96,256]{2,1,0:T(8,128)(2,1)S(1)} %get-tuple-element.61), channel_id=1, source_target_pairs={{0,16},{4,20},{8,24},{12,28},{16,0},{20,4},{24,8},{28,12},{1,17},{... | collective-permute-start | bytes 589832 | tf_op jit(solution)/shard_map/ppermute | solution.py:383
  96.0 9.1 %collective-permute-start.12 = (bf16[160,256]{1,0:T(8,128)(2,1)S(1)}, bf16[160,256]{1,0:T(8,128)(2,1)S(1)}, u32[]{:S(2)}, u32[]{:S(2)}) collective-permute-start(bf16[160,256]{1,0:T(8,128)(2,1)S(1)} %get-tuple-element.65), channel_id=1, source_target_pairs={{0,4},{4,8},{8,12},{12,0},{16,20},{20,24},{24,28},{28,16},{1,5},{5... | collective-permute-start | bytes 245768 | tf_op jit(solution)/shard_map/ppermute | solution.py:368
  96.0 9.1 %collective-permute-start.13 = (bf16[160,256]{1,0:T(8,128)(2,1)S(1)}, bf16[160,256]{1,0:T(8,128)(2,1)S(1)}, u32[]{:S(2)}, u32[]{:S(2)}) collective-permute-start(bf16[160,256]{1,0:T(8,128)(2,1)S(1)} %get-tuple-element.66), channel_id=1, source_target_pairs={{0,8},{4,12},{8,0},{12,4},{16,24},{20,28},{24,16},{28,20},{1,9},{5... | collective-permute-start | bytes 245768 | tf_op jit(solution)/shard_map/ppermute | solution.py:368
  97.5 7.6 %collective-permute-start.14 = (bf16[160,256]{1,0:T(8,128)(2,1)S(1)}, bf16[160,256]{1,0:T(8,128)(2,1)S(1)}, u32[]{:S(2)}, u32[]{:S(2)}) collective-permute-start(bf16[160,256]{1,0:T(8,128)(2,1)S(1)} %get-tuple-element.67), channel_id=1, source_target_pairs={{0,12},{4,0},{8,4},{12,8},{16,28},{20,16},{24,20},{28,24},{1,13},{... | collective-permute-start | bytes 245768 | tf_op jit(solution)/shard_map/ppermute | solution.py:368
  105.2 5.0 %collective-permute-start.15 = (bf16[96,256]{1,0:T(8,128)(2,1)S(1)}, bf16[96,256]{1,0:T(8,128)(2,1)S(1)}, u32[]{:S(2)}, u32[]{:S(2)}) collective-permute-start(bf16[96,256]{1,0:T(8,128)(2,1)S(1)} %get-tuple-element.75), channel_id=1, source_target_pairs={{0,4},{4,8},{8,12},{12,0},{16,20},{20,24},{24,28},{28,16},{1,5},{5... | collective-permute-start | bytes 147464 | tf_op jit(solution)/shard_map/ppermute | solution.py:368
  107.1 4.1 %collective-permute-start.16 = (bf16[96,256]{1,0:T(8,128)(2,1)S(1)}, bf16[96,256]{1,0:T(8,128)(2,1)S(1)}, u32[]{:S(2)}, u32[]{:S(2)}) collective-permute-start(bf16[96,256]{1,0:T(8,128)(2,1)S(1)} %get-tuple-element.76), channel_id=1, source_target_pairs={{0,8},{4,12},{8,0},{12,4},{16,24},{20,28},{24,16},{28,20},{1,9},{5... | collective-permute-start | bytes 147464 | tf_op jit(solution)/shard_map/ppermute | solution.py:368
  107.1 4.1 %collective-permute-start.17 = (bf16[96,256]{1,0:T(8,128)(2,1)S(1)}, bf16[96,256]{1,0:T(8,128)(2,1)S(1)}, u32[]{:S(2)}, u32[]{:S(2)}) collective-permute-start(bf16[96,256]{1,0:T(8,128)(2,1)S(1)} %get-tuple-element.77), channel_id=1, source_target_pairs={{0,12},{4,0},{8,4},{12,8},{16,28},{20,16},{24,20},{28,24},{1,13},{... | collective-permute-start | bytes 147464 | tf_op jit(solution)/shard_map/ppermute | solution.py:368

commit v3 on v2

--- a/solution.py
+++ b/solution.py
@@ -17,7 +17,6 @@
 PAD = 16
 AMP_SCALE = 4096.0
 LAST = 6
-UNROLL = 4
 VMEM = pl.BlockSpec(memory_space=pltpu.VMEM)
 SMEM = pl.BlockSpec(memory_space=pltpu.SMEM)
 
@@ -57,34 +56,40 @@
     )(me, amplitude, delay_bin)
 
 
-def rows_kernel(field_ref, mask_ref, visc_ref, coded_ref, first_ref, last_ref):
-    length = field_ref.shape[0]
-    coded = jnp.where(mask_ref[...] != 0, visc_ref[...], 0.0)
-    coded_ref[...] = coded
-    first_ref[:STEPS] = field_ref[:STEPS]
-    first_ref[STEPS:] = coded[:STEPS]
-    last_ref[:STEPS] = field_ref[length - STEPS :]
-    last_ref[STEPS:] = coded[length - STEPS :]
-
-
-def columns_kernel(field_ref, coded_ref, before_ref, after_ref, first_ref, last_ref, tall):
+def coded(mask, visc):
+    return jnp.where(mask != 0, visc, 0.0)
+
+
+def rows_kernel(f_top, m_top, v_top, f_end, m_end, v_end, first_ref, last_ref):
+    first_ref[:STEPS] = f_top[:STEPS]
+    first_ref[STEPS:] = coded(m_top[:STEPS], v_top[:STEPS])
+    last_ref[:STEPS] = f_end[8 - STEPS :]
+    last_ref[STEPS:] = coded(m_end[8 - STEPS :], v_end[8 - STEPS :])
+
+
+def columns_kernel(
+    field_ref, mask_ref, visc_ref, before_ref, after_ref, first_ref, last_ref, tall
+):
     rows, cols = field_ref.shape
     tall[...] = jnp.zeros_like(tall)
-    for part, ref in enumerate((field_ref, coded_ref)):
+    for part in range(2):
         halo = slice(part * STEPS, (part + 1) * STEPS)
         for start, low, out in ((0, 0, first_ref), (cols - LANES, LANES - STEPS, last_ref)):
             lanes = slice(start, start + LANES)
-            tall[:rows] = ref[:, lanes]
+            if part:
+                tall[:rows] = coded(mask_ref[:, lanes], visc_ref[:, lanes])
+            else:
+                tall[:rows] = field_ref[:, lanes]
             tall[rows : rows + STEPS] = after_ref[halo, lanes]
             tall[rows + STEPS : rows + EDGE] = before_ref[halo, lanes]
             out[halo] = jnp.transpose(tall[...])[low : low + STEPS]
 
 
 def step_kernel(
-    cell_smem,
     cell_ref,
     field_ref,
-    coded_ref,
+    mask_ref,
+    visc_ref,
     before_ref,
     after_ref,
     south_ref,
@@ -94,21 +99,23 @@
     fields,
     visc,
     wide,
-    picked,
 ):
     rows, cols = field_ref.shape
-    panels = cell_ref.shape[1]
+    panels = sample_ref.shape[1]
     height, width = visc.shape
     wide[...] = jnp.zeros_like(wide)
     blank = jnp.zeros((PAD, width), F32)
-    for part, (ref, buf) in enumerate(((field_ref, fields.at[0]), (coded_ref, visc))):
+    for part, buf in enumerate((fields.at[0], visc)):
         halo = slice(part * STEPS, (part + 1) * STEPS)
         wide[:STEPS] = north_ref[halo]
         wide[LANES - STEPS :] = south_ref[halo]
         side = jnp.transpose(wide[...])
         buf[:PAD] = blank
         buf[PAD + rows :] = blank
-        buf[PAD : PAD + rows, :cols] = ref[...]
+        if part:
+            buf[PAD : PAD + rows, :cols] = coded(mask_ref[...], visc_ref[...])
+        else:
+            buf[PAD : PAD + rows, :cols] = field_ref[...]
         buf[PAD + rows : PAD + rows + STEPS, :cols] = after_ref[halo]
         buf[PAD - STEPS : PAD, :cols] = before_ref[halo]
         buf[PAD : PAD + rows, cols:] = side[:rows]
@@ -126,36 +133,49 @@
             window = old[pl.ds(top, strip + 16), :]
             base = visc[pl.ds(top + 8, strip), :]
             center = window[8 : 8 + strip]
-            west = window[7 : 7 + strip]
-            east = window[9 : 9 + strip]
+            west = pltpu.roll(window, 1, 0)[8 : 8 + strip]
+            east = pltpu.roll(window, strip + 15, 0)[8 : 8 + strip]
             south = pltpu.roll(center, 1, 1)
             north = pltpu.roll(center, width - 1, 1)
-            grad_x = 0.5 * (east - west)
-            grad_y = 0.5 * (north - south)
-            grad_norm = jnp.sqrt(grad_x * grad_x + grad_y * grad_y)
-            viscosity = base + 0.05 * grad_norm / (1.0 + grad_norm)
-            update = center + viscosity * (east + west + north + south - 4.0 * center)
-            update = update - 0.15 * (center - west) - 0.1 * (center - south)
+            diff_x = east - west
+            diff_y = north - south
+            square = diff_x * diff_x + diff_y * diff_y
+            norm = square * lax.rsqrt(jnp.maximum(square, 1e-37))
+            viscosity = base + 0.05 * norm / (2.0 + norm)
+            around = (east + west) + (north + south)
+            update = 0.75 * center + 0.15 * west + 0.1 * south
+            update = update + viscosity * (around - 4.0 * center)
             new[pl.ds(top + 8, strip), :] = jnp.where(base > 0.0, update, 0.0)
             return carry
 
         lax.fori_loop(0, (height - 16) // strip, one_strip, 0)
     end_ref[...] = fields[STEPS, PAD : PAD + rows, :cols]
 
-    def one_panel(k, carry):
-        cell = cell_smem[0, k]
-        row = cell // cols + PAD
-        for step in range(STEPS):
-            picked[step, pl.ds(k, 1), :] = fields[step + 1, pl.ds(row, 1), :cols]
-        return carry
-
-    lax.fori_loop(0, panels, one_panel, 0, unroll=4)
-    column = lax.rem(cell_ref[...], cols)
-    chosen = lax.broadcasted_iota(jnp.int32, (cols, panels), 0) == column
-    for step in range(STEPS):
-        turned = jnp.transpose(picked[step])
-        value = jnp.sum(jnp.where(chosen, turned, 0.0), axis=0, keepdims=True)
-        sample_ref[step : step + 1, :] = value
+    lane = lax.broadcasted_iota(jnp.int32, (8, LANES), 1)
+    line = lax.broadcasted_iota(jnp.int32, (8, LANES), 0)
+    for base in range(0, panels, LANES):
+
+        def one_panel(k, found):
+            cell = cell_ref[0, base + k]
+            row = cell // cols
+            col = cell - row * cols
+            top = pl.multiple_of(row // 8 * 8 + PAD, 8)
+            left = pl.multiple_of(col // LANES * LANES, LANES)
+            here = (lane == k) & (line == row % 8)
+            turn = (k - col) & (LANES - 1)
+            return tuple(
+                jnp.where(
+                    here,
+                    pltpu.roll(fields[t + 1, pl.ds(top, 8), pl.ds(left, LANES)], turn, 1),
+                    found[t],
+                )
+                for t in range(STEPS)
+            )
+
+        none = (jnp.zeros((8, LANES), F32),) * STEPS
+        found = lax.fori_loop(0, LANES, one_panel, none, unroll=8)
+        for t in range(STEPS):
+            sample_ref[t : t + 1, base : base + LANES] = jnp.sum(found[t], axis=0, keepdims=True)
 
 
 def edges(field, mask, visc):
@@ -163,12 +183,14 @@
     edge_rows = jax.ShapeDtypeStruct((EDGE, cols), F32)
     return pl.pallas_call(
         rows_kernel,
-        in_specs=[VMEM] * 3,
-        out_specs=[VMEM] * 3,
-        out_shape=[jax.ShapeDtypeStruct((rows, cols), F32), edge_rows, edge_rows],
-        compiler_params=params(16),
-        cost_estimate=cost(rows * cols, 16 * rows * cols),
-    )(field, mask, visc)
+        grid=(1,),
+        in_specs=[pl.BlockSpec((8, cols), lambda i: (0, 0))] * 3
+        + [pl.BlockSpec((8, cols), lambda i: (rows // 8 - 1, 0))] * 3,
+        out_specs=[pl.BlockSpec((EDGE, cols), lambda i: (0, 0))] * 2,
+        out_shape=[edge_rows, edge_rows],
+        compiler_params=params(56),
+        cost_estimate=cost(16 * cols, 256 * cols),
+    )(field, mask, visc, field, mask, visc)
 
 
 def shifted(axis, first, last):
@@ -178,20 +200,20 @@
     return lax.ppermute(last, axis, up), lax.ppermute(first, axis, down)
 
 
-def field_window(field, coded, before, after, panel_cell):
+def field_window(field, mask, visc, before, after, panel_cell):
     rows, cols = field.shape
     tall = -(-(rows + EDGE) // LANES) * LANES
     edge_cols = jax.ShapeDtypeStruct((EDGE, tall), F32)
 
     first, last = pl.pallas_call(
         columns_kernel,
-        in_specs=[VMEM] * 4,
+        in_specs=[VMEM] * 5,
         out_specs=[VMEM] * 2,
         out_shape=[edge_cols, edge_cols],
         scratch_shapes=[pltpu.VMEM((tall, LANES), F32)],
         compiler_params=params(16),
         cost_estimate=cost(rows * cols, 4 * rows * cols),
-    )(field, coded, before, after)
+    )(field, mask, visc, before, after)
     south, north = shifted("panel", first, last)
     panels = panel_cell.shape[0]
     cells = panel_cell.reshape(1, panels)
@@ -208,11 +230,10 @@
             pltpu.VMEM((STEPS + 1, height, width), F32),
             pltpu.VMEM((height, width), F32),
             pltpu.VMEM((LANES, tall), F32),
-            pltpu.VMEM((STEPS, panels, cols), F32),
         ],
         compiler_params=params(24),
         cost_estimate=cost(100 * rows * cols, 800 * rows * cols),
-    )(cells, cells, field, coded, before, after, south, north)
+    )(cells, field, mask, visc, before, after, south, north)
 
 
 def bin_kernel(half_ref, *refs):
@@ -222,7 +243,9 @@
     block, local = words[0].shape
     parts = local // LANES
     high = NB // LOW
-    span = LOW + 16
+    per_row = LANES // LOW
+    half_rows = NB // LANES // 8
+    low_tiles = LOW // 8 + 1
     depth = 2 * LANES
     shift = LOW.bit_length() - 1
     for s in range(members):
@@ -237,57 +260,60 @@
 
     one = jnp.ones((), BF16)
     zero = jnp.zeros((), BF16)
-    high_ids = lax.broadcasted_iota(jnp.int32, (high, depth), 0).astype(F32).astype(BF16)
-    low_ids = [
-        (lax.broadcasted_iota(jnp.int32, (span, depth), 0) - t).astype(F32).astype(BF16)
-        for t in range(STEPS)
+    sub = lax.broadcasted_iota(jnp.int32, (16, depth), 0) & 7
+
+    def number(x):
+        return x.astype(F32).astype(BF16)
+
+    high_ids = [
+        number(per_row * (8 * (k % half_rows) + sub) + k // half_rows) for k in range(high // 8)
     ]
-    lane = lax.broadcasted_iota(jnp.int32, (NB // LANES, LANES), 1)
+    low_ids = [[number(8 * k + sub - t) for t in range(STEPS)] for k in range(low_tiles)]
+    lane = lax.broadcasted_iota(jnp.int32, (8, LANES), 1)
+    lanes = lax.broadcasted_iota(jnp.int32, (NB // LANES, LANES), 1)
     acc_s[...] = jnp.zeros_like(acc_s)
 
-    def spread(row):
-        return jnp.broadcast_to(row, (16, depth)).astype(BF16)
-
-    def one_observer(o, u):
+    def two_observers(o, u):
+        def spread(ref, *lead):
+            rows = [
+                jnp.broadcast_to(ref[(*lead, slice(o + e, o + e + 1), at)], (8, depth))
+                for e in range(2)
+            ]
+            return jnp.concatenate(rows).astype(BF16)
+
         acc = None
         for c in range(members * local // depth):
             at = slice(c * depth, (c + 1) * depth)
-            low_row = spread(low_s[pl.ds(o, 1), at])
-            high_row = spread(high_s[pl.ds(o, 1), at])
-            weights = [spread(weight_s[t, pl.ds(o, 1), at]) for t in range(STEPS)]
-            left = jnp.concatenate(
-                [jnp.where(high_ids[k : k + 16] == high_row, one, zero) for k in range(0, high, 16)]
-            )
+            low_row, high_row = spread(low_s), spread(high_s)
+            weights = [spread(weight_s, t) for t in range(STEPS)]
+            left = jnp.concatenate([jnp.where(ids == high_row, one, zero) for ids in high_ids])
             right = []
-            for k in range(0, span, 16):
+            for k in range(low_tiles):
                 placed = zero
-                for t in range(1 if k >= LOW else 0, STEPS):
-                    placed = jnp.where(low_ids[t][k : k + 16] == low_row, weights[t], placed)
+                for t in range(1 if k * 8 >= LOW else 0, STEPS):
+                    placed = jnp.where(low_ids[k][t] == low_row, weights[t], placed)
                 right.append(placed)
             term = lax.dot_general(
                 left, jnp.concatenate(right), (((1,), (1,)), ((), ())), preferred_element_type=F32
             )
             acc = term if acc is None else acc + term
-        acc_s[u, :, :span] = acc
-        per_row = LANES // LOW
-        total = None
-        for j in range(per_row):
-            x = acc_s[u, pl.ds(j, NB // LANES, stride=per_row), :]
-            if j:
-                x = pltpu.roll(x, LOW * j, 1)
-            if j == per_row - 1:
-                x = jnp.where(lane < 16, pltpu.roll(x, 1, 0), x)
-            total = x if total is None else total + x
-        sig_s[:, pl.ds(o, 1), :] = total[:, None, :]
-
-    unroll = acc_s.shape[0]
-
-    def some_observers(i, carry):
-        for u in range(unroll):
-            one_observer(i * unroll + u, u)
-        return carry
-
-    lax.fori_loop(0, block // unroll, some_observers, 0)
+        acc_s[u, :, : 16 * low_tiles] = acc
+        for e in range(2):
+            total = None
+            for j in range(per_row):
+                low = (lane - LOW * j) & (LANES - 1)
+                source = jnp.where(low < 8 * low_tiles, 16 * (low // 8) + 8 * e + (low & 7), LANES - 1)
+                tops = [16 * (j * half_rows + g) + 8 * e for g in range(half_rows)]
+                x = jnp.concatenate(
+                    [jnp.take_along_axis(acc_s[u, top : top + 8], source, axis=1) for top in tops]
+                )
+                if j == per_row - 1:
+                    x = jnp.where(lanes < LOW, pltpu.roll(x, 1, 0), x)
+                total = x if total is None else total + x
+            sig_s[:, o + e : o + e + 1, :] = total[:, None, :]
+
+    for u in range(block // 2):
+        two_observers(2 * u, u)
     tiles = NB // LANES // 2
     per_owner = tiles // keep_ref.shape[0]
     for r in range(tiles):
@@ -319,7 +345,7 @@
             pltpu.VMEM((block, panels), F32),
             pltpu.VMEM((block, panels), F32),
             pltpu.VMEM((STEPS, block, panels), F32),
-            pltpu.VMEM((UNROLL, NB // LOW, LANES), F32),
+            pltpu.VMEM((block // 2, 2 * NB // LOW, LANES), F32),
             pltpu.VMEM((NB // LANES, block, LANES), F32),
         ],
         compiler_params=params(40),
@@ -367,13 +393,15 @@
 
         return [lax.ppermute(x, "box", perm(k)) if k else x for k, x in enumerate(parts)]
 
-    coded, *ends = edges(field_start, fluid_mask, base_visc)
+    ends = edges(field_start, fluid_mask, base_visc)
     amplitude, delay_bin, *ends = lax.optimization_barrier((amplitude, delay_bin, *ends))
     before, after = shifted("box", *ends)
     packed = pack(me, amplitude, delay_bin, members)
     before, after, *packed = lax.optimization_barrier((before, after, *packed))
     words = spread(packed)
-    field, sample = field_window(field_start, coded, before, after, panel_cell)
+    field, sample = field_window(
+        field_start, fluid_mask, base_visc, before, after, panel_cell
+    )
     samples = spread([lax.all_gather(sample, "panel")] * members)
     observers = words[0].shape[0]
     across = [(i, (i + members) % peers) for i in range(peers)]

time: 113 us -> 105 us (0.929)
  Pallas kernels: 56.4 us -> 46.5 us
  waiting for transfers between devices: 19.7 us -> 24 us
  local copies, waits for them, and re-layouts: 3.13 us -> 0.02 us
    pallas_call x2, Pallas kernels: 37.5 us -> 26.8 us  [binned(): pl.pallas_call(bin_kernel, grid=(count // block,), in_specs=[SMEM] + [pl....]
    ppermute x12, waiting for transfers between devices: 10.2 us -> 13.7 us  [spread(): lax.ppermute(x, 'box', perm(k))]
    unnamed x12 -> x10, local copies, waits for them, and re-layouts: 3.13 us -> 0.02 us
    pallas_call x2, Pallas kernels: 0.33 us -> 1.7 us  [the longest x1 1.43 us: edges(): pl.pallas_call(rows_kernel, grid=(1,), in_specs=[pl.BlockSpec((8, cols),...]
  transfers between devices with their start and end apart: 18 -> 18, of which waited for: 6 -> 11; matrix products, arithmetic and copies ran while one was open for 0% -> 0% of each run, Pallas kernels for 28% -> 26%
where the time goes in v3:
time: 105 us; the launch traced here: 104 us
  Pallas kernels  46.5 us (44%)
  starting transfers between devices  26.6 us (25%)
  waiting for transfers between devices  24 us (23%)
  blocking collectives  6.53 us (6%)
    pallas_call x2, Pallas kernels, binned(): pl.pallas_call(bin_kernel, grid=(count // block,), in_specs=[SMEM] + [pl....  26.8 us
    ppermute x12, starting transfers between devices, spread(): lax.ppermute(x, 'box', perm(k))  14.7 us
    ppermute x12, waiting for transfers between devices, spread(): lax.ppermute(x, 'box', perm(k))  13.7 us
    pallas_call x1, Pallas kernels, field_window(): pl.pallas_call(step_kernel, in_specs=[SMEM] + [VMEM] * 7, out_specs=[VMEM...  12.4 us
    ppermute x4, starting transfers between devices, shifted(): return (lax.ppermute(last, axis, up), lax.ppermute(first, axis, down))  8.88 us
    ppermute x2, waiting for transfers between devices, on_device(): got = lax.ppermute(send, 'box', across)  6.79 us
    all_gather x1, blocking collectives, on_device(): samples = spread([lax.all_gather(sample, 'panel')] * members)  6.53 us
    pallas_call x1, Pallas kernels, pack(): pl.pallas_call(pack_kernel, grid=(panels // LANES,), in_specs=[SMEM, bloc...  4.47 us
  transfers between devices with their start and end apart: 18, of which 11 were waited for; matrix products, arithmetic and copies ran while one was open for 0% of the time, Pallas kernels for 26%

profile of v3, /device:TPU:0, one launch (start us, length us, event | category | flops | bytes accessed | tf_op | source)
XLA Modules:
  0.0 104.4 jit_solution(11373402025222823213)
XLA Ops:
  0.6 1.4 %shard_map.77 = (f32[8,512]{1,0:T(8,128)}, f32[8,512]{1,0:T(8,128)}) custom-call(f32[256,512]{1,0:T(8,128)} %field_ref.3, s32[256,512]{1,0:T(8,128)} %mask_ref.3, f32[256,512]{1,0:T(8,128)} %visc_ref.3, f32[256,512]{1,0:T(8,128)} %field_ref.3, s32[256,512]{1,0:T(8,128)} %mask_ref.3, f32[256,512]{1,0:T(8,128)} %visc_ref.3), custom_call_target="tpu_custom_call" | custom-call | flops 8192 | bytes 131072 | tf_op jit(solution)/shard_map/pallas_call | solution.py:184
  2.1 5.0 %collective-permute-start = (f32[8,512]{1,0:T(8,128)}, f32[8,512]{1,0:T(8,128)S(1)}, u32[]{:S(2)}, u32[]{:S(2)}) collective-permute-start(f32[8,512]{1,0:T(8,128)} %get-tuple-element.41), channel_id=1, source_target_pairs={{0,4},{4,8},{8,12},{12,16},{16,20},{20,24},{24,28},{1,5},{5,9},{9,... | collective-permute-start | bytes 49160 | tf_op jit(solution)/shard_map/ppermute | solution.py:200
  7.1 1.3 %collective-permute-start.1 = (f32[8,512]{1,0:T(8,128)}, f32[8,512]{1,0:T(8,128)S(1)}, u32[]{:S(2)}, u32[]{:S(2)}) collective-permute-start(f32[8,512]{1,0:T(8,128)} %get-tuple-element.42), channel_id=1, source_target_pairs={{4,0},{8,4},{12,8},{16,12},{20,16},{24,20},{28,24},{5,1},{9,5},{13... | collective-permute-start | bytes 49160 | tf_op jit(solution)/shard_map/ppermute | solution.py:200
  8.4 4.5 %shard_map.78 = (s32[256,512]{1,0:T(8,128)}, s32[256,512]{1,0:T(8,128)}, s32[256,512]{1,0:T(8,128)}, s32[256,512]{1,0:T(8,128)}) custom-call(s32[1]{0:T(128)S(6)} %rem.22.me_ref, bf16[512,1024]{1,0:T(8,128)(2,1)} %amp_ref, s32[512,1024]{1,0:T(8,128)} %bin_ref), custom_call_target="tpu_custom_call" | custom-call | flops 524288 | bytes 5242880 | tf_op jit(solution)/shard_map/pallas_call | solution.py:47
  12.9 2.7 %collective-permute-start.4 = (s32[256,512]{1,0:T(8,128)}, s32[256,512]{1,0:T(8,128)S(1)}, u32[]{:S(2)}, u32[]{:S(2)}) collective-permute-start(s32[256,512]{1,0:T(8,128)} %get-tuple-element.55), channel_id=1, source_target_pairs={{0,4},{4,8},{8,12},{12,0},{16,20},{20,24},{24,28},{28,16},{1,5},{5... | collective-permute-start | bytes 1572872 | tf_op jit(solution)/shard_map/ppermute | solution.py:394
  15.6 1.6 %collective-permute-start.5 = (s32[256,512]{1,0:T(8,128)}, s32[256,512]{1,0:T(8,128)S(1)}, u32[]{:S(2)}, u32[]{:S(2)}) collective-permute-start(s32[256,512]{1,0:T(8,128)} %get-tuple-element.56), channel_id=1, source_target_pairs={{0,8},{4,12},{8,0},{12,4},{16,24},{20,28},{24,16},{28,20},{1,9},{5... | collective-permute-start | bytes 1572872 | tf_op jit(solution)/shard_map/ppermute | solution.py:394
  17.2 2.3 %collective-permute-start.6 = (s32[256,512]{1,0:T(8,128)}, s32[256,512]{1,0:T(8,128)S(1)}, u32[]{:S(2)}, u32[]{:S(2)}) collective-permute-start(s32[256,512]{1,0:T(8,128)} %get-tuple-element.57), channel_id=1, source_target_pairs={{0,12},{4,0},{8,4},{12,8},{16,28},{20,16},{24,20},{28,24},{1,13},{... | collective-permute-start | bytes 1572872 | tf_op jit(solution)/shard_map/ppermute | solution.py:394
  19.7 1.3 %collective-permute-start.2 = (f32[8,384]{1,0:T(8,128)S(1)}, f32[8,384]{1,0:T(8,128)S(1)}, u32[]{:S(2)}, u32[]{:S(2)}) collective-permute-start(f32[8,384]{1,0:T(8,128)S(1)} %get-tuple-element.51), channel_id=1, source_target_pairs={{0,1},{1,2},{2,3},{4,5},{5,6},{6,7},{8,9},{9,10},{10,11},{12,13},{... | collective-permute-start | bytes 36872 | tf_op jit(solution)/shard_map/ppermute | solution.py:200
  21.0 1.3 %collective-permute-start.3 = (f32[8,384]{1,0:T(8,128)S(1)}, f32[8,384]{1,0:T(8,128)S(1)}, u32[]{:S(2)}, u32[]{:S(2)}) collective-permute-start(f32[8,384]{1,0:T(8,128)S(1)} %get-tuple-element.52), channel_id=1, source_target_pairs={{1,0},{2,1},{3,2},{5,4},{6,5},{7,6},{9,8},{10,9},{11,10},{13,12},{... | collective-permute-start | bytes 36872 | tf_op jit(solution)/shard_map/ppermute | solution.py:200
  22.4 3.5 %collective-permute-done.3.north_ref = f32[8,384]{1,0:T(8,128)S(1)} collective-permute-done((f32[8,384]{1,0:T(8,128)S(1)}, f32[8,384]{1,0:T(8,128)S(1)}, u32[]{:S(2)}, u32[]{:S(2)}) %collective-permute-start.3) | collective-permute-done | bytes 12320 | tf_op jit(solution)/shard_map/ppermute | solution.py:200
  25.8 12.4 %shard_map.80 = (f32[256,512]{1,0:T(8,128)}, f32[4,128]{1,0:T(4,128)S(1)}) custom-call(s32[1,128]{1,0:T(1,128)S(1)} %bitcast.4, f32[256,512]{1,0:T(8,128)S(1)} %copy-done, s32[256,512]{1,0:T(8,128)S(1)} %copy-done.1, f32[256,512]{1,0:T(8,128)S(1)} %copy-done.2, f32[8,512]{1,0:T(8,128)S(1)} %collective-permute-done.before_ref, ...), custom_call_target="tpu_custom_call" | custom-call | flops 13107200 | bytes 104857600 | tf_op jit(solution)/shard_map/pallas_call | solution.py:221
  38.3 6.5 %all-gather.1.refs_4_ = f32[4,4,128]{2,1,0:T(4,128)S(1)} all-gather(f32[1,4,128]{2,1,0:T(4,128)S(1)} %bitcast.3), channel_id=2, replica_groups=mesh['box'=8,'panel'=4] {'panel'}, dimensions={0}, use_global_device_ids=true | all-gather | bytes 10240 | tf_op jit(solution)/shard_map/all_gather | solution.py:405
  44.8 0.6 collective-permute-start.8
  45.4 4.0 %collective-permute-done.7.refs_5_ = f32[4,4,128]{2,1,0:T(4,128)S(1)} collective-permute-done((f32[4,4,128]{2,1,0:T(4,128)S(1)}, f32[4,4,128]{2,1,0:T(4,128)S(1)}, u32[]{:S(2)}, u32[]{:S(2)}) %collective-permute-start.7) | collective-permute-done | bytes 8224 | tf_op jit(solution)/shard_map/ppermute | solution.py:394
  49.4 3.6 %collective-permute-done.9.refs_7_ = f32[4,4,128]{2,1,0:T(4,128)S(1)} collective-permute-done((f32[4,4,128]{2,1,0:T(4,128)S(1)}, f32[4,4,128]{2,1,0:T(4,128)S(1)}, u32[]{:S(2)}, u32[]{:S(2)}) %collective-permute-start.9) | collective-permute-done | bytes 8224 | tf_op jit(solution)/shard_map/ppermute | solution.py:394
  53.0 16.6 %shard_map.82 = (f32[4,160,256]{2,1,0:T(8,128)S(1)}, bf16[4,160,256]{2,1,0:T(8,128)(2,1)S(1)}) custom-call(s32[1]{0:T(128)S(6)} %select_n.5.half_ref, s32[256,512]{1,0:T(8,128)S(1)} %copy-done.4, s32[256,512]{1,0:T(8,128)S(1)} %collective-permute-done.4.refs_1_, s32[256,512]{1,0:T(8,128)S(1)} %collective-permute-done.5.refs_2_, ...), custom_call_target="tpu_custom_call" | custom-call | flops 21474836480 | bytes 2621440 | tf_op jit(solution)/shard_map/pallas_call | solution.py:333
  69.7 2.7 %collective-permute-start.11 = (bf16[4,160,256]{2,1,0:T(8,128)(2,1)S(1)}, bf16[4,160,256]{2,1,0:T(8,128)(2,1)S(1)}, u32[]{:S(2)}, u32[]{:S(2)}) collective-permute-start(bf16[4,160,256]{2,1,0:T(8,128)(2,1)S(1)} %get-tuple-element.61), channel_id=1, source_target_pairs={{0,16},{4,20},{8,24},{12,28},{16,0},{20,4},{24,8},{28,12},{1,17},{... | collective-permute-start | bytes 983048 | tf_op jit(solution)/shard_map/ppermute | solution.py:411
  72.4 10.1 %shard_map.81 = (f32[4,96,256]{2,1,0:T(8,128)S(1)}, bf16[4,96,256]{2,1,0:T(8,128)(2,1)S(1)}) custom-call(s32[1]{0:T(128)S(6)} %select_n.5.half_ref, s32[256,512]{1,0:T(8,128)S(1)} %copy-done.4, s32[256,512]{1,0:T(8,128)S(1)} %collective-permute-done.4.refs_1_, s32[256,512]{1,0:T(8,128)S(1)} %collective-permute-done.5.refs_2_, ...), custom_call_target="tpu_custom_call" | custom-call | flops 12884901888 | bytes 1572864 | tf_op jit(solution)/shard_map/pallas_call | solution.py:333
  82.5 0.4 collective-permute-start.10
  82.9 6.5 %collective-permute-done.11.got_ref = bf16[4,160,256]{2,1,0:T(8,128)(2,1)S(1)} collective-permute-done((bf16[4,160,256]{2,1,0:T(8,128)(2,1)S(1)}, bf16[4,160,256]{2,1,0:T(8,128)(2,1)S(1)}, u32[]{:S(2)}, u32[]{:S(2)}) %collective-permute-start.11) | collective-permute-done | bytes 327712 | tf_op jit(solution)/shard_map/ppermute | solution.py:411
  89.4 1.5 %collective-permute-start.12 = (bf16[160,256]{1,0:T(8,128)(2,1)S(1)}, bf16[160,256]{1,0:T(8,128)(2,1)S(1)}, u32[]{:S(2)}, u32[]{:S(2)}) collective-permute-start(bf16[160,256]{1,0:T(8,128)(2,1)S(1)} %get-tuple-element.63), channel_id=1, source_target_pairs={{0,4},{4,8},{8,12},{12,0},{16,20},{20,24},{24,28},{28,16},{1,5},{5... | collective-permute-start | bytes 245768 | tf_op jit(solution)/shard_map/ppermute | solution.py:394
  90.9 2.4 %collective-permute-start.14 = (bf16[160,256]{1,0:T(8,128)(2,1)S(1)}, bf16[160,256]{1,0:T(8,128)(2,1)S(1)}, u32[]{:S(2)}, u32[]{:S(2)}) collective-permute-start(bf16[160,256]{1,0:T(8,128)(2,1)S(1)} %get-tuple-element.65), channel_id=1, source_target_pairs={{0,12},{4,0},{8,4},{12,8},{16,28},{20,16},{24,20},{28,24},{1,13},{... | collective-permute-start | bytes 245768 | tf_op jit(solution)/shard_map/ppermute | solution.py:394
  93.6 2.2 %collective-permute-done.12.refs_1_ = bf16[160,256]{1,0:T(8,128)(2,1)S(1)} collective-permute-done((bf16[160,256]{1,0:T(8,128)(2,1)S(1)}, bf16[160,256]{1,0:T(8,128)(2,1)S(1)}, u32[]{:S(2)}, u32[]{:S(2)}) %collective-permute-start.12) | collective-permute-done | bytes 81952 | tf_op jit(solution)/shard_map/ppermute | solution.py:394
  95.7 0.4 collective-permute-done.13.refs_2_
  96.1 0.5 collective-permute-done.14.refs_3_
  96.7 1.8 %collective-permute-start.15 = (bf16[96,256]{1,0:T(8,128)(2,1)S(1)}, bf16[96,256]{1,0:T(8,128)(2,1)S(1)}, u32[]{:S(2)}, u32[]{:S(2)}) collective-permute-start(bf16[96,256]{1,0:T(8,128)(2,1)S(1)} %get-tuple-element.73), channel_id=1, source_target_pairs={{0,4},{4,8},{8,12},{12,0},{16,20},{20,24},{24,28},{28,16},{1,5},{5... | collective-permute-start | bytes 147464 | tf_op jit(solution)/shard_map/ppermute | solution.py:394
  98.6 0.7 collective-permute-start.16
  99.3 1.1 %collective-permute-start.17 = (bf16[96,256]{1,0:T(8,128)(2,1)S(1)}, bf16[96,256]{1,0:T(8,128)(2,1)S(1)}, u32[]{:S(2)}, u32[]{:S(2)}) collective-permute-start(bf16[96,256]{1,0:T(8,128)(2,1)S(1)} %get-tuple-element.75), channel_id=1, source_target_pairs={{0,12},{4,0},{8,4},{12,8},{16,28},{20,16},{24,20},{28,24},{1,13},{... | collective-permute-start | bytes 147464 | tf_op jit(solution)/shard_map/ppermute | solution.py:394
  100.4 1.4 %collective-permute-done.15.refs_5_ = bf16[96,256]{1,0:T(8,128)(2,1)S(1)} collective-permute-done((bf16[96,256]{1,0:T(8,128)(2,1)S(1)}, bf16[96,256]{1,0:T(8,128)(2,1)S(1)}, u32[]{:S(2)}, u32[]{:S(2)}) %collective-permute-start.15) | collective-permute-done | bytes 49184 | tf_op jit(solution)/shard_map/ppermute | solution.py:394
  101.7 0.9 collective-permute-done.16.refs_6_
  102.6 0.7 collective-permute-done.17.refs_7_
  103.4 1.0 shard_map.85
  (24 shorter events, 0.7 us)
Async XLA Ops:
  2.1 17.4 %copy-start = (f32[256,512]{1,0:T(8,128)S(1)}, f32[256,512]{1,0:T(8,128)}, u32[]{:S(2)}) copy-start(f32[256,512]{1,0:T(8,128)} %field_ref.3) | copy-start | bytes 1572868
  2.1 17.4 %copy-start.1 = (s32[256,512]{1,0:T(8,128)S(1)}, s32[256,512]{1,0:T(8,128)}, u32[]{:S(2)}) copy-start(s32[256,512]{1,0:T(8,128)} %mask_ref.3) | copy-start | bytes 1572868
  2.1 17.4 %copy-start.2 = (f32[256,512]{1,0:T(8,128)S(1)}, f32[256,512]{1,0:T(8,128)}, u32[]{:S(2)}) copy-start(f32[256,512]{1,0:T(8,128)} %visc_ref.3) | copy-start | bytes 1572868
  2.1 10.8 %collective-permute-start = (f32[8,512]{1,0:T(8,128)}, f32[8,512]{1,0:T(8,128)S(1)}, u32[]{:S(2)}, u32[]{:S(2)}) collective-permute-start(f32[8,512]{1,0:T(8,128)} %get-tuple-element.41), channel_id=1, source_target_pairs={{0,4},{4,8},{8,12},{12,16},{16,20},{20,24},{24,28},{1,5},{5,9},{9,... | collective-permute-start | bytes 49160 | tf_op jit(solution)/shard_map/ppermute | solution.py:200
  7.1 5.8 %collective-permute-start.1 = (f32[8,512]{1,0:T(8,128)}, f32[8,512]{1,0:T(8,128)S(1)}, u32[]{:S(2)}, u32[]{:S(2)}) collective-permute-start(f32[8,512]{1,0:T(8,128)} %get-tuple-element.42), channel_id=1, source_target_pairs={{4,0},{8,4},{12,8},{16,12},{20,16},{24,20},{28,24},{5,1},{9,5},{13... | collective-permute-start | bytes 49160 | tf_op jit(solution)/shard_map/ppermute | solution.py:200
  8.4 17.5 %copy-start.3 = (s32[128]{0:T(128)S(1)}, s32[128]{0:T(128)}, u32[]{:S(2)}) copy-start(s32[128]{0:T(128)} %param.9) | copy-start | bytes 1540
  12.9 40.2 %copy-start.4 = (s32[256,512]{1,0:T(8,128)S(1)}, s32[256,512]{1,0:T(8,128)}, u32[]{:S(2)}) copy-start(s32[256,512]{1,0:T(8,128)} %get-tuple-element.54.refs_0_) | copy-start | bytes 1572868
  12.9 40.1 %collective-permute-start.4 = (s32[256,512]{1,0:T(8,128)}, s32[256,512]{1,0:T(8,128)S(1)}, u32[]{:S(2)}, u32[]{:S(2)}) collective-permute-start(s32[256,512]{1,0:T(8,128)} %get-tuple-element.55), channel_id=1, source_target_pairs={{0,4},{4,8},{8,12},{12,0},{16,20},{20,24},{24,28},{28,16},{1,5},{5... | collective-permute-start | bytes 1572872 | tf_op jit(solution)/shard_map/ppermute | solution.py:394
  15.6 37.4 %collective-permute-start.5 = (s32[256,512]{1,0:T(8,128)}, s32[256,512]{1,0:T(8,128)S(1)}, u32[]{:S(2)}, u32[]{:S(2)}) collective-permute-start(s32[256,512]{1,0:T(8,128)} %get-tuple-element.56), channel_id=1, source_target_pairs={{0,8},{4,12},{8,0},{12,4},{16,24},{20,28},{24,16},{28,20},{1,9},{5... | collective-permute-start | bytes 1572872 | tf_op jit(solution)/shard_map/ppermute | solution.py:394
  17.2 35.9 %collective-permute-start.6 = (s32[256,512]{1,0:T(8,128)}, s32[256,512]{1,0:T(8,128)S(1)}, u32[]{:S(2)}, u32[]{:S(2)}) collective-permute-start(s32[256,512]{1,0:T(8,128)} %get-tuple-element.57), channel_id=1, source_target_pairs={{0,12},{4,0},{8,4},{12,8},{16,28},{20,16},{24,20},{28,24},{1,13},{... | collective-permute-start | bytes 1572872 | tf_op jit(solution)/shard_map/ppermute | solution.py:394
  19.7 2.6 %collective-permute-start.2 = (f32[8,384]{1,0:T(8,128)S(1)}, f32[8,384]{1,0:T(8,128)S(1)}, u32[]{:S(2)}, u32[]{:S(2)}) collective-permute-start(f32[8,384]{1,0:T(8,128)S(1)} %get-tuple-element.51), channel_id=1, source_target_pairs={{0,1},{1,2},{2,3},{4,5},{5,6},{6,7},{8,9},{9,10},{10,11},{12,13},{... | collective-permute-start | bytes 36872 | tf_op jit(solution)/shard_map/ppermute | solution.py:200
  21.0 4.8 %collective-permute-start.3 = (f32[8,384]{1,0:T(8,128)S(1)}, f32[8,384]{1,0:T(8,128)S(1)}, u32[]{:S(2)}, u32[]{:S(2)}) collective-permute-start(f32[8,384]{1,0:T(8,128)S(1)} %get-tuple-element.52), channel_id=1, source_target_pairs={{1,0},{2,1},{3,2},{5,4},{6,5},{7,6},{9,8},{10,9},{11,10},{13,12},{... | collective-permute-start | bytes 36872 | tf_op jit(solution)/shard_map/ppermute | solution.py:200
  44.8 4.6 %collective-permute-start.7 = (f32[4,4,128]{2,1,0:T(4,128)S(1)}, f32[4,4,128]{2,1,0:T(4,128)S(1)}, u32[]{:S(2)}, u32[]{:S(2)}) collective-permute-start(f32[4,4,128]{2,1,0:T(4,128)S(1)} %all-gather.1.refs_4_), channel_id=1, source_target_pairs={{0,4},{4,8},{8,12},{12,0},{16,20},{20,24},{24,28},{28,16},{1,5},{5... | collective-permute-start | bytes 24584 | tf_op jit(solution)/shard_map/ppermute | solution.py:394
  44.8 4.6 %collective-permute-start.8 = (f32[4,4,128]{2,1,0:T(4,128)S(1)}, f32[4,4,128]{2,1,0:T(4,128)S(1)}, u32[]{:S(2)}, u32[]{:S(2)}) collective-permute-start(f32[4,4,128]{2,1,0:T(4,128)S(1)} %all-gather.1.refs_4_), channel_id=1, source_target_pairs={{0,8},{4,12},{8,0},{12,4},{16,24},{20,28},{24,16},{28,20},{1,9},{5... | collective-permute-start | bytes 24584 | tf_op jit(solution)/shard_map/ppermute | solution.py:394
  49.4 3.7 %collective-permute-start.9 = (f32[4,4,128]{2,1,0:T(4,128)S(1)}, f32[4,4,128]{2,1,0:T(4,128)S(1)}, u32[]{:S(2)}, u32[]{:S(2)}) collective-permute-start(f32[4,4,128]{2,1,0:T(4,128)S(1)} %all-gather.1.refs_4_), channel_id=1, source_target_pairs={{0,12},{4,0},{8,4},{12,8},{16,28},{20,16},{24,20},{28,24},{1,13},{... | collective-permute-start | bytes 24584 | tf_op jit(solution)/shard_map/ppermute | solution.py:394
  69.7 19.7 %collective-permute-start.11 = (bf16[4,160,256]{2,1,0:T(8,128)(2,1)S(1)}, bf16[4,160,256]{2,1,0:T(8,128)(2,1)S(1)}, u32[]{:S(2)}, u32[]{:S(2)}) collective-permute-start(bf16[4,160,256]{2,1,0:T(8,128)(2,1)S(1)} %get-tuple-element.61), channel_id=1, source_target_pairs={{0,16},{4,20},{8,24},{12,28},{16,0},{20,4},{24,8},{28,12},{1,17},{... | collective-permute-start | bytes 983048 | tf_op jit(solution)/shard_map/ppermute | solution.py:411
  82.5 11.1 %collective-permute-start.10 = (bf16[4,96,256]{2,1,0:T(8,128)(2,1)S(1)}, bf16[4,96,256]{2,1,0:T(8,128)(2,1)S(1)}, u32[]{:S(2)}, u32[]{:S(2)}) collective-permute-start(bf16[4,96,256]{2,1,0:T(8,128)(2,1)S(1)} %get-tuple-element.59), channel_id=1, source_target_pairs={{0,16},{4,20},{8,24},{12,28},{16,0},{20,4},{24,8},{28,12},{1,17},{... | collective-permute-start | bytes 589832 | tf_op jit(solution)/shard_map/ppermute | solution.py:411
  89.4 6.3 %collective-permute-start.12 = (bf16[160,256]{1,0:T(8,128)(2,1)S(1)}, bf16[160,256]{1,0:T(8,128)(2,1)S(1)}, u32[]{:S(2)}, u32[]{:S(2)}) collective-permute-start(bf16[160,256]{1,0:T(8,128)(2,1)S(1)} %get-tuple-element.63), channel_id=1, source_target_pairs={{0,4},{4,8},{8,12},{12,0},{16,20},{20,24},{24,28},{28,16},{1,5},{5... | collective-permute-start | bytes 245768 | tf_op jit(solution)/shard_map/ppermute | solution.py:394
  90.9 5.2 %collective-permute-start.13 = (bf16[160,256]{1,0:T(8,128)(2,1)S(1)}, bf16[160,256]{1,0:T(8,128)(2,1)S(1)}, u32[]{:S(2)}, u32[]{:S(2)}) collective-permute-start(bf16[160,256]{1,0:T(8,128)(2,1)S(1)} %get-tuple-element.64), channel_id=1, source_target_pairs={{0,8},{4,12},{8,0},{12,4},{16,24},{20,28},{24,16},{28,20},{1,9},{5... | collective-permute-start | bytes 245768 | tf_op jit(solution)/shard_map/ppermute | solution.py:394
  90.9 5.8 %collective-permute-start.14 = (bf16[160,256]{1,0:T(8,128)(2,1)S(1)}, bf16[160,256]{1,0:T(8,128)(2,1)S(1)}, u32[]{:S(2)}, u32[]{:S(2)}) collective-permute-start(bf16[160,256]{1,0:T(8,128)(2,1)S(1)} %get-tuple-element.65), channel_id=1, source_target_pairs={{0,12},{4,0},{8,4},{12,8},{16,28},{20,16},{24,20},{28,24},{1,13},{... | collective-permute-start | bytes 245768 | tf_op jit(solution)/shard_map/ppermute | solution.py:394
  96.7 5.0 %collective-permute-start.15 = (bf16[96,256]{1,0:T(8,128)(2,1)S(1)}, bf16[96,256]{1,0:T(8,128)(2,1)S(1)}, u32[]{:S(2)}, u32[]{:S(2)}) collective-permute-start(bf16[96,256]{1,0:T(8,128)(2,1)S(1)} %get-tuple-element.73), channel_id=1, source_target_pairs={{0,4},{4,8},{8,12},{12,0},{16,20},{20,24},{24,28},{28,16},{1,5},{5... | collective-permute-start | bytes 147464 | tf_op jit(solution)/shard_map/ppermute | solution.py:394
  98.6 4.1 %collective-permute-start.16 = (bf16[96,256]{1,0:T(8,128)(2,1)S(1)}, bf16[96,256]{1,0:T(8,128)(2,1)S(1)}, u32[]{:S(2)}, u32[]{:S(2)}) collective-permute-start(bf16[96,256]{1,0:T(8,128)(2,1)S(1)} %get-tuple-element.74), channel_id=1, source_target_pairs={{0,8},{4,12},{8,0},{12,4},{16,24},{20,28},{24,16},{28,20},{1,9},{5... | collective-permute-start | bytes 147464 | tf_op jit(solution)/shard_map/ppermute | solution.py:394
  99.3 4.1 %collective-permute-start.17 = (bf16[96,256]{1,0:T(8,128)(2,1)S(1)}, bf16[96,256]{1,0:T(8,128)(2,1)S(1)}, u32[]{:S(2)}, u32[]{:S(2)}) collective-permute-start(bf16[96,256]{1,0:T(8,128)(2,1)S(1)} %get-tuple-element.75), channel_id=1, source_target_pairs={{0,12},{4,0},{8,4},{12,8},{16,28},{20,16},{24,20},{28,24},{1,13},{... | collective-permute-start | bytes 147464 | tf_op jit(solution)/shard_map/ppermute | solution.py:394

commit v4 on v3

--- a/solution.py
+++ b/solution.py
@@ -15,6 +15,7 @@
 LANES = 128
 EDGE = 2 * STEPS
 PAD = 16
+STRIP = 32
 AMP_SCALE = 4096.0
 LAST = 6
 VMEM = pl.BlockSpec(memory_space=pltpu.VMEM)
@@ -29,8 +30,16 @@
     return pl.CostEstimate(flops=flops, bytes_accessed=size, transcendentals=0)
 
 
-def pack_kernel(me_ref, amp_ref, bin_ref, *refs):
+def pack_kernel(cols, me_ref, cell_ref, amp_ref, bin_ref, place_ref, *refs):
     outs, turned = refs[:-1], refs[-1]
+    cell = cell_ref[...]
+    row = lax.div(cell, cols)
+    col = cell - row * cols
+    panel = lax.broadcasted_iota(jnp.int32, cell.shape, 1)
+    place_ref[0:1] = col // LANES
+    place_ref[1:2] = row // 8 * 8 + PAD
+    place_ref[2:3] = row & 7
+    place_ref[3:4] = (panel - col) & (LANES - 1)
     scaled = (amp_ref[...].astype(F32) * AMP_SCALE).astype(jnp.int32)
     turned[...] = jnp.transpose((scaled << 16) | bin_ref[...])
     width = outs[0].shape[0]
@@ -39,21 +48,24 @@
         out[...] = turned[pl.ds(first, width), :]
 
 
-def pack(me, amplitude, delay_bin, members):
+def pack(me, panel_cell, cols, amplitude, delay_bin, members):
     panels, observers = amplitude.shape
+    cells = panel_cell.reshape(1, -1)
     width = observers // members
     block = pl.BlockSpec((LANES, observers), lambda i: (i, 0))
     out = jax.ShapeDtypeStruct((width, panels), jnp.int32)
-    return pl.pallas_call(
-        pack_kernel,
+    whole = pl.BlockSpec(cells.shape, lambda i: (0, 0))
+    return pl.pallas_call(
+        functools.partial(pack_kernel, cols),
         grid=(panels // LANES,),
-        in_specs=[SMEM, block, block],
-        out_specs=[pl.BlockSpec((width, LANES), lambda i: (0, i))] * members,
-        out_shape=[out] * members,
+        in_specs=[SMEM, whole, block, block],
+        out_specs=[pl.BlockSpec((4, cells.shape[1]), lambda i: (0, 0))]
+        + [pl.BlockSpec((width, LANES), lambda i: (0, i))] * members,
+        out_shape=[jax.ShapeDtypeStruct((4, cells.shape[1]), jnp.int32)] + [out] * members,
         scratch_shapes=[pltpu.VMEM((observers, LANES), jnp.int32)],
         compiler_params=params(56),
         cost_estimate=cost(panels * observers, 10 * panels * observers),
-    )(me, amplitude, delay_bin)
+    )(me, cells, amplitude, delay_bin)
 
 
 def coded(mask, visc):
@@ -102,78 +114,84 @@
 ):
     rows, cols = field_ref.shape
     panels = sample_ref.shape[1]
-    height, width = visc.shape
+    tiles, height, _ = visc.shape
     wide[...] = jnp.zeros_like(wide)
-    blank = jnp.zeros((PAD, width), F32)
     for part, buf in enumerate((fields.at[0], visc)):
         halo = slice(part * STEPS, (part + 1) * STEPS)
         wide[:STEPS] = north_ref[halo]
         wide[LANES - STEPS :] = south_ref[halo]
         side = jnp.transpose(wide[...])
-        buf[:PAD] = blank
-        buf[PAD + rows :] = blank
-        if part:
-            buf[PAD : PAD + rows, :cols] = coded(mask_ref[...], visc_ref[...])
-        else:
-            buf[PAD : PAD + rows, :cols] = field_ref[...]
-        buf[PAD + rows : PAD + rows + STEPS, :cols] = after_ref[halo]
-        buf[PAD - STEPS : PAD, :cols] = before_ref[halo]
-        buf[PAD : PAD + rows, cols:] = side[:rows]
-        buf[PAD + rows : PAD + rows + STEPS, cols:] = side[rows : rows + STEPS]
-        buf[PAD - STEPS : PAD, cols:] = side[rows + STEPS : rows + EDGE]
-
-    strip = 16
+        for k in range(tiles):
+            at = slice(k * LANES, (k + 1) * LANES)
+            buf[k, :PAD] = jnp.zeros((PAD, LANES), F32)
+            buf[k, PAD + rows :] = jnp.zeros((height - PAD - rows, LANES), F32)
+            if k == tiles - 1:
+                inside, before, after = (
+                    side[:rows],
+                    side[rows + STEPS : rows + EDGE],
+                    side[rows : rows + STEPS],
+                )
+            else:
+                inside = coded(mask_ref[:, at], visc_ref[:, at]) if part else field_ref[:, at]
+                before, after = before_ref[halo, at], after_ref[halo, at]
+            buf[k, PAD : PAD + rows] = inside
+            buf[k, PAD - STEPS : PAD] = before
+            buf[k, PAD + rows : PAD + rows + STEPS] = after
+
+    first_lane = lax.broadcasted_iota(jnp.int32, (STRIP, LANES), 1) == 0
+    last_lane = lax.broadcasted_iota(jnp.int32, (STRIP, LANES), 1) == LANES - 1
     for step in range(STEPS):
         old, new = fields.at[step], fields.at[step + 1]
-        new[:8] = jnp.zeros((8, width), F32)
-        new[height - 8 :] = jnp.zeros((8, width), F32)
+        for k in range(tiles):
+            new[k, :8] = jnp.zeros((8, LANES), F32)
+            new[k, height - 8 :] = jnp.zeros((8, LANES), F32)
 
         def one_strip(i, carry):
-            top = pl.multiple_of(i * strip, 8)
-            window = old[pl.ds(top, strip + 16), :]
-            base = visc[pl.ds(top + 8, strip), :]
-            center = window[8 : 8 + strip]
-            west = pltpu.roll(window, 1, 0)[8 : 8 + strip]
-            east = pltpu.roll(window, strip + 15, 0)[8 : 8 + strip]
-            south = pltpu.roll(center, 1, 1)
-            north = pltpu.roll(center, width - 1, 1)
-            diff_x = east - west
-            diff_y = north - south
-            square = diff_x * diff_x + diff_y * diff_y
-            norm = square * lax.rsqrt(jnp.maximum(square, 1e-37))
-            viscosity = base + 0.05 * norm / (2.0 + norm)
-            around = (east + west) + (north + south)
-            update = 0.75 * center + 0.15 * west + 0.1 * south
-            update = update + viscosity * (around - 4.0 * center)
-            new[pl.ds(top + 8, strip), :] = jnp.where(base > 0.0, update, 0.0)
+            top = pl.multiple_of(i * STRIP, 8)
+            centers = [old[k, pl.ds(top + 8, STRIP), :] for k in range(tiles)]
+            right = [pltpu.roll(x, 1, 1) for x in centers]
+            left = [pltpu.roll(x, LANES - 1, 1) for x in centers]
+            for k in range(tiles):
+                window = old[k, pl.ds(top, STRIP + 16), :]
+                base = visc[k, pl.ds(top + 8, STRIP), :]
+                center = centers[k]
+                west = pltpu.roll(window, 1, 0)[8 : 8 + STRIP]
+                east = pltpu.roll(window, STRIP + 15, 0)[8 : 8 + STRIP]
+                south = jnp.where(first_lane, right[k - 1], right[k])
+                north = jnp.where(last_lane, left[(k + 1) % tiles], left[k])
+                diff_x = east - west
+                diff_y = north - south
+                square = diff_x * diff_x + diff_y * diff_y
+                norm = square * lax.rsqrt(jnp.maximum(square, 1e-37))
+                viscosity = base + 0.05 * norm / (2.0 + norm)
+                around = (east + west) + (north + south)
+                update = 0.75 * center + 0.15 * west + 0.1 * south
+                update = update + viscosity * (around - 4.0 * center)
+                new[k, pl.ds(top + 8, STRIP), :] = jnp.where(base > 0.0, update, 0.0)
             return carry
 
-        lax.fori_loop(0, (height - 16) // strip, one_strip, 0)
-    end_ref[...] = fields[STEPS, PAD : PAD + rows, :cols]
+        strips = (height - 16) // STRIP
+        lax.fori_loop(0, strips, one_strip, 0, unroll=strips)
+    for k in range(tiles - 1):
+        end_ref[:, k * LANES : (k + 1) * LANES] = fields[STEPS, k, PAD : PAD + rows, :]
 
     lane = lax.broadcasted_iota(jnp.int32, (8, LANES), 1)
     line = lax.broadcasted_iota(jnp.int32, (8, LANES), 0)
     for base in range(0, panels, LANES):
 
         def one_panel(k, found):
-            cell = cell_ref[0, base + k]
-            row = cell // cols
-            col = cell - row * cols
-            top = pl.multiple_of(row // 8 * 8 + PAD, 8)
-            left = pl.multiple_of(col // LANES * LANES, LANES)
-            here = (lane == k) & (line == row % 8)
-            turn = (k - col) & (LANES - 1)
+            tile, top, row, turn = [cell_ref[c, base + k] for c in range(4)]
+            top = pl.multiple_of(top, 8)
+            here = (lane == k) & (line == row)
             return tuple(
                 jnp.where(
-                    here,
-                    pltpu.roll(fields[t + 1, pl.ds(top, 8), pl.ds(left, LANES)], turn, 1),
-                    found[t],
+                    here, pltpu.roll(fields[t + 1, tile, pl.ds(top, 8), :], turn, 1), found[t]
                 )
                 for t in range(STEPS)
             )
 
         none = (jnp.zeros((8, LANES), F32),) * STEPS
-        found = lax.fori_loop(0, LANES, one_panel, none, unroll=8)
+        found = lax.fori_loop(0, LANES, one_panel, none, unroll=32)
         for t in range(STEPS):
             sample_ref[t : t + 1, base : base + LANES] = jnp.sum(found[t], axis=0, keepdims=True)
 
@@ -200,7 +218,7 @@
     return lax.ppermute(last, axis, up), lax.ppermute(first, axis, down)
 
 
-def field_window(field, mask, visc, before, after, panel_cell):
+def field_window(field, mask, visc, before, after, places):
     rows, cols = field.shape
     tall = -(-(rows + EDGE) // LANES) * LANES
     edge_cols = jax.ShapeDtypeStruct((EDGE, tall), F32)
@@ -215,9 +233,9 @@
         cost_estimate=cost(rows * cols, 4 * rows * cols),
     )(field, mask, visc, before, after)
     south, north = shifted("panel", first, last)
-    panels = panel_cell.shape[0]
-    cells = panel_cell.reshape(1, panels)
-    height, width = rows + 2 * PAD, cols + LANES
+    panels = places.shape[1]
+    tiles = cols // LANES + 1
+    height = 16 + -(-(rows + 2 * PAD - 16) // STRIP) * STRIP
     return pl.pallas_call(
         step_kernel,
         in_specs=[SMEM] + [VMEM] * 7,
@@ -227,13 +245,13 @@
             jax.ShapeDtypeStruct((STEPS, panels), F32),
         ],
         scratch_shapes=[
-            pltpu.VMEM((STEPS + 1, height, width), F32),
-            pltpu.VMEM((height, width), F32),
+            pltpu.VMEM((STEPS + 1, tiles, height, LANES), F32),
+            pltpu.VMEM((tiles, height, LANES), F32),
             pltpu.VMEM((LANES, tall), F32),
         ],
         compiler_params=params(24),
         cost_estimate=cost(100 * rows * cols, 800 * rows * cols),
-    )(cells, field, mask, visc, before, after, south, north)
+    )(places, field, mask, visc, before, after, south, north)
 
 
 def bin_kernel(half_ref, *refs):
@@ -371,14 +389,39 @@
     )(me, keep, got)
 
 
-def place_kernel(firsts, width, me_ref, *refs):
-    out_ref, members = refs[-1], (len(refs) - 1) // len(firsts)
-    for c, first in enumerate(firsts):
-        for k in range(members):
-            ref = refs[c * members + k]
-            owner = lax.rem(me_ref[0] - k + members, members)
-            start = pl.multiple_of(owner * width + first, 16)
-            out_ref[pl.ds(start, ref.shape[0]), :] = ref[...].astype(F32)
+def place_kernel(first, width, me_ref, *refs):
+    members, count, _ = refs[-2].shape
+    pieces, (out_ref, wide, sems) = refs[:members], refs[-3:]
+    copies = []
+    for k, ref in enumerate(pieces):
+        owner = lax.rem(me_ref[0] - k + members, members)
+        start = pl.multiple_of(owner * width + first, 16)
+        wide[k] = ref[...].astype(F32)
+        copies.append(
+            pltpu.make_async_copy(wide.at[k], out_ref.at[pl.ds(start, count), :], sems.at[k])
+        )
+        copies[-1].start()
+    for copy in copies:
+        copy.wait()
+
+
+def place(me, pieces, signals, first, width):
+    members = len(pieces)
+    count, bins = pieces[0].shape
+    before = [] if signals is None else [signals]
+    return pl.pallas_call(
+        functools.partial(place_kernel, first, width),
+        in_specs=[SMEM] + [VMEM] * members + [pl.BlockSpec(memory_space=pl.ANY)] * len(before),
+        out_specs=pl.BlockSpec(memory_space=pl.ANY),
+        out_shape=jax.ShapeDtypeStruct((width * members, bins), F32),
+        input_output_aliases={members + 1: 0} if before else {},
+        scratch_shapes=[
+            pltpu.VMEM((members, count, bins), F32),
+            pltpu.SemaphoreType.DMA((members,)),
+        ],
+        compiler_params=params(16),
+        cost_estimate=cost(members * count * bins, 6 * members * count * bins),
+    )(me, *pieces, *before)
 
 
 def on_device(field_start, fluid_mask, base_visc, panel_cell, amplitude, delay_bin):
@@ -396,31 +439,33 @@
     ends = edges(field_start, fluid_mask, base_visc)
     amplitude, delay_bin, *ends = lax.optimization_barrier((amplitude, delay_bin, *ends))
     before, after = shifted("box", *ends)
-    packed = pack(me, amplitude, delay_bin, members)
+    places, *packed = pack(
+        me, panel_cell, field_start.shape[1], amplitude, delay_bin, members
+    )
     before, after, *packed = lax.optimization_barrier((before, after, *packed))
     words = spread(packed)
     field, sample = field_window(
-        field_start, fluid_mask, base_visc, before, after, panel_cell
+        field_start, fluid_mask, base_visc, before, after, places
     )
     samples = spread([lax.all_gather(sample, "panel")] * members)
     observers = words[0].shape[0]
     across = [(i, (i + members) % peers) for i in range(peers)]
-    pieces, firsts, first = [], [], 0
+    first, joined, signals = 0, None, None
+    waiting = []
     for count in sizes(observers):
         keep, send = binned(half, words, samples, first, count)
         got = lax.ppermute(send, "box", across)
-        if pieces:
-            got, *pieces = lax.optimization_barrier((got, *pieces))
-        pieces += spread(join(me, keep, got))
-        firsts.append(first)
+        if joined:
+            pieces = spread(joined)
+            got, pieces[members // 2] = lax.optimization_barrier((got, pieces[members // 2]))
+            waiting.append(pieces)
+        joined = join(me, keep, got)
         first += count
-    signals = pl.pallas_call(
-        functools.partial(place_kernel, firsts, observers),
-        in_specs=[SMEM] + [VMEM] * len(pieces),
-        out_specs=VMEM,
-        out_shape=jax.ShapeDtypeStruct((observers * members, pieces[0].shape[1]), F32),
-        compiler_params=params(16),
-    )(me, *pieces)
+    waiting.append(spread(joined))
+    first = 0
+    for pieces in waiting:
+        signals = place(me, pieces, signals, first, observers)
+        first += pieces[0].shape[0]
     return (field, signals)
 
 

time: 105 us -> 96.2 us (0.916)
  Pallas kernels: 46.5 us -> 40.4 us
  waiting for transfers between devices: 24 us -> 21.3 us
    pallas_call x1, Pallas kernels: 12.4 us -> 5.62 us  [field_window(): pl.pallas_call(step_kernel, in_specs=[SMEM] + [VMEM] * 7, out_specs=[VMEM...]
    ppermute x12, waiting for transfers between devices: 13.7 us -> 11.2 us  [spread(): lax.ppermute(x, 'box', perm(k))]
    pallas_call x2 -> x3, Pallas kernels: 5.51 us -> 6.13 us  [the longest x1 4.47 us: pack(): pl.pallas_call(functools.partial(pack_kernel, cols), grid=(panels // LANE...]
  transfers between devices with their start and end apart: 18 -> 18, of which waited for: 11 -> 9; matrix products, arithmetic and copies ran while one was open for 0% -> 0% of each run, Pallas kernels for 26% -> 22%
where the time goes in v4:
time: 96.2 us; the launch traced here: 95.8 us
  Pallas kernels  40.4 us (42%)
  starting transfers between devices  25.9 us (27%)
  waiting for transfers between devices  21.3 us (22%)
  blocking collectives  6.74 us (7%)
    pallas_call x2, Pallas kernels, binned(): pl.pallas_call(bin_kernel, grid=(count // block,), in_specs=[SMEM] + [pl....  26.9 us
    ppermute x12, starting transfers between devices, spread(): lax.ppermute(x, 'box', perm(k))  14 us
    ppermute x12, waiting for transfers between devices, spread(): lax.ppermute(x, 'box', perm(k))  11.2 us
    ppermute x4, starting transfers between devices, shifted(): return (lax.ppermute(last, axis, up), lax.ppermute(first, axis, down))  8.88 us
    all_gather x1, blocking collectives, on_device(): samples = spread([lax.all_gather(sample, 'panel')] * members)  6.74 us
    ppermute x2, waiting for transfers between devices, on_device(): got = lax.ppermute(send, 'box', across)  6.57 us
    pallas_call x1, Pallas kernels, field_window(): pl.pallas_call(step_kernel, in_specs=[SMEM] + [VMEM] * 7, out_specs=[VMEM...  5.62 us
    pallas_call x1, Pallas kernels, pack(): pl.pallas_call(functools.partial(pack_kernel, cols), grid=(panels // LANE...  4.47 us
  transfers between devices with their start and end apart: 18, of which 9 were waited for; matrix products, arithmetic and copies ran while one was open for 0% of the time, Pallas kernels for 22%

profile of v4, /device:TPU:0, one launch (start us, length us, event | category | flops | bytes accessed | tf_op | source)
XLA Modules:
  0.0 95.8 jit_solution(7944835276662337757)
XLA Ops:
  0.6 1.4 %shard_map.77 = (f32[8,512]{1,0:T(8,128)}, f32[8,512]{1,0:T(8,128)}) custom-call(f32[256,512]{1,0:T(8,128)} %field_ref.3, s32[256,512]{1,0:T(8,128)} %mask_ref.3, f32[256,512]{1,0:T(8,128)} %visc_ref.3, f32[256,512]{1,0:T(8,128)} %field_ref.3, s32[256,512]{1,0:T(8,128)} %mask_ref.3, f32[256,512]{1,0:T(8,128)} %visc_ref.3), custom_call_target="tpu_custom_call" | custom-call | flops 8192 | bytes 131072 | tf_op jit(solution)/shard_map/pallas_call | solution.py:202
  2.1 5.0 %collective-permute-start = (f32[8,512]{1,0:T(8,128)}, f32[8,512]{1,0:T(8,128)S(1)}, u32[]{:S(2)}, u32[]{:S(2)}) collective-permute-start(f32[8,512]{1,0:T(8,128)} %get-tuple-element.42), channel_id=1, source_target_pairs={{0,4},{4,8},{8,12},{12,16},{16,20},{20,24},{24,28},{1,5},{5,9},{9,... | collective-permute-start | bytes 49160 | tf_op jit(solution)/shard_map/ppermute | solution.py:218
  7.1 1.3 %collective-permute-start.1 = (f32[8,512]{1,0:T(8,128)}, f32[8,512]{1,0:T(8,128)S(1)}, u32[]{:S(2)}, u32[]{:S(2)}) collective-permute-start(f32[8,512]{1,0:T(8,128)} %get-tuple-element.43), channel_id=1, source_target_pairs={{4,0},{8,4},{12,8},{16,12},{20,16},{24,20},{28,24},{5,1},{9,5},{13... | collective-permute-start | bytes 49160 | tf_op jit(solution)/shard_map/ppermute | solution.py:218
  8.4 4.5 %shard_map.78 = (s32[4,128]{1,0:T(4,128)}, s32[256,512]{1,0:T(8,128)}, s32[256,512]{1,0:T(8,128)}, s32[256,512]{1,0:T(8,128)}, s32[256,512]{1,0:T(8,128)}) custom-call(s32[1]{0:T(128)S(6)} %rem.22.me_ref, s32[1,128]{1,0:T(1,128)} %bitcast.4, bf16[512,1024]{1,0:T(8,128)(2,1)} %amp_ref, s32[512,1024]{1,0:T(8,128)} %bin_ref), custom_call_target="tpu_custom_call" | custom-call | flops 524288 | bytes 5242880 | tf_op jit(solution)/shard_map/pallas_call | solution.py:58
  12.9 2.7 %collective-permute-start.4 = (s32[256,512]{1,0:T(8,128)}, s32[256,512]{1,0:T(8,128)S(1)}, u32[]{:S(2)}, u32[]{:S(2)}) collective-permute-start(s32[256,512]{1,0:T(8,128)} %get-tuple-element.54), channel_id=1, source_target_pairs={{0,4},{4,8},{8,12},{12,0},{16,20},{20,24},{24,28},{28,16},{1,5},{5... | collective-permute-start | bytes 1572872 | tf_op jit(solution)/shard_map/ppermute | solution.py:437
  15.6 1.6 %collective-permute-start.5 = (s32[256,512]{1,0:T(8,128)}, s32[256,512]{1,0:T(8,128)S(1)}, u32[]{:S(2)}, u32[]{:S(2)}) collective-permute-start(s32[256,512]{1,0:T(8,128)} %get-tuple-element.55), channel_id=1, source_target_pairs={{0,8},{4,12},{8,0},{12,4},{16,24},{20,28},{24,16},{28,20},{1,9},{5... | collective-permute-start | bytes 1572872 | tf_op jit(solution)/shard_map/ppermute | solution.py:437
  17.2 2.3 %collective-permute-start.6 = (s32[256,512]{1,0:T(8,128)}, s32[256,512]{1,0:T(8,128)S(1)}, u32[]{:S(2)}, u32[]{:S(2)}) collective-permute-start(s32[256,512]{1,0:T(8,128)} %get-tuple-element.56), channel_id=1, source_target_pairs={{0,12},{4,0},{8,4},{12,8},{16,28},{20,16},{24,20},{28,24},{1,13},{... | collective-permute-start | bytes 1572872 | tf_op jit(solution)/shard_map/ppermute | solution.py:437
  19.5 0.3 shard_map.79
  19.7 1.3 %collective-permute-start.2 = (f32[8,384]{1,0:T(8,128)S(1)}, f32[8,384]{1,0:T(8,128)S(1)}, u32[]{:S(2)}, u32[]{:S(2)}) collective-permute-start(f32[8,384]{1,0:T(8,128)S(1)} %get-tuple-element.50), channel_id=1, source_target_pairs={{0,1},{1,2},{2,3},{4,5},{5,6},{6,7},{8,9},{9,10},{10,11},{12,13},{... | collective-permute-start | bytes 36872 | tf_op jit(solution)/shard_map/ppermute | solution.py:218
  21.0 1.3 %collective-permute-start.3 = (f32[8,384]{1,0:T(8,128)S(1)}, f32[8,384]{1,0:T(8,128)S(1)}, u32[]{:S(2)}, u32[]{:S(2)}) collective-permute-start(f32[8,384]{1,0:T(8,128)S(1)} %get-tuple-element.51), channel_id=1, source_target_pairs={{1,0},{2,1},{3,2},{5,4},{6,5},{7,6},{9,8},{10,9},{11,10},{13,12},{... | collective-permute-start | bytes 36872 | tf_op jit(solution)/shard_map/ppermute | solution.py:218
  22.4 3.5 %collective-permute-done.3.north_ref = f32[8,384]{1,0:T(8,128)S(1)} collective-permute-done((f32[8,384]{1,0:T(8,128)S(1)}, f32[8,384]{1,0:T(8,128)S(1)}, u32[]{:S(2)}, u32[]{:S(2)}) %collective-permute-start.3) | collective-permute-done | bytes 12320 | tf_op jit(solution)/shard_map/ppermute | solution.py:218
  25.8 0.7 copy-done.3
  26.5 5.6 %shard_map.80 = (f32[256,512]{1,0:T(8,128)}, f32[4,128]{1,0:T(4,128)S(1)}) custom-call(s32[4,128]{1,0:T(4,128)S(1)} %copy-done.3, f32[256,512]{1,0:T(8,128)S(1)} %copy-done, s32[256,512]{1,0:T(8,128)S(1)} %copy-done.1, f32[256,512]{1,0:T(8,128)S(1)} %copy-done.2, f32[8,512]{1,0:T(8,128)S(1)} %collective-permute-done.before_ref, ...), custom_call_target="tpu_custom_call" | custom-call | flops 13107200 | bytes 104857600 | tf_op jit(solution)/shard_map/pallas_call | solution.py:239
  32.1 6.7 %all-gather.1.refs_4_ = f32[4,4,128]{2,1,0:T(4,128)S(1)} all-gather(f32[1,4,128]{2,1,0:T(4,128)S(1)} %bitcast.3), channel_id=2, replica_groups=mesh['box'=8,'panel'=4] {'panel'}, dimensions={0}, use_global_device_ids=true | all-gather | bytes 10240 | tf_op jit(solution)/shard_map/all_gather | solution.py:450
  38.9 0.6 collective-permute-start.8
  39.5 4.0 %collective-permute-done.7.refs_5_ = f32[4,4,128]{2,1,0:T(4,128)S(1)} collective-permute-done((f32[4,4,128]{2,1,0:T(4,128)S(1)}, f32[4,4,128]{2,1,0:T(4,128)S(1)}, u32[]{:S(2)}, u32[]{:S(2)}) %collective-permute-start.7) | collective-permute-done | bytes 8224 | tf_op jit(solution)/shard_map/ppermute | solution.py:437
  43.5 3.6 %collective-permute-done.9.refs_7_ = f32[4,4,128]{2,1,0:T(4,128)S(1)} collective-permute-done((f32[4,4,128]{2,1,0:T(4,128)S(1)}, f32[4,4,128]{2,1,0:T(4,128)S(1)}, u32[]{:S(2)}, u32[]{:S(2)}) %collective-permute-start.9) | collective-permute-done | bytes 8224 | tf_op jit(solution)/shard_map/ppermute | solution.py:437
  47.1 16.8 %shard_map.82 = (f32[4,160,256]{2,1,0:T(8,128)S(1)}, bf16[4,160,256]{2,1,0:T(8,128)(2,1)S(1)}) custom-call(s32[1]{0:T(128)S(6)} %select_n.5.half_ref, s32[256,512]{1,0:T(8,128)S(1)} %copy-done.4, s32[256,512]{1,0:T(8,128)S(1)} %collective-permute-done.4.refs_1_, s32[256,512]{1,0:T(8,128)S(1)} %collective-permute-done.5.refs_2_, ...), custom_call_target="tpu_custom_call" | custom-call | flops 21474836480 | bytes 2621440 | tf_op jit(solution)/shard_map/pallas_call | solution.py:351
  63.9 2.5 %collective-permute-start.11 = (bf16[4,160,256]{2,1,0:T(8,128)(2,1)S(1)}, bf16[4,160,256]{2,1,0:T(8,128)(2,1)S(1)}, u32[]{:S(2)}, u32[]{:S(2)}) collective-permute-start(bf16[4,160,256]{2,1,0:T(8,128)(2,1)S(1)} %get-tuple-element.61), channel_id=1, source_target_pairs={{0,16},{4,20},{8,24},{12,28},{16,0},{20,4},{24,8},{28,12},{1,17},{... | collective-permute-start | bytes 983048 | tf_op jit(solution)/shard_map/ppermute | solution.py:457
  66.4 10.1 %shard_map.81 = (f32[4,96,256]{2,1,0:T(8,128)S(1)}, bf16[4,96,256]{2,1,0:T(8,128)(2,1)S(1)}) custom-call(s32[1]{0:T(128)S(6)} %select_n.5.half_ref, s32[256,512]{1,0:T(8,128)S(1)} %copy-done.4, s32[256,512]{1,0:T(8,128)S(1)} %collective-permute-done.4.refs_1_, s32[256,512]{1,0:T(8,128)S(1)} %collective-permute-done.5.refs_2_, ...), custom_call_target="tpu_custom_call" | custom-call | flops 12884901888 | bytes 1572864 | tf_op jit(solution)/shard_map/pallas_call | solution.py:351
  76.5 0.5 collective-permute-start.10
  77.0 6.3 %collective-permute-done.11.got_ref = bf16[4,160,256]{2,1,0:T(8,128)(2,1)S(1)} collective-permute-done((bf16[4,160,256]{2,1,0:T(8,128)(2,1)S(1)}, bf16[4,160,256]{2,1,0:T(8,128)(2,1)S(1)}, u32[]{:S(2)}, u32[]{:S(2)}) %collective-permute-start.11) | collective-permute-done | bytes 327712 | tf_op jit(solution)/shard_map/ppermute | solution.py:457
  83.4 1.0 %collective-permute-start.12 = (bf16[160,256]{1,0:T(8,128)(2,1)S(1)}, bf16[160,256]{1,0:T(8,128)(2,1)S(1)}, u32[]{:S(2)}, u32[]{:S(2)}) collective-permute-start(bf16[160,256]{1,0:T(8,128)(2,1)S(1)} %get-tuple-element.62), channel_id=1, source_target_pairs={{0,8},{4,12},{8,0},{12,4},{16,24},{20,28},{24,16},{28,20},{1,9},{5... | collective-permute-start | bytes 245768 | tf_op jit(solution)/shard_map/ppermute | solution.py:437
  84.4 0.8 collective-permute-start.16
  85.2 2.1 %collective-permute-start.17 = (bf16[160,256]{1,0:T(8,128)(2,1)S(1)}, bf16[160,256]{1,0:T(8,128)(2,1)S(1)}, u32[]{:S(2)}, u32[]{:S(2)}) collective-permute-start(bf16[160,256]{1,0:T(8,128)(2,1)S(1)} %get-tuple-element.71), channel_id=1, source_target_pairs={{0,12},{4,0},{8,4},{12,8},{16,28},{20,16},{24,20},{28,24},{1,13},{... | collective-permute-start | bytes 245768 | tf_op jit(solution)/shard_map/ppermute | solution.py:437
  87.6 1.7 %collective-permute-done.12.refs_2_ = bf16[160,256]{1,0:T(8,128)(2,1)S(1)} collective-permute-done((bf16[160,256]{1,0:T(8,128)(2,1)S(1)}, bf16[160,256]{1,0:T(8,128)(2,1)S(1)}, u32[]{:S(2)}, u32[]{:S(2)}) %collective-permute-start.12) | collective-permute-done | bytes 81952 | tf_op jit(solution)/shard_map/ppermute | solution.py:437
  89.3 1.2 %collective-permute-start.13 = (bf16[96,256]{1,0:T(8,128)(2,1)S(1)}, bf16[96,256]{1,0:T(8,128)(2,1)S(1)}, u32[]{:S(2)}, u32[]{:S(2)}) collective-permute-start(bf16[96,256]{1,0:T(8,128)(2,1)S(1)} %get-tuple-element.65), channel_id=1, source_target_pairs={{0,4},{4,8},{8,12},{12,0},{16,20},{20,24},{24,28},{28,16},{1,5},{5... | collective-permute-start | bytes 147464 | tf_op jit(solution)/shard_map/ppermute | solution.py:437
  90.6 1.7 %collective-permute-start.15 = (bf16[96,256]{1,0:T(8,128)(2,1)S(1)}, bf16[96,256]{1,0:T(8,128)(2,1)S(1)}, u32[]{:S(2)}, u32[]{:S(2)}) collective-permute-start(bf16[96,256]{1,0:T(8,128)(2,1)S(1)} %get-tuple-element.67), channel_id=1, source_target_pairs={{0,12},{4,0},{8,4},{12,8},{16,28},{20,16},{24,20},{28,24},{1,13},{... | collective-permute-start | bytes 147464 | tf_op jit(solution)/shard_map/ppermute | solution.py:437
  92.3 0.9 shard_map.85.refs_4_
  93.2 1.2 %collective-permute-done.13.refs_1_ = bf16[96,256]{1,0:T(8,128)(2,1)S(1)} collective-permute-done((bf16[96,256]{1,0:T(8,128)(2,1)S(1)}, bf16[96,256]{1,0:T(8,128)(2,1)S(1)}, u32[]{:S(2)}, u32[]{:S(2)}) %collective-permute-start.13) | collective-permute-done | bytes 49184 | tf_op jit(solution)/shard_map/ppermute | solution.py:437
  94.4 0.7 collective-permute-done.14.refs_2_
  95.0 0.8 shard_map.86
  (25 shorter events, 0.5 us)
Async XLA Ops:
  2.1 17.4 %copy-start = (f32[256,512]{1,0:T(8,128)S(1)}, f32[256,512]{1,0:T(8,128)}, u32[]{:S(2)}) copy-start(f32[256,512]{1,0:T(8,128)} %field_ref.3) | copy-start | bytes 1572868
  2.1 17.4 %copy-start.1 = (s32[256,512]{1,0:T(8,128)S(1)}, s32[256,512]{1,0:T(8,128)}, u32[]{:S(2)}) copy-start(s32[256,512]{1,0:T(8,128)} %mask_ref.3) | copy-start | bytes 1572868
  2.1 17.4 %copy-start.2 = (f32[256,512]{1,0:T(8,128)S(1)}, f32[256,512]{1,0:T(8,128)}, u32[]{:S(2)}) copy-start(f32[256,512]{1,0:T(8,128)} %visc_ref.3) | copy-start | bytes 1572868
  2.1 10.8 %collective-permute-start = (f32[8,512]{1,0:T(8,128)}, f32[8,512]{1,0:T(8,128)S(1)}, u32[]{:S(2)}, u32[]{:S(2)}) collective-permute-start(f32[8,512]{1,0:T(8,128)} %get-tuple-element.42), channel_id=1, source_target_pairs={{0,4},{4,8},{8,12},{12,16},{16,20},{20,24},{24,28},{1,5},{5,9},{9,... | collective-permute-start | bytes 49160 | tf_op jit(solution)/shard_map/ppermute | solution.py:218
  7.1 5.8 %collective-permute-start.1 = (f32[8,512]{1,0:T(8,128)}, f32[8,512]{1,0:T(8,128)S(1)}, u32[]{:S(2)}, u32[]{:S(2)}) collective-permute-start(f32[8,512]{1,0:T(8,128)} %get-tuple-element.43), channel_id=1, source_target_pairs={{4,0},{8,4},{12,8},{16,12},{20,16},{24,20},{28,24},{5,1},{9,5},{13... | collective-permute-start | bytes 49160 | tf_op jit(solution)/shard_map/ppermute | solution.py:218
  12.9 34.3 %copy-start.4 = (s32[256,512]{1,0:T(8,128)S(1)}, s32[256,512]{1,0:T(8,128)}, u32[]{:S(2)}) copy-start(s32[256,512]{1,0:T(8,128)} %get-tuple-element.53.refs_0_) | copy-start | bytes 1572868
  12.9 34.2 %collective-permute-start.4 = (s32[256,512]{1,0:T(8,128)}, s32[256,512]{1,0:T(8,128)S(1)}, u32[]{:S(2)}, u32[]{:S(2)}) collective-permute-start(s32[256,512]{1,0:T(8,128)} %get-tuple-element.54), channel_id=1, source_target_pairs={{0,4},{4,8},{8,12},{12,0},{16,20},{20,24},{24,28},{28,16},{1,5},{5... | collective-permute-start | bytes 1572872 | tf_op jit(solution)/shard_map/ppermute | solution.py:437
  15.6 31.5 %collective-permute-start.5 = (s32[256,512]{1,0:T(8,128)}, s32[256,512]{1,0:T(8,128)S(1)}, u32[]{:S(2)}, u32[]{:S(2)}) collective-permute-start(s32[256,512]{1,0:T(8,128)} %get-tuple-element.55), channel_id=1, source_target_pairs={{0,8},{4,12},{8,0},{12,4},{16,24},{20,28},{24,16},{28,20},{1,9},{5... | collective-permute-start | bytes 1572872 | tf_op jit(solution)/shard_map/ppermute | solution.py:437
  17.2 29.9 %collective-permute-start.6 = (s32[256,512]{1,0:T(8,128)}, s32[256,512]{1,0:T(8,128)S(1)}, u32[]{:S(2)}, u32[]{:S(2)}) collective-permute-start(s32[256,512]{1,0:T(8,128)} %get-tuple-element.56), channel_id=1, source_target_pairs={{0,12},{4,0},{8,4},{12,8},{16,28},{20,16},{24,20},{28,24},{1,13},{... | collective-permute-start | bytes 1572872 | tf_op jit(solution)/shard_map/ppermute | solution.py:437
  19.7 2.6 %collective-permute-start.2 = (f32[8,384]{1,0:T(8,128)S(1)}, f32[8,384]{1,0:T(8,128)S(1)}, u32[]{:S(2)}, u32[]{:S(2)}) collective-permute-start(f32[8,384]{1,0:T(8,128)S(1)} %get-tuple-element.50), channel_id=1, source_target_pairs={{0,1},{1,2},{2,3},{4,5},{5,6},{6,7},{8,9},{9,10},{10,11},{12,13},{... | collective-permute-start | bytes 36872 | tf_op jit(solution)/shard_map/ppermute | solution.py:218
  21.0 4.8 %collective-permute-start.3 = (f32[8,384]{1,0:T(8,128)S(1)}, f32[8,384]{1,0:T(8,128)S(1)}, u32[]{:S(2)}, u32[]{:S(2)}) collective-permute-start(f32[8,384]{1,0:T(8,128)S(1)} %get-tuple-element.51), channel_id=1, source_target_pairs={{1,0},{2,1},{3,2},{5,4},{6,5},{7,6},{9,8},{10,9},{11,10},{13,12},{... | collective-permute-start | bytes 36872 | tf_op jit(solution)/shard_map/ppermute | solution.py:218
  25.8 0.7 copy-start.3
  38.9 4.6 %collective-permute-start.7 = (f32[4,4,128]{2,1,0:T(4,128)S(1)}, f32[4,4,128]{2,1,0:T(4,128)S(1)}, u32[]{:S(2)}, u32[]{:S(2)}) collective-permute-start(f32[4,4,128]{2,1,0:T(4,128)S(1)} %all-gather.1.refs_4_), channel_id=1, source_target_pairs={{0,4},{4,8},{8,12},{12,0},{16,20},{20,24},{24,28},{28,16},{1,5},{5... | collective-permute-start | bytes 24584 | tf_op jit(solution)/shard_map/ppermute | solution.py:437
  38.9 4.5 %collective-permute-start.8 = (f32[4,4,128]{2,1,0:T(4,128)S(1)}, f32[4,4,128]{2,1,0:T(4,128)S(1)}, u32[]{:S(2)}, u32[]{:S(2)}) collective-permute-start(f32[4,4,128]{2,1,0:T(4,128)S(1)} %all-gather.1.refs_4_), channel_id=1, source_target_pairs={{0,8},{4,12},{8,0},{12,4},{16,24},{20,28},{24,16},{28,20},{1,9},{5... | collective-permute-start | bytes 24584 | tf_op jit(solution)/shard_map/ppermute | solution.py:437
  43.5 3.7 %collective-permute-start.9 = (f32[4,4,128]{2,1,0:T(4,128)S(1)}, f32[4,4,128]{2,1,0:T(4,128)S(1)}, u32[]{:S(2)}, u32[]{:S(2)}) collective-permute-start(f32[4,4,128]{2,1,0:T(4,128)S(1)} %all-gather.1.refs_4_), channel_id=1, source_target_pairs={{0,12},{4,0},{8,4},{12,8},{16,28},{20,16},{24,20},{28,24},{1,13},{... | collective-permute-start | bytes 24584 | tf_op jit(solution)/shard_map/ppermute | solution.py:437
  63.9 19.4 %collective-permute-start.11 = (bf16[4,160,256]{2,1,0:T(8,128)(2,1)S(1)}, bf16[4,160,256]{2,1,0:T(8,128)(2,1)S(1)}, u32[]{:S(2)}, u32[]{:S(2)}) collective-permute-start(bf16[4,160,256]{2,1,0:T(8,128)(2,1)S(1)} %get-tuple-element.61), channel_id=1, source_target_pairs={{0,16},{4,20},{8,24},{12,28},{16,0},{20,4},{24,8},{28,12},{1,17},{... | collective-permute-start | bytes 983048 | tf_op jit(solution)/shard_map/ppermute | solution.py:457
  76.5 11.0 %collective-permute-start.10 = (bf16[4,96,256]{2,1,0:T(8,128)(2,1)S(1)}, bf16[4,96,256]{2,1,0:T(8,128)(2,1)S(1)}, u32[]{:S(2)}, u32[]{:S(2)}) collective-permute-start(bf16[4,96,256]{2,1,0:T(8,128)(2,1)S(1)} %get-tuple-element.59), channel_id=1, source_target_pairs={{0,16},{4,20},{8,24},{12,28},{16,0},{20,4},{24,8},{28,12},{1,17},{... | collective-permute-start | bytes 589832 | tf_op jit(solution)/shard_map/ppermute | solution.py:457
  83.4 5.9 %collective-permute-start.12 = (bf16[160,256]{1,0:T(8,128)(2,1)S(1)}, bf16[160,256]{1,0:T(8,128)(2,1)S(1)}, u32[]{:S(2)}, u32[]{:S(2)}) collective-permute-start(bf16[160,256]{1,0:T(8,128)(2,1)S(1)} %get-tuple-element.62), channel_id=1, source_target_pairs={{0,8},{4,12},{8,0},{12,4},{16,24},{20,28},{24,16},{28,20},{1,9},{5... | collective-permute-start | bytes 245768 | tf_op jit(solution)/shard_map/ppermute | solution.py:437
  84.4 8.0 %collective-permute-start.16 = (bf16[160,256]{1,0:T(8,128)(2,1)S(1)}, bf16[160,256]{1,0:T(8,128)(2,1)S(1)}, u32[]{:S(2)}, u32[]{:S(2)}) collective-permute-start(bf16[160,256]{1,0:T(8,128)(2,1)S(1)} %get-tuple-element.69), channel_id=1, source_target_pairs={{0,4},{4,8},{8,12},{12,0},{16,20},{20,24},{24,28},{28,16},{1,5},{5... | collective-permute-start | bytes 245768 | tf_op jit(solution)/shard_map/ppermute | solution.py:437
  85.2 7.2 %collective-permute-start.17 = (bf16[160,256]{1,0:T(8,128)(2,1)S(1)}, bf16[160,256]{1,0:T(8,128)(2,1)S(1)}, u32[]{:S(2)}, u32[]{:S(2)}) collective-permute-start(bf16[160,256]{1,0:T(8,128)(2,1)S(1)} %get-tuple-element.71), channel_id=1, source_target_pairs={{0,12},{4,0},{8,4},{12,8},{16,28},{20,16},{24,20},{28,24},{1,13},{... | collective-permute-start | bytes 245768 | tf_op jit(solution)/shard_map/ppermute | solution.py:437
  89.3 5.0 %collective-permute-start.13 = (bf16[96,256]{1,0:T(8,128)(2,1)S(1)}, bf16[96,256]{1,0:T(8,128)(2,1)S(1)}, u32[]{:S(2)}, u32[]{:S(2)}) collective-permute-start(bf16[96,256]{1,0:T(8,128)(2,1)S(1)} %get-tuple-element.65), channel_id=1, source_target_pairs={{0,4},{4,8},{8,12},{12,0},{16,20},{20,24},{24,28},{28,16},{1,5},{5... | collective-permute-start | bytes 147464 | tf_op jit(solution)/shard_map/ppermute | solution.py:437
  90.6 4.5 %collective-permute-start.14 = (bf16[96,256]{1,0:T(8,128)(2,1)S(1)}, bf16[96,256]{1,0:T(8,128)(2,1)S(1)}, u32[]{:S(2)}, u32[]{:S(2)}) collective-permute-start(bf16[96,256]{1,0:T(8,128)(2,1)S(1)} %get-tuple-element.66), channel_id=1, source_target_pairs={{0,8},{4,12},{8,0},{12,4},{16,24},{20,28},{24,16},{28,20},{1,9},{5... | collective-permute-start | bytes 147464 | tf_op jit(solution)/shard_map/ppermute | solution.py:437
  90.6 4.5 %collective-permute-start.15 = (bf16[96,256]{1,0:T(8,128)(2,1)S(1)}, bf16[96,256]{1,0:T(8,128)(2,1)S(1)}, u32[]{:S(2)}, u32[]{:S(2)}) collective-permute-start(bf16[96,256]{1,0:T(8,128)(2,1)S(1)} %get-tuple-element.67), channel_id=1, source_target_pairs={{0,12},{4,0},{8,4},{12,8},{16,28},{20,16},{24,20},{28,24},{1,13},{... | collective-permute-start | bytes 147464 | tf_op jit(solution)/shard_map/ppermute | solution.py:437

commit v5 on v4

--- a/solution.py
+++ b/solution.py
@@ -30,8 +30,48 @@
     return pl.CostEstimate(flops=flops, bytes_accessed=size, transcendentals=0)
 
 
-def pack_kernel(cols, me_ref, cell_ref, amp_ref, bin_ref, place_ref, *refs):
+def pack_kernel(me_ref, amp_ref, bin_ref, *refs):
     outs, turned = refs[:-1], refs[-1]
+    scaled = (amp_ref[...].astype(F32) * AMP_SCALE).astype(jnp.int32)
+    turned[...] = jnp.transpose((scaled << 16) | bin_ref[...])
+    width = outs[0].shape[0]
+    for k, out in enumerate(outs):
+        first = pl.multiple_of(lax.rem(me_ref[0] + k, len(outs)) * width, 8)
+        out[...] = turned[pl.ds(first, width), :]
+
+
+def pack(me, amplitude, delay_bin, members):
+    panels, observers = amplitude.shape
+    width = observers // members
+    block = pl.BlockSpec((LANES, observers), lambda i: (i, 0))
+    out = jax.ShapeDtypeStruct((width, panels), jnp.int32)
+    return pl.pallas_call(
+        pack_kernel,
+        grid=(panels // LANES,),
+        in_specs=[SMEM, block, block],
+        out_specs=[pl.BlockSpec((width, LANES), lambda i: (0, i))] * members,
+        out_shape=[out] * members,
+        scratch_shapes=[pltpu.VMEM((observers, LANES), jnp.int32)],
+        compiler_params=params(56),
+        cost_estimate=cost(panels * observers, 10 * panels * observers),
+    )(me, amplitude, delay_bin)
+
+
+def coded(mask, visc):
+    return jnp.where(mask != 0, visc, 0.0)
+
+
+def rows_kernel(f_top, m_top, v_top, f_end, m_end, v_end, first_ref, last_ref):
+    first_ref[:STEPS] = f_top[:STEPS]
+    first_ref[STEPS:] = coded(m_top[:STEPS], v_top[:STEPS])
+    last_ref[:STEPS] = f_end[8 - STEPS :]
+    last_ref[STEPS:] = coded(m_end[8 - STEPS :], v_end[8 - STEPS :])
+
+
+def columns_kernel(
+    cell_ref, field_ref, mask_ref, visc_ref, before_ref, after_ref, first_ref, last_ref, place_ref, tall
+):
+    rows, cols = field_ref.shape
     cell = cell_ref[...]
     row = lax.div(cell, cols)
     col = cell - row * cols
@@ -40,49 +80,6 @@
     place_ref[1:2] = row // 8 * 8 + PAD
     place_ref[2:3] = row & 7
     place_ref[3:4] = (panel - col) & (LANES - 1)
-    scaled = (amp_ref[...].astype(F32) * AMP_SCALE).astype(jnp.int32)
-    turned[...] = jnp.transpose((scaled << 16) | bin_ref[...])
-    width = outs[0].shape[0]
-    for k, out in enumerate(outs):
-        first = pl.multiple_of(lax.rem(me_ref[0] + k, len(outs)) * width, 8)
-        out[...] = turned[pl.ds(first, width), :]
-
-
-def pack(me, panel_cell, cols, amplitude, delay_bin, members):
-    panels, observers = amplitude.shape
-    cells = panel_cell.reshape(1, -1)
-    width = observers // members
-    block = pl.BlockSpec((LANES, observers), lambda i: (i, 0))
-    out = jax.ShapeDtypeStruct((width, panels), jnp.int32)
-    whole = pl.BlockSpec(cells.shape, lambda i: (0, 0))
-    return pl.pallas_call(
-        functools.partial(pack_kernel, cols),
-        grid=(panels // LANES,),
-        in_specs=[SMEM, whole, block, block],
-        out_specs=[pl.BlockSpec((4, cells.shape[1]), lambda i: (0, 0))]
-        + [pl.BlockSpec((width, LANES), lambda i: (0, i))] * members,
-        out_shape=[jax.ShapeDtypeStruct((4, cells.shape[1]), jnp.int32)] + [out] * members,
-        scratch_shapes=[pltpu.VMEM((observers, LANES), jnp.int32)],
-        compiler_params=params(56),
-        cost_estimate=cost(panels * observers, 10 * panels * observers),
-    )(me, cells, amplitude, delay_bin)
-
-
-def coded(mask, visc):
-    return jnp.where(mask != 0, visc, 0.0)
-
-
-def rows_kernel(f_top, m_top, v_top, f_end, m_end, v_end, first_ref, last_ref):
-    first_ref[:STEPS] = f_top[:STEPS]
-    first_ref[STEPS:] = coded(m_top[:STEPS], v_top[:STEPS])
-    last_ref[:STEPS] = f_end[8 - STEPS :]
-    last_ref[STEPS:] = coded(m_end[8 - STEPS :], v_end[8 - STEPS :])
-
-
-def columns_kernel(
-    field_ref, mask_ref, visc_ref, before_ref, after_ref, first_ref, last_ref, tall
-):
-    rows, cols = field_ref.shape
     tall[...] = jnp.zeros_like(tall)
     for part in range(2):
         halo = slice(part * STEPS, (part + 1) * STEPS)
@@ -218,22 +215,22 @@
     return lax.ppermute(last, axis, up), lax.ppermute(first, axis, down)
 
 
-def field_window(field, mask, visc, before, after, places):
+def field_window(field, mask, visc, before, after, panel_cell):
     rows, cols = field.shape
     tall = -(-(rows + EDGE) // LANES) * LANES
     edge_cols = jax.ShapeDtypeStruct((EDGE, tall), F32)
 
-    first, last = pl.pallas_call(
+    panels = panel_cell.shape[0]
+    first, last, places = pl.pallas_call(
         columns_kernel,
-        in_specs=[VMEM] * 5,
-        out_specs=[VMEM] * 2,
-        out_shape=[edge_cols, edge_cols],
+        in_specs=[VMEM] * 6,
+        out_specs=[VMEM] * 3,
+        out_shape=[edge_cols, edge_cols, jax.ShapeDtypeStruct((4, panels), jnp.int32)],
         scratch_shapes=[pltpu.VMEM((tall, LANES), F32)],
         compiler_params=params(16),
         cost_estimate=cost(rows * cols, 4 * rows * cols),
-    )(field, mask, visc, before, after)
+    )(panel_cell.reshape(1, panels), field, mask, visc, before, after)
     south, north = shifted("panel", first, last)
-    panels = places.shape[1]
     tiles = cols // LANES + 1
     height = 16 + -(-(rows + 2 * PAD - 16) // STRIP) * STRIP
     return pl.pallas_call(
@@ -439,15 +436,16 @@
     ends = edges(field_start, fluid_mask, base_visc)
     amplitude, delay_bin, *ends = lax.optimization_barrier((amplitude, delay_bin, *ends))
     before, after = shifted("box", *ends)
-    places, *packed = pack(
-        me, panel_cell, field_start.shape[1], amplitude, delay_bin, members
-    )
+    packed = pack(me, amplitude, delay_bin, members)
     before, after, *packed = lax.optimization_barrier((before, after, *packed))
     words = spread(packed)
     field, sample = field_window(
-        field_start, fluid_mask, base_visc, before, after, places
+        field_start, fluid_mask, base_visc, before, after, panel_cell
     )
-    samples = spread([lax.all_gather(sample, "panel")] * members)
+    sample = lax.all_gather(sample, "panel")
+    middle = members // 2
+    sample, words[middle] = lax.optimization_barrier((sample, words[middle]))
+    samples = spread([sample] * members)
     observers = words[0].shape[0]
     across = [(i, (i + members) % peers) for i in range(peers)]
     first, joined, signals = 0, None, None
@@ -457,7 +455,7 @@
         got = lax.ppermute(send, "box", across)
         if joined:
             pieces = spread(joined)
-            got, pieces[members // 2] = lax.optimization_barrier((got, pieces[members // 2]))
+            got, pieces[middle] = lax.optimization_barrier((got, pieces[middle]))
             waiting.append(pieces)
         joined = join(me, keep, got)
         first += count

time: 96.2 us -> 94.5 us (0.982)
  waiting for transfers between devices: 21.3 us -> 17.8 us
  starting transfers between devices: 25.9 us -> 28.4 us
    ppermute x12, waiting for transfers between devices: 11.2 us -> 5.9 us  [spread(): lax.ppermute(x, 'box', perm(k))]
    ppermute x12, starting transfers between devices: 14 us -> 16.4 us  [spread(): lax.ppermute(x, 'box', perm(k))]
    ppermute x2, waiting for transfers between devices: 6.57 us -> 8.31 us  [on_device(): got = lax.ppermute(send, 'box', across)]
  transfers between devices with their start and end apart: 18 -> 18, of which waited for: 9 -> 9; matrix products, arithmetic and copies ran while one was open for 0% -> 0% of each run, Pallas kernels for 22% -> 23%
where the time goes in v5:
time: 94.5 us; the launch traced here: 94.1 us
  Pallas kernels  40.4 us (43%)
  starting transfers between devices  28.4 us (30%)
  waiting for transfers between devices  17.8 us (19%)
  blocking collectives  6.74 us (7%)
    pallas_call x2, Pallas kernels, binned(): pl.pallas_call(bin_kernel, grid=(count // block,), in_specs=[SMEM] + [pl....  27 us
    ppermute x12, starting transfers between devices, spread(): lax.ppermute(x, 'box', perm(k))  16.4 us
    ppermute x4, starting transfers between devices, shifted(): return (lax.ppermute(last, axis, up), lax.ppermute(first, axis, down))  8.88 us
    ppermute x2, waiting for transfers between devices, on_device(): got = lax.ppermute(send, 'box', across)  8.31 us
    all_gather x1, blocking collectives, on_device(): sample = lax.all_gather(sample, 'panel')  6.74 us
    ppermute x12, waiting for transfers between devices, spread(): lax.ppermute(x, 'box', perm(k))  5.9 us
    pallas_call x1, Pallas kernels, field_window(): pl.pallas_call(step_kernel, in_specs=[SMEM] + [VMEM] * 7, out_specs=[VMEM...  5.62 us
    pallas_call x1, Pallas kernels, pack(): pl.pallas_call(pack_kernel, grid=(panels // LANES,), in_specs=[SMEM, bloc...  4.41 us
  transfers between devices with their start and end apart: 18, of which 9 were waited for; matrix products, arithmetic and copies ran while one was open for 0% of the time, Pallas kernels for 23%

profile of v5, /device:TPU:0, one launch (start us, length us, event | category | flops | bytes accessed | tf_op | source)
XLA Modules:
  0.0 94.1 jit_solution(16541913190834520068)
XLA Ops:
  0.6 1.4 %shard_map.77 = (f32[8,512]{1,0:T(8,128)}, f32[8,512]{1,0:T(8,128)}) custom-call(f32[256,512]{1,0:T(8,128)} %field_ref.3, s32[256,512]{1,0:T(8,128)} %mask_ref.3, f32[256,512]{1,0:T(8,128)} %visc_ref.3, f32[256,512]{1,0:T(8,128)} %field_ref.3, s32[256,512]{1,0:T(8,128)} %mask_ref.3, f32[256,512]{1,0:T(8,128)} %visc_ref.3), custom_call_target="tpu_custom_call" | custom-call | flops 8192 | bytes 131072 | tf_op jit(solution)/shard_map/pallas_call | solution.py:199
  2.1 5.0 %collective-permute-start = (f32[8,512]{1,0:T(8,128)}, f32[8,512]{1,0:T(8,128)S(1)}, u32[]{:S(2)}, u32[]{:S(2)}) collective-permute-start(f32[8,512]{1,0:T(8,128)} %get-tuple-element.41), channel_id=1, source_target_pairs={{0,4},{4,8},{8,12},{12,16},{16,20},{20,24},{24,28},{1,5},{5,9},{9,... | collective-permute-start | bytes 49160 | tf_op jit(solution)/shard_map/ppermute | solution.py:215
  7.1 1.3 %collective-permute-start.1 = (f32[8,512]{1,0:T(8,128)}, f32[8,512]{1,0:T(8,128)S(1)}, u32[]{:S(2)}, u32[]{:S(2)}) collective-permute-start(f32[8,512]{1,0:T(8,128)} %get-tuple-element.42), channel_id=1, source_target_pairs={{4,0},{8,4},{12,8},{16,12},{20,16},{24,20},{28,24},{5,1},{9,5},{13... | collective-permute-start | bytes 49160 | tf_op jit(solution)/shard_map/ppermute | solution.py:215
  8.4 4.4 %shard_map.78 = (s32[256,512]{1,0:T(8,128)}, s32[256,512]{1,0:T(8,128)}, s32[256,512]{1,0:T(8,128)}, s32[256,512]{1,0:T(8,128)}) custom-call(s32[1]{0:T(128)S(6)} %rem.22.me_ref, bf16[512,1024]{1,0:T(8,128)(2,1)} %amp_ref, s32[512,1024]{1,0:T(8,128)} %bin_ref), custom_call_target="tpu_custom_call" | custom-call | flops 524288 | bytes 5242880 | tf_op jit(solution)/shard_map/pallas_call | solution.py:48
  12.9 3.6 %collective-permute-start.5 = (s32[256,512]{1,0:T(8,128)}, s32[256,512]{1,0:T(8,128)S(1)}, u32[]{:S(2)}, u32[]{:S(2)}) collective-permute-start(s32[256,512]{1,0:T(8,128)} %get-tuple-element.58), channel_id=1, source_target_pairs={{0,8},{4,12},{8,0},{12,4},{16,24},{20,28},{24,16},{28,20},{1,9},{5... | collective-permute-start | bytes 1572872 | tf_op jit(solution)/shard_map/ppermute | solution.py:434
  16.5 0.6 collective-permute-start.4
  17.1 2.3 %collective-permute-start.6 = (s32[256,512]{1,0:T(8,128)}, s32[256,512]{1,0:T(8,128)S(1)}, u32[]{:S(2)}, u32[]{:S(2)}) collective-permute-start(s32[256,512]{1,0:T(8,128)} %get-tuple-element.60), channel_id=1, source_target_pairs={{0,12},{4,0},{8,4},{12,8},{16,28},{20,16},{24,20},{28,24},{1,13},{... | collective-permute-start | bytes 1572872 | tf_op jit(solution)/shard_map/ppermute | solution.py:434
  19.4 0.3 shard_map.79
  19.7 1.3 %collective-permute-start.2 = (f32[8,384]{1,0:T(8,128)S(1)}, f32[8,384]{1,0:T(8,128)S(1)}, u32[]{:S(2)}, u32[]{:S(2)}) collective-permute-start(f32[8,384]{1,0:T(8,128)S(1)} %get-tuple-element.52), channel_id=1, source_target_pairs={{0,1},{1,2},{2,3},{4,5},{5,6},{6,7},{8,9},{9,10},{10,11},{12,13},{... | collective-permute-start | bytes 36872 | tf_op jit(solution)/shard_map/ppermute | solution.py:215
  21.0 1.3 %collective-permute-start.3 = (f32[8,384]{1,0:T(8,128)S(1)}, f32[8,384]{1,0:T(8,128)S(1)}, u32[]{:S(2)}, u32[]{:S(2)}) collective-permute-start(f32[8,384]{1,0:T(8,128)S(1)} %get-tuple-element.53), channel_id=1, source_target_pairs={{1,0},{2,1},{3,2},{5,4},{6,5},{7,6},{9,8},{10,9},{11,10},{13,12},{... | collective-permute-start | bytes 36872 | tf_op jit(solution)/shard_map/ppermute | solution.py:215
  22.3 3.5 %collective-permute-done.3.north_ref = f32[8,384]{1,0:T(8,128)S(1)} collective-permute-done((f32[8,384]{1,0:T(8,128)S(1)}, f32[8,384]{1,0:T(8,128)S(1)}, u32[]{:S(2)}, u32[]{:S(2)}) %collective-permute-start.3) | collective-permute-done | bytes 12320 | tf_op jit(solution)/shard_map/ppermute | solution.py:215
  25.8 5.6 %shard_map.80 = (f32[256,512]{1,0:T(8,128)}, f32[4,128]{1,0:T(4,128)S(1)}) custom-call(s32[4,128]{1,0:T(4,128)S(1)} %get-tuple-element.51.cell_ref, f32[256,512]{1,0:T(8,128)S(1)} %copy-done, s32[256,512]{1,0:T(8,128)S(1)} %copy-done.1, f32[256,512]{1,0:T(8,128)S(1)} %copy-done.2, f32[8,512]{1,0:T(8,128)S(1)} %collective-permute-done.before_ref, ...), custom_call_target="tpu_custom_call" | custom-call | flops 13107200 | bytes 104857600 | tf_op jit(solution)/shard_map/pallas_call | solution.py:236
  31.4 6.7 %all-gather.1.refs_4_ = f32[4,4,128]{2,1,0:T(4,128)S(1)} all-gather(f32[1,4,128]{2,1,0:T(4,128)S(1)} %bitcast.3), channel_id=2, replica_groups=mesh['box'=8,'panel'=4] {'panel'}, dimensions={0}, use_global_device_ids=true | all-gather | bytes 10240 | tf_op jit(solution)/shard_map/all_gather | solution.py:445
  38.2 0.6 collective-permute-start.8
  38.8 2.4 %collective-permute-start.9 = (f32[4,4,128]{2,1,0:T(4,128)S(1)}, f32[4,4,128]{2,1,0:T(4,128)S(1)}, u32[]{:S(2)}, u32[]{:S(2)}) collective-permute-start(f32[4,4,128]{2,1,0:T(4,128)S(1)} %all-gather.1.refs_4_), channel_id=1, source_target_pairs={{0,12},{4,0},{8,4},{12,8},{16,28},{20,16},{24,20},{28,24},{1,13},{... | collective-permute-start | bytes 24584 | tf_op jit(solution)/shard_map/ppermute | solution.py:434
  41.2 1.6 %collective-permute-done.7.refs_5_ = f32[4,4,128]{2,1,0:T(4,128)S(1)} collective-permute-done((f32[4,4,128]{2,1,0:T(4,128)S(1)}, f32[4,4,128]{2,1,0:T(4,128)S(1)}, u32[]{:S(2)}, u32[]{:S(2)}) %collective-permute-start.7) | collective-permute-done | bytes 8224 | tf_op jit(solution)/shard_map/ppermute | solution.py:434
  42.8 0.6 collective-permute-done.9.refs_7_
  43.3 16.9 %shard_map.82 = (f32[4,160,256]{2,1,0:T(8,128)S(1)}, bf16[4,160,256]{2,1,0:T(8,128)(2,1)S(1)}) custom-call(s32[1]{0:T(128)S(6)} %select_n.5.half_ref, s32[256,512]{1,0:T(8,128)S(1)} %copy-done.4, s32[256,512]{1,0:T(8,128)S(1)} %collective-permute-done.4.refs_1_, s32[256,512]{1,0:T(8,128)S(1)} %collective-permute-done.5.refs_2_, ...), custom_call_target="tpu_custom_call" | custom-call | flops 21474836480 | bytes 2621440 | tf_op jit(solution)/shard_map/pallas_call | solution.py:348
  60.2 2.6 %collective-permute-start.11 = (bf16[4,160,256]{2,1,0:T(8,128)(2,1)S(1)}, bf16[4,160,256]{2,1,0:T(8,128)(2,1)S(1)}, u32[]{:S(2)}, u32[]{:S(2)}) collective-permute-start(bf16[4,160,256]{2,1,0:T(8,128)(2,1)S(1)} %get-tuple-element.65), channel_id=1, source_target_pairs={{0,16},{4,20},{8,24},{12,28},{16,0},{20,4},{24,8},{28,12},{1,17},{... | collective-permute-start | bytes 983048 | tf_op jit(solution)/shard_map/ppermute | solution.py:455
  62.8 10.1 %shard_map.81 = (f32[4,96,256]{2,1,0:T(8,128)S(1)}, bf16[4,96,256]{2,1,0:T(8,128)(2,1)S(1)}) custom-call(s32[1]{0:T(128)S(6)} %select_n.5.half_ref, s32[256,512]{1,0:T(8,128)S(1)} %copy-done.4, s32[256,512]{1,0:T(8,128)S(1)} %collective-permute-done.4.refs_1_, s32[256,512]{1,0:T(8,128)S(1)} %collective-permute-done.5.refs_2_, ...), custom_call_target="tpu_custom_call" | custom-call | flops 12884901888 | bytes 1572864 | tf_op jit(solution)/shard_map/pallas_call | solution.py:348
  72.9 0.5 collective-permute-start.10
  73.4 8.2 %collective-permute-done.11.got_ref = bf16[4,160,256]{2,1,0:T(8,128)(2,1)S(1)} collective-permute-done((bf16[4,160,256]{2,1,0:T(8,128)(2,1)S(1)}, bf16[4,160,256]{2,1,0:T(8,128)(2,1)S(1)}, u32[]{:S(2)}, u32[]{:S(2)}) %collective-permute-start.11) | collective-permute-done | bytes 327712 | tf_op jit(solution)/shard_map/ppermute | solution.py:455
  81.7 2.4 %collective-permute-start.16 = (bf16[160,256]{1,0:T(8,128)(2,1)S(1)}, bf16[160,256]{1,0:T(8,128)(2,1)S(1)}, u32[]{:S(2)}, u32[]{:S(2)}) collective-permute-start(bf16[160,256]{1,0:T(8,128)(2,1)S(1)} %get-tuple-element.73), channel_id=1, source_target_pairs={{0,4},{4,8},{8,12},{12,0},{16,20},{20,24},{24,28},{28,16},{1,5},{5... | collective-permute-start | bytes 245768 | tf_op jit(solution)/shard_map/ppermute | solution.py:434
  84.1 0.7 collective-permute-start.17
  84.8 0.1 collective-permute-done.10.got_ref
  84.9 2.1 %collective-permute-done.12.refs_2_ = bf16[160,256]{1,0:T(8,128)(2,1)S(1)} collective-permute-done((bf16[160,256]{1,0:T(8,128)(2,1)S(1)}, bf16[160,256]{1,0:T(8,128)(2,1)S(1)}, u32[]{:S(2)}, u32[]{:S(2)}) %collective-permute-start.12) | collective-permute-done | bytes 81952 | tf_op jit(solution)/shard_map/ppermute | solution.py:434
  87.1 2.2 %collective-permute-start.13 = (bf16[96,256]{1,0:T(8,128)(2,1)S(1)}, bf16[96,256]{1,0:T(8,128)(2,1)S(1)}, u32[]{:S(2)}, u32[]{:S(2)}) collective-permute-start(bf16[96,256]{1,0:T(8,128)(2,1)S(1)} %get-tuple-element.69), channel_id=1, source_target_pairs={{0,4},{4,8},{8,12},{12,0},{16,20},{20,24},{24,28},{28,16},{1,5},{5... | collective-permute-start | bytes 147464 | tf_op jit(solution)/shard_map/ppermute | solution.py:434
  89.3 1.5 %collective-permute-start.15 = (bf16[96,256]{1,0:T(8,128)(2,1)S(1)}, bf16[96,256]{1,0:T(8,128)(2,1)S(1)}, u32[]{:S(2)}, u32[]{:S(2)}) collective-permute-start(bf16[96,256]{1,0:T(8,128)(2,1)S(1)} %get-tuple-element.71), channel_id=1, source_target_pairs={{0,12},{4,0},{8,4},{12,8},{16,28},{20,16},{24,20},{28,24},{1,13},{... | collective-permute-start | bytes 147464 | tf_op jit(solution)/shard_map/ppermute | solution.py:434
  90.8 0.9 shard_map.85.refs_4_
  91.7 0.8 collective-permute-done.13.refs_1_
  92.5 0.9 collective-permute-done.14.refs_2_
  93.4 0.8 shard_map.86
  (25 shorter events, 0.4 us)
Async XLA Ops:
  2.1 17.4 %copy-start = (f32[256,512]{1,0:T(8,128)S(1)}, f32[256,512]{1,0:T(8,128)}, u32[]{:S(2)}) copy-start(f32[256,512]{1,0:T(8,128)} %field_ref.3) | copy-start | bytes 1572868
  2.1 17.4 %copy-start.1 = (s32[256,512]{1,0:T(8,128)S(1)}, s32[256,512]{1,0:T(8,128)}, u32[]{:S(2)}) copy-start(s32[256,512]{1,0:T(8,128)} %mask_ref.3) | copy-start | bytes 1572868
  2.1 17.4 %copy-start.2 = (f32[256,512]{1,0:T(8,128)S(1)}, f32[256,512]{1,0:T(8,128)}, u32[]{:S(2)}) copy-start(f32[256,512]{1,0:T(8,128)} %visc_ref.3) | copy-start | bytes 1572868
  2.1 17.4 %copy-start.3 = (s32[128]{0:T(128)S(1)}, s32[128]{0:T(128)}, u32[]{:S(2)}) copy-start(s32[128]{0:T(128)} %param.9) | copy-start | bytes 1540
  2.1 10.7 %collective-permute-start = (f32[8,512]{1,0:T(8,128)}, f32[8,512]{1,0:T(8,128)S(1)}, u32[]{:S(2)}, u32[]{:S(2)}) collective-permute-start(f32[8,512]{1,0:T(8,128)} %get-tuple-element.41), channel_id=1, source_target_pairs={{0,4},{4,8},{8,12},{12,16},{16,20},{20,24},{24,28},{1,5},{5,9},{9,... | collective-permute-start | bytes 49160 | tf_op jit(solution)/shard_map/ppermute | solution.py:215
  7.1 5.8 %collective-permute-start.1 = (f32[8,512]{1,0:T(8,128)}, f32[8,512]{1,0:T(8,128)S(1)}, u32[]{:S(2)}, u32[]{:S(2)}) collective-permute-start(f32[8,512]{1,0:T(8,128)} %get-tuple-element.42), channel_id=1, source_target_pairs={{4,0},{8,4},{12,8},{16,12},{20,16},{24,20},{28,24},{5,1},{9,5},{13... | collective-permute-start | bytes 49160 | tf_op jit(solution)/shard_map/ppermute | solution.py:215
  12.8 30.5 %copy-start.4 = (s32[256,512]{1,0:T(8,128)S(1)}, s32[256,512]{1,0:T(8,128)}, u32[]{:S(2)}) copy-start(s32[256,512]{1,0:T(8,128)} %get-tuple-element.55.refs_0_) | copy-start | bytes 1572868
  12.9 25.2 %collective-permute-start.5 = (s32[256,512]{1,0:T(8,128)}, s32[256,512]{1,0:T(8,128)S(1)}, u32[]{:S(2)}, u32[]{:S(2)}) collective-permute-start(s32[256,512]{1,0:T(8,128)} %get-tuple-element.58), channel_id=1, source_target_pairs={{0,8},{4,12},{8,0},{12,4},{16,24},{20,28},{24,16},{28,20},{1,9},{5... | collective-permute-start | bytes 1572872 | tf_op jit(solution)/shard_map/ppermute | solution.py:434
  16.5 24.7 %collective-permute-start.4 = (s32[256,512]{1,0:T(8,128)}, s32[256,512]{1,0:T(8,128)S(1)}, u32[]{:S(2)}, u32[]{:S(2)}) collective-permute-start(s32[256,512]{1,0:T(8,128)} %get-tuple-element.56), channel_id=1, source_target_pairs={{0,4},{4,8},{8,12},{12,0},{16,20},{20,24},{24,28},{28,16},{1,5},{5... | collective-permute-start | bytes 1572872 | tf_op jit(solution)/shard_map/ppermute | solution.py:434
  17.1 24.1 %collective-permute-start.6 = (s32[256,512]{1,0:T(8,128)}, s32[256,512]{1,0:T(8,128)S(1)}, u32[]{:S(2)}, u32[]{:S(2)}) collective-permute-start(s32[256,512]{1,0:T(8,128)} %get-tuple-element.60), channel_id=1, source_target_pairs={{0,12},{4,0},{8,4},{12,8},{16,28},{20,16},{24,20},{28,24},{1,13},{... | collective-permute-start | bytes 1572872 | tf_op jit(solution)/shard_map/ppermute | solution.py:434
  19.7 2.6 %collective-permute-start.2 = (f32[8,384]{1,0:T(8,128)S(1)}, f32[8,384]{1,0:T(8,128)S(1)}, u32[]{:S(2)}, u32[]{:S(2)}) collective-permute-start(f32[8,384]{1,0:T(8,128)S(1)} %get-tuple-element.52), channel_id=1, source_target_pairs={{0,1},{1,2},{2,3},{4,5},{5,6},{6,7},{8,9},{9,10},{10,11},{12,13},{... | collective-permute-start | bytes 36872 | tf_op jit(solution)/shard_map/ppermute | solution.py:215
  21.0 4.8 %collective-permute-start.3 = (f32[8,384]{1,0:T(8,128)S(1)}, f32[8,384]{1,0:T(8,128)S(1)}, u32[]{:S(2)}, u32[]{:S(2)}) collective-permute-start(f32[8,384]{1,0:T(8,128)S(1)} %get-tuple-element.53), channel_id=1, source_target_pairs={{1,0},{2,1},{3,2},{5,4},{6,5},{7,6},{9,8},{10,9},{11,10},{13,12},{... | collective-permute-start | bytes 36872 | tf_op jit(solution)/shard_map/ppermute | solution.py:215
  38.2 4.6 %collective-permute-start.7 = (f32[4,4,128]{2,1,0:T(4,128)S(1)}, f32[4,4,128]{2,1,0:T(4,128)S(1)}, u32[]{:S(2)}, u32[]{:S(2)}) collective-permute-start(f32[4,4,128]{2,1,0:T(4,128)S(1)} %all-gather.1.refs_4_), channel_id=1, source_target_pairs={{0,4},{4,8},{8,12},{12,0},{16,20},{20,24},{24,28},{28,16},{1,5},{5... | collective-permute-start | bytes 24584 | tf_op jit(solution)/shard_map/ppermute | solution.py:434
  38.2 4.5 %collective-permute-start.8 = (f32[4,4,128]{2,1,0:T(4,128)S(1)}, f32[4,4,128]{2,1,0:T(4,128)S(1)}, u32[]{:S(2)}, u32[]{:S(2)}) collective-permute-start(f32[4,4,128]{2,1,0:T(4,128)S(1)} %all-gather.1.refs_4_), channel_id=1, source_target_pairs={{0,8},{4,12},{8,0},{12,4},{16,24},{20,28},{24,16},{28,20},{1,9},{5... | collective-permute-start | bytes 24584 | tf_op jit(solution)/shard_map/ppermute | solution.py:434
  38.8 4.5 %collective-permute-start.9 = (f32[4,4,128]{2,1,0:T(4,128)S(1)}, f32[4,4,128]{2,1,0:T(4,128)S(1)}, u32[]{:S(2)}, u32[]{:S(2)}) collective-permute-start(f32[4,4,128]{2,1,0:T(4,128)S(1)} %all-gather.1.refs_4_), channel_id=1, source_target_pairs={{0,12},{4,0},{8,4},{12,8},{16,28},{20,16},{24,20},{28,24},{1,13},{... | collective-permute-start | bytes 24584 | tf_op jit(solution)/shard_map/ppermute | solution.py:434
  60.2 21.3 %collective-permute-start.11 = (bf16[4,160,256]{2,1,0:T(8,128)(2,1)S(1)}, bf16[4,160,256]{2,1,0:T(8,128)(2,1)S(1)}, u32[]{:S(2)}, u32[]{:S(2)}) collective-permute-start(bf16[4,160,256]{2,1,0:T(8,128)(2,1)S(1)} %get-tuple-element.65), channel_id=1, source_target_pairs={{0,16},{4,20},{8,24},{12,28},{16,0},{20,4},{24,8},{28,12},{1,17},{... | collective-permute-start | bytes 983048 | tf_op jit(solution)/shard_map/ppermute | solution.py:455
  72.9 12.1 %collective-permute-start.10 = (bf16[4,96,256]{2,1,0:T(8,128)(2,1)S(1)}, bf16[4,96,256]{2,1,0:T(8,128)(2,1)S(1)}, u32[]{:S(2)}, u32[]{:S(2)}) collective-permute-start(bf16[4,96,256]{2,1,0:T(8,128)(2,1)S(1)} %get-tuple-element.63), channel_id=1, source_target_pairs={{0,16},{4,20},{8,24},{12,28},{16,0},{20,4},{24,8},{28,12},{1,17},{... | collective-permute-start | bytes 589832 | tf_op jit(solution)/shard_map/ppermute | solution.py:455
  81.6 5.4 %collective-permute-start.12 = (bf16[160,256]{1,0:T(8,128)(2,1)S(1)}, bf16[160,256]{1,0:T(8,128)(2,1)S(1)}, u32[]{:S(2)}, u32[]{:S(2)}) collective-permute-start(bf16[160,256]{1,0:T(8,128)(2,1)S(1)} %get-tuple-element.66), channel_id=1, source_target_pairs={{0,8},{4,12},{8,0},{12,4},{16,24},{20,28},{24,16},{28,20},{1,9},{5... | collective-permute-start | bytes 245768 | tf_op jit(solution)/shard_map/ppermute | solution.py:434
  81.7 9.1 %collective-permute-start.16 = (bf16[160,256]{1,0:T(8,128)(2,1)S(1)}, bf16[160,256]{1,0:T(8,128)(2,1)S(1)}, u32[]{:S(2)}, u32[]{:S(2)}) collective-permute-start(bf16[160,256]{1,0:T(8,128)(2,1)S(1)} %get-tuple-element.73), channel_id=1, source_target_pairs={{0,4},{4,8},{8,12},{12,0},{16,20},{20,24},{24,28},{28,16},{1,5},{5... | collective-permute-start | bytes 245768 | tf_op jit(solution)/shard_map/ppermute | solution.py:434
  84.1 6.7 %collective-permute-start.17 = (bf16[160,256]{1,0:T(8,128)(2,1)S(1)}, bf16[160,256]{1,0:T(8,128)(2,1)S(1)}, u32[]{:S(2)}, u32[]{:S(2)}) collective-permute-start(bf16[160,256]{1,0:T(8,128)(2,1)S(1)} %get-tuple-element.75), channel_id=1, source_target_pairs={{0,12},{4,0},{8,4},{12,8},{16,28},{20,16},{24,20},{28,24},{1,13},{... | collective-permute-start | bytes 245768 | tf_op jit(solution)/shard_map/ppermute | solution.py:434
  87.1 5.4 %collective-permute-start.13 = (bf16[96,256]{1,0:T(8,128)(2,1)S(1)}, bf16[96,256]{1,0:T(8,128)(2,1)S(1)}, u32[]{:S(2)}, u32[]{:S(2)}) collective-permute-start(bf16[96,256]{1,0:T(8,128)(2,1)S(1)} %get-tuple-element.69), channel_id=1, source_target_pairs={{0,4},{4,8},{8,12},{12,0},{16,20},{20,24},{24,28},{28,16},{1,5},{5... | collective-permute-start | bytes 147464 | tf_op jit(solution)/shard_map/ppermute | solution.py:434
  89.3 4.1 %collective-permute-start.14 = (bf16[96,256]{1,0:T(8,128)(2,1)S(1)}, bf16[96,256]{1,0:T(8,128)(2,1)S(1)}, u32[]{:S(2)}, u32[]{:S(2)}) collective-permute-start(bf16[96,256]{1,0:T(8,128)(2,1)S(1)} %get-tuple-element.70), channel_id=1, source_target_pairs={{0,8},{4,12},{8,0},{12,4},{16,24},{20,28},{24,16},{28,20},{1,9},{5... | collective-permute-start | bytes 147464 | tf_op jit(solution)/shard_map/ppermute | solution.py:434
  89.3 4.1 %collective-permute-start.15 = (bf16[96,256]{1,0:T(8,128)(2,1)S(1)}, bf16[96,256]{1,0:T(8,128)(2,1)S(1)}, u32[]{:S(2)}, u32[]{:S(2)}) collective-permute-start(bf16[96,256]{1,0:T(8,128)(2,1)S(1)} %get-tuple-element.71), channel_id=1, source_target_pairs={{0,12},{4,0},{8,4},{12,8},{16,28},{20,16},{24,20},{28,24},{1,13},{... | collective-permute-start | bytes 147464 | tf_op jit(solution)/shard_map/ppermute | solution.py:434

commit v6 on v5

--- a/solution.py
+++ b/solution.py
@@ -17,7 +17,7 @@
 PAD = 16
 STRIP = 32
 AMP_SCALE = 4096.0
-LAST = 6
+PARTS = (7, 12, 16)
 VMEM = pl.BlockSpec(memory_space=pltpu.VMEM)
 SMEM = pl.BlockSpec(memory_space=pltpu.SMEM)
 
@@ -108,6 +108,8 @@
     fields,
     visc,
     wide,
+    last,
+    sem,
 ):
     rows, cols = field_ref.shape
     panels = sample_ref.shape[1]
@@ -170,7 +172,9 @@
         strips = (height - 16) // STRIP
         lax.fori_loop(0, strips, one_strip, 0, unroll=strips)
     for k in range(tiles - 1):
-        end_ref[:, k * LANES : (k + 1) * LANES] = fields[STEPS, k, PAD : PAD + rows, :]
+        last[:, k * LANES : (k + 1) * LANES] = fields[STEPS, k, PAD : PAD + rows, :]
+    leave = pltpu.make_async_copy(last, end_ref, sem)
+    leave.start()
 
     lane = lax.broadcasted_iota(jnp.int32, (8, LANES), 1)
     line = lax.broadcasted_iota(jnp.int32, (8, LANES), 0)
@@ -191,6 +195,7 @@
         found = lax.fori_loop(0, LANES, one_panel, none, unroll=32)
         for t in range(STEPS):
             sample_ref[t : t + 1, base : base + LANES] = jnp.sum(found[t], axis=0, keepdims=True)
+    leave.wait()
 
 
 def edges(field, mask, visc):
@@ -236,7 +241,7 @@
     return pl.pallas_call(
         step_kernel,
         in_specs=[SMEM] + [VMEM] * 7,
-        out_specs=[VMEM] * 2,
+        out_specs=[pl.BlockSpec(memory_space=pl.ANY), VMEM],
         out_shape=[
             jax.ShapeDtypeStruct((rows, cols), F32),
             jax.ShapeDtypeStruct((STEPS, panels), F32),
@@ -245,6 +250,8 @@
             pltpu.VMEM((STEPS + 1, tiles, height, LANES), F32),
             pltpu.VMEM((tiles, height, LANES), F32),
             pltpu.VMEM((LANES, tall), F32),
+            pltpu.VMEM((rows, cols), F32),
+            pltpu.SemaphoreType.DMA,
         ],
         compiler_params=params(24),
         cost_estimate=cost(100 * rows * cols, 800 * rows * cols),
@@ -368,22 +375,28 @@
     )(half, *words, *samples)
 
 
-def join_kernel(me_ref, keep_ref, got_ref, *outs):
+def join_kernel(parts, me_ref, *refs):
+    keeps, gots, outs = refs[:parts], refs[parts : 2 * parts], refs[2 * parts :]
     for k, out in enumerate(outs):
         owner = lax.rem(me_ref[0] + k, len(outs))
-        out[...] = (keep_ref[owner] + got_ref[owner].astype(F32)).astype(BF16)
-
-
-def join(me, keep, got):
-    members, count, bins = keep.shape
+        at = 0
+        for keep, got in zip(keeps, gots):
+            count = keep.shape[1]
+            out[at : at + count] = (keep[owner] + got[owner].astype(F32)).astype(BF16)
+            at += count
+
+
+def join(me, keeps, gots):
+    members, _, bins = keeps[0].shape
+    count = sum(keep.shape[1] for keep in keeps)
     return pl.pallas_call(
-        join_kernel,
-        in_specs=[SMEM, VMEM, VMEM],
+        functools.partial(join_kernel, len(keeps)),
+        in_specs=[SMEM] + [VMEM] * (2 * len(keeps)),
         out_specs=[VMEM] * members,
         out_shape=[jax.ShapeDtypeStruct((count, bins), BF16)] * members,
         compiler_params=params(16),
-        cost_estimate=cost(keep.size, 8 * keep.size),
-    )(me, keep, got)
+        cost_estimate=cost(members * count * bins, 8 * members * count * bins),
+    )(me, *keeps, *gots)
 
 
 def place_kernel(first, width, me_ref, *refs):
@@ -448,19 +461,22 @@
     samples = spread([sample] * members)
     observers = words[0].shape[0]
     across = [(i, (i + members) % peers) for i in range(peers)]
-    first, joined, signals = 0, None, None
-    waiting = []
-    for count in sizes(observers):
-        keep, send = binned(half, words, samples, first, count)
-        got = lax.ppermute(send, "box", across)
-        if joined:
-            pieces = spread(joined)
-            got, pieces[middle] = lax.optimization_barrier((got, pieces[middle]))
-            waiting.append(pieces)
-        joined = join(me, keep, got)
-        first += count
-    waiting.append(spread(joined))
-    first = 0
+    first, groups = 0, []
+    for chunks in sizes(observers):
+        groups.append([])
+        for count in chunks:
+            keep, send = binned(half, words, samples, first, count)
+            keep, half = lax.optimization_barrier((keep, half))
+            groups[-1].append((keep, lax.ppermute(send, "box", across)))
+            first += count
+    pieces, waiting = None, []
+    for group in groups:
+        keeps, gots = [x[0] for x in group], [x[1] for x in group]
+        if pieces is not None:
+            gots[-1], pieces[middle] = lax.optimization_barrier((gots[-1], pieces[middle]))
+        pieces = spread(join(me, keeps, gots))
+        waiting.append(pieces)
+    first, signals = 0, None
     for pieces in waiting:
         signals = place(me, pieces, signals, first, observers)
         first += pieces[0].shape[0]
@@ -468,8 +484,10 @@
 
 
 def sizes(observers):
-    last = -(-observers * LAST // 16 // 16) * 16
-    return [observers - last, last]
+    units = observers // 16
+    ends = [-(-units * part // 16) * 16 for part in PARTS]
+    counts = [end - start for start, end in zip([0] + ends, ends)]
+    return [[c for c in group if c] for group in (counts[:2], counts[2:]) if any(group)]
 
 
 def solution(mesh):

time: 94.5 us -> 89.1 us (0.943)
  waiting for transfers between devices: 17.8 us -> 9.66 us
  starting transfers between devices: 28.4 us -> 31.7 us
    ppermute x2 -> x3, waiting for transfers between devices: 8.31 us -> 0.82 us  [on_device(): groups[-1].append((keep, lax.ppermute(send, 'box', across)))]
    ppermute x2 -> x3, starting transfers between devices: 3.05 us -> 5.65 us  [on_device(): groups[-1].append((keep, lax.ppermute(send, 'box', across)))]
    pallas_call x2 -> x3, Pallas kernels: 27 us -> 27 us  [binned(): pl.pallas_call(bin_kernel, grid=(count // block,), in_specs=[SMEM] + [pl....]
  transfers between devices with their start and end apart: 18 -> 19, of which waited for: 9 -> 8; matrix products, arithmetic and copies ran while one was open for 0% -> 0% of each run, Pallas kernels for 23% -> 29%
where the time goes in v6:
time: 89.1 us; the launch traced here: 88.7 us
  Pallas kernels  39.8 us (45%)
  starting transfers between devices  31.7 us (36%)
  waiting for transfers between devices  9.66 us (11%)
  blocking collectives  6.75 us (8%)
    pallas_call x3, Pallas kernels, binned(): pl.pallas_call(bin_kernel, grid=(count // block,), in_specs=[SMEM] + [pl....  27 us
    ppermute x12, starting transfers between devices, spread(): lax.ppermute(x, 'box', perm(k))  17.2 us
    ppermute x4, starting transfers between devices, shifted(): return (lax.ppermute(last, axis, up), lax.ppermute(first, axis, down))  8.88 us
    all_gather x1, blocking collectives, on_device(): sample = lax.all_gather(sample, 'panel')  6.75 us
    ppermute x3, starting transfers between devices, on_device(): groups[-1].append((keep, lax.ppermute(send, 'box', across)))  5.65 us
    ppermute x12, waiting for transfers between devices, spread(): lax.ppermute(x, 'box', perm(k))  5.26 us
    pallas_call x1, Pallas kernels, field_window(): pl.pallas_call(step_kernel, in_specs=[SMEM] + [VMEM] * 7, out_specs=[pl.B...  4.9 us
    pallas_call x1, Pallas kernels, pack(): pl.pallas_call(pack_kernel, grid=(panels // LANES,), in_specs=[SMEM, bloc...  4.44 us
  transfers between devices with their start and end apart: 19, of which 8 were waited for; matrix products, arithmetic and copies ran while one was open for 0% of the time, Pallas kernels for 29%

profile of v6, /device:TPU:0, one launch (start us, length us, event | category | flops | bytes accessed | tf_op | source)
XLA Modules:
  0.0 88.7 jit_solution(9448923099098538969)
XLA Ops:
  0.6 1.4 %shard_map.77 = (f32[8,512]{1,0:T(8,128)}, f32[8,512]{1,0:T(8,128)}) custom-call(f32[256,512]{1,0:T(8,128)} %field_ref.3, s32[256,512]{1,0:T(8,128)} %mask_ref.3, f32[256,512]{1,0:T(8,128)} %visc_ref.3, f32[256,512]{1,0:T(8,128)} %field_ref.3, s32[256,512]{1,0:T(8,128)} %mask_ref.3, f32[256,512]{1,0:T(8,128)} %visc_ref.3), custom_call_target="tpu_custom_call" | custom-call | flops 8192 | bytes 131072 | tf_op jit(solution)/shard_map/pallas_call | solution.py:204
  2.1 5.0 %collective-permute-start = (f32[8,512]{1,0:T(8,128)}, f32[8,512]{1,0:T(8,128)S(1)}, u32[]{:S(2)}, u32[]{:S(2)}) collective-permute-start(f32[8,512]{1,0:T(8,128)} %get-tuple-element.48), channel_id=1, source_target_pairs={{0,4},{4,8},{8,12},{12,16},{16,20},{20,24},{24,28},{1,5},{5,9},{9,... | collective-permute-start | bytes 49160 | tf_op jit(solution)/shard_map/ppermute | solution.py:220
  7.1 1.3 %collective-permute-start.1 = (f32[8,512]{1,0:T(8,128)}, f32[8,512]{1,0:T(8,128)S(1)}, u32[]{:S(2)}, u32[]{:S(2)}) collective-permute-start(f32[8,512]{1,0:T(8,128)} %get-tuple-element.49), channel_id=1, source_target_pairs={{4,0},{8,4},{12,8},{16,12},{20,16},{24,20},{28,24},{5,1},{9,5},{13... | collective-permute-start | bytes 49160 | tf_op jit(solution)/shard_map/ppermute | solution.py:220
  8.4 4.4 %shard_map.78 = (s32[256,512]{1,0:T(8,128)}, s32[256,512]{1,0:T(8,128)}, s32[256,512]{1,0:T(8,128)}, s32[256,512]{1,0:T(8,128)}) custom-call(s32[1]{0:T(128)S(6)} %rem.22.me_ref, bf16[512,1024]{1,0:T(8,128)(2,1)} %amp_ref, s32[512,1024]{1,0:T(8,128)} %bin_ref), custom_call_target="tpu_custom_call" | custom-call | flops 524288 | bytes 5242880 | tf_op jit(solution)/shard_map/pallas_call | solution.py:48
  12.9 3.6 %collective-permute-start.5 = (s32[256,512]{1,0:T(8,128)}, s32[256,512]{1,0:T(8,128)S(1)}, u32[]{:S(2)}, u32[]{:S(2)}) collective-permute-start(s32[256,512]{1,0:T(8,128)} %get-tuple-element.65), channel_id=1, source_target_pairs={{0,8},{4,12},{8,0},{12,4},{16,24},{20,28},{24,16},{28,20},{1,9},{5... | collective-permute-start | bytes 1572872 | tf_op jit(solution)/shard_map/ppermute | solution.py:447
  16.5 0.6 collective-permute-start.4
  17.1 2.3 %collective-permute-start.6 = (s32[256,512]{1,0:T(8,128)}, s32[256,512]{1,0:T(8,128)S(1)}, u32[]{:S(2)}, u32[]{:S(2)}) collective-permute-start(s32[256,512]{1,0:T(8,128)} %get-tuple-element.67), channel_id=1, source_target_pairs={{0,12},{4,0},{8,4},{12,8},{16,28},{20,16},{24,20},{28,24},{1,13},{... | collective-permute-start | bytes 1572872 | tf_op jit(solution)/shard_map/ppermute | solution.py:447
  19.7 1.3 %collective-permute-start.2 = (f32[8,384]{1,0:T(8,128)S(1)}, f32[8,384]{1,0:T(8,128)S(1)}, u32[]{:S(2)}, u32[]{:S(2)}) collective-permute-start(f32[8,384]{1,0:T(8,128)S(1)} %get-tuple-element.59), channel_id=1, source_target_pairs={{0,1},{1,2},{2,3},{4,5},{5,6},{6,7},{8,9},{9,10},{10,11},{12,13},{... | collective-permute-start | bytes 36872 | tf_op jit(solution)/shard_map/ppermute | solution.py:220
  21.0 1.3 %collective-permute-start.3 = (f32[8,384]{1,0:T(8,128)S(1)}, f32[8,384]{1,0:T(8,128)S(1)}, u32[]{:S(2)}, u32[]{:S(2)}) collective-permute-start(f32[8,384]{1,0:T(8,128)S(1)} %get-tuple-element.60), channel_id=1, source_target_pairs={{1,0},{2,1},{3,2},{5,4},{6,5},{7,6},{9,8},{10,9},{11,10},{13,12},{... | collective-permute-start | bytes 36872 | tf_op jit(solution)/shard_map/ppermute | solution.py:220
  22.3 3.5 %collective-permute-done.3.north_ref = f32[8,384]{1,0:T(8,128)S(1)} collective-permute-done((f32[8,384]{1,0:T(8,128)S(1)}, f32[8,384]{1,0:T(8,128)S(1)}, u32[]{:S(2)}, u32[]{:S(2)}) %collective-permute-start.3) | collective-permute-done | bytes 12320 | tf_op jit(solution)/shard_map/ppermute | solution.py:220
  25.8 4.9 %shard_map.80 = (f32[256,512]{1,0:T(8,128)}, f32[4,128]{1,0:T(4,128)S(1)}) custom-call(s32[4,128]{1,0:T(4,128)S(1)} %get-tuple-element.58.cell_ref, f32[256,512]{1,0:T(8,128)S(1)} %copy-done, s32[256,512]{1,0:T(8,128)S(1)} %copy-done.1, f32[256,512]{1,0:T(8,128)S(1)} %copy-done.2, f32[8,512]{1,0:T(8,128)S(1)} %collective-permute-done.before_ref, ...), custom_call_target="tpu_custom_call" | custom-call | flops 13107200 | bytes 104857600 | tf_op jit(solution)/shard_map/pallas_call | solution.py:241
  30.7 6.8 %all-gather.1.refs_4_ = f32[4,4,128]{2,1,0:T(4,128)S(1)} all-gather(f32[1,4,128]{2,1,0:T(4,128)S(1)} %bitcast.3), channel_id=2, replica_groups=mesh['box'=8,'panel'=4] {'panel'}, dimensions={0}, use_global_device_ids=true | all-gather | bytes 10240 | tf_op jit(solution)/shard_map/all_gather | solution.py:458
  37.6 1.2 %collective-permute-start.8 = (f32[4,4,128]{2,1,0:T(4,128)S(1)}, f32[4,4,128]{2,1,0:T(4,128)S(1)}, u32[]{:S(2)}, u32[]{:S(2)}) collective-permute-start(f32[4,4,128]{2,1,0:T(4,128)S(1)} %all-gather.1.refs_4_), channel_id=1, source_target_pairs={{0,8},{4,12},{8,0},{12,4},{16,24},{20,28},{24,16},{28,20},{1,9},{5... | collective-permute-start | bytes 24584 | tf_op jit(solution)/shard_map/ppermute | solution.py:447
  38.7 0.9 %collective-permute-start.7 = (f32[4,4,128]{2,1,0:T(4,128)S(1)}, f32[4,4,128]{2,1,0:T(4,128)S(1)}, u32[]{:S(2)}, u32[]{:S(2)}) collective-permute-start(f32[4,4,128]{2,1,0:T(4,128)S(1)} %all-gather.1.refs_4_), channel_id=1, source_target_pairs={{0,4},{4,8},{8,12},{12,0},{16,20},{20,24},{24,28},{28,16},{1,5},{5... | collective-permute-start | bytes 24584 | tf_op jit(solution)/shard_map/ppermute | solution.py:447
  39.7 1.6 %collective-permute-done.6.refs_3_ = s32[256,512]{1,0:T(8,128)S(1)} collective-permute-done((s32[256,512]{1,0:T(8,128)}, s32[256,512]{1,0:T(8,128)S(1)}, u32[]{:S(2)}, u32[]{:S(2)}) %collective-permute-start.6) | collective-permute-done | bytes 524320 | tf_op jit(solution)/shard_map/ppermute | solution.py:447
  41.3 2.0 %collective-permute-done.7.refs_5_ = f32[4,4,128]{2,1,0:T(4,128)S(1)} collective-permute-done((f32[4,4,128]{2,1,0:T(4,128)S(1)}, f32[4,4,128]{2,1,0:T(4,128)S(1)}, u32[]{:S(2)}, u32[]{:S(2)}) %collective-permute-start.7) | collective-permute-done | bytes 8224 | tf_op jit(solution)/shard_map/ppermute | solution.py:447
  43.3 11.8 %shard_map.81 = (f32[4,112,256]{2,1,0:T(8,128)S(1)}, bf16[4,112,256]{2,1,0:T(8,128)(2,1)S(1)}) custom-call(s32[1]{0:T(128)S(6)} %select_n.5.half_ref, s32[256,512]{1,0:T(8,128)S(1)} %copy-done.4, s32[256,512]{1,0:T(8,128)S(1)} %collective-permute-done.4.refs_1_, s32[256,512]{1,0:T(8,128)S(1)} %collective-permute-done.5.refs_2_, ...), custom_call_target="tpu_custom_call" | custom-call | flops 15032385536 | bytes 1835008 | tf_op jit(solution)/shard_map/pallas_call | solution.py:355
  55.1 2.6 %collective-permute-start.11 = (bf16[4,112,256]{2,1,0:T(8,128)(2,1)S(1)}, bf16[4,112,256]{2,1,0:T(8,128)(2,1)S(1)}, u32[]{:S(2)}, u32[]{:S(2)}) collective-permute-start(bf16[4,112,256]{2,1,0:T(8,128)(2,1)S(1)} %get-tuple-element.78), channel_id=1, source_target_pairs={{0,16},{4,20},{8,24},{12,28},{16,0},{20,4},{24,8},{28,12},{1,17},{... | collective-permute-start | bytes 688136 | tf_op jit(solution)/shard_map/ppermute | solution.py:470
  57.7 8.4 %shard_map.82 = (f32[4,80,256]{2,1,0:T(8,128)S(1)}, bf16[4,80,256]{2,1,0:T(8,128)(2,1)S(1)}) custom-call(s32[1]{0:T(128)S(6)} %select_n.5.half_ref, s32[256,512]{1,0:T(8,128)S(1)} %copy-done.4, s32[256,512]{1,0:T(8,128)S(1)} %collective-permute-done.4.refs_1_, s32[256,512]{1,0:T(8,128)S(1)} %collective-permute-done.5.refs_2_, ...), custom_call_target="tpu_custom_call" | custom-call | flops 10737418240 | bytes 1310720 | tf_op jit(solution)/shard_map/pallas_call | solution.py:355
  66.1 0.5 collective-permute-start.12
  66.6 6.7 %shard_map.83 = (f32[4,64,256]{2,1,0:T(8,128)S(1)}, bf16[4,64,256]{2,1,0:T(8,128)(2,1)S(1)}) custom-call(s32[1]{0:T(128)S(6)} %select_n.5.half_ref, s32[256,512]{1,0:T(8,128)S(1)} %copy-done.4, s32[256,512]{1,0:T(8,128)S(1)} %collective-permute-done.4.refs_1_, s32[256,512]{1,0:T(8,128)S(1)} %collective-permute-done.5.refs_2_, ...), custom_call_target="tpu_custom_call" | custom-call | flops 8589934592 | bytes 1048576 | tf_op jit(solution)/shard_map/pallas_call | solution.py:355
  73.3 2.6 %collective-permute-start.10 = (bf16[4,64,256]{2,1,0:T(8,128)(2,1)S(1)}, bf16[4,64,256]{2,1,0:T(8,128)(2,1)S(1)}, u32[]{:S(2)}, u32[]{:S(2)}) collective-permute-start(bf16[4,64,256]{2,1,0:T(8,128)(2,1)S(1)} %get-tuple-element.75), channel_id=1, source_target_pairs={{0,16},{4,20},{8,24},{12,28},{16,0},{20,4},{24,8},{28,12},{1,17},{... | collective-permute-start | bytes 393224 | tf_op jit(solution)/shard_map/ppermute | solution.py:470
  76.0 1.0 %collective-permute-start.13 = (bf16[192,256]{1,0:T(8,128)(2,1)S(1)}, bf16[192,256]{1,0:T(8,128)(2,1)S(1)}, u32[]{:S(2)}, u32[]{:S(2)}) collective-permute-start(bf16[192,256]{1,0:T(8,128)(2,1)S(1)} %get-tuple-element.80), channel_id=1, source_target_pairs={{0,8},{4,12},{8,0},{12,4},{16,24},{20,28},{24,16},{28,20},{1,9},{5... | collective-permute-start | bytes 294920 | tf_op jit(solution)/shard_map/ppermute | solution.py:447
  77.0 1.0 %collective-permute-start.17 = (bf16[192,256]{1,0:T(8,128)(2,1)S(1)}, bf16[192,256]{1,0:T(8,128)(2,1)S(1)}, u32[]{:S(2)}, u32[]{:S(2)}) collective-permute-start(bf16[192,256]{1,0:T(8,128)(2,1)S(1)} %get-tuple-element.87), channel_id=1, source_target_pairs={{0,4},{4,8},{8,12},{12,0},{16,20},{20,24},{24,28},{28,16},{1,5},{5... | collective-permute-start | bytes 294920 | tf_op jit(solution)/shard_map/ppermute | solution.py:447
  78.1 1.9 %collective-permute-start.18 = (bf16[192,256]{1,0:T(8,128)(2,1)S(1)}, bf16[192,256]{1,0:T(8,128)(2,1)S(1)}, u32[]{:S(2)}, u32[]{:S(2)}) collective-permute-start(bf16[192,256]{1,0:T(8,128)(2,1)S(1)} %get-tuple-element.89), channel_id=1, source_target_pairs={{0,12},{4,0},{8,4},{12,8},{16,28},{20,16},{24,20},{28,24},{1,13},{... | collective-permute-start | bytes 294920 | tf_op jit(solution)/shard_map/ppermute | solution.py:447
  79.9 0.8 collective-permute-done.10.refs_1_
  80.8 1.0 %collective-permute-done.13.refs_2_ = bf16[192,256]{1,0:T(8,128)(2,1)S(1)} collective-permute-done((bf16[192,256]{1,0:T(8,128)(2,1)S(1)}, bf16[192,256]{1,0:T(8,128)(2,1)S(1)}, u32[]{:S(2)}, u32[]{:S(2)}) %collective-permute-start.13) | collective-permute-done | bytes 98336 | tf_op jit(solution)/shard_map/ppermute | solution.py:447
  81.8 1.7 %collective-permute-start.15 = (bf16[64,256]{1,0:T(8,128)(2,1)S(1)}, bf16[64,256]{1,0:T(8,128)(2,1)S(1)}, u32[]{:S(2)}, u32[]{:S(2)}) collective-permute-start(bf16[64,256]{1,0:T(8,128)(2,1)S(1)} %get-tuple-element.84), channel_id=1, source_target_pairs={{0,8},{4,12},{8,0},{12,4},{16,24},{20,28},{24,16},{28,20},{1,9},{5... | collective-permute-start | bytes 98312 | tf_op jit(solution)/shard_map/ppermute | solution.py:447
  83.5 2.8 %collective-permute-start.16 = (bf16[64,256]{1,0:T(8,128)(2,1)S(1)}, bf16[64,256]{1,0:T(8,128)(2,1)S(1)}, u32[]{:S(2)}, u32[]{:S(2)}) collective-permute-start(bf16[64,256]{1,0:T(8,128)(2,1)S(1)} %get-tuple-element.85), channel_id=1, source_target_pairs={{0,12},{4,0},{8,4},{12,8},{16,28},{20,16},{24,20},{28,24},{1,13},{... | collective-permute-start | bytes 98312 | tf_op jit(solution)/shard_map/ppermute | solution.py:447
  86.4 0.9 %shard_map.86.refs_4_ = f32[1024,256]{1,0:T(8,128)} custom-call(s32[1]{0:T(128)S(6)} %rem.22.me_ref, bf16[192,256]{1,0:T(8,128)(2,1)S(1)} %get-tuple-element.86.refs_0_, bf16[192,256]{1,0:T(8,128)(2,1)S(1)} %collective-permute-done.17.refs_1_, bf16[192,256]{1,0:T(8,128)(2,1)S(1)} %collective-permute-done.13.refs_2_, ...), custom_call_target="tpu_custom_call" | custom-call | flops 196608 | bytes 1179648 | tf_op jit(solution)/shard_map/pallas_call | solution.py:422
  87.3 0.6 collective-permute-done.16.refs_3_
  88.0 0.7 shard_map.87
  (28 shorter events, 0.7 us)
Async XLA Ops:
  2.1 17.4 %copy-start = (f32[256,512]{1,0:T(8,128)S(1)}, f32[256,512]{1,0:T(8,128)}, u32[]{:S(2)}) copy-start(f32[256,512]{1,0:T(8,128)} %field_ref.3) | copy-start | bytes 1572868
  2.1 17.4 %copy-start.1 = (s32[256,512]{1,0:T(8,128)S(1)}, s32[256,512]{1,0:T(8,128)}, u32[]{:S(2)}) copy-start(s32[256,512]{1,0:T(8,128)} %mask_ref.3) | copy-start | bytes 1572868
  2.1 17.4 %copy-start.2 = (f32[256,512]{1,0:T(8,128)S(1)}, f32[256,512]{1,0:T(8,128)}, u32[]{:S(2)}) copy-start(f32[256,512]{1,0:T(8,128)} %visc_ref.3) | copy-start | bytes 1572868
  2.1 17.4 %copy-start.3 = (s32[128]{0:T(128)S(1)}, s32[128]{0:T(128)}, u32[]{:S(2)}) copy-start(s32[128]{0:T(128)} %param.9) | copy-start | bytes 1540
  2.1 10.8 %collective-permute-start = (f32[8,512]{1,0:T(8,128)}, f32[8,512]{1,0:T(8,128)S(1)}, u32[]{:S(2)}, u32[]{:S(2)}) collective-permute-start(f32[8,512]{1,0:T(8,128)} %get-tuple-element.48), channel_id=1, source_target_pairs={{0,4},{4,8},{8,12},{12,16},{16,20},{20,24},{24,28},{1,5},{5,9},{9,... | collective-permute-start | bytes 49160 | tf_op jit(solution)/shard_map/ppermute | solution.py:220
  7.1 5.8 %collective-permute-start.1 = (f32[8,512]{1,0:T(8,128)}, f32[8,512]{1,0:T(8,128)S(1)}, u32[]{:S(2)}, u32[]{:S(2)}) collective-permute-start(f32[8,512]{1,0:T(8,128)} %get-tuple-element.49), channel_id=1, source_target_pairs={{4,0},{8,4},{12,8},{16,12},{20,16},{24,20},{28,24},{5,1},{9,5},{13... | collective-permute-start | bytes 49160 | tf_op jit(solution)/shard_map/ppermute | solution.py:220
  12.8 30.4 %copy-start.4 = (s32[256,512]{1,0:T(8,128)S(1)}, s32[256,512]{1,0:T(8,128)}, u32[]{:S(2)}) copy-start(s32[256,512]{1,0:T(8,128)} %get-tuple-element.62.refs_0_) | copy-start | bytes 1572868
  12.9 24.6 %collective-permute-start.5 = (s32[256,512]{1,0:T(8,128)}, s32[256,512]{1,0:T(8,128)S(1)}, u32[]{:S(2)}, u32[]{:S(2)}) collective-permute-start(s32[256,512]{1,0:T(8,128)} %get-tuple-element.65), channel_id=1, source_target_pairs={{0,8},{4,12},{8,0},{12,4},{16,24},{20,28},{24,16},{28,20},{1,9},{5... | collective-permute-start | bytes 1572872 | tf_op jit(solution)/shard_map/ppermute | solution.py:447
  16.5 23.1 %collective-permute-start.4 = (s32[256,512]{1,0:T(8,128)}, s32[256,512]{1,0:T(8,128)S(1)}, u32[]{:S(2)}, u32[]{:S(2)}) collective-permute-start(s32[256,512]{1,0:T(8,128)} %get-tuple-element.63), channel_id=1, source_target_pairs={{0,4},{4,8},{8,12},{12,0},{16,20},{20,24},{24,28},{28,16},{1,5},{5... | collective-permute-start | bytes 1572872 | tf_op jit(solution)/shard_map/ppermute | solution.py:447
  17.1 24.1 %collective-permute-start.6 = (s32[256,512]{1,0:T(8,128)}, s32[256,512]{1,0:T(8,128)S(1)}, u32[]{:S(2)}, u32[]{:S(2)}) collective-permute-start(s32[256,512]{1,0:T(8,128)} %get-tuple-element.67), channel_id=1, source_target_pairs={{0,12},{4,0},{8,4},{12,8},{16,28},{20,16},{24,20},{28,24},{1,13},{... | collective-permute-start | bytes 1572872 | tf_op jit(solution)/shard_map/ppermute | solution.py:447
  19.7 2.6 %collective-permute-start.2 = (f32[8,384]{1,0:T(8,128)S(1)}, f32[8,384]{1,0:T(8,128)S(1)}, u32[]{:S(2)}, u32[]{:S(2)}) collective-permute-start(f32[8,384]{1,0:T(8,128)S(1)} %get-tuple-element.59), channel_id=1, source_target_pairs={{0,1},{1,2},{2,3},{4,5},{5,6},{6,7},{8,9},{9,10},{10,11},{12,13},{... | collective-permute-start | bytes 36872 | tf_op jit(solution)/shard_map/ppermute | solution.py:220
  21.0 4.8 %collective-permute-start.3 = (f32[8,384]{1,0:T(8,128)S(1)}, f32[8,384]{1,0:T(8,128)S(1)}, u32[]{:S(2)}, u32[]{:S(2)}) collective-permute-start(f32[8,384]{1,0:T(8,128)S(1)} %get-tuple-element.60), channel_id=1, source_target_pairs={{1,0},{2,1},{3,2},{5,4},{6,5},{7,6},{9,8},{10,9},{11,10},{13,12},{... | collective-permute-start | bytes 36872 | tf_op jit(solution)/shard_map/ppermute | solution.py:220
  37.5 3.8 %collective-permute-start.9 = (f32[4,4,128]{2,1,0:T(4,128)S(1)}, f32[4,4,128]{2,1,0:T(4,128)S(1)}, u32[]{:S(2)}, u32[]{:S(2)}) collective-permute-start(f32[4,4,128]{2,1,0:T(4,128)S(1)} %all-gather.1.refs_4_), channel_id=1, source_target_pairs={{0,12},{4,0},{8,4},{12,8},{16,28},{20,16},{24,20},{28,24},{1,13},{... | collective-permute-start | bytes 24584 | tf_op jit(solution)/shard_map/ppermute | solution.py:447
  37.6 3.8 %collective-permute-start.8 = (f32[4,4,128]{2,1,0:T(4,128)S(1)}, f32[4,4,128]{2,1,0:T(4,128)S(1)}, u32[]{:S(2)}, u32[]{:S(2)}) collective-permute-start(f32[4,4,128]{2,1,0:T(4,128)S(1)} %all-gather.1.refs_4_), channel_id=1, source_target_pairs={{0,8},{4,12},{8,0},{12,4},{16,24},{20,28},{24,16},{28,20},{1,9},{5... | collective-permute-start | bytes 24584 | tf_op jit(solution)/shard_map/ppermute | solution.py:447
  38.7 4.5 %collective-permute-start.7 = (f32[4,4,128]{2,1,0:T(4,128)S(1)}, f32[4,4,128]{2,1,0:T(4,128)S(1)}, u32[]{:S(2)}, u32[]{:S(2)}) collective-permute-start(f32[4,4,128]{2,1,0:T(4,128)S(1)} %all-gather.1.refs_4_), channel_id=1, source_target_pairs={{0,4},{4,8},{8,12},{12,0},{16,20},{20,24},{24,28},{28,16},{1,5},{5... | collective-permute-start | bytes 24584 | tf_op jit(solution)/shard_map/ppermute | solution.py:447
  55.1 20.9 %collective-permute-start.11 = (bf16[4,112,256]{2,1,0:T(8,128)(2,1)S(1)}, bf16[4,112,256]{2,1,0:T(8,128)(2,1)S(1)}, u32[]{:S(2)}, u32[]{:S(2)}) collective-permute-start(bf16[4,112,256]{2,1,0:T(8,128)(2,1)S(1)} %get-tuple-element.78), channel_id=1, source_target_pairs={{0,16},{4,20},{8,24},{12,28},{16,0},{20,4},{24,8},{28,12},{1,17},{... | collective-permute-start | bytes 688136 | tf_op jit(solution)/shard_map/ppermute | solution.py:470
  66.1 9.8 %collective-permute-start.12 = (bf16[4,80,256]{2,1,0:T(8,128)(2,1)S(1)}, bf16[4,80,256]{2,1,0:T(8,128)(2,1)S(1)}, u32[]{:S(2)}, u32[]{:S(2)}) collective-permute-start(bf16[4,80,256]{2,1,0:T(8,128)(2,1)S(1)} %get-tuple-element.79), channel_id=1, source_target_pairs={{0,16},{4,20},{8,24},{12,28},{16,0},{20,4},{24,8},{28,12},{1,17},{... | collective-permute-start | bytes 491528 | tf_op jit(solution)/shard_map/ppermute | solution.py:470
  73.3 7.4 %collective-permute-start.10 = (bf16[4,64,256]{2,1,0:T(8,128)(2,1)S(1)}, bf16[4,64,256]{2,1,0:T(8,128)(2,1)S(1)}, u32[]{:S(2)}, u32[]{:S(2)}) collective-permute-start(bf16[4,64,256]{2,1,0:T(8,128)(2,1)S(1)} %get-tuple-element.75), channel_id=1, source_target_pairs={{0,16},{4,20},{8,24},{12,28},{16,0},{20,4},{24,8},{28,12},{1,17},{... | collective-permute-start | bytes 393224 | tf_op jit(solution)/shard_map/ppermute | solution.py:470
  76.0 5.7 %collective-permute-start.13 = (bf16[192,256]{1,0:T(8,128)(2,1)S(1)}, bf16[192,256]{1,0:T(8,128)(2,1)S(1)}, u32[]{:S(2)}, u32[]{:S(2)}) collective-permute-start(bf16[192,256]{1,0:T(8,128)(2,1)S(1)} %get-tuple-element.80), channel_id=1, source_target_pairs={{0,8},{4,12},{8,0},{12,4},{16,24},{20,28},{24,16},{28,20},{1,9},{5... | collective-permute-start | bytes 294920 | tf_op jit(solution)/shard_map/ppermute | solution.py:447
  77.0 9.4 %collective-permute-start.17 = (bf16[192,256]{1,0:T(8,128)(2,1)S(1)}, bf16[192,256]{1,0:T(8,128)(2,1)S(1)}, u32[]{:S(2)}, u32[]{:S(2)}) collective-permute-start(bf16[192,256]{1,0:T(8,128)(2,1)S(1)} %get-tuple-element.87), channel_id=1, source_target_pairs={{0,4},{4,8},{8,12},{12,0},{16,20},{20,24},{24,28},{28,16},{1,5},{5... | collective-permute-start | bytes 294920 | tf_op jit(solution)/shard_map/ppermute | solution.py:447
  78.1 8.3 %collective-permute-start.18 = (bf16[192,256]{1,0:T(8,128)(2,1)S(1)}, bf16[192,256]{1,0:T(8,128)(2,1)S(1)}, u32[]{:S(2)}, u32[]{:S(2)}) collective-permute-start(bf16[192,256]{1,0:T(8,128)(2,1)S(1)} %get-tuple-element.89), channel_id=1, source_target_pairs={{0,12},{4,0},{8,4},{12,8},{16,28},{20,16},{24,20},{28,24},{1,13},{... | collective-permute-start | bytes 294920 | tf_op jit(solution)/shard_map/ppermute | solution.py:447
  81.7 5.6 %collective-permute-start.14 = (bf16[64,256]{1,0:T(8,128)(2,1)S(1)}, bf16[64,256]{1,0:T(8,128)(2,1)S(1)}, u32[]{:S(2)}, u32[]{:S(2)}) collective-permute-start(bf16[64,256]{1,0:T(8,128)(2,1)S(1)} %get-tuple-element.83), channel_id=1, source_target_pairs={{0,4},{4,8},{8,12},{12,0},{16,20},{20,24},{24,28},{28,16},{1,5},{5... | collective-permute-start | bytes 98312 | tf_op jit(solution)/shard_map/ppermute | solution.py:447
  81.8 5.5 %collective-permute-start.15 = (bf16[64,256]{1,0:T(8,128)(2,1)S(1)}, bf16[64,256]{1,0:T(8,128)(2,1)S(1)}, u32[]{:S(2)}, u32[]{:S(2)}) collective-permute-start(bf16[64,256]{1,0:T(8,128)(2,1)S(1)} %get-tuple-element.84), channel_id=1, source_target_pairs={{0,8},{4,12},{8,0},{12,4},{16,24},{20,28},{24,16},{28,20},{1,9},{5... | collective-permute-start | bytes 98312 | tf_op jit(solution)/shard_map/ppermute | solution.py:447
  83.5 4.4 %collective-permute-start.16 = (bf16[64,256]{1,0:T(8,128)(2,1)S(1)}, bf16[64,256]{1,0:T(8,128)(2,1)S(1)}, u32[]{:S(2)}, u32[]{:S(2)}) collective-permute-start(bf16[64,256]{1,0:T(8,128)(2,1)S(1)} %get-tuple-element.85), channel_id=1, source_target_pairs={{0,12},{4,0},{8,4},{12,8},{16,28},{20,16},{24,20},{28,24},{1,13},{... | collective-permute-start | bytes 98312 | tf_op jit(solution)/shard_map/ppermute | solution.py:447

commit v7 on v6

--- a/solution.py
+++ b/solution.py
@@ -30,13 +30,21 @@
     return pl.CostEstimate(flops=flops, bytes_accessed=size, transcendentals=0)
 
 
+def target(me, k, members):
+    return me ^ k if members & (members - 1) == 0 else (me + k) % members
+
+
+def source(me, k, members):
+    return me ^ k if members & (members - 1) == 0 else (me + members - k) % members
+
+
 def pack_kernel(me_ref, amp_ref, bin_ref, *refs):
     outs, turned = refs[:-1], refs[-1]
     scaled = (amp_ref[...].astype(F32) * AMP_SCALE).astype(jnp.int32)
     turned[...] = jnp.transpose((scaled << 16) | bin_ref[...])
     width = outs[0].shape[0]
     for k, out in enumerate(outs):
-        first = pl.multiple_of(lax.rem(me_ref[0] + k, len(outs)) * width, 8)
+        first = pl.multiple_of(target(me_ref[0], k, len(outs)) * width, 8)
         out[...] = turned[pl.ds(first, width), :]
 
 
@@ -378,7 +386,7 @@
 def join_kernel(parts, me_ref, *refs):
     keeps, gots, outs = refs[:parts], refs[parts : 2 * parts], refs[2 * parts :]
     for k, out in enumerate(outs):
-        owner = lax.rem(me_ref[0] + k, len(outs))
+        owner = target(me_ref[0], k, len(outs))
         at = 0
         for keep, got in zip(keeps, gots):
             count = keep.shape[1]
@@ -404,7 +412,7 @@
     pieces, (out_ref, wide, sems) = refs[:members], refs[-3:]
     copies = []
     for k, ref in enumerate(pieces):
-        owner = lax.rem(me_ref[0] - k + members, members)
+        owner = source(me_ref[0], k, members)
         start = pl.multiple_of(owner * width + first, 16)
         wide[k] = ref[...].astype(F32)
         copies.append(
@@ -442,7 +450,9 @@
 
     def spread(parts):
         def perm(k):
-            return [(i, i // members * members + (i + k) % members) for i in range(peers)]
+            return [
+                (i, i // members * members + target(i % members, k, members)) for i in range(peers)
+            ]
 
         return [lax.ppermute(x, "box", perm(k)) if k else x for k, x in enumerate(parts)]
 

time: 89.1 us -> 89.2 us (level)
  waiting for transfers between devices: 9.66 us -> 11.5 us
  starting transfers between devices: 31.7 us -> 30.2 us
    ppermute x12, waiting for transfers between devices: 5.26 us -> 7.19 us  [spread(): lax.ppermute(x, 'box', perm(k))]
    ppermute x12, starting transfers between devices: 17.2 us -> 15.7 us  [spread(): lax.ppermute(x, 'box', perm(k))]
  transfers between devices with their start and end apart: 19 -> 19, of which waited for: 8 -> 9; matrix products, arithmetic and copies ran while one was open for 0% -> 0% of each run, Pallas kernels for 29% -> 29%
where the time goes in v7:
time: 89.2 us; the launch traced here: 88.9 us
  Pallas kernels  39.7 us (45%)
  starting transfers between devices  30.2 us (34%)
  waiting for transfers between devices  11.5 us (13%)
  blocking collectives  6.75 us (8%)
    pallas_call x3, Pallas kernels, binned(): pl.pallas_call(bin_kernel, grid=(count // block,), in_specs=[SMEM] + [pl....  26.9 us
    ppermute x12, starting transfers between devices, spread(): lax.ppermute(x, 'box', perm(k))  15.7 us
    ppermute x4, starting transfers between devices, shifted(): return (lax.ppermute(last, axis, up), lax.ppermute(first, axis, down))  8.88 us
    ppermute x12, waiting for transfers between devices, spread(): lax.ppermute(x, 'box', perm(k))  7.19 us
    all_gather x1, blocking collectives, on_device(): sample = lax.all_gather(sample, 'panel')  6.75 us
    ppermute x3, starting transfers between devices, on_device(): groups[-1].append((keep, lax.ppermute(send, 'box', across)))  5.58 us
    pallas_call x1, Pallas kernels, field_window(): pl.pallas_call(step_kernel, in_specs=[SMEM] + [VMEM] * 7, out_specs=[pl.B...  4.9 us
    pallas_call x1, Pallas kernels, pack(): pl.pallas_call(pack_kernel, grid=(panels // LANES,), in_specs=[SMEM, bloc...  4.37 us
  transfers between devices with their start and end apart: 19, of which 9 were waited for; matrix products, arithmetic and copies ran while one was open for 0% of the time, Pallas kernels for 29%

profile of v7, /device:TPU:0, one launch (start us, length us, event | category | flops | bytes accessed | tf_op | source)
XLA Modules:
  0.0 88.9 jit_solution(6123772345925293552)
XLA Ops:
  0.6 1.4 %shard_map.77 = (f32[8,512]{1,0:T(8,128)}, f32[8,512]{1,0:T(8,128)}) custom-call(f32[256,512]{1,0:T(8,128)} %field_ref.3, s32[256,512]{1,0:T(8,128)} %mask_ref.3, f32[256,512]{1,0:T(8,128)} %visc_ref.3, f32[256,512]{1,0:T(8,128)} %field_ref.3, s32[256,512]{1,0:T(8,128)} %mask_ref.3, f32[256,512]{1,0:T(8,128)} %visc_ref.3), custom_call_target="tpu_custom_call" | custom-call | flops 8192 | bytes 131072 | tf_op jit(solution)/shard_map/pallas_call | solution.py:212
  2.1 5.0 %collective-permute-start = (f32[8,512]{1,0:T(8,128)}, f32[8,512]{1,0:T(8,128)S(1)}, u32[]{:S(2)}, u32[]{:S(2)}) collective-permute-start(f32[8,512]{1,0:T(8,128)} %get-tuple-element.48), channel_id=1, source_target_pairs={{0,4},{4,8},{8,12},{12,16},{16,20},{20,24},{24,28},{1,5},{5,9},{9,... | collective-permute-start | bytes 49160 | tf_op jit(solution)/shard_map/ppermute | solution.py:228
  7.1 1.3 %collective-permute-start.1 = (f32[8,512]{1,0:T(8,128)}, f32[8,512]{1,0:T(8,128)S(1)}, u32[]{:S(2)}, u32[]{:S(2)}) collective-permute-start(f32[8,512]{1,0:T(8,128)} %get-tuple-element.49), channel_id=1, source_target_pairs={{4,0},{8,4},{12,8},{16,12},{20,16},{24,20},{28,24},{5,1},{9,5},{13... | collective-permute-start | bytes 49160 | tf_op jit(solution)/shard_map/ppermute | solution.py:228
  8.4 4.4 %shard_map.78 = (s32[256,512]{1,0:T(8,128)}, s32[256,512]{1,0:T(8,128)}, s32[256,512]{1,0:T(8,128)}, s32[256,512]{1,0:T(8,128)}) custom-call(s32[1]{0:T(128)S(6)} %rem.22.me_ref, bf16[512,1024]{1,0:T(8,128)(2,1)} %amp_ref, s32[512,1024]{1,0:T(8,128)} %bin_ref), custom_call_target="tpu_custom_call" | custom-call | flops 524288 | bytes 5242880 | tf_op jit(solution)/shard_map/pallas_call | solution.py:56
  12.9 3.5 %collective-permute-start.5 = (s32[256,512]{1,0:T(8,128)}, s32[256,512]{1,0:T(8,128)S(1)}, u32[]{:S(2)}, u32[]{:S(2)}) collective-permute-start(s32[256,512]{1,0:T(8,128)} %get-tuple-element.65), channel_id=1, source_target_pairs={{0,8},{4,12},{8,0},{12,4},{16,24},{20,28},{24,16},{28,20},{1,9},{5... | collective-permute-start | bytes 1572872 | tf_op jit(solution)/shard_map/ppermute | solution.py:457
  16.5 0.6 collective-permute-start.4
  17.1 0.9 %collective-permute-start.6 = (s32[256,512]{1,0:T(8,128)}, s32[256,512]{1,0:T(8,128)S(1)}, u32[]{:S(2)}, u32[]{:S(2)}) collective-permute-start(s32[256,512]{1,0:T(8,128)} %get-tuple-element.67), channel_id=1, source_target_pairs={{0,12},{4,8},{8,4},{12,0},{16,28},{20,24},{24,20},{28,16},{1,13},{... | collective-permute-start | bytes 1572872 | tf_op jit(solution)/shard_map/ppermute | solution.py:457
  18.3 1.3 %collective-permute-start.2 = (f32[8,384]{1,0:T(8,128)S(1)}, f32[8,384]{1,0:T(8,128)S(1)}, u32[]{:S(2)}, u32[]{:S(2)}) collective-permute-start(f32[8,384]{1,0:T(8,128)S(1)} %get-tuple-element.59), channel_id=1, source_target_pairs={{0,1},{1,2},{2,3},{4,5},{5,6},{6,7},{8,9},{9,10},{10,11},{12,13},{... | collective-permute-start | bytes 36872 | tf_op jit(solution)/shard_map/ppermute | solution.py:228
  19.6 1.3 %collective-permute-start.3 = (f32[8,384]{1,0:T(8,128)S(1)}, f32[8,384]{1,0:T(8,128)S(1)}, u32[]{:S(2)}, u32[]{:S(2)}) collective-permute-start(f32[8,384]{1,0:T(8,128)S(1)} %get-tuple-element.60), channel_id=1, source_target_pairs={{1,0},{2,1},{3,2},{5,4},{6,5},{7,6},{9,8},{10,9},{11,10},{13,12},{... | collective-permute-start | bytes 36872 | tf_op jit(solution)/shard_map/ppermute | solution.py:228
  20.9 3.5 %collective-permute-done.3.north_ref = f32[8,384]{1,0:T(8,128)S(1)} collective-permute-done((f32[8,384]{1,0:T(8,128)S(1)}, f32[8,384]{1,0:T(8,128)S(1)}, u32[]{:S(2)}, u32[]{:S(2)}) %collective-permute-start.3) | collective-permute-done | bytes 12320 | tf_op jit(solution)/shard_map/ppermute | solution.py:228
  24.4 4.9 %shard_map.80 = (f32[256,512]{1,0:T(8,128)}, f32[4,128]{1,0:T(4,128)S(1)}) custom-call(s32[4,128]{1,0:T(4,128)S(1)} %get-tuple-element.58.cell_ref, f32[256,512]{1,0:T(8,128)S(1)} %copy-done, s32[256,512]{1,0:T(8,128)S(1)} %copy-done.1, f32[256,512]{1,0:T(8,128)S(1)} %copy-done.2, f32[8,512]{1,0:T(8,128)S(1)} %collective-permute-done.before_ref, ...), custom_call_target="tpu_custom_call" | custom-call | flops 13107200 | bytes 104857600 | tf_op jit(solution)/shard_map/pallas_call | solution.py:249
  29.3 6.8 %all-gather.1.refs_4_ = f32[4,4,128]{2,1,0:T(4,128)S(1)} all-gather(f32[1,4,128]{2,1,0:T(4,128)S(1)} %bitcast.3), channel_id=2, replica_groups=mesh['box'=8,'panel'=4] {'panel'}, dimensions={0}, use_global_device_ids=true | all-gather | bytes 10240 | tf_op jit(solution)/shard_map/all_gather | solution.py:468
  36.0 2.0 %collective-permute-start.9 = (f32[4,4,128]{2,1,0:T(4,128)S(1)}, f32[4,4,128]{2,1,0:T(4,128)S(1)}, u32[]{:S(2)}, u32[]{:S(2)}) collective-permute-start(f32[4,4,128]{2,1,0:T(4,128)S(1)} %all-gather.1.refs_4_), channel_id=1, source_target_pairs={{0,12},{4,8},{8,4},{12,0},{16,28},{20,24},{24,20},{28,16},{1,13},{... | collective-permute-start | bytes 24584 | tf_op jit(solution)/shard_map/ppermute | solution.py:457
  38.5 1.0 %collective-permute-start.7 = (f32[4,4,128]{2,1,0:T(4,128)S(1)}, f32[4,4,128]{2,1,0:T(4,128)S(1)}, u32[]{:S(2)}, u32[]{:S(2)}) collective-permute-start(f32[4,4,128]{2,1,0:T(4,128)S(1)} %all-gather.1.refs_4_), channel_id=1, source_target_pairs={{0,4},{4,0},{8,12},{12,8},{16,20},{20,16},{24,28},{28,24},{1,5},{5... | collective-permute-start | bytes 24584 | tf_op jit(solution)/shard_map/ppermute | solution.py:457
  39.6 1.4 %collective-permute-done.4.refs_1_ = s32[256,512]{1,0:T(8,128)S(1)} collective-permute-done((s32[256,512]{1,0:T(8,128)}, s32[256,512]{1,0:T(8,128)S(1)}, u32[]{:S(2)}, u32[]{:S(2)}) %collective-permute-start.4) | collective-permute-done | bytes 524320 | tf_op jit(solution)/shard_map/ppermute | solution.py:457
  41.0 0.7 collective-permute-done.8.refs_6_
  42.2 11.8 %shard_map.81 = (f32[4,112,256]{2,1,0:T(8,128)S(1)}, bf16[4,112,256]{2,1,0:T(8,128)(2,1)S(1)}) custom-call(s32[1]{0:T(128)S(6)} %select_n.5.half_ref, s32[256,512]{1,0:T(8,128)S(1)} %copy-done.4, s32[256,512]{1,0:T(8,128)S(1)} %collective-permute-done.4.refs_1_, s32[256,512]{1,0:T(8,128)S(1)} %collective-permute-done.5.refs_2_, ...), custom_call_target="tpu_custom_call" | custom-call | flops 15032385536 | bytes 1835008 | tf_op jit(solution)/shard_map/pallas_call | solution.py:363
  54.0 2.5 %collective-permute-start.11 = (bf16[4,112,256]{2,1,0:T(8,128)(2,1)S(1)}, bf16[4,112,256]{2,1,0:T(8,128)(2,1)S(1)}, u32[]{:S(2)}, u32[]{:S(2)}) collective-permute-start(bf16[4,112,256]{2,1,0:T(8,128)(2,1)S(1)} %get-tuple-element.78), channel_id=1, source_target_pairs={{0,16},{4,20},{8,24},{12,28},{16,0},{20,4},{24,8},{28,12},{1,17},{... | collective-permute-start | bytes 688136 | tf_op jit(solution)/shard_map/ppermute | solution.py:480
  56.5 8.4 %shard_map.82 = (f32[4,80,256]{2,1,0:T(8,128)S(1)}, bf16[4,80,256]{2,1,0:T(8,128)(2,1)S(1)}) custom-call(s32[1]{0:T(128)S(6)} %select_n.5.half_ref, s32[256,512]{1,0:T(8,128)S(1)} %copy-done.4, s32[256,512]{1,0:T(8,128)S(1)} %collective-permute-done.4.refs_1_, s32[256,512]{1,0:T(8,128)S(1)} %collective-permute-done.5.refs_2_, ...), custom_call_target="tpu_custom_call" | custom-call | flops 10737418240 | bytes 1310720 | tf_op jit(solution)/shard_map/pallas_call | solution.py:363
  64.9 0.5 collective-permute-start.12
  65.5 6.7 %shard_map.83 = (f32[4,64,256]{2,1,0:T(8,128)S(1)}, bf16[4,64,256]{2,1,0:T(8,128)(2,1)S(1)}) custom-call(s32[1]{0:T(128)S(6)} %select_n.5.half_ref, s32[256,512]{1,0:T(8,128)S(1)} %copy-done.4, s32[256,512]{1,0:T(8,128)S(1)} %collective-permute-done.4.refs_1_, s32[256,512]{1,0:T(8,128)S(1)} %collective-permute-done.5.refs_2_, ...), custom_call_target="tpu_custom_call" | custom-call | flops 8589934592 | bytes 1048576 | tf_op jit(solution)/shard_map/pallas_call | solution.py:363
  72.2 2.5 %collective-permute-start.10 = (bf16[4,64,256]{2,1,0:T(8,128)(2,1)S(1)}, bf16[4,64,256]{2,1,0:T(8,128)(2,1)S(1)}, u32[]{:S(2)}, u32[]{:S(2)}) collective-permute-start(bf16[4,64,256]{2,1,0:T(8,128)(2,1)S(1)} %get-tuple-element.75), channel_id=1, source_target_pairs={{0,16},{4,20},{8,24},{12,28},{16,0},{20,4},{24,8},{28,12},{1,17},{... | collective-permute-start | bytes 393224 | tf_op jit(solution)/shard_map/ppermute | solution.py:480
  74.8 1.6 %collective-permute-start.13 = (bf16[192,256]{1,0:T(8,128)(2,1)S(1)}, bf16[192,256]{1,0:T(8,128)(2,1)S(1)}, u32[]{:S(2)}, u32[]{:S(2)}) collective-permute-start(bf16[192,256]{1,0:T(8,128)(2,1)S(1)} %get-tuple-element.80), channel_id=1, source_target_pairs={{0,8},{4,12},{8,0},{12,4},{16,24},{20,28},{24,16},{28,20},{1,9},{5... | collective-permute-start | bytes 294920 | tf_op jit(solution)/shard_map/ppermute | solution.py:457
  76.5 1.5 %collective-permute-start.17 = (bf16[192,256]{1,0:T(8,128)(2,1)S(1)}, bf16[192,256]{1,0:T(8,128)(2,1)S(1)}, u32[]{:S(2)}, u32[]{:S(2)}) collective-permute-start(bf16[192,256]{1,0:T(8,128)(2,1)S(1)} %get-tuple-element.87), channel_id=1, source_target_pairs={{0,4},{4,0},{8,12},{12,8},{16,20},{20,16},{24,28},{28,24},{1,5},{5... | collective-permute-start | bytes 294920 | tf_op jit(solution)/shard_map/ppermute | solution.py:457
  78.4 0.6 collective-permute-done.10.refs_1_
  79.0 1.9 %collective-permute-done.13.refs_2_ = bf16[192,256]{1,0:T(8,128)(2,1)S(1)} collective-permute-done((bf16[192,256]{1,0:T(8,128)(2,1)S(1)}, bf16[192,256]{1,0:T(8,128)(2,1)S(1)}, u32[]{:S(2)}, u32[]{:S(2)}) %collective-permute-start.13) | collective-permute-done | bytes 98336 | tf_op jit(solution)/shard_map/ppermute | solution.py:457
  81.0 0.9 collective-permute-start.14
  81.8 1.5 %collective-permute-start.15 = (bf16[64,256]{1,0:T(8,128)(2,1)S(1)}, bf16[64,256]{1,0:T(8,128)(2,1)S(1)}, u32[]{:S(2)}, u32[]{:S(2)}) collective-permute-start(bf16[64,256]{1,0:T(8,128)(2,1)S(1)} %get-tuple-element.84), channel_id=1, source_target_pairs={{0,8},{4,12},{8,0},{12,4},{16,24},{20,28},{24,16},{28,20},{1,9},{5... | collective-permute-start | bytes 98312 | tf_op jit(solution)/shard_map/ppermute | solution.py:457
  83.3 1.2 %collective-permute-start.16 = (bf16[64,256]{1,0:T(8,128)(2,1)S(1)}, bf16[64,256]{1,0:T(8,128)(2,1)S(1)}, u32[]{:S(2)}, u32[]{:S(2)}) collective-permute-start(bf16[64,256]{1,0:T(8,128)(2,1)S(1)} %get-tuple-element.85), channel_id=1, source_target_pairs={{0,12},{4,8},{8,4},{12,0},{16,28},{20,24},{24,20},{28,16},{1,13},{... | collective-permute-start | bytes 98312 | tf_op jit(solution)/shard_map/ppermute | solution.py:457
  84.5 0.9 %shard_map.86.refs_4_ = f32[1024,256]{1,0:T(8,128)} custom-call(s32[1]{0:T(128)S(6)} %rem.22.me_ref, bf16[192,256]{1,0:T(8,128)(2,1)S(1)} %get-tuple-element.86.refs_0_, bf16[192,256]{1,0:T(8,128)(2,1)S(1)} %collective-permute-done.17.refs_1_, bf16[192,256]{1,0:T(8,128)(2,1)S(1)} %collective-permute-done.13.refs_2_, ...), custom_call_target="tpu_custom_call" | custom-call | flops 196608 | bytes 1179648 | tf_op jit(solution)/shard_map/pallas_call | solution.py:430
  85.7 2.4 %collective-permute-done.16.refs_3_ = bf16[64,256]{1,0:T(8,128)(2,1)S(1)} collective-permute-done((bf16[64,256]{1,0:T(8,128)(2,1)S(1)}, bf16[64,256]{1,0:T(8,128)(2,1)S(1)}, u32[]{:S(2)}, u32[]{:S(2)}) %collective-permute-start.16) | collective-permute-done | bytes 32800 | tf_op jit(solution)/shard_map/ppermute | solution.py:457
  88.1 0.7 shard_map.87
  (28 shorter events, 2.1 us)
Async XLA Ops:
  2.1 15.9 %copy-start = (f32[256,512]{1,0:T(8,128)S(1)}, f32[256,512]{1,0:T(8,128)}, u32[]{:S(2)}) copy-start(f32[256,512]{1,0:T(8,128)} %field_ref.3) | copy-start | bytes 1572868
  2.1 15.9 %copy-start.1 = (s32[256,512]{1,0:T(8,128)S(1)}, s32[256,512]{1,0:T(8,128)}, u32[]{:S(2)}) copy-start(s32[256,512]{1,0:T(8,128)} %mask_ref.3) | copy-start | bytes 1572868
  2.1 15.9 %copy-start.2 = (f32[256,512]{1,0:T(8,128)S(1)}, f32[256,512]{1,0:T(8,128)}, u32[]{:S(2)}) copy-start(f32[256,512]{1,0:T(8,128)} %visc_ref.3) | copy-start | bytes 1572868
  2.1 15.9 %copy-start.3 = (s32[128]{0:T(128)S(1)}, s32[128]{0:T(128)}, u32[]{:S(2)}) copy-start(s32[128]{0:T(128)} %param.9) | copy-start | bytes 1540
  2.1 10.7 %collective-permute-start = (f32[8,512]{1,0:T(8,128)}, f32[8,512]{1,0:T(8,128)S(1)}, u32[]{:S(2)}, u32[]{:S(2)}) collective-permute-start(f32[8,512]{1,0:T(8,128)} %get-tuple-element.48), channel_id=1, source_target_pairs={{0,4},{4,8},{8,12},{12,16},{16,20},{20,24},{24,28},{1,5},{5,9},{9,... | collective-permute-start | bytes 49160 | tf_op jit(solution)/shard_map/ppermute | solution.py:228
  7.1 5.8 %collective-permute-start.1 = (f32[8,512]{1,0:T(8,128)}, f32[8,512]{1,0:T(8,128)S(1)}, u32[]{:S(2)}, u32[]{:S(2)}) collective-permute-start(f32[8,512]{1,0:T(8,128)} %get-tuple-element.49), channel_id=1, source_target_pairs={{4,0},{8,4},{12,8},{16,12},{20,16},{24,20},{28,24},{5,1},{9,5},{13... | collective-permute-start | bytes 49160 | tf_op jit(solution)/shard_map/ppermute | solution.py:228
  12.8 29.4 %copy-start.4 = (s32[256,512]{1,0:T(8,128)S(1)}, s32[256,512]{1,0:T(8,128)}, u32[]{:S(2)}) copy-start(s32[256,512]{1,0:T(8,128)} %get-tuple-element.62.refs_0_) | copy-start | bytes 1572868
  12.9 23.1 %collective-permute-start.5 = (s32[256,512]{1,0:T(8,128)}, s32[256,512]{1,0:T(8,128)S(1)}, u32[]{:S(2)}, u32[]{:S(2)}) collective-permute-start(s32[256,512]{1,0:T(8,128)} %get-tuple-element.65), channel_id=1, source_target_pairs={{0,8},{4,12},{8,0},{12,4},{16,24},{20,28},{24,16},{28,20},{1,9},{5... | collective-permute-start | bytes 1572872 | tf_op jit(solution)/shard_map/ppermute | solution.py:457
  16.5 24.5 %collective-permute-start.4 = (s32[256,512]{1,0:T(8,128)}, s32[256,512]{1,0:T(8,128)S(1)}, u32[]{:S(2)}, u32[]{:S(2)}) collective-permute-start(s32[256,512]{1,0:T(8,128)} %get-tuple-element.63), channel_id=1, source_target_pairs={{0,4},{4,0},{8,12},{12,8},{16,20},{20,16},{24,28},{28,24},{1,5},{5... | collective-permute-start | bytes 1572872 | tf_op jit(solution)/shard_map/ppermute | solution.py:457
  17.1 23.9 %collective-permute-start.6 = (s32[256,512]{1,0:T(8,128)}, s32[256,512]{1,0:T(8,128)S(1)}, u32[]{:S(2)}, u32[]{:S(2)}) collective-permute-start(s32[256,512]{1,0:T(8,128)} %get-tuple-element.67), channel_id=1, source_target_pairs={{0,12},{4,8},{8,4},{12,0},{16,28},{20,24},{24,20},{28,16},{1,13},{... | collective-permute-start | bytes 1572872 | tf_op jit(solution)/shard_map/ppermute | solution.py:457
  18.3 2.6 %collective-permute-start.2 = (f32[8,384]{1,0:T(8,128)S(1)}, f32[8,384]{1,0:T(8,128)S(1)}, u32[]{:S(2)}, u32[]{:S(2)}) collective-permute-start(f32[8,384]{1,0:T(8,128)S(1)} %get-tuple-element.59), channel_id=1, source_target_pairs={{0,1},{1,2},{2,3},{4,5},{5,6},{6,7},{8,9},{9,10},{10,11},{12,13},{... | collective-permute-start | bytes 36872 | tf_op jit(solution)/shard_map/ppermute | solution.py:228
  19.6 4.8 %collective-permute-start.3 = (f32[8,384]{1,0:T(8,128)S(1)}, f32[8,384]{1,0:T(8,128)S(1)}, u32[]{:S(2)}, u32[]{:S(2)}) collective-permute-start(f32[8,384]{1,0:T(8,128)S(1)} %get-tuple-element.60), channel_id=1, source_target_pairs={{1,0},{2,1},{3,2},{5,4},{6,5},{7,6},{9,8},{10,9},{11,10},{13,12},{... | collective-permute-start | bytes 36872 | tf_op jit(solution)/shard_map/ppermute | solution.py:228
  36.0 5.0 %collective-permute-start.9 = (f32[4,4,128]{2,1,0:T(4,128)S(1)}, f32[4,4,128]{2,1,0:T(4,128)S(1)}, u32[]{:S(2)}, u32[]{:S(2)}) collective-permute-start(f32[4,4,128]{2,1,0:T(4,128)S(1)} %all-gather.1.refs_4_), channel_id=1, source_target_pairs={{0,12},{4,8},{8,4},{12,0},{16,28},{20,24},{24,20},{28,16},{1,13},{... | collective-permute-start | bytes 24584 | tf_op jit(solution)/shard_map/ppermute | solution.py:457
  38.1 3.7 %collective-permute-start.8 = (f32[4,4,128]{2,1,0:T(4,128)S(1)}, f32[4,4,128]{2,1,0:T(4,128)S(1)}, u32[]{:S(2)}, u32[]{:S(2)}) collective-permute-start(f32[4,4,128]{2,1,0:T(4,128)S(1)} %all-gather.1.refs_4_), channel_id=1, source_target_pairs={{0,8},{4,12},{8,0},{12,4},{16,24},{20,28},{24,16},{28,20},{1,9},{5... | collective-permute-start | bytes 24584 | tf_op jit(solution)/shard_map/ppermute | solution.py:457
  38.5 3.7 %collective-permute-start.7 = (f32[4,4,128]{2,1,0:T(4,128)S(1)}, f32[4,4,128]{2,1,0:T(4,128)S(1)}, u32[]{:S(2)}, u32[]{:S(2)}) collective-permute-start(f32[4,4,128]{2,1,0:T(4,128)S(1)} %all-gather.1.refs_4_), channel_id=1, source_target_pairs={{0,4},{4,0},{8,12},{12,8},{16,20},{20,16},{24,28},{28,24},{1,5},{5... | collective-permute-start | bytes 24584 | tf_op jit(solution)/shard_map/ppermute | solution.py:457
  54.0 20.8 %collective-permute-start.11 = (bf16[4,112,256]{2,1,0:T(8,128)(2,1)S(1)}, bf16[4,112,256]{2,1,0:T(8,128)(2,1)S(1)}, u32[]{:S(2)}, u32[]{:S(2)}) collective-permute-start(bf16[4,112,256]{2,1,0:T(8,128)(2,1)S(1)} %get-tuple-element.78), channel_id=1, source_target_pairs={{0,16},{4,20},{8,24},{12,28},{16,0},{20,4},{24,8},{28,12},{1,17},{... | collective-permute-start | bytes 688136 | tf_op jit(solution)/shard_map/ppermute | solution.py:480
  64.9 9.8 %collective-permute-start.12 = (bf16[4,80,256]{2,1,0:T(8,128)(2,1)S(1)}, bf16[4,80,256]{2,1,0:T(8,128)(2,1)S(1)}, u32[]{:S(2)}, u32[]{:S(2)}) collective-permute-start(bf16[4,80,256]{2,1,0:T(8,128)(2,1)S(1)} %get-tuple-element.79), channel_id=1, source_target_pairs={{0,16},{4,20},{8,24},{12,28},{16,0},{20,4},{24,8},{28,12},{1,17},{... | collective-permute-start | bytes 491528 | tf_op jit(solution)/shard_map/ppermute | solution.py:480
  72.2 6.8 %collective-permute-start.10 = (bf16[4,64,256]{2,1,0:T(8,128)(2,1)S(1)}, bf16[4,64,256]{2,1,0:T(8,128)(2,1)S(1)}, u32[]{:S(2)}, u32[]{:S(2)}) collective-permute-start(bf16[4,64,256]{2,1,0:T(8,128)(2,1)S(1)} %get-tuple-element.75), channel_id=1, source_target_pairs={{0,16},{4,20},{8,24},{12,28},{16,0},{20,4},{24,8},{28,12},{1,17},{... | collective-permute-start | bytes 393224 | tf_op jit(solution)/shard_map/ppermute | solution.py:480
  74.8 6.1 %collective-permute-start.13 = (bf16[192,256]{1,0:T(8,128)(2,1)S(1)}, bf16[192,256]{1,0:T(8,128)(2,1)S(1)}, u32[]{:S(2)}, u32[]{:S(2)}) collective-permute-start(bf16[192,256]{1,0:T(8,128)(2,1)S(1)} %get-tuple-element.80), channel_id=1, source_target_pairs={{0,8},{4,12},{8,0},{12,4},{16,24},{20,28},{24,16},{28,20},{1,9},{5... | collective-permute-start | bytes 294920 | tf_op jit(solution)/shard_map/ppermute | solution.py:457
  76.5 8.0 %collective-permute-start.17 = (bf16[192,256]{1,0:T(8,128)(2,1)S(1)}, bf16[192,256]{1,0:T(8,128)(2,1)S(1)}, u32[]{:S(2)}, u32[]{:S(2)}) collective-permute-start(bf16[192,256]{1,0:T(8,128)(2,1)S(1)} %get-tuple-element.87), channel_id=1, source_target_pairs={{0,4},{4,0},{8,12},{12,8},{16,20},{20,16},{24,28},{28,24},{1,5},{5... | collective-permute-start | bytes 294920 | tf_op jit(solution)/shard_map/ppermute | solution.py:457
  78.0 6.5 %collective-permute-start.18 = (bf16[192,256]{1,0:T(8,128)(2,1)S(1)}, bf16[192,256]{1,0:T(8,128)(2,1)S(1)}, u32[]{:S(2)}, u32[]{:S(2)}) collective-permute-start(bf16[192,256]{1,0:T(8,128)(2,1)S(1)} %get-tuple-element.89), channel_id=1, source_target_pairs={{0,12},{4,8},{8,4},{12,0},{16,28},{20,24},{24,20},{28,16},{1,13},{... | collective-permute-start | bytes 294920 | tf_op jit(solution)/shard_map/ppermute | solution.py:457
  81.0 4.5 %collective-permute-start.14 = (bf16[64,256]{1,0:T(8,128)(2,1)S(1)}, bf16[64,256]{1,0:T(8,128)(2,1)S(1)}, u32[]{:S(2)}, u32[]{:S(2)}) collective-permute-start(bf16[64,256]{1,0:T(8,128)(2,1)S(1)} %get-tuple-element.83), channel_id=1, source_target_pairs={{0,4},{4,0},{8,12},{12,8},{16,20},{20,16},{24,28},{28,24},{1,5},{5... | collective-permute-start | bytes 98312 | tf_op jit(solution)/shard_map/ppermute | solution.py:457
  81.8 3.9 %collective-permute-start.15 = (bf16[64,256]{1,0:T(8,128)(2,1)S(1)}, bf16[64,256]{1,0:T(8,128)(2,1)S(1)}, u32[]{:S(2)}, u32[]{:S(2)}) collective-permute-start(bf16[64,256]{1,0:T(8,128)(2,1)S(1)} %get-tuple-element.84), channel_id=1, source_target_pairs={{0,8},{4,12},{8,0},{12,4},{16,24},{20,28},{24,16},{28,20},{1,9},{5... | collective-permute-start | bytes 98312 | tf_op jit(solution)/shard_map/ppermute | solution.py:457
  83.3 4.8 %collective-permute-start.16 = (bf16[64,256]{1,0:T(8,128)(2,1)S(1)}, bf16[64,256]{1,0:T(8,128)(2,1)S(1)}, u32[]{:S(2)}, u32[]{:S(2)}) collective-permute-start(bf16[64,256]{1,0:T(8,128)(2,1)S(1)} %get-tuple-element.85), channel_id=1, source_target_pairs={{0,12},{4,8},{8,4},{12,0},{16,28},{20,24},{24,20},{28,16},{1,13},{... | collective-permute-start | bytes 98312 | tf_op jit(solution)/shard_map/ppermute | solution.py:457

commit v8 on v7

--- a/solution.py
+++ b/solution.py
@@ -483,7 +483,7 @@
     for group in groups:
         keeps, gots = [x[0] for x in group], [x[1] for x in group]
         if pieces is not None:
-            gots[-1], pieces[middle] = lax.optimization_barrier((gots[-1], pieces[middle]))
+            gots[-1], pieces[1] = lax.optimization_barrier((gots[-1], pieces[1]))
         pieces = spread(join(me, keeps, gots))
         waiting.append(pieces)
     first, signals = 0, None

time: 89.2 us -> 89.9 us (level)
  transfers between devices with their start and end apart: 19 -> 19, of which waited for: 9 -> 8; matrix products, arithmetic and copies ran while one was open for 0% -> 0% of each run, Pallas kernels for 29% -> 29%
where the time goes in v8:
time: 89.9 us; the launch traced here: 89.5 us
  Pallas kernels  39.7 us (44%)
  starting transfers between devices  31 us (34%)
  waiting for transfers between devices  11.3 us (13%)
  blocking collectives  6.75 us (8%)
    pallas_call x3, Pallas kernels, binned(): pl.pallas_call(bin_kernel, grid=(count // block,), in_specs=[SMEM] + [pl....  26.9 us
    ppermute x12, starting transfers between devices, spread(): lax.ppermute(x, 'box', perm(k))  16.5 us
    ppermute x4, starting transfers between devices, shifted(): return (lax.ppermute(last, axis, up), lax.ppermute(first, axis, down))  8.88 us
    all_gather x1, blocking collectives, on_device(): sample = lax.all_gather(sample, 'panel')  6.75 us
    ppermute x12, waiting for transfers between devices, spread(): lax.ppermute(x, 'box', perm(k))  6.48 us
    ppermute x3, starting transfers between devices, on_device(): groups[-1].append((keep, lax.ppermute(send, 'box', across)))  5.58 us
    pallas_call x1, Pallas kernels, field_window(): pl.pallas_call(step_kernel, in_specs=[SMEM] + [VMEM] * 7, out_specs=[pl.B...  4.9 us
    pallas_call x1, Pallas kernels, pack(): pl.pallas_call(pack_kernel, grid=(panels // LANES,), in_specs=[SMEM, bloc...  4.37 us
  transfers between devices with their start and end apart: 19, of which 8 were waited for; matrix products, arithmetic and copies ran while one was open for 0% of the time, Pallas kernels for 29%

profile of v8, /device:TPU:0, one launch (start us, length us, event | category | flops | bytes accessed | tf_op | source)
XLA Modules:
  0.0 89.5 jit_solution(2747543775734085906)
XLA Ops:
  0.6 1.4 %shard_map.77 = (f32[8,512]{1,0:T(8,128)}, f32[8,512]{1,0:T(8,128)}) custom-call(f32[256,512]{1,0:T(8,128)} %field_ref.3, s32[256,512]{1,0:T(8,128)} %mask_ref.3, f32[256,512]{1,0:T(8,128)} %visc_ref.3, f32[256,512]{1,0:T(8,128)} %field_ref.3, s32[256,512]{1,0:T(8,128)} %mask_ref.3, f32[256,512]{1,0:T(8,128)} %visc_ref.3), custom_call_target="tpu_custom_call" | custom-call | flops 8192 | bytes 131072 | tf_op jit(solution)/shard_map/pallas_call | solution.py:212
  2.1 5.0 %collective-permute-start = (f32[8,512]{1,0:T(8,128)}, f32[8,512]{1,0:T(8,128)S(1)}, u32[]{:S(2)}, u32[]{:S(2)}) collective-permute-start(f32[8,512]{1,0:T(8,128)} %get-tuple-element.48), channel_id=1, source_target_pairs={{0,4},{4,8},{8,12},{12,16},{16,20},{20,24},{24,28},{1,5},{5,9},{9,... | collective-permute-start | bytes 49160 | tf_op jit(solution)/shard_map/ppermute | solution.py:228
  7.1 1.3 %collective-permute-start.1 = (f32[8,512]{1,0:T(8,128)}, f32[8,512]{1,0:T(8,128)S(1)}, u32[]{:S(2)}, u32[]{:S(2)}) collective-permute-start(f32[8,512]{1,0:T(8,128)} %get-tuple-element.49), channel_id=1, source_target_pairs={{4,0},{8,4},{12,8},{16,12},{20,16},{24,20},{28,24},{5,1},{9,5},{13... | collective-permute-start | bytes 49160 | tf_op jit(solution)/shard_map/ppermute | solution.py:228
  8.4 4.4 %shard_map.78 = (s32[256,512]{1,0:T(8,128)}, s32[256,512]{1,0:T(8,128)}, s32[256,512]{1,0:T(8,128)}, s32[256,512]{1,0:T(8,128)}) custom-call(s32[1]{0:T(128)S(6)} %rem.22.me_ref, bf16[512,1024]{1,0:T(8,128)(2,1)} %amp_ref, s32[512,1024]{1,0:T(8,128)} %bin_ref), custom_call_target="tpu_custom_call" | custom-call | flops 524288 | bytes 5242880 | tf_op jit(solution)/shard_map/pallas_call | solution.py:56
  12.9 3.5 %collective-permute-start.5 = (s32[256,512]{1,0:T(8,128)}, s32[256,512]{1,0:T(8,128)S(1)}, u32[]{:S(2)}, u32[]{:S(2)}) collective-permute-start(s32[256,512]{1,0:T(8,128)} %get-tuple-element.65), channel_id=1, source_target_pairs={{0,8},{4,12},{8,0},{12,4},{16,24},{20,28},{24,16},{28,20},{1,9},{5... | collective-permute-start | bytes 1572872 | tf_op jit(solution)/shard_map/ppermute | solution.py:457
  16.5 0.6 collective-permute-start.4
  17.1 0.9 %collective-permute-start.6 = (s32[256,512]{1,0:T(8,128)}, s32[256,512]{1,0:T(8,128)S(1)}, u32[]{:S(2)}, u32[]{:S(2)}) collective-permute-start(s32[256,512]{1,0:T(8,128)} %get-tuple-element.67), channel_id=1, source_target_pairs={{0,12},{4,8},{8,4},{12,0},{16,28},{20,24},{24,20},{28,16},{1,13},{... | collective-permute-start | bytes 1572872 | tf_op jit(solution)/shard_map/ppermute | solution.py:457
  18.3 1.3 %collective-permute-start.2 = (f32[8,384]{1,0:T(8,128)S(1)}, f32[8,384]{1,0:T(8,128)S(1)}, u32[]{:S(2)}, u32[]{:S(2)}) collective-permute-start(f32[8,384]{1,0:T(8,128)S(1)} %get-tuple-element.59), channel_id=1, source_target_pairs={{0,1},{1,2},{2,3},{4,5},{5,6},{6,7},{8,9},{9,10},{10,11},{12,13},{... | collective-permute-start | bytes 36872 | tf_op jit(solution)/shard_map/ppermute | solution.py:228
  19.6 1.3 %collective-permute-start.3 = (f32[8,384]{1,0:T(8,128)S(1)}, f32[8,384]{1,0:T(8,128)S(1)}, u32[]{:S(2)}, u32[]{:S(2)}) collective-permute-start(f32[8,384]{1,0:T(8,128)S(1)} %get-tuple-element.60), channel_id=1, source_target_pairs={{1,0},{2,1},{3,2},{5,4},{6,5},{7,6},{9,8},{10,9},{11,10},{13,12},{... | collective-permute-start | bytes 36872 | tf_op jit(solution)/shard_map/ppermute | solution.py:228
  20.9 3.5 %collective-permute-done.3.north_ref = f32[8,384]{1,0:T(8,128)S(1)} collective-permute-done((f32[8,384]{1,0:T(8,128)S(1)}, f32[8,384]{1,0:T(8,128)S(1)}, u32[]{:S(2)}, u32[]{:S(2)}) %collective-permute-start.3) | collective-permute-done | bytes 12320 | tf_op jit(solution)/shard_map/ppermute | solution.py:228
  24.4 4.9 %shard_map.80 = (f32[256,512]{1,0:T(8,128)}, f32[4,128]{1,0:T(4,128)S(1)}) custom-call(s32[4,128]{1,0:T(4,128)S(1)} %get-tuple-element.58.cell_ref, f32[256,512]{1,0:T(8,128)S(1)} %copy-done, s32[256,512]{1,0:T(8,128)S(1)} %copy-done.1, f32[256,512]{1,0:T(8,128)S(1)} %copy-done.2, f32[8,512]{1,0:T(8,128)S(1)} %collective-permute-done.before_ref, ...), custom_call_target="tpu_custom_call" | custom-call | flops 13107200 | bytes 104857600 | tf_op jit(solution)/shard_map/pallas_call | solution.py:249
  29.3 6.8 %all-gather.1.refs_4_ = f32[4,4,128]{2,1,0:T(4,128)S(1)} all-gather(f32[1,4,128]{2,1,0:T(4,128)S(1)} %bitcast.3), channel_id=2, replica_groups=mesh['box'=8,'panel'=4] {'panel'}, dimensions={0}, use_global_device_ids=true | all-gather | bytes 10240 | tf_op jit(solution)/shard_map/all_gather | solution.py:468
  36.0 2.0 %collective-permute-start.9 = (f32[4,4,128]{2,1,0:T(4,128)S(1)}, f32[4,4,128]{2,1,0:T(4,128)S(1)}, u32[]{:S(2)}, u32[]{:S(2)}) collective-permute-start(f32[4,4,128]{2,1,0:T(4,128)S(1)} %all-gather.1.refs_4_), channel_id=1, source_target_pairs={{0,12},{4,8},{8,4},{12,0},{16,28},{20,24},{24,20},{28,16},{1,13},{... | collective-permute-start | bytes 24584 | tf_op jit(solution)/shard_map/ppermute | solution.py:457
  38.1 0.4 collective-permute-start.8
  38.5 1.0 %collective-permute-start.7 = (f32[4,4,128]{2,1,0:T(4,128)S(1)}, f32[4,4,128]{2,1,0:T(4,128)S(1)}, u32[]{:S(2)}, u32[]{:S(2)}) collective-permute-start(f32[4,4,128]{2,1,0:T(4,128)S(1)} %all-gather.1.refs_4_), channel_id=1, source_target_pairs={{0,4},{4,0},{8,12},{12,8},{16,20},{20,16},{24,28},{28,24},{1,5},{5... | collective-permute-start | bytes 24584 | tf_op jit(solution)/shard_map/ppermute | solution.py:457
  39.6 1.4 %collective-permute-done.4.refs_1_ = s32[256,512]{1,0:T(8,128)S(1)} collective-permute-done((s32[256,512]{1,0:T(8,128)}, s32[256,512]{1,0:T(8,128)S(1)}, u32[]{:S(2)}, u32[]{:S(2)}) %collective-permute-start.4) | collective-permute-done | bytes 524320 | tf_op jit(solution)/shard_map/ppermute | solution.py:457
  41.0 0.7 collective-permute-done.8.refs_6_
  42.2 11.8 %shard_map.81 = (f32[4,112,256]{2,1,0:T(8,128)S(1)}, bf16[4,112,256]{2,1,0:T(8,128)(2,1)S(1)}) custom-call(s32[1]{0:T(128)S(6)} %select_n.5.half_ref, s32[256,512]{1,0:T(8,128)S(1)} %copy-done.4, s32[256,512]{1,0:T(8,128)S(1)} %collective-permute-done.4.refs_1_, s32[256,512]{1,0:T(8,128)S(1)} %collective-permute-done.5.refs_2_, ...), custom_call_target="tpu_custom_call" | custom-call | flops 15032385536 | bytes 1835008 | tf_op jit(solution)/shard_map/pallas_call | solution.py:363
  54.0 2.5 %collective-permute-start.11 = (bf16[4,112,256]{2,1,0:T(8,128)(2,1)S(1)}, bf16[4,112,256]{2,1,0:T(8,128)(2,1)S(1)}, u32[]{:S(2)}, u32[]{:S(2)}) collective-permute-start(bf16[4,112,256]{2,1,0:T(8,128)(2,1)S(1)} %get-tuple-element.78), channel_id=1, source_target_pairs={{0,16},{4,20},{8,24},{12,28},{16,0},{20,4},{24,8},{28,12},{1,17},{... | collective-permute-start | bytes 688136 | tf_op jit(solution)/shard_map/ppermute | solution.py:480
  56.5 8.4 %shard_map.82 = (f32[4,80,256]{2,1,0:T(8,128)S(1)}, bf16[4,80,256]{2,1,0:T(8,128)(2,1)S(1)}) custom-call(s32[1]{0:T(128)S(6)} %select_n.5.half_ref, s32[256,512]{1,0:T(8,128)S(1)} %copy-done.4, s32[256,512]{1,0:T(8,128)S(1)} %collective-permute-done.4.refs_1_, s32[256,512]{1,0:T(8,128)S(1)} %collective-permute-done.5.refs_2_, ...), custom_call_target="tpu_custom_call" | custom-call | flops 10737418240 | bytes 1310720 | tf_op jit(solution)/shard_map/pallas_call | solution.py:363
  64.9 0.5 collective-permute-start.12
  65.5 6.7 %shard_map.83 = (f32[4,64,256]{2,1,0:T(8,128)S(1)}, bf16[4,64,256]{2,1,0:T(8,128)(2,1)S(1)}) custom-call(s32[1]{0:T(128)S(6)} %select_n.5.half_ref, s32[256,512]{1,0:T(8,128)S(1)} %copy-done.4, s32[256,512]{1,0:T(8,128)S(1)} %collective-permute-done.4.refs_1_, s32[256,512]{1,0:T(8,128)S(1)} %collective-permute-done.5.refs_2_, ...), custom_call_target="tpu_custom_call" | custom-call | flops 8589934592 | bytes 1048576 | tf_op jit(solution)/shard_map/pallas_call | solution.py:363
  72.2 2.5 %collective-permute-start.10 = (bf16[4,64,256]{2,1,0:T(8,128)(2,1)S(1)}, bf16[4,64,256]{2,1,0:T(8,128)(2,1)S(1)}, u32[]{:S(2)}, u32[]{:S(2)}) collective-permute-start(bf16[4,64,256]{2,1,0:T(8,128)(2,1)S(1)} %get-tuple-element.75), channel_id=1, source_target_pairs={{0,16},{4,20},{8,24},{12,28},{16,0},{20,4},{24,8},{28,12},{1,17},{... | collective-permute-start | bytes 393224 | tf_op jit(solution)/shard_map/ppermute | solution.py:480
  74.8 1.6 %collective-permute-start.13 = (bf16[192,256]{1,0:T(8,128)(2,1)S(1)}, bf16[192,256]{1,0:T(8,128)(2,1)S(1)}, u32[]{:S(2)}, u32[]{:S(2)}) collective-permute-start(bf16[192,256]{1,0:T(8,128)(2,1)S(1)} %get-tuple-element.80), channel_id=1, source_target_pairs={{0,4},{4,0},{8,12},{12,8},{16,20},{20,16},{24,28},{28,24},{1,5},{5... | collective-permute-start | bytes 294920 | tf_op jit(solution)/shard_map/ppermute | solution.py:457
  76.4 1.6 %collective-permute-start.17 = (bf16[192,256]{1,0:T(8,128)(2,1)S(1)}, bf16[192,256]{1,0:T(8,128)(2,1)S(1)}, u32[]{:S(2)}, u32[]{:S(2)}) collective-permute-start(bf16[192,256]{1,0:T(8,128)(2,1)S(1)} %get-tuple-element.88), channel_id=1, source_target_pairs={{0,8},{4,12},{8,0},{12,4},{16,24},{20,28},{24,16},{28,20},{1,9},{5... | collective-permute-start | bytes 294920 | tf_op jit(solution)/shard_map/ppermute | solution.py:457
  78.4 1.2 %collective-permute-done.10.refs_1_ = bf16[4,64,256]{2,1,0:T(8,128)(2,1)S(1)} collective-permute-done((bf16[4,64,256]{2,1,0:T(8,128)(2,1)S(1)}, bf16[4,64,256]{2,1,0:T(8,128)(2,1)S(1)}, u32[]{:S(2)}, u32[]{:S(2)}) %collective-permute-start.10) | collective-permute-done | bytes 131104 | tf_op jit(solution)/shard_map/ppermute | solution.py:480
  79.6 2.8 %collective-permute-start.14 = (bf16[64,256]{1,0:T(8,128)(2,1)S(1)}, bf16[64,256]{1,0:T(8,128)(2,1)S(1)}, u32[]{:S(2)}, u32[]{:S(2)}) collective-permute-start(bf16[64,256]{1,0:T(8,128)(2,1)S(1)} %get-tuple-element.83), channel_id=1, source_target_pairs={{0,4},{4,0},{8,12},{12,8},{16,20},{20,16},{24,28},{28,24},{1,5},{5... | collective-permute-start | bytes 98312 | tf_op jit(solution)/shard_map/ppermute | solution.py:457
  82.4 1.6 %collective-permute-start.15 = (bf16[64,256]{1,0:T(8,128)(2,1)S(1)}, bf16[64,256]{1,0:T(8,128)(2,1)S(1)}, u32[]{:S(2)}, u32[]{:S(2)}) collective-permute-start(bf16[64,256]{1,0:T(8,128)(2,1)S(1)} %get-tuple-element.84), channel_id=1, source_target_pairs={{0,8},{4,12},{8,0},{12,4},{16,24},{20,28},{24,16},{28,20},{1,9},{5... | collective-permute-start | bytes 98312 | tf_op jit(solution)/shard_map/ppermute | solution.py:457
  84.0 0.9 %shard_map.86.refs_4_ = f32[1024,256]{1,0:T(8,128)} custom-call(s32[1]{0:T(128)S(6)} %rem.22.me_ref, bf16[192,256]{1,0:T(8,128)(2,1)S(1)} %get-tuple-element.86.refs_0_, bf16[192,256]{1,0:T(8,128)(2,1)S(1)} %collective-permute-done.13.refs_1_, bf16[192,256]{1,0:T(8,128)(2,1)S(1)} %collective-permute-done.17.refs_2_, ...), custom_call_target="tpu_custom_call" | custom-call | flops 196608 | bytes 1179648 | tf_op jit(solution)/shard_map/pallas_call | solution.py:430
  84.9 1.3 %collective-permute-done.15.refs_2_ = bf16[64,256]{1,0:T(8,128)(2,1)S(1)} collective-permute-done((bf16[64,256]{1,0:T(8,128)(2,1)S(1)}, bf16[64,256]{1,0:T(8,128)(2,1)S(1)}, u32[]{:S(2)}, u32[]{:S(2)}) %collective-permute-start.15) | collective-permute-done | bytes 32800 | tf_op jit(solution)/shard_map/ppermute | solution.py:457
  86.3 2.5 %collective-permute-done.16.refs_3_ = bf16[64,256]{1,0:T(8,128)(2,1)S(1)} collective-permute-done((bf16[64,256]{1,0:T(8,128)(2,1)S(1)}, bf16[64,256]{1,0:T(8,128)(2,1)S(1)}, u32[]{:S(2)}, u32[]{:S(2)}) %collective-permute-start.16) | collective-permute-done | bytes 32800 | tf_op jit(solution)/shard_map/ppermute | solution.py:457
  88.8 0.7 shard_map.87
  (28 shorter events, 1.4 us)
Async XLA Ops:
  2.1 15.9 %copy-start = (f32[256,512]{1,0:T(8,128)S(1)}, f32[256,512]{1,0:T(8,128)}, u32[]{:S(2)}) copy-start(f32[256,512]{1,0:T(8,128)} %field_ref.3) | copy-start | bytes 1572868
  2.1 15.9 %copy-start.1 = (s32[256,512]{1,0:T(8,128)S(1)}, s32[256,512]{1,0:T(8,128)}, u32[]{:S(2)}) copy-start(s32[256,512]{1,0:T(8,128)} %mask_ref.3) | copy-start | bytes 1572868
  2.1 15.9 %copy-start.2 = (f32[256,512]{1,0:T(8,128)S(1)}, f32[256,512]{1,0:T(8,128)}, u32[]{:S(2)}) copy-start(f32[256,512]{1,0:T(8,128)} %visc_ref.3) | copy-start | bytes 1572868
  2.1 15.9 %copy-start.3 = (s32[128]{0:T(128)S(1)}, s32[128]{0:T(128)}, u32[]{:S(2)}) copy-start(s32[128]{0:T(128)} %param.9) | copy-start | bytes 1540
  2.1 10.7 %collective-permute-start = (f32[8,512]{1,0:T(8,128)}, f32[8,512]{1,0:T(8,128)S(1)}, u32[]{:S(2)}, u32[]{:S(2)}) collective-permute-start(f32[8,512]{1,0:T(8,128)} %get-tuple-element.48), channel_id=1, source_target_pairs={{0,4},{4,8},{8,12},{12,16},{16,20},{20,24},{24,28},{1,5},{5,9},{9,... | collective-permute-start | bytes 49160 | tf_op jit(solution)/shard_map/ppermute | solution.py:228
  7.1 5.8 %collective-permute-start.1 = (f32[8,512]{1,0:T(8,128)}, f32[8,512]{1,0:T(8,128)S(1)}, u32[]{:S(2)}, u32[]{:S(2)}) collective-permute-start(f32[8,512]{1,0:T(8,128)} %get-tuple-element.49), channel_id=1, source_target_pairs={{4,0},{8,4},{12,8},{16,12},{20,16},{24,20},{28,24},{5,1},{9,5},{13... | collective-permute-start | bytes 49160 | tf_op jit(solution)/shard_map/ppermute | solution.py:228
  12.8 29.4 %copy-start.4 = (s32[256,512]{1,0:T(8,128)S(1)}, s32[256,512]{1,0:T(8,128)}, u32[]{:S(2)}) copy-start(s32[256,512]{1,0:T(8,128)} %get-tuple-element.62.refs_0_) | copy-start | bytes 1572868
  12.9 23.1 %collective-permute-start.5 = (s32[256,512]{1,0:T(8,128)}, s32[256,512]{1,0:T(8,128)S(1)}, u32[]{:S(2)}, u32[]{:S(2)}) collective-permute-start(s32[256,512]{1,0:T(8,128)} %get-tuple-element.65), channel_id=1, source_target_pairs={{0,8},{4,12},{8,0},{12,4},{16,24},{20,28},{24,16},{28,20},{1,9},{5... | collective-permute-start | bytes 1572872 | tf_op jit(solution)/shard_map/ppermute | solution.py:457
  16.5 24.5 %collective-permute-start.4 = (s32[256,512]{1,0:T(8,128)}, s32[256,512]{1,0:T(8,128)S(1)}, u32[]{:S(2)}, u32[]{:S(2)}) collective-permute-start(s32[256,512]{1,0:T(8,128)} %get-tuple-element.63), channel_id=1, source_target_pairs={{0,4},{4,0},{8,12},{12,8},{16,20},{20,16},{24,28},{28,24},{1,5},{5... | collective-permute-start | bytes 1572872 | tf_op jit(solution)/shard_map/ppermute | solution.py:457
  17.1 23.9 %collective-permute-start.6 = (s32[256,512]{1,0:T(8,128)}, s32[256,512]{1,0:T(8,128)S(1)}, u32[]{:S(2)}, u32[]{:S(2)}) collective-permute-start(s32[256,512]{1,0:T(8,128)} %get-tuple-element.67), channel_id=1, source_target_pairs={{0,12},{4,8},{8,4},{12,0},{16,28},{20,24},{24,20},{28,16},{1,13},{... | collective-permute-start | bytes 1572872 | tf_op jit(solution)/shard_map/ppermute | solution.py:457
  18.3 2.6 %collective-permute-start.2 = (f32[8,384]{1,0:T(8,128)S(1)}, f32[8,384]{1,0:T(8,128)S(1)}, u32[]{:S(2)}, u32[]{:S(2)}) collective-permute-start(f32[8,384]{1,0:T(8,128)S(1)} %get-tuple-element.59), channel_id=1, source_target_pairs={{0,1},{1,2},{2,3},{4,5},{5,6},{6,7},{8,9},{9,10},{10,11},{12,13},{... | collective-permute-start | bytes 36872 | tf_op jit(solution)/shard_map/ppermute | solution.py:228
  19.6 4.8 %collective-permute-start.3 = (f32[8,384]{1,0:T(8,128)S(1)}, f32[8,384]{1,0:T(8,128)S(1)}, u32[]{:S(2)}, u32[]{:S(2)}) collective-permute-start(f32[8,384]{1,0:T(8,128)S(1)} %get-tuple-element.60), channel_id=1, source_target_pairs={{1,0},{2,1},{3,2},{5,4},{6,5},{7,6},{9,8},{10,9},{11,10},{13,12},{... | collective-permute-start | bytes 36872 | tf_op jit(solution)/shard_map/ppermute | solution.py:228
  36.0 5.0 %collective-permute-start.9 = (f32[4,4,128]{2,1,0:T(4,128)S(1)}, f32[4,4,128]{2,1,0:T(4,128)S(1)}, u32[]{:S(2)}, u32[]{:S(2)}) collective-permute-start(f32[4,4,128]{2,1,0:T(4,128)S(1)} %all-gather.1.refs_4_), channel_id=1, source_target_pairs={{0,12},{4,8},{8,4},{12,0},{16,28},{20,24},{24,20},{28,16},{1,13},{... | collective-permute-start | bytes 24584 | tf_op jit(solution)/shard_map/ppermute | solution.py:457
  38.1 3.7 %collective-permute-start.8 = (f32[4,4,128]{2,1,0:T(4,128)S(1)}, f32[4,4,128]{2,1,0:T(4,128)S(1)}, u32[]{:S(2)}, u32[]{:S(2)}) collective-permute-start(f32[4,4,128]{2,1,0:T(4,128)S(1)} %all-gather.1.refs_4_), channel_id=1, source_target_pairs={{0,8},{4,12},{8,0},{12,4},{16,24},{20,28},{24,16},{28,20},{1,9},{5... | collective-permute-start | bytes 24584 | tf_op jit(solution)/shard_map/ppermute | solution.py:457
  38.5 3.7 %collective-permute-start.7 = (f32[4,4,128]{2,1,0:T(4,128)S(1)}, f32[4,4,128]{2,1,0:T(4,128)S(1)}, u32[]{:S(2)}, u32[]{:S(2)}) collective-permute-start(f32[4,4,128]{2,1,0:T(4,128)S(1)} %all-gather.1.refs_4_), channel_id=1, source_target_pairs={{0,4},{4,0},{8,12},{12,8},{16,20},{20,16},{24,28},{28,24},{1,5},{5... | collective-permute-start | bytes 24584 | tf_op jit(solution)/shard_map/ppermute | solution.py:457
  54.0 20.8 %collective-permute-start.11 = (bf16[4,112,256]{2,1,0:T(8,128)(2,1)S(1)}, bf16[4,112,256]{2,1,0:T(8,128)(2,1)S(1)}, u32[]{:S(2)}, u32[]{:S(2)}) collective-permute-start(bf16[4,112,256]{2,1,0:T(8,128)(2,1)S(1)} %get-tuple-element.78), channel_id=1, source_target_pairs={{0,16},{4,20},{8,24},{12,28},{16,0},{20,4},{24,8},{28,12},{1,17},{... | collective-permute-start | bytes 688136 | tf_op jit(solution)/shard_map/ppermute | solution.py:480
  64.9 9.8 %collective-permute-start.12 = (bf16[4,80,256]{2,1,0:T(8,128)(2,1)S(1)}, bf16[4,80,256]{2,1,0:T(8,128)(2,1)S(1)}, u32[]{:S(2)}, u32[]{:S(2)}) collective-permute-start(bf16[4,80,256]{2,1,0:T(8,128)(2,1)S(1)} %get-tuple-element.79), channel_id=1, source_target_pairs={{0,16},{4,20},{8,24},{12,28},{16,0},{20,4},{24,8},{28,12},{1,17},{... | collective-permute-start | bytes 491528 | tf_op jit(solution)/shard_map/ppermute | solution.py:480
  72.2 7.4 %collective-permute-start.10 = (bf16[4,64,256]{2,1,0:T(8,128)(2,1)S(1)}, bf16[4,64,256]{2,1,0:T(8,128)(2,1)S(1)}, u32[]{:S(2)}, u32[]{:S(2)}) collective-permute-start(bf16[4,64,256]{2,1,0:T(8,128)(2,1)S(1)} %get-tuple-element.75), channel_id=1, source_target_pairs={{0,16},{4,20},{8,24},{12,28},{16,0},{20,4},{24,8},{28,12},{1,17},{... | collective-permute-start | bytes 393224 | tf_op jit(solution)/shard_map/ppermute | solution.py:480
  74.8 4.7 %collective-permute-start.13 = (bf16[192,256]{1,0:T(8,128)(2,1)S(1)}, bf16[192,256]{1,0:T(8,128)(2,1)S(1)}, u32[]{:S(2)}, u32[]{:S(2)}) collective-permute-start(bf16[192,256]{1,0:T(8,128)(2,1)S(1)} %get-tuple-element.80), channel_id=1, source_target_pairs={{0,4},{4,0},{8,12},{12,8},{16,20},{20,16},{24,28},{28,24},{1,5},{5... | collective-permute-start | bytes 294920 | tf_op jit(solution)/shard_map/ppermute | solution.py:457
  76.4 7.6 %collective-permute-start.17 = (bf16[192,256]{1,0:T(8,128)(2,1)S(1)}, bf16[192,256]{1,0:T(8,128)(2,1)S(1)}, u32[]{:S(2)}, u32[]{:S(2)}) collective-permute-start(bf16[192,256]{1,0:T(8,128)(2,1)S(1)} %get-tuple-element.88), channel_id=1, source_target_pairs={{0,8},{4,12},{8,0},{12,4},{16,24},{20,28},{24,16},{28,20},{1,9},{5... | collective-permute-start | bytes 294920 | tf_op jit(solution)/shard_map/ppermute | solution.py:457
  78.0 6.0 %collective-permute-start.18 = (bf16[192,256]{1,0:T(8,128)(2,1)S(1)}, bf16[192,256]{1,0:T(8,128)(2,1)S(1)}, u32[]{:S(2)}, u32[]{:S(2)}) collective-permute-start(bf16[192,256]{1,0:T(8,128)(2,1)S(1)} %get-tuple-element.89), channel_id=1, source_target_pairs={{0,12},{4,8},{8,4},{12,0},{16,28},{20,24},{24,20},{28,16},{1,13},{... | collective-permute-start | bytes 294920 | tf_op jit(solution)/shard_map/ppermute | solution.py:457
  79.6 5.3 %collective-permute-start.14 = (bf16[64,256]{1,0:T(8,128)(2,1)S(1)}, bf16[64,256]{1,0:T(8,128)(2,1)S(1)}, u32[]{:S(2)}, u32[]{:S(2)}) collective-permute-start(bf16[64,256]{1,0:T(8,128)(2,1)S(1)} %get-tuple-element.83), channel_id=1, source_target_pairs={{0,4},{4,0},{8,12},{12,8},{16,20},{20,16},{24,28},{28,24},{1,5},{5... | collective-permute-start | bytes 98312 | tf_op jit(solution)/shard_map/ppermute | solution.py:457
  82.4 3.9 %collective-permute-start.15 = (bf16[64,256]{1,0:T(8,128)(2,1)S(1)}, bf16[64,256]{1,0:T(8,128)(2,1)S(1)}, u32[]{:S(2)}, u32[]{:S(2)}) collective-permute-start(bf16[64,256]{1,0:T(8,128)(2,1)S(1)} %get-tuple-element.84), channel_id=1, source_target_pairs={{0,8},{4,12},{8,0},{12,4},{16,24},{20,28},{24,16},{28,20},{1,9},{5... | collective-permute-start | bytes 98312 | tf_op jit(solution)/shard_map/ppermute | solution.py:457
  84.0 4.8 %collective-permute-start.16 = (bf16[64,256]{1,0:T(8,128)(2,1)S(1)}, bf16[64,256]{1,0:T(8,128)(2,1)S(1)}, u32[]{:S(2)}, u32[]{:S(2)}) collective-permute-start(bf16[64,256]{1,0:T(8,128)(2,1)S(1)} %get-tuple-element.85), channel_id=1, source_target_pairs={{0,12},{4,8},{8,4},{12,0},{16,28},{20,24},{24,20},{28,16},{1,13},{... | collective-permute-start | bytes 98312 | tf_op jit(solution)/shard_map/ppermute | solution.py:457

commit v9 on v6

--- a/solution.py
+++ b/solution.py
@@ -30,13 +30,17 @@
     return pl.CostEstimate(flops=flops, bytes_accessed=size, transcendentals=0)
 
 
+def target(me, k, members):
+    return me ^ k if members & (members - 1) == 0 else (me + k) % members
+
+
 def pack_kernel(me_ref, amp_ref, bin_ref, *refs):
     outs, turned = refs[:-1], refs[-1]
     scaled = (amp_ref[...].astype(F32) * AMP_SCALE).astype(jnp.int32)
     turned[...] = jnp.transpose((scaled << 16) | bin_ref[...])
     width = outs[0].shape[0]
     for k, out in enumerate(outs):
-        first = pl.multiple_of(lax.rem(me_ref[0] + k, len(outs)) * width, 8)
+        first = pl.multiple_of(target(me_ref[0], k, len(outs)) * width, 8)
         out[...] = turned[pl.ds(first, width), :]
 
 
@@ -440,9 +444,9 @@
     index = lax.axis_index("box").astype(jnp.int32).reshape(1)
     me, half = lax.rem(index, members), index // members
 
-    def spread(parts):
+    def spread(parts, to):
         def perm(k):
-            return [(i, i // members * members + (i + k) % members) for i in range(peers)]
+            return [(i, i // members * members + to(i % members, k, members)) for i in range(peers)]
 
         return [lax.ppermute(x, "box", perm(k)) if k else x for k, x in enumerate(parts)]
 
@@ -451,14 +455,14 @@
     before, after = shifted("box", *ends)
     packed = pack(me, amplitude, delay_bin, members)
     before, after, *packed = lax.optimization_barrier((before, after, *packed))
-    words = spread(packed)
+    words = spread(packed, target)
     field, sample = field_window(
         field_start, fluid_mask, base_visc, before, after, panel_cell
     )
     sample = lax.all_gather(sample, "panel")
     middle = members // 2
     sample, words[middle] = lax.optimization_barrier((sample, words[middle]))
-    samples = spread([sample] * members)
+    samples = spread([sample] * members, target)
     observers = words[0].shape[0]
     across = [(i, (i + members) % peers) for i in range(peers)]
     first, groups = 0, []
@@ -474,7 +478,7 @@
         keeps, gots = [x[0] for x in group], [x[1] for x in group]
         if pieces is not None:
             gots[-1], pieces[middle] = lax.optimization_barrier((gots[-1], pieces[middle]))
-        pieces = spread(join(me, keeps, gots))
+        pieces = spread(join(me, keeps, gots), lambda i, k, n: (i + k) % n)
         waiting.append(pieces)
     first, signals = 0, None
     for pieces in waiting:

time: 89.1 us -> 88.1 us (0.989)
  transfers between devices with their start and end apart: 19 -> 19, of which waited for: 8 -> 7; matrix products, arithmetic and copies ran while one was open for 0% -> 0% of each run, Pallas kernels for 29% -> 29%
where the time goes in v9:
time: 88.1 us; the launch traced here: 87.7 us
  Pallas kernels  39.7 us (45%)
  starting transfers between devices  31.5 us (36%)
  waiting for transfers between devices  8.94 us (10%)
  blocking collectives  6.75 us (8%)
    pallas_call x3, Pallas kernels, binned(): pl.pallas_call(bin_kernel, grid=(count // block,), in_specs=[SMEM] + [pl....  26.9 us
    ppermute x12, starting transfers between devices, spread(): lax.ppermute(x, 'box', perm(k))  17.1 us
    ppermute x4, starting transfers between devices, shifted(): return (lax.ppermute(last, axis, up), lax.ppermute(first, axis, down))  8.88 us
    all_gather x1, blocking collectives, on_device(): sample = lax.all_gather(sample, 'panel')  6.75 us
    ppermute x3, starting transfers between devices, on_device(): groups[-1].append((keep, lax.ppermute(send, 'box', across)))  5.58 us
    ppermute x12, waiting for transfers between devices, spread(): lax.ppermute(x, 'box', perm(k))  5.27 us
    pallas_call x1, Pallas kernels, field_window(): pl.pallas_call(step_kernel, in_specs=[SMEM] + [VMEM] * 7, out_specs=[pl.B...  4.9 us
    pallas_call x1, Pallas kernels, pack(): pl.pallas_call(pack_kernel, grid=(panels // LANES,), in_specs=[SMEM, bloc...  4.37 us
  transfers between devices with their start and end apart: 19, of which 7 were waited for; matrix products, arithmetic and copies ran while one was open for 0% of the time, Pallas kernels for 29%

profile of v9, /device:TPU:0, one launch (start us, length us, event | category | flops | bytes accessed | tf_op | source)
XLA Modules:
  0.0 87.7 jit_solution(6465392879160653110)
XLA Ops:
  0.6 1.4 %shard_map.77 = (f32[8,512]{1,0:T(8,128)}, f32[8,512]{1,0:T(8,128)}) custom-call(f32[256,512]{1,0:T(8,128)} %field_ref.3, s32[256,512]{1,0:T(8,128)} %mask_ref.3, f32[256,512]{1,0:T(8,128)} %visc_ref.3, f32[256,512]{1,0:T(8,128)} %field_ref.3, s32[256,512]{1,0:T(8,128)} %mask_ref.3, f32[256,512]{1,0:T(8,128)} %visc_ref.3), custom_call_target="tpu_custom_call" | custom-call | flops 8192 | bytes 131072 | tf_op jit(solution)/shard_map/pallas_call | solution.py:208
  2.1 5.0 %collective-permute-start = (f32[8,512]{1,0:T(8,128)}, f32[8,512]{1,0:T(8,128)S(1)}, u32[]{:S(2)}, u32[]{:S(2)}) collective-permute-start(f32[8,512]{1,0:T(8,128)} %get-tuple-element.48), channel_id=1, source_target_pairs={{0,4},{4,8},{8,12},{12,16},{16,20},{20,24},{24,28},{1,5},{5,9},{9,... | collective-permute-start | bytes 49160 | tf_op jit(solution)/shard_map/ppermute | solution.py:224
  7.1 1.3 %collective-permute-start.1 = (f32[8,512]{1,0:T(8,128)}, f32[8,512]{1,0:T(8,128)S(1)}, u32[]{:S(2)}, u32[]{:S(2)}) collective-permute-start(f32[8,512]{1,0:T(8,128)} %get-tuple-element.49), channel_id=1, source_target_pairs={{4,0},{8,4},{12,8},{16,12},{20,16},{24,20},{28,24},{5,1},{9,5},{13... | collective-permute-start | bytes 49160 | tf_op jit(solution)/shard_map/ppermute | solution.py:224
  8.4 4.4 %shard_map.78 = (s32[256,512]{1,0:T(8,128)}, s32[256,512]{1,0:T(8,128)}, s32[256,512]{1,0:T(8,128)}, s32[256,512]{1,0:T(8,128)}) custom-call(s32[1]{0:T(128)S(6)} %rem.22.me_ref, bf16[512,1024]{1,0:T(8,128)(2,1)} %amp_ref, s32[512,1024]{1,0:T(8,128)} %bin_ref), custom_call_target="tpu_custom_call" | custom-call | flops 524288 | bytes 5242880 | tf_op jit(solution)/shard_map/pallas_call | solution.py:52
  12.9 3.5 %collective-permute-start.5 = (s32[256,512]{1,0:T(8,128)}, s32[256,512]{1,0:T(8,128)S(1)}, u32[]{:S(2)}, u32[]{:S(2)}) collective-permute-start(s32[256,512]{1,0:T(8,128)} %get-tuple-element.65), channel_id=1, source_target_pairs={{0,8},{4,12},{8,0},{12,4},{16,24},{20,28},{24,16},{28,20},{1,9},{5... | collective-permute-start | bytes 1572872 | tf_op jit(solution)/shard_map/ppermute | solution.py:451
  16.5 0.6 collective-permute-start.4
  17.1 0.9 %collective-permute-start.6 = (s32[256,512]{1,0:T(8,128)}, s32[256,512]{1,0:T(8,128)S(1)}, u32[]{:S(2)}, u32[]{:S(2)}) collective-permute-start(s32[256,512]{1,0:T(8,128)} %get-tuple-element.67), channel_id=1, source_target_pairs={{0,12},{4,8},{8,4},{12,0},{16,28},{20,24},{24,20},{28,16},{1,13},{... | collective-permute-start | bytes 1572872 | tf_op jit(solution)/shard_map/ppermute | solution.py:451
  18.3 1.3 %collective-permute-start.2 = (f32[8,384]{1,0:T(8,128)S(1)}, f32[8,384]{1,0:T(8,128)S(1)}, u32[]{:S(2)}, u32[]{:S(2)}) collective-permute-start(f32[8,384]{1,0:T(8,128)S(1)} %get-tuple-element.59), channel_id=1, source_target_pairs={{0,1},{1,2},{2,3},{4,5},{5,6},{6,7},{8,9},{9,10},{10,11},{12,13},{... | collective-permute-start | bytes 36872 | tf_op jit(solution)/shard_map/ppermute | solution.py:224
  19.6 1.3 %collective-permute-start.3 = (f32[8,384]{1,0:T(8,128)S(1)}, f32[8,384]{1,0:T(8,128)S(1)}, u32[]{:S(2)}, u32[]{:S(2)}) collective-permute-start(f32[8,384]{1,0:T(8,128)S(1)} %get-tuple-element.60), channel_id=1, source_target_pairs={{1,0},{2,1},{3,2},{5,4},{6,5},{7,6},{9,8},{10,9},{11,10},{13,12},{... | collective-permute-start | bytes 36872 | tf_op jit(solution)/shard_map/ppermute | solution.py:224
  20.9 3.5 %collective-permute-done.3.north_ref = f32[8,384]{1,0:T(8,128)S(1)} collective-permute-done((f32[8,384]{1,0:T(8,128)S(1)}, f32[8,384]{1,0:T(8,128)S(1)}, u32[]{:S(2)}, u32[]{:S(2)}) %collective-permute-start.3) | collective-permute-done | bytes 12320 | tf_op jit(solution)/shard_map/ppermute | solution.py:224
  24.4 4.9 %shard_map.80 = (f32[256,512]{1,0:T(8,128)}, f32[4,128]{1,0:T(4,128)S(1)}) custom-call(s32[4,128]{1,0:T(4,128)S(1)} %get-tuple-element.58.cell_ref, f32[256,512]{1,0:T(8,128)S(1)} %copy-done, s32[256,512]{1,0:T(8,128)S(1)} %copy-done.1, f32[256,512]{1,0:T(8,128)S(1)} %copy-done.2, f32[8,512]{1,0:T(8,128)S(1)} %collective-permute-done.before_ref, ...), custom_call_target="tpu_custom_call" | custom-call | flops 13107200 | bytes 104857600 | tf_op jit(solution)/shard_map/pallas_call | solution.py:245
  29.3 6.8 %all-gather.1.refs_4_ = f32[4,4,128]{2,1,0:T(4,128)S(1)} all-gather(f32[1,4,128]{2,1,0:T(4,128)S(1)} %bitcast.3), channel_id=2, replica_groups=mesh['box'=8,'panel'=4] {'panel'}, dimensions={0}, use_global_device_ids=true | all-gather | bytes 10240 | tf_op jit(solution)/shard_map/all_gather | solution.py:462
  36.0 2.0 %collective-permute-start.9 = (f32[4,4,128]{2,1,0:T(4,128)S(1)}, f32[4,4,128]{2,1,0:T(4,128)S(1)}, u32[]{:S(2)}, u32[]{:S(2)}) collective-permute-start(f32[4,4,128]{2,1,0:T(4,128)S(1)} %all-gather.1.refs_4_), channel_id=1, source_target_pairs={{0,12},{4,8},{8,4},{12,0},{16,28},{20,24},{24,20},{28,16},{1,13},{... | collective-permute-start | bytes 24584 | tf_op jit(solution)/shard_map/ppermute | solution.py:451
  38.5 1.0 %collective-permute-start.7 = (f32[4,4,128]{2,1,0:T(4,128)S(1)}, f32[4,4,128]{2,1,0:T(4,128)S(1)}, u32[]{:S(2)}, u32[]{:S(2)}) collective-permute-start(f32[4,4,128]{2,1,0:T(4,128)S(1)} %all-gather.1.refs_4_), channel_id=1, source_target_pairs={{0,4},{4,0},{8,12},{12,8},{16,20},{20,16},{24,28},{28,24},{1,5},{5... | collective-permute-start | bytes 24584 | tf_op jit(solution)/shard_map/ppermute | solution.py:451
  39.6 1.4 %collective-permute-done.4.refs_1_ = s32[256,512]{1,0:T(8,128)S(1)} collective-permute-done((s32[256,512]{1,0:T(8,128)}, s32[256,512]{1,0:T(8,128)S(1)}, u32[]{:S(2)}, u32[]{:S(2)}) %collective-permute-start.4) | collective-permute-done | bytes 524320 | tf_op jit(solution)/shard_map/ppermute | solution.py:451
  41.0 0.7 collective-permute-done.8.refs_6_
  42.2 11.8 %shard_map.81 = (f32[4,112,256]{2,1,0:T(8,128)S(1)}, bf16[4,112,256]{2,1,0:T(8,128)(2,1)S(1)}) custom-call(s32[1]{0:T(128)S(6)} %select_n.5.half_ref, s32[256,512]{1,0:T(8,128)S(1)} %copy-done.4, s32[256,512]{1,0:T(8,128)S(1)} %collective-permute-done.4.refs_1_, s32[256,512]{1,0:T(8,128)S(1)} %collective-permute-done.5.refs_2_, ...), custom_call_target="tpu_custom_call" | custom-call | flops 15032385536 | bytes 1835008 | tf_op jit(solution)/shard_map/pallas_call | solution.py:359
  54.0 2.5 %collective-permute-start.11 = (bf16[4,112,256]{2,1,0:T(8,128)(2,1)S(1)}, bf16[4,112,256]{2,1,0:T(8,128)(2,1)S(1)}, u32[]{:S(2)}, u32[]{:S(2)}) collective-permute-start(bf16[4,112,256]{2,1,0:T(8,128)(2,1)S(1)} %get-tuple-element.78), channel_id=1, source_target_pairs={{0,16},{4,20},{8,24},{12,28},{16,0},{20,4},{24,8},{28,12},{1,17},{... | collective-permute-start | bytes 688136 | tf_op jit(solution)/shard_map/ppermute | solution.py:474
  56.5 8.4 %shard_map.82 = (f32[4,80,256]{2,1,0:T(8,128)S(1)}, bf16[4,80,256]{2,1,0:T(8,128)(2,1)S(1)}) custom-call(s32[1]{0:T(128)S(6)} %select_n.5.half_ref, s32[256,512]{1,0:T(8,128)S(1)} %copy-done.4, s32[256,512]{1,0:T(8,128)S(1)} %collective-permute-done.4.refs_1_, s32[256,512]{1,0:T(8,128)S(1)} %collective-permute-done.5.refs_2_, ...), custom_call_target="tpu_custom_call" | custom-call | flops 10737418240 | bytes 1310720 | tf_op jit(solution)/shard_map/pallas_call | solution.py:359
  64.9 0.5 collective-permute-start.12
  65.5 6.7 %shard_map.83 = (f32[4,64,256]{2,1,0:T(8,128)S(1)}, bf16[4,64,256]{2,1,0:T(8,128)(2,1)S(1)}) custom-call(s32[1]{0:T(128)S(6)} %select_n.5.half_ref, s32[256,512]{1,0:T(8,128)S(1)} %copy-done.4, s32[256,512]{1,0:T(8,128)S(1)} %collective-permute-done.4.refs_1_, s32[256,512]{1,0:T(8,128)S(1)} %collective-permute-done.5.refs_2_, ...), custom_call_target="tpu_custom_call" | custom-call | flops 8589934592 | bytes 1048576 | tf_op jit(solution)/shard_map/pallas_call | solution.py:359
  72.2 2.5 %collective-permute-start.10 = (bf16[4,64,256]{2,1,0:T(8,128)(2,1)S(1)}, bf16[4,64,256]{2,1,0:T(8,128)(2,1)S(1)}, u32[]{:S(2)}, u32[]{:S(2)}) collective-permute-start(bf16[4,64,256]{2,1,0:T(8,128)(2,1)S(1)} %get-tuple-element.75), channel_id=1, source_target_pairs={{0,16},{4,20},{8,24},{12,28},{16,0},{20,4},{24,8},{28,12},{1,17},{... | collective-permute-start | bytes 393224 | tf_op jit(solution)/shard_map/ppermute | solution.py:474
  74.8 1.6 %collective-permute-start.13 = (bf16[192,256]{1,0:T(8,128)(2,1)S(1)}, bf16[192,256]{1,0:T(8,128)(2,1)S(1)}, u32[]{:S(2)}, u32[]{:S(2)}) collective-permute-start(bf16[192,256]{1,0:T(8,128)(2,1)S(1)} %get-tuple-element.80), channel_id=1, source_target_pairs={{0,8},{4,12},{8,0},{12,4},{16,24},{20,28},{24,16},{28,20},{1,9},{5... | collective-permute-start | bytes 294920 | tf_op jit(solution)/shard_map/ppermute | solution.py:451
  76.5 1.5 %collective-permute-start.17 = (bf16[192,256]{1,0:T(8,128)(2,1)S(1)}, bf16[192,256]{1,0:T(8,128)(2,1)S(1)}, u32[]{:S(2)}, u32[]{:S(2)}) collective-permute-start(bf16[192,256]{1,0:T(8,128)(2,1)S(1)} %get-tuple-element.87), channel_id=1, source_target_pairs={{0,4},{4,8},{8,12},{12,0},{16,20},{20,24},{24,28},{28,16},{1,5},{5... | collective-permute-start | bytes 294920 | tf_op jit(solution)/shard_map/ppermute | solution.py:451
  78.0 1.4 %collective-permute-start.18 = (bf16[192,256]{1,0:T(8,128)(2,1)S(1)}, bf16[192,256]{1,0:T(8,128)(2,1)S(1)}, u32[]{:S(2)}, u32[]{:S(2)}) collective-permute-start(bf16[192,256]{1,0:T(8,128)(2,1)S(1)} %get-tuple-element.89), channel_id=1, source_target_pairs={{0,12},{4,0},{8,4},{12,8},{16,28},{20,16},{24,20},{28,24},{1,13},{... | collective-permute-start | bytes 294920 | tf_op jit(solution)/shard_map/ppermute | solution.py:451
  79.4 1.5 %collective-permute-done.13.refs_2_ = bf16[192,256]{1,0:T(8,128)(2,1)S(1)} collective-permute-done((bf16[192,256]{1,0:T(8,128)(2,1)S(1)}, bf16[192,256]{1,0:T(8,128)(2,1)S(1)}, u32[]{:S(2)}, u32[]{:S(2)}) %collective-permute-start.13) | collective-permute-done | bytes 98336 | tf_op jit(solution)/shard_map/ppermute | solution.py:451
  81.0 0.9 collective-permute-start.14
  81.8 1.2 %collective-permute-start.15 = (bf16[64,256]{1,0:T(8,128)(2,1)S(1)}, bf16[64,256]{1,0:T(8,128)(2,1)S(1)}, u32[]{:S(2)}, u32[]{:S(2)}) collective-permute-start(bf16[64,256]{1,0:T(8,128)(2,1)S(1)} %get-tuple-element.84), channel_id=1, source_target_pairs={{0,8},{4,12},{8,0},{12,4},{16,24},{20,28},{24,16},{28,20},{1,9},{5... | collective-permute-start | bytes 98312 | tf_op jit(solution)/shard_map/ppermute | solution.py:451
  83.0 1.8 %collective-permute-start.16 = (bf16[64,256]{1,0:T(8,128)(2,1)S(1)}, bf16[64,256]{1,0:T(8,128)(2,1)S(1)}, u32[]{:S(2)}, u32[]{:S(2)}) collective-permute-start(bf16[64,256]{1,0:T(8,128)(2,1)S(1)} %get-tuple-element.85), channel_id=1, source_target_pairs={{0,12},{4,0},{8,4},{12,8},{16,28},{20,16},{24,20},{28,24},{1,13},{... | collective-permute-start | bytes 98312 | tf_op jit(solution)/shard_map/ppermute | solution.py:451
  84.9 0.9 %shard_map.86.refs_4_ = f32[1024,256]{1,0:T(8,128)} custom-call(s32[1]{0:T(128)S(6)} %rem.22.me_ref, bf16[192,256]{1,0:T(8,128)(2,1)S(1)} %get-tuple-element.86.refs_0_, bf16[192,256]{1,0:T(8,128)(2,1)S(1)} %collective-permute-done.17.refs_1_, bf16[192,256]{1,0:T(8,128)(2,1)S(1)} %collective-permute-done.13.refs_2_, ...), custom_call_target="tpu_custom_call" | custom-call | flops 196608 | bytes 1179648 | tf_op jit(solution)/shard_map/pallas_call | solution.py:426
  85.8 1.1 %collective-permute-done.16.refs_3_ = bf16[64,256]{1,0:T(8,128)(2,1)S(1)} collective-permute-done((bf16[64,256]{1,0:T(8,128)(2,1)S(1)}, bf16[64,256]{1,0:T(8,128)(2,1)S(1)}, u32[]{:S(2)}, u32[]{:S(2)}) %collective-permute-start.16) | collective-permute-done | bytes 32800 | tf_op jit(solution)/shard_map/ppermute | solution.py:451
  87.0 0.7 shard_map.87
  (28 shorter events, 1.5 us)
Async XLA Ops:
  2.1 15.9 %copy-start = (f32[256,512]{1,0:T(8,128)S(1)}, f32[256,512]{1,0:T(8,128)}, u32[]{:S(2)}) copy-start(f32[256,512]{1,0:T(8,128)} %field_ref.3) | copy-start | bytes 1572868
  2.1 15.9 %copy-start.1 = (s32[256,512]{1,0:T(8,128)S(1)}, s32[256,512]{1,0:T(8,128)}, u32[]{:S(2)}) copy-start(s32[256,512]{1,0:T(8,128)} %mask_ref.3) | copy-start | bytes 1572868
  2.1 15.9 %copy-start.2 = (f32[256,512]{1,0:T(8,128)S(1)}, f32[256,512]{1,0:T(8,128)}, u32[]{:S(2)}) copy-start(f32[256,512]{1,0:T(8,128)} %visc_ref.3) | copy-start | bytes 1572868
  2.1 15.9 %copy-start.3 = (s32[128]{0:T(128)S(1)}, s32[128]{0:T(128)}, u32[]{:S(2)}) copy-start(s32[128]{0:T(128)} %param.9) | copy-start | bytes 1540
  2.1 10.7 %collective-permute-start = (f32[8,512]{1,0:T(8,128)}, f32[8,512]{1,0:T(8,128)S(1)}, u32[]{:S(2)}, u32[]{:S(2)}) collective-permute-start(f32[8,512]{1,0:T(8,128)} %get-tuple-element.48), channel_id=1, source_target_pairs={{0,4},{4,8},{8,12},{12,16},{16,20},{20,24},{24,28},{1,5},{5,9},{9,... | collective-permute-start | bytes 49160 | tf_op jit(solution)/shard_map/ppermute | solution.py:224
  7.1 5.8 %collective-permute-start.1 = (f32[8,512]{1,0:T(8,128)}, f32[8,512]{1,0:T(8,128)S(1)}, u32[]{:S(2)}, u32[]{:S(2)}) collective-permute-start(f32[8,512]{1,0:T(8,128)} %get-tuple-element.49), channel_id=1, source_target_pairs={{4,0},{8,4},{12,8},{16,12},{20,16},{24,20},{28,24},{5,1},{9,5},{13... | collective-permute-start | bytes 49160 | tf_op jit(solution)/shard_map/ppermute | solution.py:224
  12.8 29.4 %copy-start.4 = (s32[256,512]{1,0:T(8,128)S(1)}, s32[256,512]{1,0:T(8,128)}, u32[]{:S(2)}) copy-start(s32[256,512]{1,0:T(8,128)} %get-tuple-element.62.refs_0_) | copy-start | bytes 1572868
  12.9 23.1 %collective-permute-start.5 = (s32[256,512]{1,0:T(8,128)}, s32[256,512]{1,0:T(8,128)S(1)}, u32[]{:S(2)}, u32[]{:S(2)}) collective-permute-start(s32[256,512]{1,0:T(8,128)} %get-tuple-element.65), channel_id=1, source_target_pairs={{0,8},{4,12},{8,0},{12,4},{16,24},{20,28},{24,16},{28,20},{1,9},{5... | collective-permute-start | bytes 1572872 | tf_op jit(solution)/shard_map/ppermute | solution.py:451
  16.5 24.5 %collective-permute-start.4 = (s32[256,512]{1,0:T(8,128)}, s32[256,512]{1,0:T(8,128)S(1)}, u32[]{:S(2)}, u32[]{:S(2)}) collective-permute-start(s32[256,512]{1,0:T(8,128)} %get-tuple-element.63), channel_id=1, source_target_pairs={{0,4},{4,0},{8,12},{12,8},{16,20},{20,16},{24,28},{28,24},{1,5},{5... | collective-permute-start | bytes 1572872 | tf_op jit(solution)/shard_map/ppermute | solution.py:451
  17.1 23.9 %collective-permute-start.6 = (s32[256,512]{1,0:T(8,128)}, s32[256,512]{1,0:T(8,128)S(1)}, u32[]{:S(2)}, u32[]{:S(2)}) collective-permute-start(s32[256,512]{1,0:T(8,128)} %get-tuple-element.67), channel_id=1, source_target_pairs={{0,12},{4,8},{8,4},{12,0},{16,28},{20,24},{24,20},{28,16},{1,13},{... | collective-permute-start | bytes 1572872 | tf_op jit(solution)/shard_map/ppermute | solution.py:451
  18.3 2.6 %collective-permute-start.2 = (f32[8,384]{1,0:T(8,128)S(1)}, f32[8,384]{1,0:T(8,128)S(1)}, u32[]{:S(2)}, u32[]{:S(2)}) collective-permute-start(f32[8,384]{1,0:T(8,128)S(1)} %get-tuple-element.59), channel_id=1, source_target_pairs={{0,1},{1,2},{2,3},{4,5},{5,6},{6,7},{8,9},{9,10},{10,11},{12,13},{... | collective-permute-start | bytes 36872 | tf_op jit(solution)/shard_map/ppermute | solution.py:224
  19.6 4.8 %collective-permute-start.3 = (f32[8,384]{1,0:T(8,128)S(1)}, f32[8,384]{1,0:T(8,128)S(1)}, u32[]{:S(2)}, u32[]{:S(2)}) collective-permute-start(f32[8,384]{1,0:T(8,128)S(1)} %get-tuple-element.60), channel_id=1, source_target_pairs={{1,0},{2,1},{3,2},{5,4},{6,5},{7,6},{9,8},{10,9},{11,10},{13,12},{... | collective-permute-start | bytes 36872 | tf_op jit(solution)/shard_map/ppermute | solution.py:224
  36.0 5.0 %collective-permute-start.9 = (f32[4,4,128]{2,1,0:T(4,128)S(1)}, f32[4,4,128]{2,1,0:T(4,128)S(1)}, u32[]{:S(2)}, u32[]{:S(2)}) collective-permute-start(f32[4,4,128]{2,1,0:T(4,128)S(1)} %all-gather.1.refs_4_), channel_id=1, source_target_pairs={{0,12},{4,8},{8,4},{12,0},{16,28},{20,24},{24,20},{28,16},{1,13},{... | collective-permute-start | bytes 24584 | tf_op jit(solution)/shard_map/ppermute | solution.py:451
  38.1 3.7 %collective-permute-start.8 = (f32[4,4,128]{2,1,0:T(4,128)S(1)}, f32[4,4,128]{2,1,0:T(4,128)S(1)}, u32[]{:S(2)}, u32[]{:S(2)}) collective-permute-start(f32[4,4,128]{2,1,0:T(4,128)S(1)} %all-gather.1.refs_4_), channel_id=1, source_target_pairs={{0,8},{4,12},{8,0},{12,4},{16,24},{20,28},{24,16},{28,20},{1,9},{5... | collective-permute-start | bytes 24584 | tf_op jit(solution)/shard_map/ppermute | solution.py:451
  38.5 3.7 %collective-permute-start.7 = (f32[4,4,128]{2,1,0:T(4,128)S(1)}, f32[4,4,128]{2,1,0:T(4,128)S(1)}, u32[]{:S(2)}, u32[]{:S(2)}) collective-permute-start(f32[4,4,128]{2,1,0:T(4,128)S(1)} %all-gather.1.refs_4_), channel_id=1, source_target_pairs={{0,4},{4,0},{8,12},{12,8},{16,20},{20,16},{24,28},{28,24},{1,5},{5... | collective-permute-start | bytes 24584 | tf_op jit(solution)/shard_map/ppermute | solution.py:451
  54.0 20.8 %collective-permute-start.11 = (bf16[4,112,256]{2,1,0:T(8,128)(2,1)S(1)}, bf16[4,112,256]{2,1,0:T(8,128)(2,1)S(1)}, u32[]{:S(2)}, u32[]{:S(2)}) collective-permute-start(bf16[4,112,256]{2,1,0:T(8,128)(2,1)S(1)} %get-tuple-element.78), channel_id=1, source_target_pairs={{0,16},{4,20},{8,24},{12,28},{16,0},{20,4},{24,8},{28,12},{1,17},{... | collective-permute-start | bytes 688136 | tf_op jit(solution)/shard_map/ppermute | solution.py:474
  64.9 9.8 %collective-permute-start.12 = (bf16[4,80,256]{2,1,0:T(8,128)(2,1)S(1)}, bf16[4,80,256]{2,1,0:T(8,128)(2,1)S(1)}, u32[]{:S(2)}, u32[]{:S(2)}) collective-permute-start(bf16[4,80,256]{2,1,0:T(8,128)(2,1)S(1)} %get-tuple-element.79), channel_id=1, source_target_pairs={{0,16},{4,20},{8,24},{12,28},{16,0},{20,4},{24,8},{28,12},{1,17},{... | collective-permute-start | bytes 491528 | tf_op jit(solution)/shard_map/ppermute | solution.py:474
  72.2 7.2 %collective-permute-start.10 = (bf16[4,64,256]{2,1,0:T(8,128)(2,1)S(1)}, bf16[4,64,256]{2,1,0:T(8,128)(2,1)S(1)}, u32[]{:S(2)}, u32[]{:S(2)}) collective-permute-start(bf16[4,64,256]{2,1,0:T(8,128)(2,1)S(1)} %get-tuple-element.75), channel_id=1, source_target_pairs={{0,16},{4,20},{8,24},{12,28},{16,0},{20,4},{24,8},{28,12},{1,17},{... | collective-permute-start | bytes 393224 | tf_op jit(solution)/shard_map/ppermute | solution.py:474
  74.8 6.1 %collective-permute-start.13 = (bf16[192,256]{1,0:T(8,128)(2,1)S(1)}, bf16[192,256]{1,0:T(8,128)(2,1)S(1)}, u32[]{:S(2)}, u32[]{:S(2)}) collective-permute-start(bf16[192,256]{1,0:T(8,128)(2,1)S(1)} %get-tuple-element.80), channel_id=1, source_target_pairs={{0,8},{4,12},{8,0},{12,4},{16,24},{20,28},{24,16},{28,20},{1,9},{5... | collective-permute-start | bytes 294920 | tf_op jit(solution)/shard_map/ppermute | solution.py:451
  76.5 8.4 %collective-permute-start.17 = (bf16[192,256]{1,0:T(8,128)(2,1)S(1)}, bf16[192,256]{1,0:T(8,128)(2,1)S(1)}, u32[]{:S(2)}, u32[]{:S(2)}) collective-permute-start(bf16[192,256]{1,0:T(8,128)(2,1)S(1)} %get-tuple-element.87), channel_id=1, source_target_pairs={{0,4},{4,8},{8,12},{12,0},{16,20},{20,24},{24,28},{28,16},{1,5},{5... | collective-permute-start | bytes 294920 | tf_op jit(solution)/shard_map/ppermute | solution.py:451
  78.0 6.9 %collective-permute-start.18 = (bf16[192,256]{1,0:T(8,128)(2,1)S(1)}, bf16[192,256]{1,0:T(8,128)(2,1)S(1)}, u32[]{:S(2)}, u32[]{:S(2)}) collective-permute-start(bf16[192,256]{1,0:T(8,128)(2,1)S(1)} %get-tuple-element.89), channel_id=1, source_target_pairs={{0,12},{4,0},{8,4},{12,8},{16,28},{20,16},{24,20},{28,24},{1,13},{... | collective-permute-start | bytes 294920 | tf_op jit(solution)/shard_map/ppermute | solution.py:451
  81.0 4.9 %collective-permute-start.14 = (bf16[64,256]{1,0:T(8,128)(2,1)S(1)}, bf16[64,256]{1,0:T(8,128)(2,1)S(1)}, u32[]{:S(2)}, u32[]{:S(2)}) collective-permute-start(bf16[64,256]{1,0:T(8,128)(2,1)S(1)} %get-tuple-element.83), channel_id=1, source_target_pairs={{0,4},{4,8},{8,12},{12,0},{16,20},{20,24},{24,28},{28,16},{1,5},{5... | collective-permute-start | bytes 98312 | tf_op jit(solution)/shard_map/ppermute | solution.py:451
  81.8 4.0 %collective-permute-start.15 = (bf16[64,256]{1,0:T(8,128)(2,1)S(1)}, bf16[64,256]{1,0:T(8,128)(2,1)S(1)}, u32[]{:S(2)}, u32[]{:S(2)}) collective-permute-start(bf16[64,256]{1,0:T(8,128)(2,1)S(1)} %get-tuple-element.84), channel_id=1, source_target_pairs={{0,8},{4,12},{8,0},{12,4},{16,24},{20,28},{24,16},{28,20},{1,9},{5... | collective-permute-start | bytes 98312 | tf_op jit(solution)/shard_map/ppermute | solution.py:451
  83.0 3.9 %collective-permute-start.16 = (bf16[64,256]{1,0:T(8,128)(2,1)S(1)}, bf16[64,256]{1,0:T(8,128)(2,1)S(1)}, u32[]{:S(2)}, u32[]{:S(2)}) collective-permute-start(bf16[64,256]{1,0:T(8,128)(2,1)S(1)} %get-tuple-element.85), channel_id=1, source_target_pairs={{0,12},{4,0},{8,4},{12,8},{16,28},{20,16},{24,20},{28,24},{1,13},{... | collective-permute-start | bytes 98312 | tf_op jit(solution)/shard_map/ppermute | solution.py:451

commit v10 on v9

--- a/solution.py
+++ b/solution.py
@@ -491,7 +491,7 @@
     units = observers // 16
     ends = [-(-units * part // 16) * 16 for part in PARTS]
     counts = [end - start for start, end in zip([0] + ends, ends)]
-    return [[c for c in group if c] for group in (counts[:2], counts[2:]) if any(group)]
+    return [[c for c in counts if c]]
 
 
 def solution(mesh):

time: 88.1 us -> 88.6 us (level)
  waiting for transfers between devices: 8.94 us -> 15 us
  starting transfers between devices: 31.5 us -> 26.6 us
    ppermute x12 -> x9, starting transfers between devices: 17.1 us -> 12.1 us  [spread(): lax.ppermute(x, 'box', perm(k))]
    ppermute x3, waiting for transfers between devices: 0.01 us -> 4.94 us  [on_device(): groups[-1].append((keep, lax.ppermute(send, 'box', across)))]
    ppermute x12 -> x9, waiting for transfers between devices: 5.27 us -> 6.42 us  [spread(): lax.ppermute(x, 'box', perm(k))]
  transfers between devices with their start and end apart: 19 -> 16, of which waited for: 7 -> 9; matrix products, arithmetic and copies ran while one was open for 0% -> 0% of each run, Pallas kernels for 29% -> 28%
where the time goes in v10:
time: 88.6 us; the launch traced here: 88.2 us
  Pallas kernels  39 us (44%)
  starting transfers between devices  26.6 us (30%)
  waiting for transfers between devices  15 us (17%)
  blocking collectives  6.75 us (8%)
    pallas_call x3, Pallas kernels, binned(): pl.pallas_call(bin_kernel, grid=(count // block,), in_specs=[SMEM] + [pl....  27 us
    ppermute x9, starting transfers between devices, spread(): lax.ppermute(x, 'box', perm(k))  12.1 us
    ppermute x4, starting transfers between devices, shifted(): return (lax.ppermute(last, axis, up), lax.ppermute(first, axis, down))  8.88 us
    all_gather x1, blocking collectives, on_device(): sample = lax.all_gather(sample, 'panel')  6.75 us
    ppermute x9, waiting for transfers between devices, spread(): lax.ppermute(x, 'box', perm(k))  6.42 us
    ppermute x3, starting transfers between devices, on_device(): groups[-1].append((keep, lax.ppermute(send, 'box', across)))  5.66 us
    ppermute x3, waiting for transfers between devices, on_device(): groups[-1].append((keep, lax.ppermute(send, 'box', across)))  4.94 us
    pallas_call x1, Pallas kernels, field_window(): pl.pallas_call(step_kernel, in_specs=[SMEM] + [VMEM] * 7, out_specs=[pl.B...  4.9 us
  transfers between devices with their start and end apart: 16, of which 9 were waited for; matrix products, arithmetic and copies ran while one was open for 0% of the time, Pallas kernels for 28%

profile of v10, /device:TPU:0, one launch (start us, length us, event | category | flops | bytes accessed | tf_op | source)
XLA Modules:
  0.0 88.2 jit_solution(10682529943677967364)
XLA Ops:
  0.6 1.4 %shard_map.77 = (f32[8,512]{1,0:T(8,128)}, f32[8,512]{1,0:T(8,128)}) custom-call(f32[256,512]{1,0:T(8,128)} %field_ref.3, s32[256,512]{1,0:T(8,128)} %mask_ref.3, f32[256,512]{1,0:T(8,128)} %visc_ref.3, f32[256,512]{1,0:T(8,128)} %field_ref.3, s32[256,512]{1,0:T(8,128)} %mask_ref.3, f32[256,512]{1,0:T(8,128)} %visc_ref.3), custom_call_target="tpu_custom_call" | custom-call | flops 8192 | bytes 131072 | tf_op jit(solution)/shard_map/pallas_call | solution.py:208
  2.1 5.0 %collective-permute-start = (f32[8,512]{1,0:T(8,128)}, f32[8,512]{1,0:T(8,128)S(1)}, u32[]{:S(2)}, u32[]{:S(2)}) collective-permute-start(f32[8,512]{1,0:T(8,128)} %get-tuple-element.42), channel_id=1, source_target_pairs={{0,4},{4,8},{8,12},{12,16},{16,20},{20,24},{24,28},{1,5},{5,9},{9,... | collective-permute-start | bytes 49160 | tf_op jit(solution)/shard_map/ppermute | solution.py:224
  7.1 1.3 %collective-permute-start.1 = (f32[8,512]{1,0:T(8,128)}, f32[8,512]{1,0:T(8,128)S(1)}, u32[]{:S(2)}, u32[]{:S(2)}) collective-permute-start(f32[8,512]{1,0:T(8,128)} %get-tuple-element.43), channel_id=1, source_target_pairs={{4,0},{8,4},{12,8},{16,12},{20,16},{24,20},{28,24},{5,1},{9,5},{13... | collective-permute-start | bytes 49160 | tf_op jit(solution)/shard_map/ppermute | solution.py:224
  8.4 4.3 %shard_map.78 = (s32[256,512]{1,0:T(8,128)}, s32[256,512]{1,0:T(8,128)}, s32[256,512]{1,0:T(8,128)}, s32[256,512]{1,0:T(8,128)}) custom-call(s32[1]{0:T(128)S(6)} %rem.22.me_ref, bf16[512,1024]{1,0:T(8,128)(2,1)} %amp_ref, s32[512,1024]{1,0:T(8,128)} %bin_ref), custom_call_target="tpu_custom_call" | custom-call | flops 524288 | bytes 5242880 | tf_op jit(solution)/shard_map/pallas_call | solution.py:52
  12.9 3.5 %collective-permute-start.5 = (s32[256,512]{1,0:T(8,128)}, s32[256,512]{1,0:T(8,128)S(1)}, u32[]{:S(2)}, u32[]{:S(2)}) collective-permute-start(s32[256,512]{1,0:T(8,128)} %get-tuple-element.59), channel_id=1, source_target_pairs={{0,8},{4,12},{8,0},{12,4},{16,24},{20,28},{24,16},{28,20},{1,9},{5... | collective-permute-start | bytes 1572872 | tf_op jit(solution)/shard_map/ppermute | solution.py:451
  16.4 0.6 collective-permute-start.4
  17.1 0.9 %collective-permute-start.6 = (s32[256,512]{1,0:T(8,128)}, s32[256,512]{1,0:T(8,128)S(1)}, u32[]{:S(2)}, u32[]{:S(2)}) collective-permute-start(s32[256,512]{1,0:T(8,128)} %get-tuple-element.61), channel_id=1, source_target_pairs={{0,12},{4,8},{8,4},{12,0},{16,28},{20,24},{24,20},{28,16},{1,13},{... | collective-permute-start | bytes 1572872 | tf_op jit(solution)/shard_map/ppermute | solution.py:451
  18.0 0.3 shard_map.79
  18.3 1.3 %collective-permute-start.2 = (f32[8,384]{1,0:T(8,128)S(1)}, f32[8,384]{1,0:T(8,128)S(1)}, u32[]{:S(2)}, u32[]{:S(2)}) collective-permute-start(f32[8,384]{1,0:T(8,128)S(1)} %get-tuple-element.53), channel_id=1, source_target_pairs={{0,1},{1,2},{2,3},{4,5},{5,6},{6,7},{8,9},{9,10},{10,11},{12,13},{... | collective-permute-start | bytes 36872 | tf_op jit(solution)/shard_map/ppermute | solution.py:224
  19.6 1.3 %collective-permute-start.3 = (f32[8,384]{1,0:T(8,128)S(1)}, f32[8,384]{1,0:T(8,128)S(1)}, u32[]{:S(2)}, u32[]{:S(2)}) collective-permute-start(f32[8,384]{1,0:T(8,128)S(1)} %get-tuple-element.54), channel_id=1, source_target_pairs={{1,0},{2,1},{3,2},{5,4},{6,5},{7,6},{9,8},{10,9},{11,10},{13,12},{... | collective-permute-start | bytes 36872 | tf_op jit(solution)/shard_map/ppermute | solution.py:224
  20.9 3.5 %collective-permute-done.3.north_ref = f32[8,384]{1,0:T(8,128)S(1)} collective-permute-done((f32[8,384]{1,0:T(8,128)S(1)}, f32[8,384]{1,0:T(8,128)S(1)}, u32[]{:S(2)}, u32[]{:S(2)}) %collective-permute-start.3) | collective-permute-done | bytes 12320 | tf_op jit(solution)/shard_map/ppermute | solution.py:224
  24.4 4.9 %shard_map.80 = (f32[256,512]{1,0:T(8,128)}, f32[4,128]{1,0:T(4,128)S(1)}) custom-call(s32[4,128]{1,0:T(4,128)S(1)} %get-tuple-element.52.cell_ref, f32[256,512]{1,0:T(8,128)S(1)} %copy-done, s32[256,512]{1,0:T(8,128)S(1)} %copy-done.1, f32[256,512]{1,0:T(8,128)S(1)} %copy-done.2, f32[8,512]{1,0:T(8,128)S(1)} %collective-permute-done.before_ref, ...), custom_call_target="tpu_custom_call" | custom-call | flops 13107200 | bytes 104857600 | tf_op jit(solution)/shard_map/pallas_call | solution.py:245
  29.3 6.8 %all-gather.1.refs_4_ = f32[4,4,128]{2,1,0:T(4,128)S(1)} all-gather(f32[1,4,128]{2,1,0:T(4,128)S(1)} %bitcast.3), channel_id=2, replica_groups=mesh['box'=8,'panel'=4] {'panel'}, dimensions={0}, use_global_device_ids=true | all-gather | bytes 10240 | tf_op jit(solution)/shard_map/all_gather | solution.py:462
  36.0 2.0 %collective-permute-start.9 = (f32[4,4,128]{2,1,0:T(4,128)S(1)}, f32[4,4,128]{2,1,0:T(4,128)S(1)}, u32[]{:S(2)}, u32[]{:S(2)}) collective-permute-start(f32[4,4,128]{2,1,0:T(4,128)S(1)} %all-gather.1.refs_4_), channel_id=1, source_target_pairs={{0,12},{4,8},{8,4},{12,0},{16,28},{20,24},{24,20},{28,16},{1,13},{... | collective-permute-start | bytes 24584 | tf_op jit(solution)/shard_map/ppermute | solution.py:451
  38.1 0.4 collective-permute-start.8
  38.5 1.0 %collective-permute-start.7 = (f32[4,4,128]{2,1,0:T(4,128)S(1)}, f32[4,4,128]{2,1,0:T(4,128)S(1)}, u32[]{:S(2)}, u32[]{:S(2)}) collective-permute-start(f32[4,4,128]{2,1,0:T(4,128)S(1)} %all-gather.1.refs_4_), channel_id=1, source_target_pairs={{0,4},{4,0},{8,12},{12,8},{16,20},{20,16},{24,28},{28,24},{1,5},{5... | collective-permute-start | bytes 24584 | tf_op jit(solution)/shard_map/ppermute | solution.py:451
  39.6 1.4 %collective-permute-done.4.refs_1_ = s32[256,512]{1,0:T(8,128)S(1)} collective-permute-done((s32[256,512]{1,0:T(8,128)}, s32[256,512]{1,0:T(8,128)S(1)}, u32[]{:S(2)}, u32[]{:S(2)}) %collective-permute-start.4) | collective-permute-done | bytes 524320 | tf_op jit(solution)/shard_map/ppermute | solution.py:451
  41.0 0.7 collective-permute-done.8.refs_6_
  41.7 0.4 collective-permute-done.7.refs_5_
  42.2 11.8 %shard_map.81 = (f32[4,112,256]{2,1,0:T(8,128)S(1)}, bf16[4,112,256]{2,1,0:T(8,128)(2,1)S(1)}) custom-call(s32[1]{0:T(128)S(6)} %select_n.5.half_ref, s32[256,512]{1,0:T(8,128)S(1)} %copy-done.4, s32[256,512]{1,0:T(8,128)S(1)} %collective-permute-done.4.refs_1_, s32[256,512]{1,0:T(8,128)S(1)} %collective-permute-done.5.refs_2_, ...), custom_call_target="tpu_custom_call" | custom-call | flops 15032385536 | bytes 1835008 | tf_op jit(solution)/shard_map/pallas_call | solution.py:359
  54.0 2.6 %collective-permute-start.10 = (bf16[4,112,256]{2,1,0:T(8,128)(2,1)S(1)}, bf16[4,112,256]{2,1,0:T(8,128)(2,1)S(1)}, u32[]{:S(2)}, u32[]{:S(2)}) collective-permute-start(bf16[4,112,256]{2,1,0:T(8,128)(2,1)S(1)} %get-tuple-element.71), channel_id=1, source_target_pairs={{0,16},{4,20},{8,24},{12,28},{16,0},{20,4},{24,8},{28,12},{1,17},{... | collective-permute-start | bytes 688136 | tf_op jit(solution)/shard_map/ppermute | solution.py:474
  56.6 8.4 %shard_map.82 = (f32[4,80,256]{2,1,0:T(8,128)S(1)}, bf16[4,80,256]{2,1,0:T(8,128)(2,1)S(1)}) custom-call(s32[1]{0:T(128)S(6)} %select_n.5.half_ref, s32[256,512]{1,0:T(8,128)S(1)} %copy-done.4, s32[256,512]{1,0:T(8,128)S(1)} %collective-permute-done.4.refs_1_, s32[256,512]{1,0:T(8,128)S(1)} %collective-permute-done.5.refs_2_, ...), custom_call_target="tpu_custom_call" | custom-call | flops 10737418240 | bytes 1310720 | tf_op jit(solution)/shard_map/pallas_call | solution.py:359
  65.0 0.4 collective-permute-start.11
  65.5 6.7 %shard_map.83 = (f32[4,64,256]{2,1,0:T(8,128)S(1)}, bf16[4,64,256]{2,1,0:T(8,128)(2,1)S(1)}) custom-call(s32[1]{0:T(128)S(6)} %select_n.5.half_ref, s32[256,512]{1,0:T(8,128)S(1)} %copy-done.4, s32[256,512]{1,0:T(8,128)S(1)} %collective-permute-done.4.refs_1_, s32[256,512]{1,0:T(8,128)S(1)} %collective-permute-done.5.refs_2_, ...), custom_call_target="tpu_custom_call" | custom-call | flops 8589934592 | bytes 1048576 | tf_op jit(solution)/shard_map/pallas_call | solution.py:359
  72.2 2.6 %collective-permute-start.12 = (bf16[4,64,256]{2,1,0:T(8,128)(2,1)S(1)}, bf16[4,64,256]{2,1,0:T(8,128)(2,1)S(1)}, u32[]{:S(2)}, u32[]{:S(2)}) collective-permute-start(bf16[4,64,256]{2,1,0:T(8,128)(2,1)S(1)} %get-tuple-element.73), channel_id=1, source_target_pairs={{0,16},{4,20},{8,24},{12,28},{16,0},{20,4},{24,8},{28,12},{1,17},{... | collective-permute-start | bytes 393224 | tf_op jit(solution)/shard_map/ppermute | solution.py:474
  74.8 4.9 %collective-permute-done.12.refs_5_ = bf16[4,64,256]{2,1,0:T(8,128)(2,1)S(1)} collective-permute-done((bf16[4,64,256]{2,1,0:T(8,128)(2,1)S(1)}, bf16[4,64,256]{2,1,0:T(8,128)(2,1)S(1)}, u32[]{:S(2)}, u32[]{:S(2)}) %collective-permute-start.12) | collective-permute-done | bytes 131104 | tf_op jit(solution)/shard_map/ppermute | solution.py:474
  79.9 1.1 %collective-permute-start.13 = (bf16[256,256]{1,0:T(8,128)(2,1)S(1)}, bf16[256,256]{1,0:T(8,128)(2,1)S(1)}, u32[]{:S(2)}, u32[]{:S(2)}) collective-permute-start(bf16[256,256]{1,0:T(8,128)(2,1)S(1)} %get-tuple-element.75), channel_id=1, source_target_pairs={{0,4},{4,8},{8,12},{12,0},{16,20},{20,24},{24,28},{28,16},{1,5},{5... | collective-permute-start | bytes 393224 | tf_op jit(solution)/shard_map/ppermute | solution.py:451
  80.9 0.8 collective-permute-start.14
  81.8 1.6 %collective-permute-start.15 = (bf16[256,256]{1,0:T(8,128)(2,1)S(1)}, bf16[256,256]{1,0:T(8,128)(2,1)S(1)}, u32[]{:S(2)}, u32[]{:S(2)}) collective-permute-start(bf16[256,256]{1,0:T(8,128)(2,1)S(1)} %get-tuple-element.77), channel_id=1, source_target_pairs={{0,12},{4,0},{8,4},{12,8},{16,28},{20,16},{24,20},{28,24},{1,13},{... | collective-permute-start | bytes 393224 | tf_op jit(solution)/shard_map/ppermute | solution.py:451
  83.4 2.5 %collective-permute-done.13.refs_1_ = bf16[256,256]{1,0:T(8,128)(2,1)S(1)} collective-permute-done((bf16[256,256]{1,0:T(8,128)(2,1)S(1)}, bf16[256,256]{1,0:T(8,128)(2,1)S(1)}, u32[]{:S(2)}, u32[]{:S(2)}) %collective-permute-start.13) | collective-permute-done | bytes 131104 | tf_op jit(solution)/shard_map/ppermute | solution.py:451
  85.9 1.3 %collective-permute-done.15.refs_3_ = bf16[256,256]{1,0:T(8,128)(2,1)S(1)} collective-permute-done((bf16[256,256]{1,0:T(8,128)(2,1)S(1)}, bf16[256,256]{1,0:T(8,128)(2,1)S(1)}, u32[]{:S(2)}, u32[]{:S(2)}) %collective-permute-start.15) | collective-permute-done | bytes 131104 | tf_op jit(solution)/shard_map/ppermute | solution.py:451
  87.2 1.0 %shard_map.85 = f32[1024,256]{1,0:T(8,128)} custom-call(s32[1]{0:T(128)S(6)} %rem.22.me_ref, bf16[256,256]{1,0:T(8,128)(2,1)S(1)} %get-tuple-element.74.refs_0_, bf16[256,256]{1,0:T(8,128)(2,1)S(1)} %collective-permute-done.13.refs_1_, bf16[256,256]{1,0:T(8,128)(2,1)S(1)} %collective-permute-done.14.refs_2_, bf16[256,256]{1,0:T(8,128)(2,1)S(1)} %collective-permute-done.15.refs_3_), custom_call_target="tpu_custom_call" | custom-call | flops 262144 | bytes 1572864 | tf_op jit(solution)/shard_map/pallas_call | solution.py:426
  (20 shorter events, 0.4 us)
Async XLA Ops:
  2.1 15.9 %copy-start = (f32[256,512]{1,0:T(8,128)S(1)}, f32[256,512]{1,0:T(8,128)}, u32[]{:S(2)}) copy-start(f32[256,512]{1,0:T(8,128)} %field_ref.3) | copy-start | bytes 1572868
  2.1 15.9 %copy-start.1 = (s32[256,512]{1,0:T(8,128)S(1)}, s32[256,512]{1,0:T(8,128)}, u32[]{:S(2)}) copy-start(s32[256,512]{1,0:T(8,128)} %mask_ref.3) | copy-start | bytes 1572868
  2.1 15.9 %copy-start.2 = (f32[256,512]{1,0:T(8,128)S(1)}, f32[256,512]{1,0:T(8,128)}, u32[]{:S(2)}) copy-start(f32[256,512]{1,0:T(8,128)} %visc_ref.3) | copy-start | bytes 1572868
  2.1 15.9 %copy-start.3 = (s32[128]{0:T(128)S(1)}, s32[128]{0:T(128)}, u32[]{:S(2)}) copy-start(s32[128]{0:T(128)} %param.9) | copy-start | bytes 1540
  2.1 10.7 %collective-permute-start = (f32[8,512]{1,0:T(8,128)}, f32[8,512]{1,0:T(8,128)S(1)}, u32[]{:S(2)}, u32[]{:S(2)}) collective-permute-start(f32[8,512]{1,0:T(8,128)} %get-tuple-element.42), channel_id=1, source_target_pairs={{0,4},{4,8},{8,12},{12,16},{16,20},{20,24},{24,28},{1,5},{5,9},{9,... | collective-permute-start | bytes 49160 | tf_op jit(solution)/shard_map/ppermute | solution.py:224
  7.1 5.8 %collective-permute-start.1 = (f32[8,512]{1,0:T(8,128)}, f32[8,512]{1,0:T(8,128)S(1)}, u32[]{:S(2)}, u32[]{:S(2)}) collective-permute-start(f32[8,512]{1,0:T(8,128)} %get-tuple-element.43), channel_id=1, source_target_pairs={{4,0},{8,4},{12,8},{16,12},{20,16},{24,20},{28,24},{5,1},{9,5},{13... | collective-permute-start | bytes 49160 | tf_op jit(solution)/shard_map/ppermute | solution.py:224
  12.7 29.4 %copy-start.4 = (s32[256,512]{1,0:T(8,128)S(1)}, s32[256,512]{1,0:T(8,128)}, u32[]{:S(2)}) copy-start(s32[256,512]{1,0:T(8,128)} %get-tuple-element.56.refs_0_) | copy-start | bytes 1572868
  12.9 23.1 %collective-permute-start.5 = (s32[256,512]{1,0:T(8,128)}, s32[256,512]{1,0:T(8,128)S(1)}, u32[]{:S(2)}, u32[]{:S(2)}) collective-permute-start(s32[256,512]{1,0:T(8,128)} %get-tuple-element.59), channel_id=1, source_target_pairs={{0,8},{4,12},{8,0},{12,4},{16,24},{20,28},{24,16},{28,20},{1,9},{5... | collective-permute-start | bytes 1572872 | tf_op jit(solution)/shard_map/ppermute | solution.py:451
  16.4 24.5 %collective-permute-start.4 = (s32[256,512]{1,0:T(8,128)}, s32[256,512]{1,0:T(8,128)S(1)}, u32[]{:S(2)}, u32[]{:S(2)}) collective-permute-start(s32[256,512]{1,0:T(8,128)} %get-tuple-element.57), channel_id=1, source_target_pairs={{0,4},{4,0},{8,12},{12,8},{16,20},{20,16},{24,28},{28,24},{1,5},{5... | collective-permute-start | bytes 1572872 | tf_op jit(solution)/shard_map/ppermute | solution.py:451
  17.1 23.9 %collective-permute-start.6 = (s32[256,512]{1,0:T(8,128)}, s32[256,512]{1,0:T(8,128)S(1)}, u32[]{:S(2)}, u32[]{:S(2)}) collective-permute-start(s32[256,512]{1,0:T(8,128)} %get-tuple-element.61), channel_id=1, source_target_pairs={{0,12},{4,8},{8,4},{12,0},{16,28},{20,24},{24,20},{28,16},{1,13},{... | collective-permute-start | bytes 1572872 | tf_op jit(solution)/shard_map/ppermute | solution.py:451
  18.3 2.6 %collective-permute-start.2 = (f32[8,384]{1,0:T(8,128)S(1)}, f32[8,384]{1,0:T(8,128)S(1)}, u32[]{:S(2)}, u32[]{:S(2)}) collective-permute-start(f32[8,384]{1,0:T(8,128)S(1)} %get-tuple-element.53), channel_id=1, source_target_pairs={{0,1},{1,2},{2,3},{4,5},{5,6},{6,7},{8,9},{9,10},{10,11},{12,13},{... | collective-permute-start | bytes 36872 | tf_op jit(solution)/shard_map/ppermute | solution.py:224
  19.6 4.8 %collective-permute-start.3 = (f32[8,384]{1,0:T(8,128)S(1)}, f32[8,384]{1,0:T(8,128)S(1)}, u32[]{:S(2)}, u32[]{:S(2)}) collective-permute-start(f32[8,384]{1,0:T(8,128)S(1)} %get-tuple-element.54), channel_id=1, source_target_pairs={{1,0},{2,1},{3,2},{5,4},{6,5},{7,6},{9,8},{10,9},{11,10},{13,12},{... | collective-permute-start | bytes 36872 | tf_op jit(solution)/shard_map/ppermute | solution.py:224
  36.0 5.0 %collective-permute-start.9 = (f32[4,4,128]{2,1,0:T(4,128)S(1)}, f32[4,4,128]{2,1,0:T(4,128)S(1)}, u32[]{:S(2)}, u32[]{:S(2)}) collective-permute-start(f32[4,4,128]{2,1,0:T(4,128)S(1)} %all-gather.1.refs_4_), channel_id=1, source_target_pairs={{0,12},{4,8},{8,4},{12,0},{16,28},{20,24},{24,20},{28,16},{1,13},{... | collective-permute-start | bytes 24584 | tf_op jit(solution)/shard_map/ppermute | solution.py:451
  38.1 3.7 %collective-permute-start.8 = (f32[4,4,128]{2,1,0:T(4,128)S(1)}, f32[4,4,128]{2,1,0:T(4,128)S(1)}, u32[]{:S(2)}, u32[]{:S(2)}) collective-permute-start(f32[4,4,128]{2,1,0:T(4,128)S(1)} %all-gather.1.refs_4_), channel_id=1, source_target_pairs={{0,8},{4,12},{8,0},{12,4},{16,24},{20,28},{24,16},{28,20},{1,9},{5... | collective-permute-start | bytes 24584 | tf_op jit(solution)/shard_map/ppermute | solution.py:451
  38.5 3.7 %collective-permute-start.7 = (f32[4,4,128]{2,1,0:T(4,128)S(1)}, f32[4,4,128]{2,1,0:T(4,128)S(1)}, u32[]{:S(2)}, u32[]{:S(2)}) collective-permute-start(f32[4,4,128]{2,1,0:T(4,128)S(1)} %all-gather.1.refs_4_), channel_id=1, source_target_pairs={{0,4},{4,0},{8,12},{12,8},{16,20},{20,16},{24,28},{28,24},{1,5},{5... | collective-permute-start | bytes 24584 | tf_op jit(solution)/shard_map/ppermute | solution.py:451
  54.0 25.8 %collective-permute-start.10 = (bf16[4,112,256]{2,1,0:T(8,128)(2,1)S(1)}, bf16[4,112,256]{2,1,0:T(8,128)(2,1)S(1)}, u32[]{:S(2)}, u32[]{:S(2)}) collective-permute-start(bf16[4,112,256]{2,1,0:T(8,128)(2,1)S(1)} %get-tuple-element.71), channel_id=1, source_target_pairs={{0,16},{4,20},{8,24},{12,28},{16,0},{20,4},{24,8},{28,12},{1,17},{... | collective-permute-start | bytes 688136 | tf_op jit(solution)/shard_map/ppermute | solution.py:474
  65.0 14.7 %collective-permute-start.11 = (bf16[4,80,256]{2,1,0:T(8,128)(2,1)S(1)}, bf16[4,80,256]{2,1,0:T(8,128)(2,1)S(1)}, u32[]{:S(2)}, u32[]{:S(2)}) collective-permute-start(bf16[4,80,256]{2,1,0:T(8,128)(2,1)S(1)} %get-tuple-element.72), channel_id=1, source_target_pairs={{0,16},{4,20},{8,24},{12,28},{16,0},{20,4},{24,8},{28,12},{1,17},{... | collective-permute-start | bytes 491528 | tf_op jit(solution)/shard_map/ppermute | solution.py:474
  72.2 7.6 %collective-permute-start.12 = (bf16[4,64,256]{2,1,0:T(8,128)(2,1)S(1)}, bf16[4,64,256]{2,1,0:T(8,128)(2,1)S(1)}, u32[]{:S(2)}, u32[]{:S(2)}) collective-permute-start(bf16[4,64,256]{2,1,0:T(8,128)(2,1)S(1)} %get-tuple-element.73), channel_id=1, source_target_pairs={{0,16},{4,20},{8,24},{12,28},{16,0},{20,4},{24,8},{28,12},{1,17},{... | collective-permute-start | bytes 393224 | tf_op jit(solution)/shard_map/ppermute | solution.py:474
  79.9 6.0 %collective-permute-start.13 = (bf16[256,256]{1,0:T(8,128)(2,1)S(1)}, bf16[256,256]{1,0:T(8,128)(2,1)S(1)}, u32[]{:S(2)}, u32[]{:S(2)}) collective-permute-start(bf16[256,256]{1,0:T(8,128)(2,1)S(1)} %get-tuple-element.75), channel_id=1, source_target_pairs={{0,4},{4,8},{8,12},{12,0},{16,20},{20,24},{24,28},{28,16},{1,5},{5... | collective-permute-start | bytes 393224 | tf_op jit(solution)/shard_map/ppermute | solution.py:451
  80.9 5.0 %collective-permute-start.14 = (bf16[256,256]{1,0:T(8,128)(2,1)S(1)}, bf16[256,256]{1,0:T(8,128)(2,1)S(1)}, u32[]{:S(2)}, u32[]{:S(2)}) collective-permute-start(bf16[256,256]{1,0:T(8,128)(2,1)S(1)} %get-tuple-element.76), channel_id=1, source_target_pairs={{0,8},{4,12},{8,0},{12,4},{16,24},{20,28},{24,16},{28,20},{1,9},{5... | collective-permute-start | bytes 393224 | tf_op jit(solution)/shard_map/ppermute | solution.py:451
  81.8 5.4 %collective-permute-start.15 = (bf16[256,256]{1,0:T(8,128)(2,1)S(1)}, bf16[256,256]{1,0:T(8,128)(2,1)S(1)}, u32[]{:S(2)}, u32[]{:S(2)}) collective-permute-start(bf16[256,256]{1,0:T(8,128)(2,1)S(1)} %get-tuple-element.77), channel_id=1, source_target_pairs={{0,12},{4,0},{8,4},{12,8},{16,28},{20,16},{24,20},{28,24},{1,13},{... | collective-permute-start | bytes 393224 | tf_op jit(solution)/shard_map/ppermute | solution.py:451

commit v11 on v9

--- a/solution.py
+++ b/solution.py
@@ -17,7 +17,7 @@
 PAD = 16
 STRIP = 32
 AMP_SCALE = 4096.0
-PARTS = (7, 12, 16)
+PARTS = (8, 13, 16)
 VMEM = pl.BlockSpec(memory_space=pltpu.VMEM)
 SMEM = pl.BlockSpec(memory_space=pltpu.SMEM)
 

time: 88.1 us -> 96.6 us (1.096)
  waiting for transfers between devices: 8.94 us -> 18.7 us
  starting transfers between devices: 31.5 us -> 30.5 us
    ppermute x3, waiting for transfers between devices: 0.01 us -> 11 us  [on_device(): groups[-1].append((keep, lax.ppermute(send, 'box', across)))]
    ppermute x12, starting transfers between devices: 17.1 us -> 15.1 us  [spread(): lax.ppermute(x, 'box', perm(k))]
    ppermute x12, waiting for transfers between devices: 5.27 us -> 4.02 us  [spread(): lax.ppermute(x, 'box', perm(k))]
  transfers between devices with their start and end apart: 19 -> 19, of which waited for: 7 -> 10; matrix products, arithmetic and copies ran while one was open for 0% -> 0% of each run, Pallas kernels for 29% -> 25%
where the time goes in v11:
time: 96.6 us; the launch traced here: 96.2 us
  Pallas kernels  39.6 us (41%)
  starting transfers between devices  30.5 us (32%)
  waiting for transfers between devices  18.7 us (19%)
  blocking collectives  6.75 us (7%)
    pallas_call x3, Pallas kernels, binned(): pl.pallas_call(bin_kernel, grid=(count // block,), in_specs=[SMEM] + [pl....  26.8 us
    ppermute x12, starting transfers between devices, spread(): lax.ppermute(x, 'box', perm(k))  15.1 us
    ppermute x3, waiting for transfers between devices, on_device(): groups[-1].append((keep, lax.ppermute(send, 'box', across)))  11 us
    ppermute x4, starting transfers between devices, shifted(): return (lax.ppermute(last, axis, up), lax.ppermute(first, axis, down))  8.88 us
    all_gather x1, blocking collectives, on_device(): sample = lax.all_gather(sample, 'panel')  6.75 us
    ppermute x3, starting transfers between devices, on_device(): groups[-1].append((keep, lax.ppermute(send, 'box', across)))  6.49 us
    pallas_call x1, Pallas kernels, field_window(): pl.pallas_call(step_kernel, in_specs=[SMEM] + [VMEM] * 7, out_specs=[pl.B...  4.9 us
    pallas_call x1, Pallas kernels, pack(): pl.pallas_call(pack_kernel, grid=(panels // LANES,), in_specs=[SMEM, bloc...  4.37 us
  transfers between devices with their start and end apart: 19, of which 10 were waited for; matrix products, arithmetic and copies ran while one was open for 0% of the time, Pallas kernels for 25%

profile of v11, /device:TPU:0, one launch (start us, length us, event | category | flops | bytes accessed | tf_op | source)
XLA Modules:
  0.0 96.2 jit_solution(12596422967876258176)
XLA Ops:
  0.6 1.4 %shard_map.77 = (f32[8,512]{1,0:T(8,128)}, f32[8,512]{1,0:T(8,128)}) custom-call(f32[256,512]{1,0:T(8,128)} %field_ref.3, s32[256,512]{1,0:T(8,128)} %mask_ref.3, f32[256,512]{1,0:T(8,128)} %visc_ref.3, f32[256,512]{1,0:T(8,128)} %field_ref.3, s32[256,512]{1,0:T(8,128)} %mask_ref.3, f32[256,512]{1,0:T(8,128)} %visc_ref.3), custom_call_target="tpu_custom_call" | custom-call | flops 8192 | bytes 131072 | tf_op jit(solution)/shard_map/pallas_call | solution.py:208
  2.1 5.0 %collective-permute-start = (f32[8,512]{1,0:T(8,128)}, f32[8,512]{1,0:T(8,128)S(1)}, u32[]{:S(2)}, u32[]{:S(2)}) collective-permute-start(f32[8,512]{1,0:T(8,128)} %get-tuple-element.48), channel_id=1, source_target_pairs={{0,4},{4,8},{8,12},{12,16},{16,20},{20,24},{24,28},{1,5},{5,9},{9,... | collective-permute-start | bytes 49160 | tf_op jit(solution)/shard_map/ppermute | solution.py:224
  7.1 1.3 %collective-permute-start.1 = (f32[8,512]{1,0:T(8,128)}, f32[8,512]{1,0:T(8,128)S(1)}, u32[]{:S(2)}, u32[]{:S(2)}) collective-permute-start(f32[8,512]{1,0:T(8,128)} %get-tuple-element.49), channel_id=1, source_target_pairs={{4,0},{8,4},{12,8},{16,12},{20,16},{24,20},{28,24},{5,1},{9,5},{13... | collective-permute-start | bytes 49160 | tf_op jit(solution)/shard_map/ppermute | solution.py:224
  8.4 4.4 %shard_map.78 = (s32[256,512]{1,0:T(8,128)}, s32[256,512]{1,0:T(8,128)}, s32[256,512]{1,0:T(8,128)}, s32[256,512]{1,0:T(8,128)}) custom-call(s32[1]{0:T(128)S(6)} %rem.22.me_ref, bf16[512,1024]{1,0:T(8,128)(2,1)} %amp_ref, s32[512,1024]{1,0:T(8,128)} %bin_ref), custom_call_target="tpu_custom_call" | custom-call | flops 524288 | bytes 5242880 | tf_op jit(solution)/shard_map/pallas_call | solution.py:52
  12.9 3.5 %collective-permute-start.5 = (s32[256,512]{1,0:T(8,128)}, s32[256,512]{1,0:T(8,128)S(1)}, u32[]{:S(2)}, u32[]{:S(2)}) collective-permute-start(s32[256,512]{1,0:T(8,128)} %get-tuple-element.65), channel_id=1, source_target_pairs={{0,8},{4,12},{8,0},{12,4},{16,24},{20,28},{24,16},{28,20},{1,9},{5... | collective-permute-start | bytes 1572872 | tf_op jit(solution)/shard_map/ppermute | solution.py:451
  16.5 0.6 collective-permute-start.4
  17.1 0.9 collective-permute-start.6
  18.3 1.3 %collective-permute-start.2 = (f32[8,384]{1,0:T(8,128)S(1)}, f32[8,384]{1,0:T(8,128)S(1)}, u32[]{:S(2)}, u32[]{:S(2)}) collective-permute-start(f32[8,384]{1,0:T(8,128)S(1)} %get-tuple-element.59), channel_id=1, source_target_pairs={{0,1},{1,2},{2,3},{4,5},{5,6},{6,7},{8,9},{9,10},{10,11},{12,13},{... | collective-permute-start | bytes 36872 | tf_op jit(solution)/shard_map/ppermute | solution.py:224
  19.6 1.3 %collective-permute-start.3 = (f32[8,384]{1,0:T(8,128)S(1)}, f32[8,384]{1,0:T(8,128)S(1)}, u32[]{:S(2)}, u32[]{:S(2)}) collective-permute-start(f32[8,384]{1,0:T(8,128)S(1)} %get-tuple-element.60), channel_id=1, source_target_pairs={{1,0},{2,1},{3,2},{5,4},{6,5},{7,6},{9,8},{10,9},{11,10},{13,12},{... | collective-permute-start | bytes 36872 | tf_op jit(solution)/shard_map/ppermute | solution.py:224
  20.9 3.5 %collective-permute-done.3.north_ref = f32[8,384]{1,0:T(8,128)S(1)} collective-permute-done((f32[8,384]{1,0:T(8,128)S(1)}, f32[8,384]{1,0:T(8,128)S(1)}, u32[]{:S(2)}, u32[]{:S(2)}) %collective-permute-start.3) | collective-permute-done | bytes 12320 | tf_op jit(solution)/shard_map/ppermute | solution.py:224
  24.4 4.9 %shard_map.80 = (f32[256,512]{1,0:T(8,128)}, f32[4,128]{1,0:T(4,128)S(1)}) custom-call(s32[4,128]{1,0:T(4,128)S(1)} %get-tuple-element.58.cell_ref, f32[256,512]{1,0:T(8,128)S(1)} %copy-done, s32[256,512]{1,0:T(8,128)S(1)} %copy-done.1, f32[256,512]{1,0:T(8,128)S(1)} %copy-done.2, f32[8,512]{1,0:T(8,128)S(1)} %collective-permute-done.before_ref, ...), custom_call_target="tpu_custom_call" | custom-call | flops 13107200 | bytes 104857600 | tf_op jit(solution)/shard_map/pallas_call | solution.py:245
  29.3 6.8 %all-gather.1.refs_4_ = f32[4,4,128]{2,1,0:T(4,128)S(1)} all-gather(f32[1,4,128]{2,1,0:T(4,128)S(1)} %bitcast.3), channel_id=2, replica_groups=mesh['box'=8,'panel'=4] {'panel'}, dimensions={0}, use_global_device_ids=true | all-gather | bytes 10240 | tf_op jit(solution)/shard_map/all_gather | solution.py:462
  36.0 2.0 %collective-permute-start.9 = (f32[4,4,128]{2,1,0:T(4,128)S(1)}, f32[4,4,128]{2,1,0:T(4,128)S(1)}, u32[]{:S(2)}, u32[]{:S(2)}) collective-permute-start(f32[4,4,128]{2,1,0:T(4,128)S(1)} %all-gather.1.refs_4_), channel_id=1, source_target_pairs={{0,12},{4,8},{8,4},{12,0},{16,28},{20,24},{24,20},{28,16},{1,13},{... | collective-permute-start | bytes 24584 | tf_op jit(solution)/shard_map/ppermute | solution.py:451
  38.5 1.0 %collective-permute-start.7 = (f32[4,4,128]{2,1,0:T(4,128)S(1)}, f32[4,4,128]{2,1,0:T(4,128)S(1)}, u32[]{:S(2)}, u32[]{:S(2)}) collective-permute-start(f32[4,4,128]{2,1,0:T(4,128)S(1)} %all-gather.1.refs_4_), channel_id=1, source_target_pairs={{0,4},{4,0},{8,12},{12,8},{16,20},{20,16},{24,28},{28,24},{1,5},{5... | collective-permute-start | bytes 24584 | tf_op jit(solution)/shard_map/ppermute | solution.py:451
  39.6 1.4 %collective-permute-done.4.refs_1_ = s32[256,512]{1,0:T(8,128)S(1)} collective-permute-done((s32[256,512]{1,0:T(8,128)}, s32[256,512]{1,0:T(8,128)S(1)}, u32[]{:S(2)}, u32[]{:S(2)}) %collective-permute-start.4) | collective-permute-done | bytes 524320 | tf_op jit(solution)/shard_map/ppermute | solution.py:451
  41.0 0.7 collective-permute-done.8.refs_6_
  42.2 13.4 %shard_map.81 = (f32[4,128,256]{2,1,0:T(8,128)S(1)}, bf16[4,128,256]{2,1,0:T(8,128)(2,1)S(1)}) custom-call(s32[1]{0:T(128)S(6)} %select_n.5.half_ref, s32[256,512]{1,0:T(8,128)S(1)} %copy-done.4, s32[256,512]{1,0:T(8,128)S(1)} %collective-permute-done.4.refs_1_, s32[256,512]{1,0:T(8,128)S(1)} %collective-permute-done.5.refs_2_, ...), custom_call_target="tpu_custom_call" | custom-call | flops 17179869184 | bytes 2097152 | tf_op jit(solution)/shard_map/pallas_call | solution.py:359
  55.6 2.6 %collective-permute-start.11 = (bf16[4,128,256]{2,1,0:T(8,128)(2,1)S(1)}, bf16[4,128,256]{2,1,0:T(8,128)(2,1)S(1)}, u32[]{:S(2)}, u32[]{:S(2)}) collective-permute-start(bf16[4,128,256]{2,1,0:T(8,128)(2,1)S(1)} %get-tuple-element.78), channel_id=1, source_target_pairs={{0,16},{4,20},{8,24},{12,28},{16,0},{20,4},{24,8},{28,12},{1,17},{... | collective-permute-start | bytes 786440 | tf_op jit(solution)/shard_map/ppermute | solution.py:474
  58.1 8.4 %shard_map.82 = (f32[4,80,256]{2,1,0:T(8,128)S(1)}, bf16[4,80,256]{2,1,0:T(8,128)(2,1)S(1)}) custom-call(s32[1]{0:T(128)S(6)} %select_n.5.half_ref, s32[256,512]{1,0:T(8,128)S(1)} %copy-done.4, s32[256,512]{1,0:T(8,128)S(1)} %collective-permute-done.4.refs_1_, s32[256,512]{1,0:T(8,128)S(1)} %collective-permute-done.5.refs_2_, ...), custom_call_target="tpu_custom_call" | custom-call | flops 10737418240 | bytes 1310720 | tf_op jit(solution)/shard_map/pallas_call | solution.py:359
  66.6 0.4 collective-permute-start.12
  67.0 9.2 %collective-permute-done.12.refs_3_ = bf16[4,80,256]{2,1,0:T(8,128)(2,1)S(1)} collective-permute-done((bf16[4,80,256]{2,1,0:T(8,128)(2,1)S(1)}, bf16[4,80,256]{2,1,0:T(8,128)(2,1)S(1)}, u32[]{:S(2)}, u32[]{:S(2)}) %collective-permute-start.12) | collective-permute-done | bytes 163872 | tf_op jit(solution)/shard_map/ppermute | solution.py:474
  76.4 0.6 collective-permute-start.13
  76.9 5.1 %shard_map.83 = (f32[4,48,256]{2,1,0:T(8,128)S(1)}, bf16[4,48,256]{2,1,0:T(8,128)(2,1)S(1)}) custom-call(s32[1]{0:T(128)S(6)} %select_n.5.half_ref, s32[256,512]{1,0:T(8,128)S(1)} %copy-done.4, s32[256,512]{1,0:T(8,128)S(1)} %collective-permute-done.4.refs_1_, s32[256,512]{1,0:T(8,128)S(1)} %collective-permute-done.5.refs_2_, ...), custom_call_target="tpu_custom_call" | custom-call | flops 6442450944 | bytes 786432 | tf_op jit(solution)/shard_map/pallas_call | solution.py:359
  82.0 3.4 %collective-permute-start.10 = (bf16[4,48,256]{2,1,0:T(8,128)(2,1)S(1)}, bf16[4,48,256]{2,1,0:T(8,128)(2,1)S(1)}, u32[]{:S(2)}, u32[]{:S(2)}) collective-permute-start(bf16[4,48,256]{2,1,0:T(8,128)(2,1)S(1)} %get-tuple-element.75), channel_id=1, source_target_pairs={{0,16},{4,20},{8,24},{12,28},{16,0},{20,4},{24,8},{28,12},{1,17},{... | collective-permute-start | bytes 294920 | tf_op jit(solution)/shard_map/ppermute | solution.py:474
  85.5 1.2 %collective-permute-start.17 = (bf16[208,256]{1,0:T(8,128)(2,1)S(1)}, bf16[208,256]{1,0:T(8,128)(2,1)S(1)}, u32[]{:S(2)}, u32[]{:S(2)}) collective-permute-start(bf16[208,256]{1,0:T(8,128)(2,1)S(1)} %get-tuple-element.87), channel_id=1, source_target_pairs={{0,4},{4,8},{8,12},{12,0},{16,20},{20,24},{24,28},{28,16},{1,5},{5... | collective-permute-start | bytes 319496 | tf_op jit(solution)/shard_map/ppermute | solution.py:451
  86.6 1.8 %collective-permute-start.18 = (bf16[208,256]{1,0:T(8,128)(2,1)S(1)}, bf16[208,256]{1,0:T(8,128)(2,1)S(1)}, u32[]{:S(2)}, u32[]{:S(2)}) collective-permute-start(bf16[208,256]{1,0:T(8,128)(2,1)S(1)} %get-tuple-element.89), channel_id=1, source_target_pairs={{0,12},{4,0},{8,4},{12,8},{16,28},{20,16},{24,20},{28,24},{1,13},{... | collective-permute-start | bytes 319496 | tf_op jit(solution)/shard_map/ppermute | solution.py:451
  88.4 1.8 %collective-permute-done.10.refs_1_ = bf16[4,48,256]{2,1,0:T(8,128)(2,1)S(1)} collective-permute-done((bf16[4,48,256]{2,1,0:T(8,128)(2,1)S(1)}, bf16[4,48,256]{2,1,0:T(8,128)(2,1)S(1)}, u32[]{:S(2)}, u32[]{:S(2)}) %collective-permute-start.10) | collective-permute-done | bytes 98336 | tf_op jit(solution)/shard_map/ppermute | solution.py:474
  90.2 1.2 %collective-permute-start.14 = (bf16[48,256]{1,0:T(8,128)(2,1)S(1)}, bf16[48,256]{1,0:T(8,128)(2,1)S(1)}, u32[]{:S(2)}, u32[]{:S(2)}) collective-permute-start(bf16[48,256]{1,0:T(8,128)(2,1)S(1)} %get-tuple-element.83), channel_id=1, source_target_pairs={{0,4},{4,8},{8,12},{12,0},{16,20},{20,24},{24,28},{28,16},{1,5},{5... | collective-permute-start | bytes 73736 | tf_op jit(solution)/shard_map/ppermute | solution.py:451
  91.4 1.8 %collective-permute-start.16 = (bf16[48,256]{1,0:T(8,128)(2,1)S(1)}, bf16[48,256]{1,0:T(8,128)(2,1)S(1)}, u32[]{:S(2)}, u32[]{:S(2)}) collective-permute-start(bf16[48,256]{1,0:T(8,128)(2,1)S(1)} %get-tuple-element.85), channel_id=1, source_target_pairs={{0,12},{4,0},{8,4},{12,8},{16,28},{20,16},{24,20},{28,24},{1,13},{... | collective-permute-start | bytes 73736 | tf_op jit(solution)/shard_map/ppermute | solution.py:451
  93.2 0.9 shard_map.86.refs_4_
  94.1 0.8 collective-permute-done.14.refs_1_
  95.5 0.7 shard_map.87
  (28 shorter events, 2.0 us)
Async XLA Ops:
  2.1 15.9 %copy-start = (f32[256,512]{1,0:T(8,128)S(1)}, f32[256,512]{1,0:T(8,128)}, u32[]{:S(2)}) copy-start(f32[256,512]{1,0:T(8,128)} %field_ref.3) | copy-start | bytes 1572868
  2.1 15.9 %copy-start.1 = (s32[256,512]{1,0:T(8,128)S(1)}, s32[256,512]{1,0:T(8,128)}, u32[]{:S(2)}) copy-start(s32[256,512]{1,0:T(8,128)} %mask_ref.3) | copy-start | bytes 1572868
  2.1 15.9 %copy-start.2 = (f32[256,512]{1,0:T(8,128)S(1)}, f32[256,512]{1,0:T(8,128)}, u32[]{:S(2)}) copy-start(f32[256,512]{1,0:T(8,128)} %visc_ref.3) | copy-start | bytes 1572868
  2.1 15.9 %copy-start.3 = (s32[128]{0:T(128)S(1)}, s32[128]{0:T(128)}, u32[]{:S(2)}) copy-start(s32[128]{0:T(128)} %param.9) | copy-start | bytes 1540
  2.1 10.7 %collective-permute-start = (f32[8,512]{1,0:T(8,128)}, f32[8,512]{1,0:T(8,128)S(1)}, u32[]{:S(2)}, u32[]{:S(2)}) collective-permute-start(f32[8,512]{1,0:T(8,128)} %get-tuple-element.48), channel_id=1, source_target_pairs={{0,4},{4,8},{8,12},{12,16},{16,20},{20,24},{24,28},{1,5},{5,9},{9,... | collective-permute-start | bytes 49160 | tf_op jit(solution)/shard_map/ppermute | solution.py:224
  7.1 5.8 %collective-permute-start.1 = (f32[8,512]{1,0:T(8,128)}, f32[8,512]{1,0:T(8,128)S(1)}, u32[]{:S(2)}, u32[]{:S(2)}) collective-permute-start(f32[8,512]{1,0:T(8,128)} %get-tuple-element.49), channel_id=1, source_target_pairs={{4,0},{8,4},{12,8},{16,12},{20,16},{24,20},{28,24},{5,1},{9,5},{13... | collective-permute-start | bytes 49160 | tf_op jit(solution)/shard_map/ppermute | solution.py:224
  12.8 29.4 %copy-start.4 = (s32[256,512]{1,0:T(8,128)S(1)}, s32[256,512]{1,0:T(8,128)}, u32[]{:S(2)}) copy-start(s32[256,512]{1,0:T(8,128)} %get-tuple-element.62.refs_0_) | copy-start | bytes 1572868
  12.9 23.1 %collective-permute-start.5 = (s32[256,512]{1,0:T(8,128)}, s32[256,512]{1,0:T(8,128)S(1)}, u32[]{:S(2)}, u32[]{:S(2)}) collective-permute-start(s32[256,512]{1,0:T(8,128)} %get-tuple-element.65), channel_id=1, source_target_pairs={{0,8},{4,12},{8,0},{12,4},{16,24},{20,28},{24,16},{28,20},{1,9},{5... | collective-permute-start | bytes 1572872 | tf_op jit(solution)/shard_map/ppermute | solution.py:451
  16.5 24.5 %collective-permute-start.4 = (s32[256,512]{1,0:T(8,128)}, s32[256,512]{1,0:T(8,128)S(1)}, u32[]{:S(2)}, u32[]{:S(2)}) collective-permute-start(s32[256,512]{1,0:T(8,128)} %get-tuple-element.63), channel_id=1, source_target_pairs={{0,4},{4,0},{8,12},{12,8},{16,20},{20,16},{24,28},{28,24},{1,5},{5... | collective-permute-start | bytes 1572872 | tf_op jit(solution)/shard_map/ppermute | solution.py:451
  17.1 23.9 %collective-permute-start.6 = (s32[256,512]{1,0:T(8,128)}, s32[256,512]{1,0:T(8,128)S(1)}, u32[]{:S(2)}, u32[]{:S(2)}) collective-permute-start(s32[256,512]{1,0:T(8,128)} %get-tuple-element.67), channel_id=1, source_target_pairs={{0,12},{4,8},{8,4},{12,0},{16,28},{20,24},{24,20},{28,16},{1,13},{... | collective-permute-start | bytes 1572872 | tf_op jit(solution)/shard_map/ppermute | solution.py:451
  18.3 2.6 %collective-permute-start.2 = (f32[8,384]{1,0:T(8,128)S(1)}, f32[8,384]{1,0:T(8,128)S(1)}, u32[]{:S(2)}, u32[]{:S(2)}) collective-permute-start(f32[8,384]{1,0:T(8,128)S(1)} %get-tuple-element.59), channel_id=1, source_target_pairs={{0,1},{1,2},{2,3},{4,5},{5,6},{6,7},{8,9},{9,10},{10,11},{12,13},{... | collective-permute-start | bytes 36872 | tf_op jit(solution)/shard_map/ppermute | solution.py:224
  19.6 4.8 %collective-permute-start.3 = (f32[8,384]{1,0:T(8,128)S(1)}, f32[8,384]{1,0:T(8,128)S(1)}, u32[]{:S(2)}, u32[]{:S(2)}) collective-permute-start(f32[8,384]{1,0:T(8,128)S(1)} %get-tuple-element.60), channel_id=1, source_target_pairs={{1,0},{2,1},{3,2},{5,4},{6,5},{7,6},{9,8},{10,9},{11,10},{13,12},{... | collective-permute-start | bytes 36872 | tf_op jit(solution)/shard_map/ppermute | solution.py:224
  36.0 5.0 %collective-permute-start.9 = (f32[4,4,128]{2,1,0:T(4,128)S(1)}, f32[4,4,128]{2,1,0:T(4,128)S(1)}, u32[]{:S(2)}, u32[]{:S(2)}) collective-permute-start(f32[4,4,128]{2,1,0:T(4,128)S(1)} %all-gather.1.refs_4_), channel_id=1, source_target_pairs={{0,12},{4,8},{8,4},{12,0},{16,28},{20,24},{24,20},{28,16},{1,13},{... | collective-permute-start | bytes 24584 | tf_op jit(solution)/shard_map/ppermute | solution.py:451
  38.1 3.7 %collective-permute-start.8 = (f32[4,4,128]{2,1,0:T(4,128)S(1)}, f32[4,4,128]{2,1,0:T(4,128)S(1)}, u32[]{:S(2)}, u32[]{:S(2)}) collective-permute-start(f32[4,4,128]{2,1,0:T(4,128)S(1)} %all-gather.1.refs_4_), channel_id=1, source_target_pairs={{0,8},{4,12},{8,0},{12,4},{16,24},{20,28},{24,16},{28,20},{1,9},{5... | collective-permute-start | bytes 24584 | tf_op jit(solution)/shard_map/ppermute | solution.py:451
  38.5 3.7 %collective-permute-start.7 = (f32[4,4,128]{2,1,0:T(4,128)S(1)}, f32[4,4,128]{2,1,0:T(4,128)S(1)}, u32[]{:S(2)}, u32[]{:S(2)}) collective-permute-start(f32[4,4,128]{2,1,0:T(4,128)S(1)} %all-gather.1.refs_4_), channel_id=1, source_target_pairs={{0,4},{4,0},{8,12},{12,8},{16,20},{20,16},{24,28},{28,24},{1,5},{5... | collective-permute-start | bytes 24584 | tf_op jit(solution)/shard_map/ppermute | solution.py:451
  55.6 20.7 %collective-permute-start.11 = (bf16[4,128,256]{2,1,0:T(8,128)(2,1)S(1)}, bf16[4,128,256]{2,1,0:T(8,128)(2,1)S(1)}, u32[]{:S(2)}, u32[]{:S(2)}) collective-permute-start(bf16[4,128,256]{2,1,0:T(8,128)(2,1)S(1)} %get-tuple-element.78), channel_id=1, source_target_pairs={{0,16},{4,20},{8,24},{12,28},{16,0},{20,4},{24,8},{28,12},{1,17},{... | collective-permute-start | bytes 786440 | tf_op jit(solution)/shard_map/ppermute | solution.py:474
  66.6 9.7 %collective-permute-start.12 = (bf16[4,80,256]{2,1,0:T(8,128)(2,1)S(1)}, bf16[4,80,256]{2,1,0:T(8,128)(2,1)S(1)}, u32[]{:S(2)}, u32[]{:S(2)}) collective-permute-start(bf16[4,80,256]{2,1,0:T(8,128)(2,1)S(1)} %get-tuple-element.79), channel_id=1, source_target_pairs={{0,16},{4,20},{8,24},{12,28},{16,0},{20,4},{24,8},{28,12},{1,17},{... | collective-permute-start | bytes 491528 | tf_op jit(solution)/shard_map/ppermute | solution.py:474
  76.4 13.8 %collective-permute-start.13 = (bf16[208,256]{1,0:T(8,128)(2,1)S(1)}, bf16[208,256]{1,0:T(8,128)(2,1)S(1)}, u32[]{:S(2)}, u32[]{:S(2)}) collective-permute-start(bf16[208,256]{1,0:T(8,128)(2,1)S(1)} %get-tuple-element.80), channel_id=1, source_target_pairs={{0,8},{4,12},{8,0},{12,4},{16,24},{20,28},{24,16},{28,20},{1,9},{5... | collective-permute-start | bytes 319496 | tf_op jit(solution)/shard_map/ppermute | solution.py:451
  82.0 8.1 %collective-permute-start.10 = (bf16[4,48,256]{2,1,0:T(8,128)(2,1)S(1)}, bf16[4,48,256]{2,1,0:T(8,128)(2,1)S(1)}, u32[]{:S(2)}, u32[]{:S(2)}) collective-permute-start(bf16[4,48,256]{2,1,0:T(8,128)(2,1)S(1)} %get-tuple-element.75), channel_id=1, source_target_pairs={{0,16},{4,20},{8,24},{12,28},{16,0},{20,4},{24,8},{28,12},{1,17},{... | collective-permute-start | bytes 294920 | tf_op jit(solution)/shard_map/ppermute | solution.py:474
  85.5 7.7 %collective-permute-start.17 = (bf16[208,256]{1,0:T(8,128)(2,1)S(1)}, bf16[208,256]{1,0:T(8,128)(2,1)S(1)}, u32[]{:S(2)}, u32[]{:S(2)}) collective-permute-start(bf16[208,256]{1,0:T(8,128)(2,1)S(1)} %get-tuple-element.87), channel_id=1, source_target_pairs={{0,4},{4,8},{8,12},{12,0},{16,20},{20,24},{24,28},{28,16},{1,5},{5... | collective-permute-start | bytes 319496 | tf_op jit(solution)/shard_map/ppermute | solution.py:451
  86.6 6.5 %collective-permute-start.18 = (bf16[208,256]{1,0:T(8,128)(2,1)S(1)}, bf16[208,256]{1,0:T(8,128)(2,1)S(1)}, u32[]{:S(2)}, u32[]{:S(2)}) collective-permute-start(bf16[208,256]{1,0:T(8,128)(2,1)S(1)} %get-tuple-element.89), channel_id=1, source_target_pairs={{0,12},{4,0},{8,4},{12,8},{16,28},{20,16},{24,20},{28,24},{1,13},{... | collective-permute-start | bytes 319496 | tf_op jit(solution)/shard_map/ppermute | solution.py:451
  90.2 4.8 %collective-permute-start.14 = (bf16[48,256]{1,0:T(8,128)(2,1)S(1)}, bf16[48,256]{1,0:T(8,128)(2,1)S(1)}, u32[]{:S(2)}, u32[]{:S(2)}) collective-permute-start(bf16[48,256]{1,0:T(8,128)(2,1)S(1)} %get-tuple-element.83), channel_id=1, source_target_pairs={{0,4},{4,8},{8,12},{12,0},{16,20},{20,24},{24,28},{28,16},{1,5},{5... | collective-permute-start | bytes 73736 | tf_op jit(solution)/shard_map/ppermute | solution.py:451
  91.4 3.9 %collective-permute-start.15 = (bf16[48,256]{1,0:T(8,128)(2,1)S(1)}, bf16[48,256]{1,0:T(8,128)(2,1)S(1)}, u32[]{:S(2)}, u32[]{:S(2)}) collective-permute-start(bf16[48,256]{1,0:T(8,128)(2,1)S(1)} %get-tuple-element.84), channel_id=1, source_target_pairs={{0,8},{4,12},{8,0},{12,4},{16,24},{20,28},{24,16},{28,20},{1,9},{5... | collective-permute-start | bytes 73736 | tf_op jit(solution)/shard_map/ppermute | solution.py:451
  91.4 4.2 %collective-permute-start.16 = (bf16[48,256]{1,0:T(8,128)(2,1)S(1)}, bf16[48,256]{1,0:T(8,128)(2,1)S(1)}, u32[]{:S(2)}, u32[]{:S(2)}) collective-permute-start(bf16[48,256]{1,0:T(8,128)(2,1)S(1)} %get-tuple-element.85), channel_id=1, source_target_pairs={{0,12},{4,0},{8,4},{12,8},{16,28},{20,16},{24,20},{28,24},{1,13},{... | collective-permute-start | bytes 73736 | tf_op jit(solution)/shard_map/ppermute | solution.py:451

commit v12 on v11

--- a/solution.py
+++ b/solution.py
@@ -491,7 +491,7 @@
     units = observers // 16
     ends = [-(-units * part // 16) * 16 for part in PARTS]
     counts = [end - start for start, end in zip([0] + ends, ends)]
-    return [[c for c in group if c] for group in (counts[:2], counts[2:]) if any(group)]
+    return [[c for c in counts if c]]
 
 
 def solution(mesh):

time: 96.6 us -> 90.9 us (0.941)
  starting transfers between devices: 30.5 us -> 26.6 us
  waiting for transfers between devices: 18.7 us -> 17.3 us
    ppermute x3, waiting for transfers between devices: 11 us -> 5.77 us  [on_device(): groups[-1].append((keep, lax.ppermute(send, 'box', across)))]
    ppermute x12 -> x9, waiting for transfers between devices: 4.02 us -> 7.88 us  [spread(): lax.ppermute(x, 'box', perm(k))]
    ppermute x12 -> x9, starting transfers between devices: 15.1 us -> 12.1 us  [spread(): lax.ppermute(x, 'box', perm(k))]
  transfers between devices with their start and end apart: 19 -> 16, of which waited for: 10 -> 8; matrix products, arithmetic and copies ran while one was open for 0% -> 0% of each run, Pallas kernels for 25% -> 25%
where the time goes in v12:
time: 90.9 us; the launch traced here: 90.5 us
  Pallas kernels  39 us (43%)
  starting transfers between devices  26.6 us (29%)
  waiting for transfers between devices  17.3 us (19%)
  blocking collectives  6.75 us (7%)
    pallas_call x3, Pallas kernels, binned(): pl.pallas_call(bin_kernel, grid=(count // block,), in_specs=[SMEM] + [pl....  27 us
    ppermute x9, starting transfers between devices, spread(): lax.ppermute(x, 'box', perm(k))  12.1 us
    ppermute x4, starting transfers between devices, shifted(): return (lax.ppermute(last, axis, up), lax.ppermute(first, axis, down))  8.88 us
    ppermute x9, waiting for transfers between devices, spread(): lax.ppermute(x, 'box', perm(k))  7.88 us
    all_gather x1, blocking collectives, on_device(): sample = lax.all_gather(sample, 'panel')  6.75 us
    ppermute x3, waiting for transfers between devices, on_device(): groups[-1].append((keep, lax.ppermute(send, 'box', across)))  5.77 us
    ppermute x3, starting transfers between devices, on_device(): groups[-1].append((keep, lax.ppermute(send, 'box', across)))  5.65 us
    pallas_call x1, Pallas kernels, field_window(): pl.pallas_call(step_kernel, in_specs=[SMEM] + [VMEM] * 7, out_specs=[pl.B...  4.9 us
  transfers between devices with their start and end apart: 16, of which 8 were waited for; matrix products, arithmetic and copies ran while one was open for 0% of the time, Pallas kernels for 25%

profile of v12, /device:TPU:0, one launch (start us, length us, event | category | flops | bytes accessed | tf_op | source)
XLA Modules:
  0.0 90.5 jit_solution(5207023663374775245)
XLA Ops:
  0.6 1.4 %shard_map.77 = (f32[8,512]{1,0:T(8,128)}, f32[8,512]{1,0:T(8,128)}) custom-call(f32[256,512]{1,0:T(8,128)} %field_ref.3, s32[256,512]{1,0:T(8,128)} %mask_ref.3, f32[256,512]{1,0:T(8,128)} %visc_ref.3, f32[256,512]{1,0:T(8,128)} %field_ref.3, s32[256,512]{1,0:T(8,128)} %mask_ref.3, f32[256,512]{1,0:T(8,128)} %visc_ref.3), custom_call_target="tpu_custom_call" | custom-call | flops 8192 | bytes 131072 | tf_op jit(solution)/shard_map/pallas_call | solution.py:208
  2.1 5.0 %collective-permute-start = (f32[8,512]{1,0:T(8,128)}, f32[8,512]{1,0:T(8,128)S(1)}, u32[]{:S(2)}, u32[]{:S(2)}) collective-permute-start(f32[8,512]{1,0:T(8,128)} %get-tuple-element.42), channel_id=1, source_target_pairs={{0,4},{4,8},{8,12},{12,16},{16,20},{20,24},{24,28},{1,5},{5,9},{9,... | collective-permute-start | bytes 49160 | tf_op jit(solution)/shard_map/ppermute | solution.py:224
  7.1 1.3 %collective-permute-start.1 = (f32[8,512]{1,0:T(8,128)}, f32[8,512]{1,0:T(8,128)S(1)}, u32[]{:S(2)}, u32[]{:S(2)}) collective-permute-start(f32[8,512]{1,0:T(8,128)} %get-tuple-element.43), channel_id=1, source_target_pairs={{4,0},{8,4},{12,8},{16,12},{20,16},{24,20},{28,24},{5,1},{9,5},{13... | collective-permute-start | bytes 49160 | tf_op jit(solution)/shard_map/ppermute | solution.py:224
  8.4 4.3 %shard_map.78 = (s32[256,512]{1,0:T(8,128)}, s32[256,512]{1,0:T(8,128)}, s32[256,512]{1,0:T(8,128)}, s32[256,512]{1,0:T(8,128)}) custom-call(s32[1]{0:T(128)S(6)} %rem.22.me_ref, bf16[512,1024]{1,0:T(8,128)(2,1)} %amp_ref, s32[512,1024]{1,0:T(8,128)} %bin_ref), custom_call_target="tpu_custom_call" | custom-call | flops 524288 | bytes 5242880 | tf_op jit(solution)/shard_map/pallas_call | solution.py:52
  12.9 3.5 %collective-permute-start.5 = (s32[256,512]{1,0:T(8,128)}, s32[256,512]{1,0:T(8,128)S(1)}, u32[]{:S(2)}, u32[]{:S(2)}) collective-permute-start(s32[256,512]{1,0:T(8,128)} %get-tuple-element.59), channel_id=1, source_target_pairs={{0,8},{4,12},{8,0},{12,4},{16,24},{20,28},{24,16},{28,20},{1,9},{5... | collective-permute-start | bytes 1572872 | tf_op jit(solution)/shard_map/ppermute | solution.py:451
  16.4 0.6 collective-permute-start.4
  17.1 0.9 %collective-permute-start.6 = (s32[256,512]{1,0:T(8,128)}, s32[256,512]{1,0:T(8,128)S(1)}, u32[]{:S(2)}, u32[]{:S(2)}) collective-permute-start(s32[256,512]{1,0:T(8,128)} %get-tuple-element.61), channel_id=1, source_target_pairs={{0,12},{4,8},{8,4},{12,0},{16,28},{20,24},{24,20},{28,16},{1,13},{... | collective-permute-start | bytes 1572872 | tf_op jit(solution)/shard_map/ppermute | solution.py:451
  18.0 0.3 shard_map.79
  18.3 1.3 %collective-permute-start.2 = (f32[8,384]{1,0:T(8,128)S(1)}, f32[8,384]{1,0:T(8,128)S(1)}, u32[]{:S(2)}, u32[]{:S(2)}) collective-permute-start(f32[8,384]{1,0:T(8,128)S(1)} %get-tuple-element.53), channel_id=1, source_target_pairs={{0,1},{1,2},{2,3},{4,5},{5,6},{6,7},{8,9},{9,10},{10,11},{12,13},{... | collective-permute-start | bytes 36872 | tf_op jit(solution)/shard_map/ppermute | solution.py:224
  19.6 1.3 %collective-permute-start.3 = (f32[8,384]{1,0:T(8,128)S(1)}, f32[8,384]{1,0:T(8,128)S(1)}, u32[]{:S(2)}, u32[]{:S(2)}) collective-permute-start(f32[8,384]{1,0:T(8,128)S(1)} %get-tuple-element.54), channel_id=1, source_target_pairs={{1,0},{2,1},{3,2},{5,4},{6,5},{7,6},{9,8},{10,9},{11,10},{13,12},{... | collective-permute-start | bytes 36872 | tf_op jit(solution)/shard_map/ppermute | solution.py:224
  20.9 3.5 %collective-permute-done.3.north_ref = f32[8,384]{1,0:T(8,128)S(1)} collective-permute-done((f32[8,384]{1,0:T(8,128)S(1)}, f32[8,384]{1,0:T(8,128)S(1)}, u32[]{:S(2)}, u32[]{:S(2)}) %collective-permute-start.3) | collective-permute-done | bytes 12320 | tf_op jit(solution)/shard_map/ppermute | solution.py:224
  24.4 4.9 %shard_map.80 = (f32[256,512]{1,0:T(8,128)}, f32[4,128]{1,0:T(4,128)S(1)}) custom-call(s32[4,128]{1,0:T(4,128)S(1)} %get-tuple-element.52.cell_ref, f32[256,512]{1,0:T(8,128)S(1)} %copy-done, s32[256,512]{1,0:T(8,128)S(1)} %copy-done.1, f32[256,512]{1,0:T(8,128)S(1)} %copy-done.2, f32[8,512]{1,0:T(8,128)S(1)} %collective-permute-done.before_ref, ...), custom_call_target="tpu_custom_call" | custom-call | flops 13107200 | bytes 104857600 | tf_op jit(solution)/shard_map/pallas_call | solution.py:245
  29.3 6.8 %all-gather.1.refs_4_ = f32[4,4,128]{2,1,0:T(4,128)S(1)} all-gather(f32[1,4,128]{2,1,0:T(4,128)S(1)} %bitcast.3), channel_id=2, replica_groups=mesh['box'=8,'panel'=4] {'panel'}, dimensions={0}, use_global_device_ids=true | all-gather | bytes 10240 | tf_op jit(solution)/shard_map/all_gather | solution.py:462
  36.0 2.0 %collective-permute-start.9 = (f32[4,4,128]{2,1,0:T(4,128)S(1)}, f32[4,4,128]{2,1,0:T(4,128)S(1)}, u32[]{:S(2)}, u32[]{:S(2)}) collective-permute-start(f32[4,4,128]{2,1,0:T(4,128)S(1)} %all-gather.1.refs_4_), channel_id=1, source_target_pairs={{0,12},{4,8},{8,4},{12,0},{16,28},{20,24},{24,20},{28,16},{1,13},{... | collective-permute-start | bytes 24584 | tf_op jit(solution)/shard_map/ppermute | solution.py:451
  38.1 0.4 collective-permute-start.8
  38.5 1.0 %collective-permute-start.7 = (f32[4,4,128]{2,1,0:T(4,128)S(1)}, f32[4,4,128]{2,1,0:T(4,128)S(1)}, u32[]{:S(2)}, u32[]{:S(2)}) collective-permute-start(f32[4,4,128]{2,1,0:T(4,128)S(1)} %all-gather.1.refs_4_), channel_id=1, source_target_pairs={{0,4},{4,0},{8,12},{12,8},{16,20},{20,16},{24,28},{28,24},{1,5},{5... | collective-permute-start | bytes 24584 | tf_op jit(solution)/shard_map/ppermute | solution.py:451
  39.6 1.4 %collective-permute-done.4.refs_1_ = s32[256,512]{1,0:T(8,128)S(1)} collective-permute-done((s32[256,512]{1,0:T(8,128)}, s32[256,512]{1,0:T(8,128)S(1)}, u32[]{:S(2)}, u32[]{:S(2)}) %collective-permute-start.4) | collective-permute-done | bytes 524320 | tf_op jit(solution)/shard_map/ppermute | solution.py:451
  41.0 0.7 collective-permute-done.8.refs_6_
  41.7 0.4 collective-permute-done.7.refs_5_
  42.2 13.5 %shard_map.81 = (f32[4,128,256]{2,1,0:T(8,128)S(1)}, bf16[4,128,256]{2,1,0:T(8,128)(2,1)S(1)}) custom-call(s32[1]{0:T(128)S(6)} %select_n.5.half_ref, s32[256,512]{1,0:T(8,128)S(1)} %copy-done.4, s32[256,512]{1,0:T(8,128)S(1)} %collective-permute-done.4.refs_1_, s32[256,512]{1,0:T(8,128)S(1)} %collective-permute-done.5.refs_2_, ...), custom_call_target="tpu_custom_call" | custom-call | flops 17179869184 | bytes 2097152 | tf_op jit(solution)/shard_map/pallas_call | solution.py:359
  55.7 2.6 %collective-permute-start.10 = (bf16[4,128,256]{2,1,0:T(8,128)(2,1)S(1)}, bf16[4,128,256]{2,1,0:T(8,128)(2,1)S(1)}, u32[]{:S(2)}, u32[]{:S(2)}) collective-permute-start(bf16[4,128,256]{2,1,0:T(8,128)(2,1)S(1)} %get-tuple-element.71), channel_id=1, source_target_pairs={{0,16},{4,20},{8,24},{12,28},{16,0},{20,4},{24,8},{28,12},{1,17},{... | collective-permute-start | bytes 786440 | tf_op jit(solution)/shard_map/ppermute | solution.py:474
  58.3 8.4 %shard_map.82 = (f32[4,80,256]{2,1,0:T(8,128)S(1)}, bf16[4,80,256]{2,1,0:T(8,128)(2,1)S(1)}) custom-call(s32[1]{0:T(128)S(6)} %select_n.5.half_ref, s32[256,512]{1,0:T(8,128)S(1)} %copy-done.4, s32[256,512]{1,0:T(8,128)S(1)} %collective-permute-done.4.refs_1_, s32[256,512]{1,0:T(8,128)S(1)} %collective-permute-done.5.refs_2_, ...), custom_call_target="tpu_custom_call" | custom-call | flops 10737418240 | bytes 1310720 | tf_op jit(solution)/shard_map/pallas_call | solution.py:359
  66.7 0.5 collective-permute-start.11
  67.2 5.1 %shard_map.83 = (f32[4,48,256]{2,1,0:T(8,128)S(1)}, bf16[4,48,256]{2,1,0:T(8,128)(2,1)S(1)}) custom-call(s32[1]{0:T(128)S(6)} %select_n.5.half_ref, s32[256,512]{1,0:T(8,128)S(1)} %copy-done.4, s32[256,512]{1,0:T(8,128)S(1)} %collective-permute-done.4.refs_1_, s32[256,512]{1,0:T(8,128)S(1)} %collective-permute-done.5.refs_2_, ...), custom_call_target="tpu_custom_call" | custom-call | flops 6442450944 | bytes 786432 | tf_op jit(solution)/shard_map/pallas_call | solution.py:359
  72.2 2.6 %collective-permute-start.12 = (bf16[4,48,256]{2,1,0:T(8,128)(2,1)S(1)}, bf16[4,48,256]{2,1,0:T(8,128)(2,1)S(1)}, u32[]{:S(2)}, u32[]{:S(2)}) collective-permute-start(bf16[4,48,256]{2,1,0:T(8,128)(2,1)S(1)} %get-tuple-element.73), channel_id=1, source_target_pairs={{0,16},{4,20},{8,24},{12,28},{16,0},{20,4},{24,8},{28,12},{1,17},{... | collective-permute-start | bytes 294920 | tf_op jit(solution)/shard_map/ppermute | solution.py:474
  74.8 5.8 %collective-permute-done.12.refs_5_ = bf16[4,48,256]{2,1,0:T(8,128)(2,1)S(1)} collective-permute-done((bf16[4,48,256]{2,1,0:T(8,128)(2,1)S(1)}, bf16[4,48,256]{2,1,0:T(8,128)(2,1)S(1)}, u32[]{:S(2)}, u32[]{:S(2)}) %collective-permute-start.12) | collective-permute-done | bytes 98336 | tf_op jit(solution)/shard_map/ppermute | solution.py:474
  80.7 0.9 collective-permute-start.13
  81.6 0.7 collective-permute-start.14
  82.3 1.9 %collective-permute-start.15 = (bf16[256,256]{1,0:T(8,128)(2,1)S(1)}, bf16[256,256]{1,0:T(8,128)(2,1)S(1)}, u32[]{:S(2)}, u32[]{:S(2)}) collective-permute-start(bf16[256,256]{1,0:T(8,128)(2,1)S(1)} %get-tuple-element.77), channel_id=1, source_target_pairs={{0,12},{4,0},{8,4},{12,8},{16,28},{20,16},{24,20},{28,24},{1,13},{... | collective-permute-start | bytes 393224 | tf_op jit(solution)/shard_map/ppermute | solution.py:451
  84.2 3.9 %collective-permute-done.13.refs_1_ = bf16[256,256]{1,0:T(8,128)(2,1)S(1)} collective-permute-done((bf16[256,256]{1,0:T(8,128)(2,1)S(1)}, bf16[256,256]{1,0:T(8,128)(2,1)S(1)}, u32[]{:S(2)}, u32[]{:S(2)}) %collective-permute-start.13) | collective-permute-done | bytes 131104 | tf_op jit(solution)/shard_map/ppermute | solution.py:451
  88.1 1.4 %collective-permute-done.15.refs_3_ = bf16[256,256]{1,0:T(8,128)(2,1)S(1)} collective-permute-done((bf16[256,256]{1,0:T(8,128)(2,1)S(1)}, bf16[256,256]{1,0:T(8,128)(2,1)S(1)}, u32[]{:S(2)}, u32[]{:S(2)}) %collective-permute-start.15) | collective-permute-done | bytes 131104 | tf_op jit(solution)/shard_map/ppermute | solution.py:451
  89.5 1.0 %shard_map.85 = f32[1024,256]{1,0:T(8,128)} custom-call(s32[1]{0:T(128)S(6)} %rem.22.me_ref, bf16[256,256]{1,0:T(8,128)(2,1)S(1)} %get-tuple-element.74.refs_0_, bf16[256,256]{1,0:T(8,128)(2,1)S(1)} %collective-permute-done.13.refs_1_, bf16[256,256]{1,0:T(8,128)(2,1)S(1)} %collective-permute-done.14.refs_2_, bf16[256,256]{1,0:T(8,128)(2,1)S(1)} %collective-permute-done.15.refs_3_), custom_call_target="tpu_custom_call" | custom-call | flops 262144 | bytes 1572864 | tf_op jit(solution)/shard_map/pallas_call | solution.py:426
  (20 shorter events, 0.3 us)
Async XLA Ops:
  2.1 15.9 %copy-start = (f32[256,512]{1,0:T(8,128)S(1)}, f32[256,512]{1,0:T(8,128)}, u32[]{:S(2)}) copy-start(f32[256,512]{1,0:T(8,128)} %field_ref.3) | copy-start | bytes 1572868
  2.1 15.9 %copy-start.1 = (s32[256,512]{1,0:T(8,128)S(1)}, s32[256,512]{1,0:T(8,128)}, u32[]{:S(2)}) copy-start(s32[256,512]{1,0:T(8,128)} %mask_ref.3) | copy-start | bytes 1572868
  2.1 15.9 %copy-start.2 = (f32[256,512]{1,0:T(8,128)S(1)}, f32[256,512]{1,0:T(8,128)}, u32[]{:S(2)}) copy-start(f32[256,512]{1,0:T(8,128)} %visc_ref.3) | copy-start | bytes 1572868
  2.1 15.9 %copy-start.3 = (s32[128]{0:T(128)S(1)}, s32[128]{0:T(128)}, u32[]{:S(2)}) copy-start(s32[128]{0:T(128)} %param.9) | copy-start | bytes 1540
  2.1 10.7 %collective-permute-start = (f32[8,512]{1,0:T(8,128)}, f32[8,512]{1,0:T(8,128)S(1)}, u32[]{:S(2)}, u32[]{:S(2)}) collective-permute-start(f32[8,512]{1,0:T(8,128)} %get-tuple-element.42), channel_id=1, source_target_pairs={{0,4},{4,8},{8,12},{12,16},{16,20},{20,24},{24,28},{1,5},{5,9},{9,... | collective-permute-start | bytes 49160 | tf_op jit(solution)/shard_map/ppermute | solution.py:224
  7.1 5.8 %collective-permute-start.1 = (f32[8,512]{1,0:T(8,128)}, f32[8,512]{1,0:T(8,128)S(1)}, u32[]{:S(2)}, u32[]{:S(2)}) collective-permute-start(f32[8,512]{1,0:T(8,128)} %get-tuple-element.43), channel_id=1, source_target_pairs={{4,0},{8,4},{12,8},{16,12},{20,16},{24,20},{28,24},{5,1},{9,5},{13... | collective-permute-start | bytes 49160 | tf_op jit(solution)/shard_map/ppermute | solution.py:224
  12.7 29.4 %copy-start.4 = (s32[256,512]{1,0:T(8,128)S(1)}, s32[256,512]{1,0:T(8,128)}, u32[]{:S(2)}) copy-start(s32[256,512]{1,0:T(8,128)} %get-tuple-element.56.refs_0_) | copy-start | bytes 1572868
  12.9 23.1 %collective-permute-start.5 = (s32[256,512]{1,0:T(8,128)}, s32[256,512]{1,0:T(8,128)S(1)}, u32[]{:S(2)}, u32[]{:S(2)}) collective-permute-start(s32[256,512]{1,0:T(8,128)} %get-tuple-element.59), channel_id=1, source_target_pairs={{0,8},{4,12},{8,0},{12,4},{16,24},{20,28},{24,16},{28,20},{1,9},{5... | collective-permute-start | bytes 1572872 | tf_op jit(solution)/shard_map/ppermute | solution.py:451
  16.4 24.5 %collective-permute-start.4 = (s32[256,512]{1,0:T(8,128)}, s32[256,512]{1,0:T(8,128)S(1)}, u32[]{:S(2)}, u32[]{:S(2)}) collective-permute-start(s32[256,512]{1,0:T(8,128)} %get-tuple-element.57), channel_id=1, source_target_pairs={{0,4},{4,0},{8,12},{12,8},{16,20},{20,16},{24,28},{28,24},{1,5},{5... | collective-permute-start | bytes 1572872 | tf_op jit(solution)/shard_map/ppermute | solution.py:451
  17.1 23.9 %collective-permute-start.6 = (s32[256,512]{1,0:T(8,128)}, s32[256,512]{1,0:T(8,128)S(1)}, u32[]{:S(2)}, u32[]{:S(2)}) collective-permute-start(s32[256,512]{1,0:T(8,128)} %get-tuple-element.61), channel_id=1, source_target_pairs={{0,12},{4,8},{8,4},{12,0},{16,28},{20,24},{24,20},{28,16},{1,13},{... | collective-permute-start | bytes 1572872 | tf_op jit(solution)/shard_map/ppermute | solution.py:451
  18.3 2.6 %collective-permute-start.2 = (f32[8,384]{1,0:T(8,128)S(1)}, f32[8,384]{1,0:T(8,128)S(1)}, u32[]{:S(2)}, u32[]{:S(2)}) collective-permute-start(f32[8,384]{1,0:T(8,128)S(1)} %get-tuple-element.53), channel_id=1, source_target_pairs={{0,1},{1,2},{2,3},{4,5},{5,6},{6,7},{8,9},{9,10},{10,11},{12,13},{... | collective-permute-start | bytes 36872 | tf_op jit(solution)/shard_map/ppermute | solution.py:224
  19.6 4.8 %collective-permute-start.3 = (f32[8,384]{1,0:T(8,128)S(1)}, f32[8,384]{1,0:T(8,128)S(1)}, u32[]{:S(2)}, u32[]{:S(2)}) collective-permute-start(f32[8,384]{1,0:T(8,128)S(1)} %get-tuple-element.54), channel_id=1, source_target_pairs={{1,0},{2,1},{3,2},{5,4},{6,5},{7,6},{9,8},{10,9},{11,10},{13,12},{... | collective-permute-start | bytes 36872 | tf_op jit(solution)/shard_map/ppermute | solution.py:224
  36.0 5.0 %collective-permute-start.9 = (f32[4,4,128]{2,1,0:T(4,128)S(1)}, f32[4,4,128]{2,1,0:T(4,128)S(1)}, u32[]{:S(2)}, u32[]{:S(2)}) collective-permute-start(f32[4,4,128]{2,1,0:T(4,128)S(1)} %all-gather.1.refs_4_), channel_id=1, source_target_pairs={{0,12},{4,8},{8,4},{12,0},{16,28},{20,24},{24,20},{28,16},{1,13},{... | collective-permute-start | bytes 24584 | tf_op jit(solution)/shard_map/ppermute | solution.py:451
  38.1 3.7 %collective-permute-start.8 = (f32[4,4,128]{2,1,0:T(4,128)S(1)}, f32[4,4,128]{2,1,0:T(4,128)S(1)}, u32[]{:S(2)}, u32[]{:S(2)}) collective-permute-start(f32[4,4,128]{2,1,0:T(4,128)S(1)} %all-gather.1.refs_4_), channel_id=1, source_target_pairs={{0,8},{4,12},{8,0},{12,4},{16,24},{20,28},{24,16},{28,20},{1,9},{5... | collective-permute-start | bytes 24584 | tf_op jit(solution)/shard_map/ppermute | solution.py:451
  38.5 3.7 %collective-permute-start.7 = (f32[4,4,128]{2,1,0:T(4,128)S(1)}, f32[4,4,128]{2,1,0:T(4,128)S(1)}, u32[]{:S(2)}, u32[]{:S(2)}) collective-permute-start(f32[4,4,128]{2,1,0:T(4,128)S(1)} %all-gather.1.refs_4_), channel_id=1, source_target_pairs={{0,4},{4,0},{8,12},{12,8},{16,20},{20,16},{24,28},{28,24},{1,5},{5... | collective-permute-start | bytes 24584 | tf_op jit(solution)/shard_map/ppermute | solution.py:451
  55.7 24.9 %collective-permute-start.10 = (bf16[4,128,256]{2,1,0:T(8,128)(2,1)S(1)}, bf16[4,128,256]{2,1,0:T(8,128)(2,1)S(1)}, u32[]{:S(2)}, u32[]{:S(2)}) collective-permute-start(bf16[4,128,256]{2,1,0:T(8,128)(2,1)S(1)} %get-tuple-element.71), channel_id=1, source_target_pairs={{0,16},{4,20},{8,24},{12,28},{16,0},{20,4},{24,8},{28,12},{1,17},{... | collective-permute-start | bytes 786440 | tf_op jit(solution)/shard_map/ppermute | solution.py:474
  66.7 13.9 %collective-permute-start.11 = (bf16[4,80,256]{2,1,0:T(8,128)(2,1)S(1)}, bf16[4,80,256]{2,1,0:T(8,128)(2,1)S(1)}, u32[]{:S(2)}, u32[]{:S(2)}) collective-permute-start(bf16[4,80,256]{2,1,0:T(8,128)(2,1)S(1)} %get-tuple-element.72), channel_id=1, source_target_pairs={{0,16},{4,20},{8,24},{12,28},{16,0},{20,4},{24,8},{28,12},{1,17},{... | collective-permute-start | bytes 491528 | tf_op jit(solution)/shard_map/ppermute | solution.py:474
  72.2 8.4 %collective-permute-start.12 = (bf16[4,48,256]{2,1,0:T(8,128)(2,1)S(1)}, bf16[4,48,256]{2,1,0:T(8,128)(2,1)S(1)}, u32[]{:S(2)}, u32[]{:S(2)}) collective-permute-start(bf16[4,48,256]{2,1,0:T(8,128)(2,1)S(1)} %get-tuple-element.73), channel_id=1, source_target_pairs={{0,16},{4,20},{8,24},{12,28},{16,0},{20,4},{24,8},{28,12},{1,17},{... | collective-permute-start | bytes 294920 | tf_op jit(solution)/shard_map/ppermute | solution.py:474
  80.7 7.4 %collective-permute-start.13 = (bf16[256,256]{1,0:T(8,128)(2,1)S(1)}, bf16[256,256]{1,0:T(8,128)(2,1)S(1)}, u32[]{:S(2)}, u32[]{:S(2)}) collective-permute-start(bf16[256,256]{1,0:T(8,128)(2,1)S(1)} %get-tuple-element.75), channel_id=1, source_target_pairs={{0,4},{4,8},{8,12},{12,0},{16,20},{20,24},{24,28},{28,16},{1,5},{5... | collective-permute-start | bytes 393224 | tf_op jit(solution)/shard_map/ppermute | solution.py:451
  81.6 6.5 %collective-permute-start.14 = (bf16[256,256]{1,0:T(8,128)(2,1)S(1)}, bf16[256,256]{1,0:T(8,128)(2,1)S(1)}, u32[]{:S(2)}, u32[]{:S(2)}) collective-permute-start(bf16[256,256]{1,0:T(8,128)(2,1)S(1)} %get-tuple-element.76), channel_id=1, source_target_pairs={{0,8},{4,12},{8,0},{12,4},{16,24},{20,28},{24,16},{28,20},{1,9},{5... | collective-permute-start | bytes 393224 | tf_op jit(solution)/shard_map/ppermute | solution.py:451
  82.3 7.2 %collective-permute-start.15 = (bf16[256,256]{1,0:T(8,128)(2,1)S(1)}, bf16[256,256]{1,0:T(8,128)(2,1)S(1)}, u32[]{:S(2)}, u32[]{:S(2)}) collective-permute-start(bf16[256,256]{1,0:T(8,128)(2,1)S(1)} %get-tuple-element.77), channel_id=1, source_target_pairs={{0,12},{4,0},{8,4},{12,8},{16,28},{20,16},{24,20},{28,24},{1,13},{... | collective-permute-start | bytes 393224 | tf_op jit(solution)/shard_map/ppermute | solution.py:451
